TPU v7x, 32 devices: a whole 2x2x4 slice. The times are simulated.
32 devices in a mesh: pb: 4 (over y, core), pa: 8 (over z, x).
Axes of the slice: x: 2, y: 2, z: 4, core: 2. Of those that a mesh axis runs over, the one named last changes fastest.
Arguments:
- enc_in: bfloat16 [32768, 768], P(('pb', 'pa')), may hold values from -6 to 6
- dec_in: bfloat16 [192, 768], P('pb'), may hold values from -6 to 6
- question_of: int32 [64], P(('pb', 'pa')), may hold values from 0 to 1, as said below
- lengths: int32 [64], P(('pb', 'pa')), may hold values from 64 to 512, as said below
- enc_gain_attn: bfloat16 [768], replicated, may hold values from 0.5 to 1.5
- enc_query: bfloat16 [768, 768], replicated, may hold values from -0.21875 to 0.21875
- enc_key: bfloat16 [768, 768], replicated, may hold values from -0.21875 to 0.21875
- enc_value: bfloat16 [768, 768], replicated, may hold values from -0.21875 to 0.21875
- enc_output: bfloat16 [768, 768], replicated, may hold values from -3.5 to 3.5
- enc_bias: bfloat16 [32, 12], replicated, may hold values from -4 to 4
- enc_gain_ffn: bfloat16 [768], replicated, may hold values from 0.5 to 1.5
- enc_ff_in: bfloat16 [768, 3072], replicated, may hold values from -0.21875 to 0.21875
- enc_ff_out: bfloat16 [3072, 768], replicated, may hold values from -0.109375 to 0.109375
- enc_gain_final: bfloat16 [768], replicated, may hold values from 0.5 to 1.5
- cross_key: bfloat16 [768, 768], replicated, may hold values from -0.21875 to 0.21875
- cross_value: bfloat16 [768, 768], replicated, may hold values from -0.21875 to 0.21875
- dec_gain_self: bfloat16 [768], replicated, may hold values from 0.5 to 1.5
- dec_query: bfloat16 [768, 768], replicated, may hold values from -0.21875 to 0.21875
- dec_key: bfloat16 [768, 768], replicated, may hold values from -0.21875 to 0.21875
- dec_value: bfloat16 [768, 768], replicated, may hold values from -0.21875 to 0.21875
- dec_output: bfloat16 [768, 768], replicated, may hold values from -0.625 to 0.625
- dec_bias: bfloat16 [32, 12], replicated, may hold values from -4 to 4
- dec_gain_cross: bfloat16 [768], replicated, may hold values from 0.5 to 1.5
- cross_query: bfloat16 [768, 768], replicated, may hold values from -0.21875 to 0.21875
- cross_output: bfloat16 [768, 768], replicated, may hold values from -9 to 9
- dec_gain_ffn: bfloat16 [768], replicated, may hold values from 0.5 to 1.5
- dec_ff_in: bfloat16 [768, 3072], replicated, may hold values from -0.21875 to 0.21875
- dec_ff_out: bfloat16 [3072, 768], replicated, may hold values from -0.109375 to 0.109375
- enc_cot: bfloat16 [32768, 768], P(('pb', 'pa')), may hold values from -6 to 6
- dec_cot: bfloat16 [192, 768], P('pb'), may hold values from -6 to 6
Outputs:
- enc_out: bfloat16 [32768, 768], P(('pb', 'pa'))
- dec_out: bfloat16 [192, 768], P('pb')
- enc_in_grad: float32 [32768, 768], P(('pb', 'pa'))
- dec_in_grad: float32 [192, 768], P('pb')
- enc_gain_attn_grad: float32 [768], P(('pb', 'pa'))
- enc_query_grad: float32 [768, 768], P(('pb', 'pa'))
- enc_key_grad: float32 [768, 768], P(('pb', 'pa'))
- enc_value_grad: float32 [768, 768], P(('pb', 'pa'))
- enc_output_grad: float32 [768, 768], P(('pb', 'pa'))
- enc_bias_grad: float32 [384], P(('pb', 'pa'))
- enc_gain_ffn_grad: float32 [768], P(('pb', 'pa'))
- enc_ff_in_grad: float32 [768, 3072], P(('pb', 'pa'))
- enc_ff_out_grad: float32 [3072, 768], P(('pb', 'pa'))
- enc_gain_final_grad: float32 [768], P(('pb', 'pa'))
- cross_key_grad: float32 [768, 768], P(('pb', 'pa'))
- cross_value_grad: float32 [768, 768], P(('pb', 'pa'))
- dec_gain_self_grad: float32 [768], P(('pb', 'pa'))
- dec_query_grad: float32 [768, 768], P(('pb', 'pa'))
- dec_key_grad: float32 [768, 768], P(('pb', 'pa'))
- dec_value_grad: float32 [768, 768], P(('pb', 'pa'))
- dec_output_grad: float32 [768, 768], P(('pb', 'pa'))
- dec_bias_grad: float32 [384], P(('pb', 'pa'))
- dec_gain_cross_grad: float32 [768], P(('pb', 'pa'))
- cross_query_grad: float32 [768, 768], P(('pb', 'pa'))
- cross_output_grad: float32 [768, 768], P(('pb', 'pa'))
- dec_gain_ffn_grad: float32 [768], P(('pb', 'pa'))
- dec_ff_in_grad: float32 [768, 3072], P(('pb', 'pa'))
- dec_ff_out_grad: float32 [3072, 768], P(('pb', 'pa'))
Inputs may be any that keep to these rules, and one draw needn't show every extreme that they name: question_of[n] names a question of the passage's group (the 2 questions whose answers are rows g * 2 * 24 onward of dec_in for group g); every question of every group has at least one passage. A passage's tokens fill the first lengths[n] of its 512 slots, the rest is padding; some passage holds exactly 512 tokens.
All inputs are finite; a program needn't handle non-finite values.
Results may differ from a plain program's by a relative error of at most 0.017.
Values sent between devices are 32-bit elements; how exact they have to be, the bound alone decides.
A program may use at most 384 MiB of HBM per device.

v0:
```python
import math

import jax
import jax.numpy as jnp
import numpy as np
from jax import lax
from jax.sharding import PartitionSpec as P

D = 768
HEADS = 12
HEAD = 64
BUCKETS = 32
PL = 512
ANS = 24


far_distance = 128
epsilon = 1e-06
highest = lax.Precision.HIGHEST


def joined(array, axis, combine):
    everything = jax.tree.map(lambda part: lax.all_gather(part, axis), array)
    first = jax.tree.map(lambda part: part[0], everything)

    def lap(k, so_far):
        return combine(so_far, jax.tree.map(lambda part: part[k], everything))

    return lax.fori_loop(1, lax.axis_size(axis), lap, first)


def smooth_unit(values):
    return jax.nn.gelu(values, approximate=True)


def smooth_back(values, grad):
    return jax.vjp(smooth_unit, values)[1](grad)[0]


def bucket_of(offset, bidirectional):
    if bidirectional:
        halves = BUCKETS // 2
        base_bucket = halves if offset > 0 else 0
        distance = abs(offset)
    else:
        halves = BUCKETS
        base_bucket = 0
        distance = max(-offset, 0)
    exact_count = halves // 2
    if distance < exact_count:
        return base_bucket + distance
    scaled = (
        math.log(distance / exact_count)
        / math.log(far_distance / exact_count)
        * (halves - exact_count)
    )
    return base_bucket + min(exact_count + int(scaled), halves - 1)


def offset_onehot(length):
    table = np.zeros((2 * length - 1, BUCKETS), np.float32)
    for offset in range(-(length - 1), length):
        table[offset + length - 1, bucket_of(offset, True)] = 1.0
    return table


def causal_onehot(length):
    table = np.zeros((length * length, BUCKETS), np.float32)
    for query_pos in range(length):
        for key_pos in range(length):
            table[query_pos * length + key_pos, bucket_of(key_pos - query_pos, False)] = 1.0
    return table


def spread_offsets(per_offset):
    length = (per_offset.shape[1] + 1) // 2
    flat = jnp.tile(per_offset, (1, length))
    part_rows = flat[:, length - 1 : length - 1 + length * (2 * length - 2)]
    return part_rows.reshape(per_offset.shape[0], length, 2 * length - 2)[:, :, :length]


def fold_offsets(matrix):
    heads_here = matrix.shape[0]
    length = matrix.shape[1]
    padded = jnp.pad(matrix, ((0, 0), (0, 0), (0, length - 2)))
    flat = padded.reshape(heads_here, length * (2 * length - 2))
    whole = jnp.pad(flat, ((0, 0), (length - 1, 1)))
    return jnp.sum(whole.reshape(heads_here, length, 2 * length - 1), axis=1)


def to_low(values):
    return values.astype(jnp.bfloat16)


def product(left, right):
    return jnp.dot(left, right, preferred_element_type=jnp.float32)


def product_tn(left, right):
    return lax.dot_general(
        left, right, (((0,), (0,)), ((), ())), preferred_element_type=jnp.float32
    )


def product_nt(left, right):
    return lax.dot_general(
        left, right, (((1,), (1,)), ((), ())), preferred_element_type=jnp.float32
    )


def exact_product(left, right):
    return jnp.dot(left, right.astype(jnp.float32), precision=highest)


def exact_tn(left, right):
    return lax.dot_general(
        left.astype(jnp.float32),
        right.astype(jnp.float32),
        (((0,), (0,)), ((), ())),
        precision=highest,
    )


def exact_nt(left, right):
    return lax.dot_general(
        left, right.astype(jnp.float32), (((1,), (1,)), ((), ())), precision=highest
    )


def norm_forward(values, gain):
    scale = lax.rsqrt(jnp.mean(values * values, axis=-1, keepdims=True) + epsilon)
    return (values * scale * gain, scale)


def norm_backward(values, scale, gain, grad):
    scaled_grad = grad * gain
    gain_grad = jnp.sum(grad * values * scale, axis=0)
    inner = jnp.mean(scaled_grad * values, axis=-1, keepdims=True)
    return (scaled_grad * scale - values * (scale * scale * scale) * inner, gain_grad)


def merge_stats(earlier, later):
    top_score = jnp.maximum(earlier[0], later[0])
    return (
        top_score,
        earlier[1] * jnp.exp(earlier[0] - top_score) + later[1] * jnp.exp(later[0] - top_score),
    )


def local(
    enc_in,
    dec_in,
    question_of,
    lengths,
    enc_gain_attn,
    enc_query,
    enc_key,
    enc_value,
    enc_output,
    enc_bias,
    enc_gain_ffn,
    enc_ff_in,
    enc_ff_out,
    enc_gain_final,
    cross_key,
    cross_value,
    dec_gain_self,
    dec_query,
    dec_key,
    dec_value,
    dec_output,
    dec_bias,
    dec_gain_cross,
    cross_query,
    cross_output,
    dec_gain_ffn,
    dec_ff_in,
    dec_ff_out,
    enc_cot,
    dec_cot,
):
    passages = lengths.shape[0]
    tokens = passages * PL
    answer_rows = dec_in.shape[0]
    questions = answer_rows // ANS
    gain_attn = enc_gain_attn.astype(jnp.float32)
    gain_ffn = enc_gain_ffn.astype(jnp.float32)
    gain_final = enc_gain_final.astype(jnp.float32)
    gain_self = dec_gain_self.astype(jnp.float32)
    gain_cross = dec_gain_cross.astype(jnp.float32)
    gain_dffn = dec_gain_ffn.astype(jnp.float32)
    enc_table = jnp.asarray(offset_onehot(PL))
    dec_table = jnp.asarray(causal_onehot(ANS))
    enc_x = enc_in.astype(jnp.float32)
    attn_normed, attn_scale = norm_forward(enc_x, gain_attn)
    attn_low = to_low(attn_normed)
    enc_queries = to_low(product(attn_low, enc_query)).reshape(passages, PL, HEADS, HEAD)
    enc_keys = to_low(product(attn_low, enc_key)).reshape(passages, PL, HEADS, HEAD)
    enc_values = to_low(product(attn_low, enc_value)).reshape(passages, PL, HEADS, HEAD)
    key_valid = jnp.arange(PL)[None, :] < lengths[:, None]
    enc_position = spread_offsets(
        jnp.dot(enc_table, enc_bias.astype(jnp.float32), precision=highest).T
    )

    def enc_scores():
        raw_scores = 0.125 * jnp.einsum(
            "pqhd,pkhd->phqk", enc_queries, enc_keys, preferred_element_type=jnp.float32
        )
        return jnp.where(
            key_valid[:, None, None, :], raw_scores + enc_position[None], -1000000000.0
        )

    scores = enc_scores()
    row_top = jnp.max(scores, axis=-1, keepdims=True)
    exp_scores = jnp.exp(scores - row_top)
    row_total = jnp.sum(exp_scores, axis=-1, keepdims=True)
    enc_lse = row_top + jnp.log(row_total)
    enc_attended = to_low(
        jnp.einsum(
            "phqk,pkhd->pqhd",
            to_low(exp_scores / row_total),
            enc_values,
            preferred_element_type=jnp.float32,
        ).reshape(tokens, D)
    )
    enc_mid = enc_x + product(enc_attended, enc_output)
    ffn_normed, ffn_scale = norm_forward(enc_mid, gain_ffn)
    ffn_low = to_low(ffn_normed)
    enc_pre = product(ffn_low, enc_ff_in)
    enc_hidden = to_low(smooth_unit(enc_pre))
    enc_y = enc_mid + product(enc_hidden, enc_ff_out)
    final_normed, final_scale = norm_forward(enc_y, gain_final)
    final_low = to_low(final_normed)
    cross_keys = to_low(product(final_low, cross_key)).reshape(tokens, HEADS, HEAD)
    cross_values = to_low(product(final_low, cross_value)).reshape(tokens, HEADS, HEAD)
    dec_x = dec_in.astype(jnp.float32)
    self_normed, self_scale = norm_forward(dec_x, gain_self)
    self_low = to_low(self_normed)
    dec_queries = to_low(product(self_low, dec_query)).reshape(questions, ANS, HEADS, HEAD)
    dec_keys = to_low(product(self_low, dec_key)).reshape(questions, ANS, HEADS, HEAD)
    dec_values = to_low(product(self_low, dec_value)).reshape(questions, ANS, HEADS, HEAD)
    dec_position = jnp.dot(dec_table, dec_bias.astype(jnp.float32), precision=highest).T.reshape(
        HEADS, ANS, ANS
    )
    causal = jnp.arange(ANS)[None, :] <= jnp.arange(ANS)[:, None]

    def dec_scores():
        raw_scores = 0.125 * jnp.einsum(
            "qihd,qjhd->qhij", dec_queries, dec_keys, preferred_element_type=jnp.float32
        )
        return jnp.where(causal, raw_scores + dec_position[None], -1000000000.0)

    self_scores = dec_scores()
    self_top = jnp.max(self_scores, axis=-1, keepdims=True)
    self_exp = jnp.exp(self_scores - self_top)
    self_total = jnp.sum(self_exp, axis=-1, keepdims=True)
    dec_lse = self_top + jnp.log(self_total)
    dec_attended = to_low(
        jnp.einsum(
            "qhij,qjhd->qihd",
            to_low(self_exp / self_total),
            dec_values,
            preferred_element_type=jnp.float32,
        ).reshape(answer_rows, D)
    )
    dec_mid = dec_x + product(dec_attended, dec_output)
    cross_normed, cross_scale = norm_forward(dec_mid, gain_cross)
    cross_low = to_low(cross_normed)
    cross_queries = to_low(product(cross_low, cross_query)).reshape(answer_rows, HEADS, HEAD)
    key_question = jnp.broadcast_to(question_of[:, None], (passages, PL)).reshape(tokens)
    row_question = jnp.arange(answer_rows) // ANS
    permitted = (row_question[:, None] == key_question[None, :]) & key_valid.reshape(tokens)[
        None, :
    ]
    cross_raw = 0.125 * jnp.einsum(
        "rhd,khd->hrk", cross_queries, cross_keys, preferred_element_type=jnp.float32
    )
    cross_scores = jnp.where(permitted[None], cross_raw, -1000000000.0)
    local_top = jnp.max(cross_scores, axis=-1)
    local_total = jnp.sum(jnp.exp(cross_scores - local_top[..., None]), axis=-1)
    merged_top, merged_total = joined((local_top, local_total), "pa", merge_stats)
    cross_probs = jnp.exp(cross_scores - merged_top[..., None]) / merged_total[..., None]
    cross_low_probs = to_low(cross_probs)
    partial_out = jnp.einsum(
        "hrk,khd->rhd", cross_low_probs, cross_values, preferred_element_type=jnp.float32
    ).reshape(answer_rows, D)
    cross_attended = lax.psum(partial_out, "pa")
    dec_after = dec_mid + exact_product(cross_attended, cross_output)
    dffn_normed, dffn_scale = norm_forward(dec_after, gain_dffn)
    dffn_low = to_low(dffn_normed)
    dec_pre = product(dffn_low, dec_ff_in)
    dec_hidden = to_low(smooth_unit(dec_pre))
    dec_y = dec_after + product(dec_hidden, dec_ff_out)
    grad_dec_y = dec_cot.astype(jnp.float32)
    out_grad_low = to_low(grad_dec_y)
    pre_grad_low = to_low(smooth_back(dec_pre, product_nt(out_grad_low, dec_ff_out)))
    back_after, dec_gain_ffn_grad = norm_backward(
        dec_after, dffn_scale, gain_dffn, product_nt(pre_grad_low, dec_ff_in)
    )
    grad_after = grad_dec_y + back_after
    after_low = to_low(grad_after)
    cross_att_grad = to_low(product_nt(after_low, cross_output)).reshape(answer_rows, HEADS, HEAD)
    cross_dprob = jnp.einsum(
        "rhd,khd->hrk", cross_att_grad, cross_values, preferred_element_type=jnp.float32
    )
    cross_delta = lax.psum(jnp.sum(cross_probs * cross_dprob, axis=-1), "pa")
    cross_dscore = to_low(cross_probs * (cross_dprob - cross_delta[..., None]))
    query_part = 0.125 * jnp.einsum(
        "hrk,khd->rhd", cross_dscore, cross_keys, preferred_element_type=jnp.float32
    ).reshape(answer_rows, D)
    grad_cross_q = lax.psum(query_part, "pa")
    grad_cross_k = to_low(
        0.125
        * jnp.einsum(
            "hrk,rhd->khd", cross_dscore, cross_queries, preferred_element_type=jnp.float32
        ).reshape(tokens, D)
    )
    grad_cross_v = to_low(
        jnp.einsum(
            "hrk,rhd->khd", cross_low_probs, cross_att_grad, preferred_element_type=jnp.float32
        ).reshape(tokens, D)
    )
    back_mid, dec_gain_cross_grad = norm_backward(
        dec_mid, cross_scale, gain_cross, exact_nt(grad_cross_q, cross_query)
    )
    grad_mid = grad_after + back_mid
    mid_low = to_low(grad_mid)
    dec_att_grad = to_low(product_nt(mid_low, dec_output)).reshape(questions, ANS, HEADS, HEAD)
    dec_probs = jnp.exp(dec_scores() - dec_lse)
    dec_dprob = jnp.einsum(
        "qihd,qjhd->qhij", dec_att_grad, dec_values, preferred_element_type=jnp.float32
    )
    dec_dscore = dec_probs * (dec_dprob - jnp.sum(dec_probs * dec_dprob, axis=-1, keepdims=True))
    dec_bias_grad = jnp.dot(
        jnp.sum(dec_dscore, axis=0).reshape(HEADS, ANS * ANS), dec_table, precision=highest
    ).T.reshape(BUCKETS * HEADS)
    low_dscore = to_low(dec_dscore)
    grad_dq = to_low(
        0.125
        * jnp.einsum("qhij,qjhd->qihd", low_dscore, dec_keys, preferred_element_type=jnp.float32)
    ).reshape(answer_rows, D)
    grad_dk = to_low(
        0.125
        * jnp.einsum("qhij,qihd->qjhd", low_dscore, dec_queries, preferred_element_type=jnp.float32)
    ).reshape(answer_rows, D)
    grad_dv = to_low(
        jnp.einsum(
            "qhij,qihd->qjhd", to_low(dec_probs), dec_att_grad, preferred_element_type=jnp.float32
        )
    ).reshape(answer_rows, D)
    self_back = (
        product_nt(grad_dq, dec_query)
        + product_nt(grad_dk, dec_key)
        + product_nt(grad_dv, dec_value)
    )
    back_dec_in, dec_gain_self_grad = norm_backward(dec_x, self_scale, gain_self, self_back)
    dec_in_grad = grad_mid + back_dec_in
    cross_key_grad = product_tn(final_low, grad_cross_k)
    cross_value_grad = product_tn(final_low, grad_cross_v)
    final_back = product_nt(grad_cross_k, cross_key) + product_nt(grad_cross_v, cross_value)
    back_final, enc_gain_final_grad = norm_backward(enc_y, final_scale, gain_final, final_back)
    grad_enc_y = enc_cot.astype(jnp.float32) + back_final
    eout_low = to_low(grad_enc_y)
    enc_ff_out_grad = product_tn(enc_hidden, eout_low)
    epre_low = to_low(smooth_back(enc_pre, product_nt(eout_low, enc_ff_out)))
    enc_ff_in_grad = product_tn(ffn_low, epre_low)
    back_enc_mid, enc_gain_ffn_grad = norm_backward(
        enc_mid, ffn_scale, gain_ffn, product_nt(epre_low, enc_ff_in)
    )
    grad_enc_mid = grad_enc_y + back_enc_mid
    emid_low = to_low(grad_enc_mid)
    enc_output_grad = product_tn(enc_attended, emid_low)
    enc_att_grad = to_low(product_nt(emid_low, enc_output)).reshape(passages, PL, HEADS, HEAD)
    enc_probs = jnp.exp(enc_scores() - enc_lse)
    enc_dprob = jnp.einsum(
        "pqhd,pkhd->phqk", enc_att_grad, enc_values, preferred_element_type=jnp.float32
    )
    enc_dscore = enc_probs * (enc_dprob - jnp.sum(enc_probs * enc_dprob, axis=-1, keepdims=True))
    enc_bias_grad = jnp.dot(
        fold_offsets(jnp.sum(enc_dscore, axis=0)), enc_table, precision=highest
    ).T.reshape(BUCKETS * HEADS)
    low_escore = to_low(enc_dscore)
    grad_eq = to_low(
        0.125
        * jnp.einsum("phqk,pkhd->pqhd", low_escore, enc_keys, preferred_element_type=jnp.float32)
    ).reshape(tokens, D)
    grad_ek = to_low(
        0.125
        * jnp.einsum("phqk,pqhd->pkhd", low_escore, enc_queries, preferred_element_type=jnp.float32)
    ).reshape(tokens, D)
    grad_ev = to_low(
        jnp.einsum(
            "phqk,pqhd->pkhd", to_low(enc_probs), enc_att_grad, preferred_element_type=jnp.float32
        )
    ).reshape(tokens, D)
    enc_query_grad = product_tn(attn_low, grad_eq)
    enc_key_grad = product_tn(attn_low, grad_ek)
    enc_value_grad = product_tn(attn_low, grad_ev)
    attn_back = (
        product_nt(grad_eq, enc_query)
        + product_nt(grad_ek, enc_key)
        + product_nt(grad_ev, enc_value)
    )
    back_enc_in, enc_gain_attn_grad = norm_backward(enc_x, attn_scale, gain_attn, attn_back)
    enc_in_grad = grad_enc_mid + back_enc_in
    enc_terms = (
        enc_gain_attn_grad,
        enc_query_grad,
        enc_key_grad,
        enc_value_grad,
        enc_output_grad,
        enc_bias_grad,
        enc_gain_ffn_grad,
        enc_ff_in_grad,
        enc_ff_out_grad,
        enc_gain_final_grad,
        cross_key_grad,
        cross_value_grad,
    )
    pick = lambda values: values
    enc_parts = (
        lax.psum_scatter(enc_terms[0], ("pb", "pa"), scatter_dimension=0, tiled=True),
        lax.psum_scatter(enc_terms[1], ("pb", "pa"), scatter_dimension=0, tiled=True),
        lax.psum_scatter(enc_terms[2], ("pb", "pa"), scatter_dimension=0, tiled=True),
        lax.psum_scatter(enc_terms[3], ("pb", "pa"), scatter_dimension=0, tiled=True),
        lax.psum_scatter(enc_terms[4], ("pb", "pa"), scatter_dimension=0, tiled=True),
        lax.psum_scatter(enc_terms[5], ("pb", "pa"), scatter_dimension=0, tiled=True),
        lax.psum_scatter(enc_terms[6], ("pb", "pa"), scatter_dimension=0, tiled=True),
        lax.psum_scatter(enc_terms[7], ("pb", "pa"), scatter_dimension=0, tiled=True),
        lax.psum_scatter(enc_terms[8], ("pb", "pa"), scatter_dimension=0, tiled=True),
        lax.psum_scatter(enc_terms[9], ("pb", "pa"), scatter_dimension=0, tiled=True),
        lax.psum_scatter(enc_terms[10], ("pb", "pa"), scatter_dimension=0, tiled=True),
        lax.psum_scatter(enc_terms[11], ("pb", "pa"), scatter_dimension=0, tiled=True),
    )
    dec_halves = (
        lax.psum_scatter(pick(dec_gain_self_grad), "pb", scatter_dimension=0, tiled=True),
        lax.psum_scatter(
            product_tn(pick(self_low), grad_dq), "pb", scatter_dimension=0, tiled=True
        ),
        lax.psum_scatter(
            product_tn(pick(self_low), grad_dk), "pb", scatter_dimension=0, tiled=True
        ),
        lax.psum_scatter(
            product_tn(pick(self_low), grad_dv), "pb", scatter_dimension=0, tiled=True
        ),
        lax.psum_scatter(
            product_tn(pick(dec_attended), mid_low), "pb", scatter_dimension=0, tiled=True
        ),
        lax.psum_scatter(pick(dec_bias_grad), "pb", scatter_dimension=0, tiled=True),
        lax.psum_scatter(pick(dec_gain_cross_grad), "pb", scatter_dimension=0, tiled=True),
        lax.psum_scatter(
            exact_tn(pick(cross_low), grad_cross_q), "pb", scatter_dimension=0, tiled=True
        ),
        lax.psum_scatter(
            exact_tn(pick(cross_attended), after_low), "pb", scatter_dimension=0, tiled=True
        ),
        lax.psum_scatter(pick(dec_gain_ffn_grad), "pb", scatter_dimension=0, tiled=True),
        lax.psum_scatter(
            product_tn(pick(dffn_low), pre_grad_low), "pb", scatter_dimension=0, tiled=True
        ),
        lax.psum_scatter(
            product_tn(pick(dec_hidden), out_grad_low), "pb", scatter_dimension=0, tiled=True
        ),
    )
    position = lax.axis_index("pa")
    pa_count = lax.axis_size("pa")
    dec_parts = tuple(
        (
            lax.dynamic_slice_in_dim(
                piece, position * (piece.shape[0] // pa_count), piece.shape[0] // pa_count, 0
            )
            for piece in dec_halves
        )
    )
    return (
        (to_low(enc_y), to_low(dec_y), enc_in_grad, dec_in_grad)
        + tuple(enc_parts)
        + tuple(dec_parts)
    )


def solution(mesh):
    return jax.shard_map(
        local,
        mesh=mesh,
        in_specs=(
            P(("pb", "pa"), None),
            P("pb", None),
            P(("pb", "pa")),
            P(("pb", "pa")),
            P(),
            P(),
            P(),
            P(),
            P(),
            P(),
            P(),
            P(),
            P(),
            P(),
            P(),
            P(),
            P(),
            P(),
            P(),
            P(),
            P(),
            P(),
            P(),
            P(),
            P(),
            P(),
            P(),
            P(),
            P(("pb", "pa"), None),
            P("pb", None),
        ),
        out_specs=(
            P(("pb", "pa"), None),
            P("pb", None),
            P(("pb", "pa"), None),
            P("pb", None),
            P(("pb", "pa")),
            P(("pb", "pa"), None),
            P(("pb", "pa"), None),
            P(("pb", "pa"), None),
            P(("pb", "pa"), None),
            P(("pb", "pa")),
            P(("pb", "pa")),
            P(("pb", "pa"), None),
            P(("pb", "pa"), None),
            P(("pb", "pa")),
            P(("pb", "pa"), None),
            P(("pb", "pa"), None),
            P(("pb", "pa")),
            P(("pb", "pa"), None),
            P(("pb", "pa"), None),
            P(("pb", "pa"), None),
            P(("pb", "pa"), None),
            P(("pb", "pa")),
            P(("pb", "pa")),
            P(("pb", "pa"), None),
            P(("pb", "pa"), None),
            P(("pb", "pa")),
            P(("pb", "pa"), None),
            P(("pb", "pa"), None),
        ),
        check_vma=False,
    )
```

profile of v0, /device:TPU:0, one launch (start us, length us, event | category | flops | bytes accessed | tf_op | source)
XLA Modules:
  0.0 1818.1 jit_solution(9271962447084214012)
XLA Ops:
  60.7 11.5 tile.4
  72.2 38.7 %tile.10 = f32[12,523776]{1,0:T(8,128)} reshape(f32[12,512,1023]{2,1,0:T(8,128)} %tile.4) | data formatting | bytes 50282496 | tf_op jit(solution)/shard_map/tile | solution.py:77
  111.0 25.7 %slice.20 = f32[12,523264]{1,0:T(8,128)} slice(f32[12,523776]{1,0:T(8,128)} %tile.10), slice={[0:12], [511:523775]} | slice | bytes 50233344 | tf_op jit(solution)/shard_map/slice | solution.py:78
  136.6 42.4 %reshape.384 = f32[12,512,1022]{2,1,0:T(8,128)} reshape(f32[12,523264]{1,0:T(8,128)} %slice.20) | data formatting | bytes 50233344 | tf_op jit(solution)/shard_map/reshape | solution.py:79
  179.0 10.6 slice.21
  189.7 12.6 copy.214
  202.3 15.2 fusion.134
  217.5 10.2 fusion.2
  227.7 10.6 fusion.36
  243.6 8.5 fusion.123
  252.2 12.0 multiply_reduce_fusion.5
  273.7 32.3 %all-gather.3 = f32[8,12,48]{2,1,0:T(8,128)S(1)} all-gather(f32[1,12,48]{2,1,0:T(8,128)S(1)} %bitcast.189), channel_id=3, replica_groups=mesh['pb'=4,'pa'=8] {'pa'}, dimensions={0}, use_global_device_ids=true | all-gather | bytes 20736 | tf_op jit(solution)/shard_map/all_gather | solution.py:23
  306.0 30.5 %all-gather.2 = f32[8,12,48]{2,1,0:T(8,128)S(1)} all-gather(f32[1,12,48]{2,1,0:T(8,128)S(1)} %bitcast.188), channel_id=2, replica_groups=mesh['pb'=4,'pa'=8] {'pa'}, dimensions={0}, use_global_device_ids=true | all-gather | bytes 20736 | tf_op jit(solution)/shard_map/all_gather | solution.py:23
  340.8 4.7 fusion.136
  346.0 65.5 %all-reduce.15.cloned.1.call-done = f32[48,768]{1,0:T(8,128)} async-done(((f32[48,768]{1,0:T(8,128)}), f32[48,768]{1,0:T(8,128)}) %all-reduce.15.cloned.1.call-update) | async-done | bytes 147472 | tf_op jit(solution)/shard_map/psum | solution.py:287
  417.6 4.8 multiply_reduce_fusion.9
  426.1 5.2 multiply_reduce_fusion.7
  431.2 20.5 %psum.22 = f32[12,48]{1,0:T(8,128)} all-reduce(f32[12,48]{1,0:T(8,128)} %get-tuple-element.342), channel_id=1, replica_groups=mesh['pb'=4,'pa'=8] {'pa'}, use_global_device_ids=true, to_apply=%region_17.18 | all-reduce | flops 576 | bytes 4608 | tf_op jit(solution)/shard_map/psum | solution.py:306
  463.1 63.3 %all-reduce.17.cloned.1.call-done = f32[48,768]{1,0:T(8,128)} async-done(((f32[48,768]{1,0:T(8,128)}), f32[48,768]{1,0:T(8,128)}) %all-reduce.17.cloned.1.call-update) | async-done | bytes 147472 | tf_op jit(solution)/shard_map/psum | solution.py:311
  563.0 5.0 fusion.112
  569.2 5.2 fusion.110
  590.5 4.7 fusion.140
  595.9 6.4 subtract_add_fusion.1
  603.9 16.3 fusion.10
  620.5 10.3 multiply_reduce_fusion.2
  642.3 5.6 fusion.56
  648.2 14.2 fusion.31
  670.1 19.7 %multiply_reduce_fusion = (f32[2,12,512]{2,1,0:T(8,128)S(1)}, f32[2,12,512,512]{2,3,1,0:T(8,128)}) fusion(f32[2,12,512,512]{2,3,1,0:T(8,128)} %get-tuple-element.326, f32[2,12,512]{2,1,0:T(8,128)S(1)} %log_add_fusion, bf16[2,512,12,64]{1,0,3,2:T(2,128)(2,1)} %reshape.381, bf16[2,512,12,64]{1,0,3,2:T(2,128)(2,1)} %reshape.393), kind=kOutput, calls=%fused_computation.6 | convolution fusion | flops 824168448 | bytes 53575680 | tf_op jit(solution)/shard_map/pqhd,pkhd->phqk/dot_general | solution.py:375
  690.3 27.5 %fusion.15 = (f32[12,512,512]{1,2,0:T(8,128)}, bf16[2,12,512,512]{2,3,1,0:T(8,128)(2,1)}) fusion(f32[2,12,512,512]{2,3,1,0:T(8,128)} %get-tuple-element.347, f32[2,12,512]{2,1,0:T(8,128)S(1)} %get-tuple-element.346, f32[2,12,512,512]{2,3,1,0:T(8,128)} %get-tuple-element.326, f32[2,12,512]{2,1,0:T(8,128)S(1)} %log_add_fusion), kind=kLoop, calls=%fused_computation.32 | loop fusion | flops 28311552 | bytes 75595776 | tf_op jit(solution)/shard_map/reduce_sum | solution.py:380
  717.8 8.5 fusion.35
  732.4 7.3 fusion.34
  746.0 15.9 fusion.59
  761.9 10.3 fusion.122
  777.4 12.7 copy.279
  803.0 14.4 pad.8.clone
  817.3 47.8 %reshape.401 = f32[12,523264]{1,0:T(8,128)} reshape(f32[12,512,1022]{2,1,0:T(8,128)} %pad.8.clone) | data formatting | bytes 50233344 | tf_op jit(solution)/shard_map/reshape | solution.py:86
  865.1 25.9 %pad.9 = f32[12,523776]{1,0:T(8,128)} pad(f32[12,523264]{1,0:T(8,128)} %reshape.401, f32[]{:T(128)} %constant.94.clone.1), padding=0_0x511_1 | pad | bytes 50257924 | tf_op jit(solution)/shard_map/jit(_pad)/pad | solution.py:87
  891.0 41.9 %reshape.402 = f32[12,512,1023]{2,1,0:T(8,128)} reshape(f32[12,523776]{1,0:T(8,128)} %pad.9) | data formatting | bytes 50282496 | tf_op jit(solution)/shard_map/reshape | solution.py:88
  933.0 9.6 reduce_sum.263
  943.7 40.7 %all-reduce.10 = (f32[768]{0:T(1024)S(1)}, f32[384]{0:T(512)S(1)}, f32[768]{0:T(1024)S(1)}, f32[768]{0:T(1024)S(1)}) all-reduce(f32[768]{0:T(1024)S(1)} %get-tuple-element.279, f32[384]{0:T(512)S(1)} %reshape.403, f32[768]{0:T(1024)S(1)} %copy-done.105, f32[768]{0:T(1024)S(1)} %copy-done.97), channel_id=4, replica_groups=mesh['pb'=4,'pa'=8] {'pb','pa'}, use_global_device_ids=true, to_apply=%region_27.28.clone | all-reduce | flops 2688 | bytes 21504
  996.2 11.1 all-reduce.11
  1023.0 88.0 %reduce-scatter.31.cloned.1.call-done = f32[24,768]{1,0:T(8,128)} async-done(((f32[768,768]{1,0:T(8,128)}), f32[24,768]{1,0:T(8,128)}) %reduce-scatter.31.cloned.1.call-update) | async-done | bytes 73744 | tf_op jit(solution)/shard_map/reduce_scatter | solution.py:433
  1111.0 104.1 %reduce-scatter.23.cloned.1.call-done = f32[24,768]{1,0:T(8,128)} async-done(((f32[768,768]{1,0:T(8,128)}), f32[24,768]{1,0:T(8,128)}) %reduce-scatter.23.cloned.1.call-update) | async-done | bytes 73744 | tf_op jit(solution)/shard_map/reduce_scatter | solution.py:426
  1215.1 104.6 %reduce-scatter.21.cloned.1.call-done = f32[24,768]{1,0:T(8,128)} async-done(((f32[768,768]{1,0:T(8,128)}), f32[24,768]{1,0:T(8,128)}) %reduce-scatter.21.cloned.1.call-update) | async-done | bytes 73744 | tf_op jit(solution)/shard_map/reduce_scatter | solution.py:425
  1319.6 103.8 %reduce-scatter.19.cloned.1.call-done = f32[24,768]{1,0:T(8,128)} async-done(((f32[768,768]{1,0:T(8,128)}), f32[24,768]{1,0:T(8,128)}) %reduce-scatter.19.cloned.1.call-update) | async-done | bytes 73744 | tf_op jit(solution)/shard_map/reduce_scatter | solution.py:424
  1423.4 104.6 %reduce-scatter.17.cloned.1.call-done = f32[24,768]{1,0:T(8,128)} async-done(((f32[768,768]{1,0:T(8,128)}), f32[24,768]{1,0:T(8,128)}) %reduce-scatter.17.cloned.1.call-update) | async-done | bytes 73744 | tf_op jit(solution)/shard_map/reduce_scatter | solution.py:423
  1528.0 141.1 %reduce-scatter.27.cloned.1.call-done = f32[96,768]{1,0:T(8,128)} async-done(((f32[3072,768]{1,0:T(8,128)}), f32[96,768]{1,0:T(8,128)}) %reduce-scatter.27.cloned.1.call-update) | async-done | bytes 294928 | tf_op jit(solution)/shard_map/reduce_scatter | solution.py:430
  1669.1 141.9 %reduce-scatter.25.cloned.1.call-done = f32[24,3072]{1,0:T(8,128)} async-done(((f32[768,3072]{1,0:T(8,128)}), f32[24,3072]{1,0:T(8,128)}) %reduce-scatter.25.cloned.1.call-update) | async-done | bytes 294928 | tf_op jit(solution)/shard_map/reduce_scatter | solution.py:429
  (445 shorter events, 226.9 us)
Async XLA Ops:
  7.2 260.9 %copy-start = (bf16[768,768]{1,0:T(8,128)(2,1)S(1)}, bf16[768,768]{1,0:T(8,128)(2,1)}, u32[]{:S(2)}) copy-start(bf16[768,768]{1,0:T(8,128)(2,1)} %param.49) | copy-start | bytes 3538948
  7.2 12.7 copy-start.53
  7.2 12.3 copy-start.16
  7.2 12.3 copy-start.33
  7.3 12.7 copy-start.103
  7.3 404.3 %all-reduce.15.cloned.1.call-start = ((), (), s32[]{:S(2)}) async-start(), calls=%async_computation.16 | async-start | bytes 294912 | tf_op jit(solution)/shard_map/psum | solution.py:287
  9.5 10.0 copy-start.91
  11.5 38.4 %copy-start.89 = (f32[768]{0:T(1024)}, f32[768]{0:T(1024)S(1)}, u32[]{:S(2)}) copy-start(f32[768]{0:T(1024)S(1)} %convert_element_type.222) | copy-start | bytes 9220
  13.6 11.3 copy-start.80
  29.2 20.8 %copy-start.87 = (f32[1024]{0:T(1024)}, f32[1024]{0:T(1024)S(1)}, u32[]{:S(2)}) copy-start(f32[1024]{0:T(1024)S(1)} %get-tuple-element.314) | copy-start | bytes 12292
  217.5 10.2 copy-start.66
  217.5 10.3 copy-start.20
  227.7 10.7 copy-start.73
  243.0 9.2 copy-start.7
  252.2 12.7 copy-start.83
  340.7 70.8 %copy-start.29 = (f32[48,768]{1,0:T(8,128)S(1)}, f32[48,768]{1,0:T(8,128)}, u32[]{:S(2)}) copy-start(f32[48,768]{1,0:T(8,128)} %copy-done.28) | copy-start | bytes 442372
  340.7 185.7 %all-reduce.17.cloned.1.call-start = ((), (), s32[]{:S(2)}) async-start(), calls=%async_computation.17 | async-start | bytes 294912 | tf_op jit(solution)/shard_map/psum | solution.py:311
  413.7 8.7 copy-start.25
  417.6 145.5 %copy-start.14 = (f32[48,3072]{1,0:T(8,128)}, f32[48,3072]{1,0:T(8,128)S(1)}, u32[]{:S(2)}) copy-start(f32[48,3072]{1,0:T(8,128)S(1)} %get-tuple-element.340) | copy-start | bytes 1769476
  459.2 551.2 %reduce-scatter.43.cloned.1.call-start = ((), (), s32[]{:S(2)}) async-start(), calls=%async_computation.31 | async-start | bytes 2949120 | tf_op jit(solution)/shard_map/reduce_scatter | solution.py:454
  463.0 548.9 %reduce-scatter.41.cloned.1.call-start = ((), (), s32[]{:S(2)}) async-start(), calls=%async_computation.30 | async-start | bytes 2949120 | tf_op jit(solution)/shard_map/reduce_scatter | solution.py:451
  530.0 483.5 %reduce-scatter.39.cloned.1.call-start = ((), (), s32[]{:S(2)}) async-start(), calls=%async_computation.29 | async-start | bytes 2949120 | tf_op jit(solution)/shard_map/reduce_scatter | solution.py:446
  537.6 477.4 %reduce-scatter.37.cloned.1.call-start = ((), (), s32[]{:S(2)}) async-start(), calls=%async_computation.28 | async-start | bytes 2949120 | tf_op jit(solution)/shard_map/reduce_scatter | solution.py:443
  546.8 469.7 %reduce-scatter.35.cloned.1.call-start = ((), (), s32[]{:S(2)}) async-start(), calls=%async_computation.27 | async-start | bytes 2949120 | tf_op jit(solution)/shard_map/reduce_scatter | solution.py:440
  556.3 461.8 %reduce-scatter.33.cloned.1.call-start = ((), (), s32[]{:S(2)}) async-start(), calls=%async_computation.26 | async-start | bytes 2949120 | tf_op jit(solution)/shard_map/reduce_scatter | solution.py:437
  563.0 456.6 %reduce-scatter.47.cloned.1.call-start = ((), (), s32[]{:S(2)}) async-start(), calls=%async_computation.33 | async-start | bytes 11796480 | tf_op jit(solution)/shard_map/reduce_scatter | solution.py:461
  568.1 453.2 %reduce-scatter.45.cloned.1.call-start = ((), (), s32[]{:S(2)}) async-start(), calls=%async_computation.32 | async-start | bytes 11796480 | tf_op jit(solution)/shard_map/reduce_scatter | solution.py:458
  574.5 448.5 %reduce-scatter.29.cloned.1.call-start = ((), (), s32[]{:S(2)}) async-start(), calls=%async_computation.24 | async-start | bytes 2433024 | tf_op jit(solution)/shard_map/reduce_scatter | solution.py:432
  595.2 515.8 %reduce-scatter.31.cloned.1.call-start = ((), (), s32[]{:S(2)}) async-start(), calls=%async_computation.25 | async-start | bytes 2433024 | tf_op jit(solution)/shard_map/reduce_scatter | solution.py:433
  620.3 10.6 copy-start.95
  620.3 594.8 %reduce-scatter.23.cloned.1.call-start = ((), (), s32[]{:S(2)}) async-start(), calls=%async_computation.21 | async-start | bytes 2433024 | tf_op jit(solution)/shard_map/reduce_scatter | solution.py:426
  620.5 10.3 copy-start.8
  620.5 10.3 copy-start.12
  647.9 671.7 %reduce-scatter.21.cloned.1.call-start = ((), (), s32[]{:S(2)}) async-start(), calls=%async_computation.20 | async-start | bytes 2433024 | tf_op jit(solution)/shard_map/reduce_scatter | solution.py:425
  689.8 733.6 %reduce-scatter.19.cloned.1.call-start = ((), (), s32[]{:S(2)}) async-start(), calls=%async_computation.19 | async-start | bytes 2433024 | tf_op jit(solution)/shard_map/reduce_scatter | solution.py:424
  690.3 27.5 %copy-start.6 = (bf16[2,512,12,64]{1,0,3,2:T(2,128)(2,1)S(1)}, bf16[2,512,12,64]{1,0,3,2:T(2,128)(2,1)}, u32[]{:S(2)}) copy-start(bf16[2,512,12,64]{1,0,3,2:T(2,128)(2,1)} %reshape.382) | copy-start | bytes 4718596
  732.3 795.7 %reduce-scatter.17.cloned.1.call-start = ((), (), s32[]{:S(2)}) async-start(), calls=%async_computation.18 | async-start | bytes 2433024 | tf_op jit(solution)/shard_map/reduce_scatter | solution.py:423
  745.8 923.3 %reduce-scatter.27.cloned.1.call-start = ((), (), s32[]{:S(2)}) async-start(), calls=%async_computation.23 | async-start | bytes 9732096 | tf_op jit(solution)/shard_map/reduce_scatter | solution.py:430
  761.9 1049.1 %reduce-scatter.25.cloned.1.call-start = ((), (), s32[]{:S(2)}) async-start(), calls=%async_computation.22 | async-start | bytes 9732096 | tf_op jit(solution)/shard_map/reduce_scatter | solution.py:429
  777.4 12.7 copy-start.114
  932.9 9.6 copy-start.40
  933.0 10.7 copy-start.97
  933.0 10.7 copy-start.105
  933.0 53.7 %copy-start.15 = (f32[48,3072]{1,0:T(8,128)S(1)}, f32[48,3072]{1,0:T(8,128)}, u32[]{:S(2)}) copy-start(f32[48,3072]{1,0:T(8,128)} %copy-done.14) | copy-start | bytes 1769476
  933.0 53.7 %copy-start.27 = (f32[48,768]{1,0:T(8,128)S(1)}, f32[48,768]{1,0:T(8,128)}, u32[]{:S(2)}) copy-start(f32[48,768]{1,0:T(8,128)} %copy-done.25) | copy-start | bytes 442372
  991.7 17.9 copy-start.37
  991.7 17.9 copy-start.108
  992.4 818.6 %copy-start.1 = (bf16[768,768]{1,0:T(8,128)(2,1)S(1)}, bf16[768,768]{1,0:T(8,128)(2,1)}, u32[]{:S(2)}) copy-start(bf16[768,768]{1,0:T(8,128)(2,1)} %param.49) | copy-start | bytes 3538948
  (89 other events, 254.9 us)
Sparse Core Ops, SparseCore 0:
  340.8 70.6 all-reduce.14
  459.3 67.0 all-reduce.16
  528.9 32.1 reduce-scatter.42
  563.6 33.0 reduce-scatter.40
  599.1 33.0 reduce-scatter.38
  634.8 33.0 reduce-scatter.36
  670.4 33.0 reduce-scatter.34
  706.2 33.0 reduce-scatter.32
  741.9 78.4 reduce-scatter.46
  822.8 78.4 reduce-scatter.44
  907.2 99.1 reduce-scatter.28
  1012.9 98.0 reduce-scatter.30
  1116.9 98.1 reduce-scatter.22
  1221.6 97.9 reduce-scatter.20
  1325.3 98.0 reduce-scatter.18
  1430.0 97.9 reduce-scatter.16
  1534.3 134.7 reduce-scatter.26
  1676.4 134.5 reduce-scatter.24
where the time goes:
time: 1820 us
  waiting for transfers between devices  917 us (50%)
  local copies, waits for them, and re-layouts  383 us (21%)
  matrix products  287 us (16%)
  blocking collectives  135 us (7%)
  other arithmetic  76 us (4%)
    reduce_scatter x1, waiting for transfers between devices, local(): lax.psum_scatter(enc_terms[7], ('pb', 'pa'), scatter_dimension=0, tiled=T...  142 us
    reduce_scatter x1, waiting for transfers between devices, local(): lax.psum_scatter(enc_terms[8], ('pb', 'pa'), scatter_dimension=0, tiled=T...  141 us
    reduce_scatter x1, waiting for transfers between devices, local(): lax.psum_scatter(enc_terms[1], ('pb', 'pa'), scatter_dimension=0, tiled=T...  105 us
    reduce_scatter x1, waiting for transfers between devices, local(): lax.psum_scatter(enc_terms[3], ('pb', 'pa'), scatter_dimension=0, tiled=T...  105 us
    reduce_scatter x1, waiting for transfers between devices, local(): lax.psum_scatter(enc_terms[4], ('pb', 'pa'), scatter_dimension=0, tiled=T...  104 us
    reduce_scatter x1, waiting for transfers between devices, local(): lax.psum_scatter(enc_terms[2], ('pb', 'pa'), scatter_dimension=0, tiled=T...  104 us
    reduce_scatter x1, waiting for transfers between devices, local(): lax.psum_scatter(enc_terms[11], ('pb', 'pa'), scatter_dimension=0, tiled=...  88 us
    dot_general x14, matrix products, product_tn(): lax.dot_general(left, right, (((0,), (0,)), ((), ())), preferred_element_...  69.2 us
  transfers between devices with their start and end apart: 18, of which 9 were waited for; matrix products, arithmetic and copies ran while one was open for 24% of the time, Pallas kernels for 0%

commit v1 on v0

v1 whole, which is shorter than its diff:
```python
import functools
import math

import jax
import jax.numpy as jnp
import numpy as np
from jax import lax
from jax.experimental import pallas as pl
from jax.experimental.pallas import tpu as pltpu
from jax.sharding import PartitionSpec as P

D = 768
HEADS = 12
HEAD = 64
BUCKETS = 32
PL = 512
ANS = 24

far_distance = 128
epsilon = 1e-06
highest = lax.Precision.HIGHEST


def smooth_unit(values):
    return jax.nn.gelu(values, approximate=True)


def smooth_back(values, grad):
    return jax.vjp(smooth_unit, values)[1](grad)[0]


def bucket_of(offset, bidirectional):
    if bidirectional:
        halves = BUCKETS // 2
        base_bucket = halves if offset > 0 else 0
        distance = abs(offset)
    else:
        halves = BUCKETS
        base_bucket = 0
        distance = max(-offset, 0)
    exact_count = halves // 2
    if distance < exact_count:
        return base_bucket + distance
    scaled = (
        math.log(distance / exact_count)
        / math.log(far_distance / exact_count)
        * (halves - exact_count)
    )
    return base_bucket + min(exact_count + int(scaled), halves - 1)


def causal_onehot(length):
    table = np.zeros((length * length, BUCKETS), np.float32)
    for query_pos in range(length):
        for key_pos in range(length):
            table[query_pos * length + key_pos, bucket_of(key_pos - query_pos, False)] = 1.0
    return table


def to_low(values):
    return values.astype(jnp.bfloat16)


def product(left, right):
    return jnp.dot(left, right, preferred_element_type=jnp.float32)


def product_tn(left, right):
    return lax.dot_general(
        left, right, (((0,), (0,)), ((), ())), preferred_element_type=jnp.float32
    )


def product_nt(left, right):
    return lax.dot_general(
        left, right, (((1,), (1,)), ((), ())), preferred_element_type=jnp.float32
    )


def exact_product(left, right):
    return jnp.dot(left, right.astype(jnp.float32), precision=highest)


def exact_tn(left, right):
    return lax.dot_general(
        left.astype(jnp.float32),
        right.astype(jnp.float32),
        (((0,), (0,)), ((), ())),
        precision=highest,
    )


def exact_nt(left, right):
    return lax.dot_general(
        left, right.astype(jnp.float32), (((1,), (1,)), ((), ())), precision=highest
    )


def norm_forward(values, gain):
    scale = lax.rsqrt(jnp.mean(values * values, axis=-1, keepdims=True) + epsilon)
    return (values * scale * gain, scale)


def norm_backward(values, scale, gain, grad):
    scaled_grad = grad * gain
    gain_grad = jnp.sum(grad * values * scale, axis=0)
    inner = jnp.mean(scaled_grad * values, axis=-1, keepdims=True)
    return (scaled_grad * scale - values * (scale * scale * scale) * inner, gain_grad)


STRIP = 128
WIDE = 1024


def strip_table():
    table = np.zeros((WIDE, BUCKETS), np.float32)
    for place in range(WIDE):
        if place < PL + STRIP * 3:
            offset = PL - STRIP - place
        else:
            offset = PL - STRIP + WIDE - place
        if abs(offset) < PL:
            table[place, bucket_of(offset, True)] = 1.0
    return table


def nn(left, right):
    return lax.dot_general(left, right, (((1,), (0,)), ((), ())), preferred_element_type=jnp.float32)


def head_lanes(values, head):
    lane = lax.broadcasted_iota(jnp.int32, values.shape, 1)
    keep = lane < HEAD if head == 0 else lane >= HEAD
    return jnp.where(keep, values, jnp.zeros_like(values))


def key_mask(length):
    place = lax.broadcasted_iota(jnp.int32, (PL, 1), 0)
    return jnp.where(place < length, 0.0, -1e9)


def build_strip(base_ref, strip_ref):
    for head in range(2):
        row = base_ref[0, head : head + 1, :]
        spread = jnp.broadcast_to(row, (STRIP, WIDE))
        strip_ref[head] = pltpu.roll(spread, 0, 1, stride=1, stride_axis=0)


def attn_forward_kernel(lengths_ref, q_ref, k_ref, v_ref, base_ref, out_ref, lse_ref, strip_ref, score_ref, outT_ref):
    passage = pl.program_id(1)

    @pl.when(passage == 0)
    def _():
        build_strip(base_ref, strip_ref)

    mask = key_mask(lengths_ref[passage])
    q_t = q_ref[...].T
    v_t = v_ref[...].T
    k = k_ref[...]
    blocks = PL // STRIP
    for head in range(2):
        k_head = head_lanes(k, head)
        top = None
        for b in range(blocks):
            rows = slice(b * STRIP, (b + 1) * STRIP)
            start = PL - STRIP - b * STRIP
            s = nn(k_head[rows], q_t) + strip_ref[head, :, start : start + PL] + mask[rows]
            score_ref[head, rows, :] = s
            here = jnp.max(s, axis=0, keepdims=True)
            top = here if top is None else jnp.maximum(top, here)
        total = None
        acc = None
        for b in range(blocks):
            rows = slice(b * STRIP, (b + 1) * STRIP)
            e = jnp.exp(score_ref[head, rows, :] - top)
            here = jnp.sum(e, axis=0, keepdims=True)
            total = here if total is None else total + here
            part = nn(v_t[head * HEAD : (head + 1) * HEAD, rows], to_low(e))
            acc = part if acc is None else acc + part
        outT_ref[head * HEAD : (head + 1) * HEAD, :] = to_low(acc * (1.0 / total))
        lse_ref[0, 0, head : head + 1, :] = top + jnp.log(total)
    out_ref[...] = outT_ref[...].T


def attn_forward(lengths, q, k, v, base):
    passages = lengths.shape[0]
    pairs = HEADS // 2
    tile = pl.BlockSpec((PL, 128), lambda h, p, *_: (p, h))
    return pl.pallas_call(
        attn_forward_kernel,
        grid_spec=pltpu.PrefetchScalarGridSpec(
            num_scalar_prefetch=1,
            grid=(pairs, passages),
            in_specs=[tile, tile, tile, pl.BlockSpec((1, 2, WIDE), lambda h, p, *_: (h, 0, 0))],
            out_specs=[tile, pl.BlockSpec((1, 1, 2, PL), lambda h, p, *_: (h, p, 0, 0))],
            scratch_shapes=[
                pltpu.VMEM((2, STRIP, WIDE), jnp.float32),
                pltpu.VMEM((2, PL, PL), jnp.float32),
                pltpu.VMEM((128, PL), jnp.bfloat16),
            ],
        ),
        out_shape=[
            jax.ShapeDtypeStruct((passages * PL, D), jnp.bfloat16),
            jax.ShapeDtypeStruct((pairs, passages, 2, PL), jnp.float32),
        ],
        compiler_params=pltpu.CompilerParams(vmem_limit_bytes=32 * 2**20),
        name="enc_attention",
    )(lengths, q, k, v, base)


def attn_backward_kernel(
    lengths_ref, q_ref, k_ref, v_ref, o_ref, do_ref, lse_ref, base_ref,
    dq_ref, dk_ref, dv_ref, fold_ref,
    strip_ref, gather_ref, dqT_ref,
):
    passage = pl.program_id(1)

    @pl.when(passage == 0)
    def _():
        build_strip(base_ref, strip_ref)
        gather_ref[...] = jnp.zeros_like(gather_ref)

    mask = key_mask(lengths_ref[passage])
    q = q_ref[...]
    k = k_ref[...]
    v = v_ref[...]
    do = do_ref[...]
    q_t = q.T
    k_t = k.T
    do_t = do.T
    o_t = o_ref[...].T
    weighed = do_t.astype(jnp.float32) * o_t.astype(jnp.float32)
    blocks = PL // STRIP
    lane = lax.broadcasted_iota(jnp.int32, (STRIP, 128), 1)
    first = lane < HEAD
    dks = []
    dvs = []
    for head in range(2):
        heads = slice(head * HEAD, (head + 1) * HEAD)
        delta = jnp.sum(weighed[heads], axis=0, keepdims=True)
        lse = lse_ref[0, 0, head : head + 1, :]
        k_head = head_lanes(k, head)
        v_head = head_lanes(v, head)
        acc = None
        for b in range(blocks):
            rows = slice(b * STRIP, (b + 1) * STRIP)
            start = PL - STRIP - b * STRIP
            s = nn(k_head[rows], q_t) + strip_ref[head, :, start : start + PL] + mask[rows]
            p = jnp.exp(s - lse)
            dp = nn(v_head[rows], do_t)
            ds = p * (dp - delta)
            gather_ref[head, :, start : start + PL] += ds
            ds_low = to_low(ds)
            dv_part = nn(to_low(p), do)
            dk_part = nn(ds_low, q)
            if head == 0:
                dvs.append(dv_part)
                dks.append(dk_part)
            else:
                dv_ref[rows, :] = to_low(jnp.where(first, dvs[b], dv_part))
                dk_ref[rows, :] = to_low(jnp.where(first, dks[b], dk_part))
            part = nn(k_t[heads, rows], ds_low)
            acc = part if acc is None else acc + part
        dqT_ref[heads, :] = to_low(0.125 * acc)
    dq_ref[...] = dqT_ref[...].T

    @pl.when(passage == pl.num_programs(1) - 1)
    def _():
        row = lax.broadcasted_iota(jnp.int32, (8, WIDE), 0)
        for head in range(2):
            total = gather_ref[head, 0:8, :]
            for group in range(1, STRIP // 8):
                total = total + pltpu.roll(gather_ref[head, group * 8 : group * 8 + 8, :], WIDE - group * 8, 1)
            for bit in (1, 2, 4):
                total = jnp.where((row // bit) % 2 == 1, pltpu.roll(total, WIDE - bit, 1), total)
            fold_ref[0, head : head + 1, :] = jnp.sum(total, axis=0, keepdims=True)


def attn_backward(lengths, q, k, v, o, do, lse, base):
    passages = lengths.shape[0]
    pairs = HEADS // 2
    tile = pl.BlockSpec((PL, 128), lambda h, p, *_: (p, h))
    row = pl.BlockSpec((1, 2, WIDE), lambda h, p, *_: (h, 0, 0))
    big = jax.ShapeDtypeStruct((passages * PL, D), jnp.bfloat16)
    return pl.pallas_call(
        attn_backward_kernel,
        grid_spec=pltpu.PrefetchScalarGridSpec(
            num_scalar_prefetch=1,
            grid=(pairs, passages),
            in_specs=[tile] * 5 + [pl.BlockSpec((1, 1, 2, PL), lambda h, p, *_: (h, p, 0, 0)), row],
            out_specs=[tile, tile, tile, row],
            scratch_shapes=[
                pltpu.VMEM((2, STRIP, WIDE), jnp.float32),
                pltpu.VMEM((2, STRIP, WIDE), jnp.float32),
                pltpu.VMEM((128, PL), jnp.bfloat16),
            ],
        ),
        out_shape=[big, big, big, jax.ShapeDtypeStruct((pairs, 2, WIDE), jnp.float32)],
        compiler_params=pltpu.CompilerParams(vmem_limit_bytes=32 * 2**20),
        name="enc_attention_back",
    )(lengths, q, k, v, o, do, lse, base)


MIB = 2**20


def nt(left, right):
    return lax.dot_general(left, right, (((1,), (1,)), ((), ())), preferred_element_type=jnp.float32)


def rms(values, gain):
    scale = lax.rsqrt(jnp.mean(values * values, axis=-1, keepdims=True) + epsilon)
    return values * scale * gain, scale


def rms_back(values, scale, gain, grad):
    scaled = grad * gain
    gain_grad = jnp.sum(grad * values * scale, axis=0, keepdims=True)
    inner = jnp.mean(scaled * values, axis=-1, keepdims=True)
    return scaled * scale - values * (scale * scale * scale) * inner, gain_grad


def gelu_both(v):
    c = math.sqrt(2.0 / math.pi)
    square = v * v
    t = jnp.tanh(v * (c + (c * 0.044715) * square))
    half = 0.5 + 0.5 * t
    slope = half + (half * (1.0 - t)) * v * (c + (3.0 * 0.044715 * c) * square)
    return v * half, slope


def whole(array):
    return pl.BlockSpec(array.shape, lambda *_: (0,) * array.ndim)


def rows_of(tile, width):
    return pl.BlockSpec((tile, width), lambda i: (i, 0))


def sds(shape, kind):
    return jax.ShapeDtypeStruct(shape, kind)


def params(mib):
    return pltpu.CompilerParams(vmem_limit_bytes=mib * MIB)


def qkv_kernel(x_ref, gain_ref, wq_ref, wk_ref, wv_ref, low_ref, q_ref, k_ref, v_ref):
    normed, _ = rms(x_ref[...].astype(jnp.float32), gain_ref[...])
    low = to_low(normed)
    low_ref[...] = low
    q_ref[...] = to_low(0.125 * to_low(nn(low, wq_ref[...])).astype(jnp.float32))
    k_ref[...] = to_low(nn(low, wk_ref[...]))
    v_ref[...] = to_low(nn(low, wv_ref[...]))


def qkv_forward(x, gain, wq, wk, wv):
    tokens = x.shape[0]
    tile = 256
    big = sds((tokens, D), jnp.bfloat16)
    return pl.pallas_call(
        qkv_kernel,
        grid=(tokens // tile,),
        in_specs=[rows_of(tile, D)] + [whole(a) for a in (gain, wq, wk, wv)],
        out_specs=[rows_of(tile, D)] * 4,
        out_shape=[big] * 4,
        compiler_params=params(40),
        name="enc_qkv",
    )(x, gain, wq, wk, wv)


def post_kernel(
    x_ref, att_ref, gain_ffn_ref, gain_final_ref, wo_ref, win_ref, wout_ref, wck_ref, wcv_ref,
    mid_ref, ffn_low_ref, hidden_ref, slope_ref, y_ref, out_ref, final_low_ref, ck_ref, cv_ref,
):
    mid = x_ref[...].astype(jnp.float32) + nn(att_ref[...], wo_ref[...])
    mid_ref[...] = mid
    normed, _ = rms(mid, gain_ffn_ref[...])
    low = to_low(normed)
    ffn_low_ref[...] = low
    y = mid
    width = 768
    for c in range(win_ref.shape[1] // width):
        cols = slice(c * width, (c + 1) * width)
        hidden, slope = gelu_both(nn(low, win_ref[:, cols]))
        hidden = to_low(hidden)
        hidden_ref[:, cols] = hidden
        slope_ref[:, cols] = to_low(slope)
        y = y + nn(hidden, wout_ref[cols, :])
    y_ref[...] = y
    out_ref[...] = to_low(y)
    final, _ = rms(y, gain_final_ref[...])
    final = to_low(final)
    final_low_ref[...] = final
    ck_ref[...] = to_low(nn(final, wck_ref[...]))
    cv_ref[...] = to_low(nn(final, wcv_ref[...]))


def post_forward(x, att, gain_ffn, gain_final, wo, win, wout, wck, wcv):
    tokens = x.shape[0]
    tile = 256
    ff = win.shape[1]
    low = sds((tokens, D), jnp.bfloat16)
    wide = sds((tokens, ff), jnp.bfloat16)
    full = sds((tokens, D), jnp.float32)
    d = rows_of(tile, D)
    f = rows_of(tile, ff)
    return pl.pallas_call(
        post_kernel,
        grid=(tokens // tile,),
        in_specs=[d, d] + [whole(a) for a in (gain_ffn, gain_final, wo, win, wout, wck, wcv)],
        out_specs=[d, d, f, f, d, d, d, d, d],
        out_shape=[full, low, wide, wide, full, low, low, low, low],
        compiler_params=params(56),
        name="enc_post",
    )(x, att, gain_ffn, gain_final, wo, win, wout, wck, wcv)


def back_kernel(
    gkv_ref, y_ref, mid_ref, slope_ref, cot_ref, gain_ffn_ref, gain_final_ref,
    wck_ref, wcv_ref, wout_ref, win_ref, wo_ref,
    eout_ref, epre_ref, emid_ref, grad_mid_ref, att_grad_ref, gain_final_grad_ref, gain_ffn_grad_ref,
):
    @pl.when(pl.program_id(0) == 0)
    def _():
        gain_final_grad_ref[...] = jnp.zeros_like(gain_final_grad_ref)
        gain_ffn_grad_ref[...] = jnp.zeros_like(gain_ffn_grad_ref)

    y = y_ref[...]
    scale = lax.rsqrt(jnp.mean(y * y, axis=-1, keepdims=True) + epsilon)
    final_back = nt(gkv_ref[0], wck_ref[...]) + nt(gkv_ref[1], wcv_ref[...])
    back, gain_grad = rms_back(y, scale, gain_final_ref[...], final_back)
    gain_final_grad_ref[...] += gain_grad
    grad_y = cot_ref[...].astype(jnp.float32) + back
    eout = to_low(grad_y)
    eout_ref[...] = eout
    width = 768
    acc = None
    for c in range(win_ref.shape[1] // width):
        cols = slice(c * width, (c + 1) * width)
        epre = to_low(slope_ref[:, cols].astype(jnp.float32) * nt(eout, wout_ref[cols, :]))
        epre_ref[:, cols] = epre
        part = nt(epre, win_ref[:, cols])
        acc = part if acc is None else acc + part
    mid = mid_ref[...]
    scale = lax.rsqrt(jnp.mean(mid * mid, axis=-1, keepdims=True) + epsilon)
    back, gain_grad = rms_back(mid, scale, gain_ffn_ref[...], acc)
    gain_ffn_grad_ref[...] += gain_grad
    grad_mid = grad_y + back
    grad_mid_ref[...] = grad_mid
    emid = to_low(grad_mid)
    emid_ref[...] = emid
    att_grad_ref[...] = to_low(nt(emid, wo_ref[...]))


def post_backward(gkv, y, mid, slope, cot, gain_ffn, gain_final, wck, wcv, wout, win, wo):
    tokens = y.shape[0]
    tile = 256
    ff = win.shape[1]
    low = sds((tokens, D), jnp.bfloat16)
    d = rows_of(tile, D)
    f = rows_of(tile, ff)
    gain = pl.BlockSpec((1, D), lambda i: (0, 0))
    return pl.pallas_call(
        back_kernel,
        grid=(tokens // tile,),
        in_specs=[pl.BlockSpec((2, tile, D), lambda i: (0, i, 0)), d, d, f, d]
        + [whole(a) for a in (gain_ffn, gain_final, wck, wcv, wout, win, wo)],
        out_specs=[d, f, d, d, d, gain, gain],
        out_shape=[low, sds((tokens, ff), jnp.bfloat16), low, sds((tokens, D), jnp.float32), low]
        + [sds((1, D), jnp.float32)] * 2,
        compiler_params=params(56),
        name="enc_post_back",
    )(gkv, y, mid, slope, cot, gain_ffn, gain_final, wck, wcv, wout, win, wo)


def qkv_back_kernel(dq_ref, dk_ref, dv_ref, x_ref, grad_mid_ref, gain_ref, wq_ref, wk_ref, wv_ref, out_ref, gain_grad_ref):
    @pl.when(pl.program_id(0) == 0)
    def _():
        gain_grad_ref[...] = jnp.zeros_like(gain_grad_ref)

    x = x_ref[...].astype(jnp.float32)
    scale = lax.rsqrt(jnp.mean(x * x, axis=-1, keepdims=True) + epsilon)
    grad = nt(dq_ref[...], wq_ref[...]) + nt(dk_ref[...], wk_ref[...]) + nt(dv_ref[...], wv_ref[...])
    back, gain_grad = rms_back(x, scale, gain_ref[...], grad)
    gain_grad_ref[...] += gain_grad
    out_ref[...] = grad_mid_ref[...] + back


def qkv_backward(dq, dk, dv, x, grad_mid, gain, wq, wk, wv):
    tokens = x.shape[0]
    tile = 256
    d = rows_of(tile, D)
    return pl.pallas_call(
        qkv_back_kernel,
        grid=(tokens // tile,),
        in_specs=[d] * 5 + [whole(a) for a in (gain, wq, wk, wv)],
        out_specs=[d, pl.BlockSpec((1, D), lambda i: (0, 0))],
        out_shape=[sds((tokens, D), jnp.float32), sds((1, D), jnp.float32)],
        compiler_params=params(40),
        name="enc_qkv_back",
    )(dq, dk, dv, x, grad_mid, gain, wq, wk, wv)


def weight_grad_kernel(rows, pb, pa, tiles, per_chain, table_ref, left_ref, *refs):
    rights = refs[: len(tiles)]
    keep_ref, send_ref, turned_ref = refs[len(tiles) :]
    step = pl.program_id(0)
    depth, height = left_ref.shape

    @pl.when(step == 0)
    def _():
        for c in range(height // 256):
            cols = slice(c * 256, (c + 1) * 256)
            turned_ref[cols, :] = left_ref[:, cols].T

    core = table_ref[0, 0]
    chain = step // per_chain
    half_rows = pa * rows

    def work(right):
        for y in range(pb // 2):
            low_part = nn(turned_ref[2 * y * half_rows : (2 * y + 1) * half_rows, :], right)
            high_part = nn(turned_ref[(2 * y + 1) * half_rows : (2 * y + 2) * half_rows, :], right)
            mine = jnp.where(core == 0, low_part, high_part)
            other = jnp.where(core == 0, high_part, low_part)
            for a in range(pa):
                slot = table_ref[chain + 1, y * pa + a]
                keep_ref[slot] = mine[a * rows : (a + 1) * rows]
                send_ref[slot] = other[a * rows : (a + 1) * rows]

    first = 0
    for right_ref, count in zip(rights, tiles):
        if len(tiles) == 1:
            work(right_ref[...])
        else:
            @pl.when((step >= first) & (step < first + count))
            def _(right_ref=right_ref):
                work(right_ref[...])
        first += count


def weight_grad(table, left, rights, pb, pa, width, per_chain):
    tokens, height = left.shape
    rows = height // (pb * pa)
    tiles = [r.shape[1] // width for r in rights]
    total = sum(tiles)
    firsts = np.cumsum([0] + tiles)[:-1]

    def spec(first, count):
        return pl.BlockSpec((tokens, width), lambda i, *_: (0, jnp.clip(i - int(first), 0, count - 1)))

    half = pb * pa // 2
    out = pl.BlockSpec((half, rows, width), lambda i, *_: (0, 0, i))
    shape = sds((half, rows, total * width), jnp.float32)
    return pl.pallas_call(
        functools.partial(weight_grad_kernel, rows, pb, pa, tiles, per_chain),
        grid_spec=pltpu.PrefetchScalarGridSpec(
            num_scalar_prefetch=1,
            grid=(total,),
            in_specs=[pl.BlockSpec((tokens, height), lambda i, *_: (0, 0))] + [spec(f, c) for f, c in zip(firsts, tiles)],
            out_specs=[out, out],
            scratch_shapes=[pltpu.VMEM((height, tokens), jnp.bfloat16)],
        ),
        out_shape=[shape, shape],
        compiler_params=params(56),
        name="weight_grad",
    )(table, left, *rights)


PACK = 896


def permitted_mask(question_ref, length_ref, answer_rows, passages):
    row = lax.broadcasted_iota(jnp.int32, (answer_rows, PL), 0)
    place = lax.broadcasted_iota(jnp.int32, (answer_rows, PL), 1)
    whose = row // ANS
    return jnp.concatenate(
        [(whose == question_ref[p]) & (place < length_ref[p]) for p in range(passages)], axis=1
    )


def cross_part_kernel(question_ref, length_ref, q_ref, ck_ref, cv_ref, part_ref):
    rows = q_ref.shape[0]
    mask = permitted_mask(question_ref, length_ref, rows, ck_ref.shape[0] // PL)
    lane = lax.broadcasted_iota(jnp.int32, (rows, 128), 1)
    stats = jnp.zeros((rows, 128), jnp.float32)
    for pair in range(HEADS // 2):
        cols = slice(pair * 128, (pair + 1) * 128)
        q = q_ref[:, cols]
        k = ck_ref[:, cols]
        v = cv_ref[:, cols]
        outs = []
        for head in range(2):
            s = jnp.where(mask, 0.125 * nt(head_lanes(q, head), k), -1e9)
            top = jnp.max(s, axis=1, keepdims=True)
            e = jnp.exp(s - top)
            total = jnp.sum(e, axis=1, keepdims=True)
            outs.append(nn(to_low(e), v))
            place = 2 * pair + head
            stats = jnp.where(lane == place, top, jnp.where(lane == HEADS + place, total, stats))
        part_ref[:, cols] = jnp.where(lane < HEAD, outs[0], outs[1])
    part_ref[:, D:] = stats


def cross_part(question_of, lengths, q, ck, cv):
    vmem = pl.BlockSpec(memory_space=pltpu.VMEM)
    smem = pl.BlockSpec(memory_space=pltpu.SMEM)
    return pl.pallas_call(
        cross_part_kernel,
        in_specs=[smem, smem, vmem, vmem, vmem],
        out_specs=vmem,
        out_shape=sds((q.shape[0], PACK), jnp.float32),
        compiler_params=params(40),
        name="cross_part",
    )(question_of, lengths, q, ck, cv)


def over_heads(stats, rows):
    lane = lax.broadcasted_iota(jnp.int32, (rows, 128), 1)
    return jnp.concatenate(
        [jnp.where(lane < HEAD, stats[:, 2 * g : 2 * g + 1], stats[:, 2 * g + 1 : 2 * g + 2]) for g in range(HEADS // 2)],
        axis=1,
    )


def merge_kernel(pa, part_ref, out_ref, recv_ref, mine_ref, send_sem, recv_sem, send2_sem, recv2_sem):
    me = lax.axis_index("pa")
    rows = part_ref.shape[1]
    barrier = pltpu.get_barrier_semaphore()
    for off in range(1, pa):
        pl.semaphore_signal(barrier, inc=1, device_id={"pa": lax.rem(me + off, pa)}, device_id_type=pl.DeviceIdType.MESH)
    pl.semaphore_wait(barrier, pa - 1)

    def first(off):
        peer = lax.rem(me + off, pa)
        return pltpu.make_async_remote_copy(
            src_ref=part_ref.at[peer], dst_ref=recv_ref.at[off], send_sem=send_sem.at[off], recv_sem=recv_sem.at[off],
            device_id={"pa": peer}, device_id_type=pl.DeviceIdType.MESH,
        )

    def second(off):
        peer = lax.rem(me + off, pa)
        return pltpu.make_async_remote_copy(
            src_ref=mine_ref, dst_ref=out_ref.at[me], send_sem=send2_sem.at[off], recv_sem=recv2_sem.at[off],
            device_id={"pa": peer}, device_id_type=pl.DeviceIdType.MESH,
        )

    for off in range(1, pa):
        first(off).start()
    recv_ref[0] = part_ref[me]
    for off in range(1, pa):
        first(off).wait()
    tops = [recv_ref[i, :, D : D + 128][:, :HEADS] for i in range(pa)]
    top = tops[0]
    for t in tops[1:]:
        top = jnp.maximum(top, t)
    total = jnp.zeros((rows, HEADS), jnp.float32)
    acc = jnp.zeros((rows, D), jnp.float32)
    for i in range(pa):
        w = jnp.exp(tops[i] - top)
        total = total + w * recv_ref[i, :, D : D + 128][:, HEADS : 2 * HEADS]
        acc = acc + over_heads(w, rows) * recv_ref[i, :, :D]
    mine_ref[:, :D] = acc / over_heads(total, rows)
    lse = top + jnp.log(total)
    mine_ref[:, D:] = jnp.concatenate([lse, jnp.zeros((rows, 128 - HEADS), jnp.float32)], axis=1)
    for off in range(1, pa):
        second(off).start()
    out_ref[me] = mine_ref[...]
    for off in range(1, pa):
        second(off).wait()


def merge(part, pa):
    answer_rows = part.shape[0]
    rows = answer_rows // pa
    block = (pa, rows, PACK)
    vmem = pl.BlockSpec(memory_space=pltpu.VMEM)
    out = pl.pallas_call(
        functools.partial(merge_kernel, pa),
        in_specs=[vmem],
        out_specs=vmem,
        out_shape=sds(block, jnp.float32),
        scratch_shapes=[
            pltpu.VMEM(block, jnp.float32),
            pltpu.VMEM((rows, PACK), jnp.float32),
            pltpu.SemaphoreType.DMA((pa,)),
            pltpu.SemaphoreType.DMA((pa,)),
            pltpu.SemaphoreType.DMA((pa,)),
            pltpu.SemaphoreType.DMA((pa,)),
        ],
        compiler_params=pltpu.CompilerParams(collective_id=0, has_side_effects=True, vmem_limit_bytes=16 * MIB),
        name="cross_merge",
    )(part.reshape(block))
    return out.reshape(answer_rows, PACK)


def cross_back_kernel(question_ref, length_ref, q_ref, ck_ref, cv_ref, grad_ref, att_ref, lse_ref, gq_ref, gkv_ref):
    rows = q_ref.shape[0]
    mask = permitted_mask(question_ref, length_ref, rows, ck_ref.shape[0] // PL)
    lane = lax.broadcasted_iota(jnp.int32, (rows, 128), 1)
    for pair in range(HEADS // 2):
        cols = slice(pair * 128, (pair + 1) * 128)
        q = q_ref[:, cols]
        k = ck_ref[:, cols]
        v = cv_ref[:, cols]
        g = grad_ref[:, cols]
        weighed = g.astype(jnp.float32) * att_ref[:, cols]
        gqs = []
        scores = []
        probs = []
        for head in range(2):
            place = 2 * pair + head
            s = jnp.where(mask, 0.125 * nt(head_lanes(q, head), k), -1e9)
            p = jnp.exp(s - lse_ref[:, place : place + 1])
            dp = nt(head_lanes(g, head), v)
            delta = jnp.sum(head_lanes(weighed, head), axis=1, keepdims=True)
            ds = to_low(p * (dp - delta))
            gqs.append(nn(ds, k))
            scores.append(ds)
            probs.append(to_low(p))
        gq_ref[:, cols] = 0.125 * jnp.where(lane < HEAD, gqs[0], gqs[1])
        both_q = jnp.concatenate([head_lanes(q, 0), head_lanes(q, 1)], axis=0)
        both_g = jnp.concatenate([head_lanes(g, 0), head_lanes(g, 1)], axis=0)
        gkv_ref[0, :, cols] = to_low(0.125 * product_tn(jnp.concatenate(scores, axis=0), both_q))
        gkv_ref[1, :, cols] = to_low(product_tn(jnp.concatenate(probs, axis=0), both_g))


def cross_back(question_of, lengths, q, ck, cv, grad, att, lse):
    vmem = pl.BlockSpec(memory_space=pltpu.VMEM)
    smem = pl.BlockSpec(memory_space=pltpu.SMEM)
    return pl.pallas_call(
        cross_back_kernel,
        in_specs=[smem, smem] + [vmem] * 6,
        out_specs=[vmem, vmem],
        out_shape=[sds((q.shape[0], D), jnp.float32), sds((2, ck.shape[0], D), jnp.bfloat16)],
        compiler_params=params(40),
        name="cross_back",
    )(question_of, lengths, q, ck, cv, grad, att, lse)


def bits_of(mesh_sizes):
    pb, pa = mesh_sizes
    pb_bits = pb.bit_length() - 1
    pa_bits = pa.bit_length() - 1
    ys = [("pb", b) for b in range(1, pb_bits)]
    xs = [("pa", b) for b in range(pa_bits - 2)]
    zs = [("pa", b) for b in range(pa_bits - 2, pa_bits)]
    return xs, ys, zs


def orders_of(mesh_sizes):
    xs, ys, zs = bits_of(mesh_sizes)
    return (xs + ys + zs, ys + xs + zs, zs[:1] + xs + ys + zs[1:])


def exchange_table(mesh_sizes, orders):
    pb, pa = mesh_sizes
    pb_me = lax.axis_index("pb")
    pa_me = lax.axis_index("pa")
    cells = np.arange(pb * pa // 2)
    pb_of = jnp.asarray(cells // pa * 2)
    pa_of = jnp.asarray(cells % pa)
    rows = [jnp.full((cells.size,), pb_me % 2, jnp.int32)]
    for order in orders:
        slot = jnp.zeros((cells.size,), jnp.int32)
        for axis, bit in order:
            far = ((pb_of if axis == "pb" else pa_of) >> bit) ^ ((pb_me if axis == "pb" else pa_me) >> bit)
            slot = slot * 2 + (far & 1).astype(jnp.int32)
        rows.append(slot)
    return jnp.stack(rows)


def swap(values, axis, bit):
    size = lax.axis_size(axis)
    return lax.ppermute(values, axis, [(i, i ^ (1 << bit)) for i in range(size)])


def summed(parts, first, last):
    total = parts[0][first:last]
    for part in parts[1:]:
        total = total + part[first:last]
    return total


def scatter_chain(parts, order):
    count = parts[0].shape[0]
    for axis, bit in order:
        count //= 2
        received = swap(summed(parts, count, 2 * count), axis, bit)
        parts = [part[:count] for part in parts] + [received]
    return summed(parts, 0, 1)[0]


def scatter(pieces, orders, widths=None):
    keep, send = pieces
    received = swap(send, "pb", 0)
    if widths is None:
        return scatter_chain([keep, received], orders[0])
    first = 0
    done = []
    for order, width in zip(orders, widths):
        cols = slice(first, first + width)
        done.append(scatter_chain([keep[:, :, cols], received[:, :, cols]], order))
        first += width
    return jnp.concatenate(done, axis=1)


def scatter_small(values, orders, mesh_sizes):
    pb, pa = mesh_sizes
    full = [("pb", 0)] + list(orders[0])
    count = pb * pa
    width = -(-values.shape[1] // 128) * 128
    values = jnp.pad(values, ((0, 0), (0, width - values.shape[1])))
    pb_me = lax.axis_index("pb")
    pa_me = lax.axis_index("pa")
    cells = np.arange(count)
    pb_of = jnp.zeros((count,), jnp.int32)
    pa_of = jnp.zeros((count,), jnp.int32)
    for place, (axis, bit) in enumerate(full):
        one = jnp.asarray((cells >> (len(full) - 1 - place) & 1) << bit, jnp.int32)
        if axis == "pb":
            pb_of = pb_of + one
        else:
            pa_of = pa_of + one
    shard = (pb_of ^ pb_me) * pa + (pa_of ^ pa_me)
    ordered = jnp.take(values, shard, axis=0).reshape(count, width // 128, 128)
    return scatter_chain([ordered], full).reshape(width)


def local(
    pb, pa,
    enc_in, dec_in, question_of, lengths, enc_gain_attn, enc_query, enc_key, enc_value, enc_output, enc_bias,
    enc_gain_ffn, enc_ff_in, enc_ff_out, enc_gain_final, cross_key, cross_value, dec_gain_self, dec_query, dec_key,
    dec_value, dec_output, dec_bias, dec_gain_cross, cross_query, cross_output, dec_gain_ffn, dec_ff_in, dec_ff_out,
    enc_cot, dec_cot,
):
    sizes = (pb, pa)
    orders = orders_of(sizes)
    answer_rows = dec_in.shape[0]
    questions = answer_rows // ANS
    gain_attn, gain_ffn, gain_final = (g.astype(jnp.float32)[None] for g in (enc_gain_attn, enc_gain_ffn, enc_gain_final))
    gain_self = dec_gain_self.astype(jnp.float32)
    gain_cross = dec_gain_cross.astype(jnp.float32)
    gain_dffn = dec_gain_ffn.astype(jnp.float32)
    table = exchange_table(sizes, orders)
    enc_table = jnp.asarray(strip_table())
    dec_table = jnp.asarray(causal_onehot(ANS))
    base = jnp.dot(enc_table, enc_bias.astype(jnp.float32), precision=highest).T.reshape(HEADS // 2, 2, WIDE)

    attn_low, enc_queries, enc_keys, enc_values = qkv_forward(enc_in, gain_attn, enc_query, enc_key, enc_value)
    enc_attended, enc_lse = attn_forward(lengths, enc_queries, enc_keys, enc_values, base)
    enc_mid, ffn_low, enc_hidden, enc_slope, enc_y, enc_out, final_low, cross_keys, cross_values = post_forward(
        enc_in, enc_attended, gain_ffn, gain_final, enc_output, enc_ff_in, enc_ff_out, cross_key, cross_value
    )

    dec_x = dec_in.astype(jnp.float32)
    self_normed, self_scale = norm_forward(dec_x, gain_self)
    self_low = to_low(self_normed)
    dec_queries = to_low(product(self_low, dec_query)).reshape(questions, ANS, HEADS, HEAD)
    dec_keys = to_low(product(self_low, dec_key)).reshape(questions, ANS, HEADS, HEAD)
    dec_values = to_low(product(self_low, dec_value)).reshape(questions, ANS, HEADS, HEAD)
    dec_position = jnp.dot(dec_table, dec_bias.astype(jnp.float32), precision=highest).T.reshape(HEADS, ANS, ANS)
    causal = jnp.arange(ANS)[None, :] <= jnp.arange(ANS)[:, None]
    raw_scores = 0.125 * jnp.einsum("qihd,qjhd->qhij", dec_queries, dec_keys, preferred_element_type=jnp.float32)
    self_scores = jnp.where(causal, raw_scores + dec_position[None], -1000000000.0)
    self_top = jnp.max(self_scores, axis=-1, keepdims=True)
    self_exp = jnp.exp(self_scores - self_top)
    dec_probs = self_exp / jnp.sum(self_exp, axis=-1, keepdims=True)
    dec_attended = to_low(
        jnp.einsum("qhij,qjhd->qihd", to_low(dec_probs), dec_values, preferred_element_type=jnp.float32).reshape(answer_rows, D)
    )
    dec_mid = dec_x + product(dec_attended, dec_output)
    cross_normed, cross_scale = norm_forward(dec_mid, gain_cross)
    cross_low = to_low(cross_normed)
    cross_queries = to_low(product(cross_low, cross_query))

    merged = merge(cross_part(question_of, lengths, cross_queries, cross_keys, cross_values), pa)
    cross_attended = merged[:, :D]
    dec_after = dec_mid + exact_product(cross_attended, cross_output)
    dffn_normed, dffn_scale = norm_forward(dec_after, gain_dffn)
    dffn_low = to_low(dffn_normed)
    dec_pre = product(dffn_low, dec_ff_in)
    dec_hidden = to_low(smooth_unit(dec_pre))
    dec_y = dec_after + product(dec_hidden, dec_ff_out)
    grad_dec_y = dec_cot.astype(jnp.float32)
    out_grad_low = dec_cot
    pre_grad_low = to_low(smooth_back(dec_pre, product_nt(out_grad_low, dec_ff_out)))
    back_after, dec_gain_ffn_grad = norm_backward(dec_after, dffn_scale, gain_dffn, product_nt(pre_grad_low, dec_ff_in))
    grad_after = grad_dec_y + back_after
    after_low = to_low(grad_after)
    cross_att_grad = to_low(product_nt(after_low, cross_output))

    query_part, grad_cross = cross_back(
        question_of, lengths, cross_queries, cross_keys, cross_values, cross_att_grad, cross_attended, merged[:, D:]
    )
    grad_cross_q = lax.psum(query_part, "pa")

    eout_low, epre_low, emid_low, grad_enc_mid, enc_att_grad, final_gain_grad, ffn_gain_grad = post_backward(
        grad_cross, enc_y, enc_mid, enc_slope, enc_cot, gain_ffn, gain_final, cross_key, cross_value, enc_ff_out, enc_ff_in, enc_output
    )
    cross_terms = scatter(weight_grad(table, final_low, [grad_cross[0], grad_cross[1]], pb, pa, 256, 99), orders)
    ff_out_term = scatter(weight_grad(table[jnp.array([0, 2])], enc_hidden, [eout_low], pb, pa, 256, 99), orders[1:])
    ff_in_term = scatter(weight_grad(table, ffn_low, [epre_low], pb, pa, 512, 2), orders, (1024, 1024, 1024))
    output_term = scatter(weight_grad(table[jnp.array([0, 3])], enc_attended, [emid_low], pb, pa, 256, 99), orders[2:])
    grad_eq, grad_ek, grad_ev, fold = attn_backward(
        lengths, enc_queries, enc_keys, enc_values, enc_attended, enc_att_grad, enc_lse, base
    )
    attn_terms = scatter(
        weight_grad(table, attn_low, [grad_eq, grad_ek, grad_ev], pb, pa, 256, 3), orders, (768, 768, 768)
    )
    enc_in_grad, attn_gain_grad = qkv_backward(
        grad_eq, grad_ek, grad_ev, enc_in, grad_enc_mid, gain_attn, enc_query, enc_key, enc_value
    )
    enc_bias_grad = jnp.dot(fold.reshape(HEADS, WIDE), enc_table, precision=highest).T.reshape(BUCKETS * HEADS)

    back_mid, dec_gain_cross_grad = norm_backward(dec_mid, cross_scale, gain_cross, exact_nt(grad_cross_q, cross_query))
    grad_mid = grad_after + back_mid
    mid_low = to_low(grad_mid)
    dec_att_grad = to_low(product_nt(mid_low, dec_output)).reshape(questions, ANS, HEADS, HEAD)
    dec_dprob = jnp.einsum("qihd,qjhd->qhij", dec_att_grad, dec_values, preferred_element_type=jnp.float32)
    dec_dscore = dec_probs * (dec_dprob - jnp.sum(dec_probs * dec_dprob, axis=-1, keepdims=True))
    dec_bias_grad = jnp.dot(
        jnp.sum(dec_dscore, axis=0).reshape(HEADS, ANS * ANS), dec_table, precision=highest
    ).T.reshape(BUCKETS * HEADS)
    low_dscore = to_low(dec_dscore)
    grad_dq = to_low(
        0.125 * jnp.einsum("qhij,qjhd->qihd", low_dscore, dec_keys, preferred_element_type=jnp.float32)
    ).reshape(answer_rows, D)
    grad_dk = to_low(
        0.125 * jnp.einsum("qhij,qihd->qjhd", low_dscore, dec_queries, preferred_element_type=jnp.float32)
    ).reshape(answer_rows, D)
    grad_dv = to_low(
        jnp.einsum("qhij,qihd->qjhd", to_low(dec_probs), dec_att_grad, preferred_element_type=jnp.float32)
    ).reshape(answer_rows, D)
    self_back = product_nt(grad_dq, dec_query) + product_nt(grad_dk, dec_key) + product_nt(grad_dv, dec_value)
    back_dec_in, dec_gain_self_grad = norm_backward(dec_x, self_scale, gain_self, self_back)
    dec_in_grad = grad_mid + back_dec_in

    column = lax.axis_index("pa")

    def own_columns(values):
        rows = values.shape[1] // (pb * pa)
        cut = values.reshape(answer_rows, pb, pa, rows)
        return lax.dynamic_slice_in_dim(cut, column, 1, 2).reshape(answer_rows, pb * rows)

    def dec_term(left, right, times=product_tn):
        left = own_columns(left)
        return times(left, right).reshape(pb, left.shape[1] // pb, right.shape[1])

    ff_rows = dec_hidden.shape[1]
    thin = [
        dec_term(self_low, grad_dq),
        dec_term(self_low, grad_dk),
        dec_term(self_low, grad_dv),
        dec_term(dec_attended, mid_low),
        dec_term(cross_low, grad_cross_q, exact_tn),
        dec_term(cross_attended, after_low, exact_tn),
        dec_term(dec_hidden, out_grad_low),
    ]
    wide = dec_term(dffn_low, pre_grad_low)
    thin += [wide[:, :, c * D : (c + 1) * D] for c in range(ff_rows // D)]
    heights = [t.shape[1] for t in thin]
    dec_sum = lax.psum_scatter(jnp.concatenate(thin, axis=1), "pb", scatter_dimension=0, tiled=False)
    cuts = np.cumsum([0] + heights)
    got = [dec_sum[a:b] for a, b in zip(cuts[:-1], cuts[1:])]
    dec_ff_in_grad = jnp.concatenate(got[7:], axis=1)

    shards = pb * pa
    share = 1.0 / pa
    small_list = [
        attn_gain_grad[0], ffn_gain_grad[0], final_gain_grad[0], enc_bias_grad,
        dec_gain_self_grad * share, dec_gain_cross_grad * share, dec_gain_ffn_grad * share, dec_bias_grad * share,
    ]
    small_rows = [s.shape[0] // shards for s in small_list]
    small = scatter_small(jnp.concatenate([s.reshape(shards, -1) for s in small_list], axis=1), orders, sizes)
    cuts = np.cumsum([0] + small_rows)
    smalls = [small[a:b] for a, b in zip(cuts[:-1], cuts[1:])]

    return (
        enc_out, to_low(dec_y), enc_in_grad, dec_in_grad,
        smalls[0], attn_terms[:, :D], attn_terms[:, D : 2 * D], attn_terms[:, 2 * D :], output_term, smalls[3],
        smalls[1], ff_in_term, ff_out_term, smalls[2], cross_terms[:, :D], cross_terms[:, D:],
        smalls[4], got[0], got[1], got[2], got[3], smalls[7], smalls[5], got[4], got[5], smalls[6], dec_ff_in_grad, got[6],
    )


def solution(mesh):
    pb, pa = mesh.shape["pb"], mesh.shape["pa"]
    rows = P(("pb", "pa"), None)
    flat = P(("pb", "pa"))
    dec = P("pb", None)
    return jax.shard_map(
        functools.partial(local, pb, pa),
        mesh=mesh,
        in_specs=(rows, dec, flat, flat) + (P(),) * 24 + (rows, dec),
        out_specs=(rows, dec, rows, dec)
        + (flat, rows, rows, rows, rows, flat, flat, rows, rows, flat, rows, rows)
        + (flat, rows, rows, rows, rows, flat, flat, rows, rows, flat, rows, rows),
        check_vma=False,
    )
```

time: 1820 us -> 597 us (0.33)
  waiting for transfers between devices: 917 us -> 127 us
  local copies, waits for them, and re-layouts: 383 us -> 79.7 us
  matrix products: 287 us -> 52 us
  Pallas kernels: 0 us -> 202 us
  blocking collectives: 135 us -> 0 us
  starting transfers between devices: 2.33 us -> 63.3 us
  other arithmetic: 76 us -> 47.1 us
    reduce_scatter x16 -> x1, waiting for transfers between devices: 788 us -> 0.01 us  [local(): lax.psum_scatter(jnp.concatenate(thin, axis=1), 'pb', scatter_dimension=0...]
    pallas_call x0 -> x14, Pallas kernels: none -> 202 us  [the longest x5 53 us: weight_grad(): pl.pallas_call(functools.partial(weight_grad_kernel, rows, pb, pa, tiles,...]
    reshape x12 -> x6, local copies, waits for them, and re-layouts: 151 us -> 1.35 us  [the longest x1 1.13 us: own_columns(): cut = values.reshape(answer_rows, pb, pa, rows)]
    ppermute x0 -> x46, waiting for transfers between devices: none -> 127 us  [swap(): return lax.ppermute(values, axis, [(i, i ^ 1 << bit) for i in range(size)])]
    dot_general x15 -> x3, matrix products: 89.4 us -> 2.11 us  [the longest x1 1.58 us: local(): jnp.dot(fold.reshape(HEADS, WIDE), enc_table, precision=highest)]
    psum x1 -> x0, waiting for transfers between devices: 65.5 us -> none  [local(): cross_attended = lax.psum(partial_out, 'pa')]
    psum x1, waiting for transfers between devices: 63.3 us -> 0.01 us  [local(): grad_cross_q = lax.psum(query_part, 'pa')]
    ppermute x0 -> x46, starting transfers between devices: none -> 63.2 us  [swap(): return lax.ppermute(values, axis, [(i, i ^ 1 << bit) for i in range(size)])]
  transfers between devices with their start and end apart: 18 -> 48, of which waited for: 9 -> 22; matrix products, arithmetic and copies ran while one was open for 24% -> 20% of each run, Pallas kernels for 0% -> 21%
where the time goes in v1:
time: 597 us; the launch traced here: 587 us
  Pallas kernels  202 us (34%)
  waiting for transfers between devices  127 us (21%)
  local copies, waits for them, and re-layouts  79.7 us (13%)
  starting transfers between devices  63.3 us (11%)
  matrix products  52 us (9%)
  other arithmetic  47.1 us (8%)
  between operations  15.8 us (3%)
    ppermute x46, waiting for transfers between devices, swap(): return lax.ppermute(values, axis, [(i, i ^ 1 << bit) for i in range(size)])  127 us
    ppermute x46, starting transfers between devices, swap(): return lax.ppermute(values, axis, [(i, i ^ 1 << bit) for i in range(size)])  63.2 us
    pallas_call x5, Pallas kernels, weight_grad(): pl.pallas_call(functools.partial(weight_grad_kernel, rows, pb, pa, tiles,...  53 us
    pallas_call x1, Pallas kernels, attn_backward(): pl.pallas_call(attn_backward_kernel, grid_spec=pltpu.PrefetchScalarGridSp...  38.6 us
    unnamed x217, local copies, waits for them, and re-layouts  31 us
    pallas_call x1, Pallas kernels, post_backward(): pl.pallas_call(back_kernel, grid=(tokens // tile,), in_specs=[pl.BlockSpe...  26.3 us
    pallas_call x1, Pallas kernels, post_forward(): pl.pallas_call(post_kernel, grid=(tokens // tile,), in_specs=[d, d] + [wh...  25.9 us
    add x24, other arithmetic, summed(): total = total + part[first:last]  25.7 us
  transfers between devices with their start and end apart: 48, of which 22 were waited for; matrix products, arithmetic and copies ran while one was open for 20% of the time, Pallas kernels for 21%

profile of v1, /device:TPU:0, one launch (start us, length us, event | category | flops | bytes accessed | tf_op | source)
XLA Modules:
  0.0 587.0 jit_solution(5544392082643303275)
XLA Ops:
  26.3 4.7 enc_qkv.1
  32.2 19.3 %enc_attention.1 = (bf16[1024,768]{1,0:T(8,128)(2,1)S(1)}, f32[6,2,2,512]{3,2,1,0:T(2,128)S(1)}) custom-call(s32[2]{0:T(128)S(1)} %copy-done.31, bf16[1024,768]{1,0:T(8,128)(2,1)S(1)} %get-tuple-element.68.q_ref, bf16[1024,768]{1,0:T(8,128)(2,1)S(1)} %get-tuple-element.69.k_ref, bf16[1024,768]{1,0:T(8,128)(2,1)S(1)} %get-tuple-element.70.v_ref, ...), custom_call_target="tpu_custom_call" | custom-call | tf_op jit(solution)/shard_map/enc_attention/pallas_call | solution.py:189
  52.7 25.9 %enc_post.1 = (f32[1024,768]{1,0:T(8,128)}, bf16[1024,768]{1,0:T(8,128)(2,1)}, bf16[1024,3072]{1,0:T(8,128)(2,1)}, bf16[1024,3072]{1,0:T(8,128)(2,1)}, f32[1024,...) custom-call(bf16[1024,768]{1,0:T(8,128)(2,1)} %x_ref.5, ...), custom_call_target="tpu_custom_call" | custom-call | tf_op jit(solution)/shard_map/enc_post/pallas_call | solution.py:408
  81.4 4.6 cross_part.1
  86.1 17.7 %cross_merge.1 = f32[8,6,896]{2,1,0:T(8,128)S(1)} custom-call(f32[8,6,896]{2,1,0:T(8,128)S(1)} %reshape.256.part_ref), custom_call_target="tpu_custom_call" | custom-call | tf_op jit(solution)/shard_map/cross_merge/pallas_call | solution.py:679
  104.8 4.3 fusion.98
  109.2 4.3 fusion.19
  115.9 5.7 cross_back.1
  123.5 3.8 slice_bitcast_fusion
  128.0 9.4 %weight_grad.9 = (f32[16,24,1536]{2,1,0:T(8,128)}, f32[16,24,1536]{2,1,0:T(8,128)}) custom-call(s32[4,16]{1,0:T(4,128)} %pad_add_fusion.table_ref, bf16[1024,768]{1,0:T(8,128)(2,1)} %get-tuple-element.105.left_ref, bf16[1024,768]{1,0:T(8,128)(2,1)} %get-tuple-element.145.refs_0_, bf16[1024,768]{1,0:T(8,128)(2,1)} %get-tuple-element.144.refs_1_), custom_call_target="tpu_custom_call" | custom-call | tf_op jit(solution)/shard_map/weight_grad/pallas_call | solution.py:556
  138.5 26.3 %enc_post_back.1 = (bf16[1024,768]{1,0:T(8,128)(2,1)}, bf16[1024,3072]{1,0:T(8,128)(2,1)}, bf16[1024,768]{1,0:T(8,128)(2,1)}, f32[1024,768]{1,0:T(8,128)}, bf16[...) custom-call(bf16[2,1024,768]{2,1,0:T(8,128)(2,1)} %copy-done.5, f32[1024,768]{1,0:T(8,128)} %get-tuple-element.76.y_ref, ...), custom_call_target="tpu_custom_call" | custom-call | tf_op jit(solution)/shard_map/enc_post_back/pallas_call | solution.py:464
  164.8 12.7 %weight_grad.8 = (f32[16,96,768]{2,1,0:T(8,128)}, f32[16,96,768]{2,1,0:T(8,128)}) custom-call(s32[2,16]{1,0:T(2,128)} %gather_fusion.2, bf16[1024,3072]{1,0:T(8,128)(2,1)} %get-tuple-element.101.left_ref, bf16[1024,768]{1,0:T(8,128)(2,1)} %get-tuple-element.102.refs_0_), custom_call_target="tpu_custom_call" | custom-call | tf_op jit(solution)/shard_map/weight_grad/pallas_call | solution.py:556
  179.1 6.4 %weight_grad.6 = (f32[16,24,768]{2,1,0:T(8,128)}, f32[16,24,768]{2,1,0:T(8,128)}) custom-call(s32[2,16]{1,0:T(2,128)} %gather_fusion.1, bf16[1024,768]{1,0:T(8,128)(2,1)} %copy-done.1, bf16[1024,768]{1,0:T(8,128)(2,1)} %get-tuple-element.94.refs_0_), custom_call_target="tpu_custom_call" | custom-call | tf_op jit(solution)/shard_map/weight_grad/pallas_call | solution.py:556
  189.7 38.6 %enc_attention_back.1 = (bf16[1024,768]{1,0:T(8,128)(2,1)S(1)}, bf16[1024,768]{1,0:T(8,128)(2,1)S(1)}, bf16[1024,768]{1,0:T(8,128)(2,1)S(1)}, f32[6,2,1024]{2,1,0:T(2,128)S(1)}) custom-call(s32[2]{0:T(128)S(1)} %copy-done.31, bf16[1024,768]{1,0:T(8,128)(2,1)S(1)} %copy-done.11, bf16[1024,768]{1,0:T(8,128)(2,1)S(1)} %copy-done.13, ...), custom_call_target="tpu_custom_call" | custom-call | tf_op jit(solution)/shard_map/enc_attention_back/pallas_call | solution.py:285
  231.8 12.3 %weight_grad.5 = (f32[16,24,2304]{2,1,0:T(8,128)}, f32[16,24,2304]{2,1,0:T(8,128)}) custom-call(s32[4,16]{1,0:T(4,128)} %pad_add_fusion.table_ref, bf16[1024,768]{1,0:T(8,128)(2,1)} %copy-done.29, bf16[1024,768]{1,0:T(8,128)(2,1)} %copy-done.16, bf16[1024,768]{1,0:T(8,128)(2,1)} %copy-done.18, bf16[1024,768]{1,0:T(8,128)(2,1)} %copy-done.20), custom_call_target="tpu_custom_call" | custom-call | tf_op jit(solution)/shard_map/weight_grad/pallas_call | solution.py:556
  248.2 3.9 fusion.11
  252.1 2.5 fusion.22
  273.6 6.2 %enc_qkv_back.1 = (f32[1024,768]{1,0:T(8,128)}, f32[1,768]{1,0:T(1,128)S(1)}) custom-call(bf16[1024,768]{1,0:T(8,128)(2,1)S(1)} %copy-done.17, bf16[1024,768]{1,0:T(8,128)(2,1)S(1)} %copy-done.19, bf16[1024,768]{1,0:T(8,128)(2,1)S(1)} %copy-done.21, bf16[1024,768]{1,0:T(8,128)(2,1)S(1)} %copy-done.4, f32[1024,768]{1,0:T(8,128)S(1)} %copy-done.28, ...), custom_call_target="tpu_custom_call" | custom-call | tf_op jit(solution)/shard_map/enc_qkv_back/pallas_call | solution.py:494
  282.6 12.3 %weight_grad.7 = (f32[16,24,3072]{2,1,0:T(8,128)}, f32[16,24,3072]{2,1,0:T(8,128)}) custom-call(s32[4,16]{1,0:T(4,128)} %pad_add_fusion.table_ref, bf16[1024,768]{1,0:T(8,128)(2,1)} %get-tuple-element.97.left_ref, bf16[1024,3072]{1,0:T(8,128)(2,1)} %get-tuple-element.98.refs_0_), custom_call_target="tpu_custom_call" | custom-call | tf_op jit(solution)/shard_map/weight_grad/pallas_call | solution.py:556
  295.5 2.7 multiply_reduce_fusion.2
  302.8 2.0 fusion.10
  362.9 10.7 %collective-permute-done.19 = f32[8,24,768]{2,1,0:T(8,128)S(1)} collective-permute-done((f32[8,24,768]{2,1,0:T(8,128)S(1)}, f32[8,24,768]{2,1,0:T(8,128)S(1)}, u32[]{:S(2)}, u32[]{:S(2)}) %collective-permute-start.19) | collective-permute-done | bytes 589856 | tf_op jit(solution)/shard_map/ppermute | solution.py:776
  373.6 3.6 collective-permute-start.4
  380.8 13.9 %collective-permute-done.20 = f32[4,24,768]{2,1,0:T(8,128)S(1)} collective-permute-done((f32[4,24,768]{2,1,0:T(8,128)S(1)}, f32[4,24,768]{2,1,0:T(8,128)S(1)}, u32[]{:S(2)}, u32[]{:S(2)}) %collective-permute-start.20) | collective-permute-done | bytes 294944 | tf_op jit(solution)/shard_map/ppermute | solution.py:776
  399.8 2.3 collective-permute-done.21
  403.0 2.6 collective-permute-start.22
  409.3 2.0 collective-permute-start.14
  411.2 3.5 collective-permute-done.43
  418.1 8.1 %collective-permute-done.10 = f32[8,24,768]{2,1,0:T(8,128)S(1)} collective-permute-done((f32[8,24,768]{2,1,0:T(8,128)S(1)}, f32[8,24,768]{2,1,0:T(8,128)S(1)}, u32[]{:S(2)}, u32[]{:S(2)}) %collective-permute-start.10) | collective-permute-done | bytes 589856 | tf_op jit(solution)/shard_map/ppermute | solution.py:776
  432.0 2.0 slice_add_fusion
  436.8 2.2 collective-permute-done.11
  439.9 5.5 collective-permute-done.15
  447.2 3.8 collective-permute-start.45
  452.2 8.7 %collective-permute-done.45 = f32[1,24,1536]{2,1,0:T(8,128)S(1)} collective-permute-done((f32[1,24,1536]{2,1,0:T(8,128)S(1)}, f32[1,24,1536]{2,1,0:T(8,128)S(1)}, u32[]{:S(2)}, u32[]{:S(2)}) %collective-permute-start.45) | collective-permute-done | bytes 147488 | tf_op jit(solution)/shard_map/ppermute | solution.py:776
  462.8 45.7 %collective-permute-done.28 = f32[8,24,1024]{2,1,0:T(8,128)S(1)} collective-permute-done((f32[8,24,1024]{2,1,0:T(8,128)S(1)}, f32[8,24,1024]{2,1,0:T(8,128)S(1)}, u32[]{:S(2)}, u32[]{:S(2)}) %collective-permute-start.28) | collective-permute-done | bytes 786464 | tf_op jit(solution)/shard_map/ppermute | solution.py:776
  514.2 2.4 collective-permute-done.25
  517.6 4.0 collective-permute-start.17
  525.8 2.0 collective-permute-done.26
  530.3 4.5 collective-permute-start.27
  536.5 2.9 collective-permute-start.9
  541.1 2.9 collective-permute-start.35
  547.3 2.2 collective-permute-done.35
  551.5 2.1 collective-permute-start.39
  556.1 2.0 slice_bitcast_fusion.6
  558.0 6.5 %collective-permute-done.39 = f32[2,96,768]{2,1,0:T(8,128)S(1)} collective-permute-done((f32[2,96,768]{2,1,0:T(8,128)S(1)}, f32[2,96,768]{2,1,0:T(8,128)S(1)}, u32[]{:S(2)}, u32[]{:S(2)}) %collective-permute-start.39) | collective-permute-done | bytes 589856 | tf_op jit(solution)/shard_map/ppermute | solution.py:776
  565.7 4.5 collective-permute-start.40
  571.0 6.8 %collective-permute-done.40 = f32[1,96,768]{2,1,0:T(8,128)S(1)} collective-permute-done((f32[1,96,768]{2,1,0:T(8,128)S(1)}, f32[1,96,768]{2,1,0:T(8,128)S(1)}, u32[]{:S(2)}, u32[]{:S(2)}) %collective-permute-start.40) | collective-permute-done | bytes 294944 | tf_op jit(solution)/shard_map/ppermute | solution.py:776
  577.7 1.9 fusion.21
  (451 shorter events, 186.5 us)
Async XLA Ops:
  7.2 288.3 %all-reduce.3.cloned.1.call-start = ((), (), s32[]{:S(2)}) async-start(), calls=%async_computation.1 | async-start | bytes 294912 | tf_op jit(solution)/shard_map/psum | solution.py:897
  123.4 431.0 %reduce-scatter.2.cloned.1.call-start = ((), (), s32[]{:S(2)}) async-start(), calls=%async_computation.2 | async-start | bytes 5160960 | tf_op jit(solution)/shard_map/reduce_scatter | solution.py:964
  137.3 220.7 %collective-permute-start.41 = (f32[16,24,1536]{2,1,0:T(8,128)}, f32[16,24,1536]{2,1,0:T(8,128)}, u32[]{:S(2)}, u32[]{:S(2)}) collective-permute-start(f32[16,24,1536]{2,1,0:T(8,128)} %get-tuple-element.107), channel_id=1, source_target_pairs={{0,8},{8,0},{16,24},{24,16},{1,9},{9,1},{17,25},{25,17},{2,10},{10... | collective-permute-start | bytes 7077896 | tf_op jit(solution)/shard_map/ppermute | solution.py:776
  177.5 253.6 %collective-permute-start.36 = (f32[16,96,768]{2,1,0:T(8,128)}, f32[16,96,768]{2,1,0:T(8,128)}, u32[]{:S(2)}, u32[]{:S(2)}) collective-permute-start(f32[16,96,768]{2,1,0:T(8,128)} %get-tuple-element.104), channel_id=1, source_target_pairs={{0,8},{8,0},{16,24},{24,16},{1,9},{9,1},{17,25},{25,17},{2,10},{10... | collective-permute-start | bytes 14155784 | tf_op jit(solution)/shard_map/ppermute | solution.py:776
  185.5 169.9 %collective-permute-start.18 = (f32[16,24,768]{2,1,0:T(8,128)}, f32[16,24,768]{2,1,0:T(8,128)}, u32[]{:S(2)}, u32[]{:S(2)}) collective-permute-start(f32[16,24,768]{2,1,0:T(8,128)} %get-tuple-element.96), channel_id=1, source_target_pairs={{0,8},{8,0},{16,24},{24,16},{1,9},{9,1},{17,25},{25,17},{2,10},{10... | collective-permute-start | bytes 3538952 | tf_op jit(solution)/shard_map/ppermute | solution.py:776
  244.2 161.4 %collective-permute-start.5 = (f32[16,24,2304]{2,1,0:T(8,128)}, f32[16,24,2304]{2,1,0:T(8,128)}, u32[]{:S(2)}, u32[]{:S(2)}) collective-permute-start(f32[16,24,2304]{2,1,0:T(8,128)} %get-tuple-element.93), channel_id=1, source_target_pairs={{0,8},{8,0},{16,24},{24,16},{1,9},{9,1},{17,25},{25,17},{2,10},{10... | collective-permute-start | bytes 10616840 | tf_op jit(solution)/shard_map/ppermute | solution.py:776
  329.3 14.6 %collective-permute-start = (f32[16,2,128]{2,1,0:T(2,128)}, f32[16,2,128]{2,1,0:T(2,128)}, u32[]{:S(2)}, u32[]{:S(2)}) collective-permute-start(f32[16,2,128]{2,1,0:T(2,128)} %slice.1029), channel_id=1, source_target_pairs={{0,8},{8,0},{16,24},{24,16},{1,9},{9,1},{17,25},{25,17},{2,10},{10... | collective-permute-start | bytes 49160 | tf_op jit(solution)/shard_map/ppermute | solution.py:776
  345.4 4.0 collective-permute-start.1
  350.6 4.1 collective-permute-start.2
  354.7 79.3 %collective-permute-start.23 = (f32[16,24,3072]{2,1,0:T(8,128)}, f32[16,24,3072]{2,1,0:T(8,128)S(1)}, u32[]{:S(2)}, u32[]{:S(2)}) collective-permute-start(f32[16,24,3072]{2,1,0:T(8,128)} %get-tuple-element.100), channel_id=1, source_target_pairs={{0,8},{8,0},{16,24},{24,16},{1,9},{9,1},{17,25},{25,17},{2,10},{10... | collective-permute-start | bytes 14155784 | tf_op jit(solution)/shard_map/ppermute | solution.py:776
  355.4 5.1 collective-permute-start.3
  358.0 15.5 %collective-permute-start.19 = (f32[8,24,768]{2,1,0:T(8,128)S(1)}, f32[8,24,768]{2,1,0:T(8,128)S(1)}, u32[]{:S(2)}, u32[]{:S(2)}) collective-permute-start(f32[8,24,768]{2,1,0:T(8,128)S(1)} %slice_add_fusion.12), channel_id=1, source_target_pairs={{0,2},{1,3},{2,0},{3,1},{4,6},{5,7},{6,4},{7,5},{8,10},{9,11},{10,... | collective-permute-start | bytes 1769480 | tf_op jit(solution)/shard_map/ppermute | solution.py:776
  360.5 36.5 %collective-permute-start.42 = (f32[8,24,1536]{2,1,0:T(8,128)S(1)}, f32[8,24,1536]{2,1,0:T(8,128)S(1)}, u32[]{:S(2)}, u32[]{:S(2)}) collective-permute-start(f32[8,24,1536]{2,1,0:T(8,128)S(1)} %slice_add_fusion.1), channel_id=1, source_target_pairs={{0,1},{1,0},{2,3},{3,2},{4,5},{5,4},{6,7},{7,6},{8,9},{9,8},{10,11... | collective-permute-start | bytes 3538952 | tf_op jit(solution)/shard_map/ppermute | solution.py:776
  373.6 5.1 collective-permute-start.4
  378.7 16.0 %collective-permute-start.20 = (f32[4,24,768]{2,1,0:T(8,128)S(1)}, f32[4,24,768]{2,1,0:T(8,128)S(1)}, u32[]{:S(2)}, u32[]{:S(2)}) collective-permute-start(f32[4,24,768]{2,1,0:T(8,128)S(1)} %slice_add_fusion.33), channel_id=1, source_target_pairs={{0,1},{1,0},{2,3},{3,2},{4,5},{5,4},{6,7},{7,6},{8,9},{9,8},{10,11... | collective-permute-start | bytes 884744 | tf_op jit(solution)/shard_map/ppermute | solution.py:776
  395.7 6.4 %collective-permute-start.21 = (f32[2,24,768]{2,1,0:T(8,128)S(1)}, f32[2,24,768]{2,1,0:T(8,128)S(1)}, u32[]{:S(2)}, u32[]{:S(2)}) collective-permute-start(f32[2,24,768]{2,1,0:T(8,128)S(1)} %slice_add_fusion.58), channel_id=1, source_target_pairs={{0,16},{8,24},{16,0},{24,8},{1,17},{9,25},{17,1},{25,9},{2,18},{10... | collective-permute-start | bytes 442376 | tf_op jit(solution)/shard_map/ppermute | solution.py:776
  398.4 16.4 %collective-permute-start.43 = (f32[4,24,1536]{2,1,0:T(8,128)S(1)}, f32[4,24,1536]{2,1,0:T(8,128)S(1)}, u32[]{:S(2)}, u32[]{:S(2)}) collective-permute-start(f32[4,24,1536]{2,1,0:T(8,128)S(1)} %slice_add_fusion.7), channel_id=1, source_target_pairs={{0,16},{8,24},{16,0},{24,8},{1,17},{9,25},{17,1},{25,9},{2,18},{10... | collective-permute-start | bytes 1769480 | tf_op jit(solution)/shard_map/ppermute | solution.py:776
  403.0 6.3 %collective-permute-start.22 = (f32[1,24,768]{2,1,0:T(8,128)S(1)}, f32[1,24,768]{2,1,0:T(8,128)S(1)}, u32[]{:S(2)}, u32[]{:S(2)}) collective-permute-start(f32[1,24,768]{2,1,0:T(8,128)S(1)} %slice_add_fusion.94), channel_id=1, source_target_pairs={{0,4},{1,5},{2,6},{3,7},{4,0},{5,1},{6,2},{7,3},{8,12},{9,13},{10,... | collective-permute-start | bytes 221192 | tf_op jit(solution)/shard_map/ppermute | solution.py:776
  407.4 18.8 %collective-permute-start.10 = (f32[8,24,768]{2,1,0:T(8,128)S(1)}, f32[8,24,768]{2,1,0:T(8,128)S(1)}, u32[]{:S(2)}, u32[]{:S(2)}) collective-permute-start(f32[8,24,768]{2,1,0:T(8,128)S(1)} %get-tuple-element.140), channel_id=1, source_target_pairs={{0,16},{8,24},{16,0},{24,8},{1,17},{9,25},{17,1},{25,9},{2,18},{10... | collective-permute-start | bytes 1769480 | tf_op jit(solution)/shard_map/ppermute | solution.py:776
  409.3 17.9 %collective-permute-start.14 = (f32[8,24,768]{2,1,0:T(8,128)S(1)}, f32[8,24,768]{2,1,0:T(8,128)S(1)}, u32[]{:S(2)}, u32[]{:S(2)}) collective-permute-start(f32[8,24,768]{2,1,0:T(8,128)S(1)} %get-tuple-element.139), channel_id=1, source_target_pairs={{0,2},{1,3},{2,0},{3,1},{4,6},{5,7},{6,4},{7,5},{8,10},{9,11},{10,... | collective-permute-start | bytes 1769480 | tf_op jit(solution)/shard_map/ppermute | solution.py:776
  414.7 13.0 %collective-permute-start.6 = (f32[8,24,768]{2,1,0:T(8,128)S(1)}, f32[8,24,768]{2,1,0:T(8,128)S(1)}, u32[]{:S(2)}, u32[]{:S(2)}) collective-permute-start(f32[8,24,768]{2,1,0:T(8,128)S(1)} %get-tuple-element.141), channel_id=1, source_target_pairs={{0,1},{1,0},{2,3},{3,2},{4,5},{5,4},{6,7},{7,6},{8,9},{9,8},{10,11... | collective-permute-start | bytes 1769480 | tf_op jit(solution)/shard_map/ppermute | solution.py:776
  426.2 9.7 %collective-permute-start.44 = (f32[2,24,1536]{2,1,0:T(8,128)S(1)}, f32[2,24,1536]{2,1,0:T(8,128)S(1)}, u32[]{:S(2)}, u32[]{:S(2)}) collective-permute-start(f32[2,24,1536]{2,1,0:T(8,128)S(1)} %slice_add_fusion.22), channel_id=1, source_target_pairs={{0,2},{1,3},{2,0},{3,1},{4,6},{5,7},{6,4},{7,5},{8,10},{9,11},{10,... | collective-permute-start | bytes 884744 | tf_op jit(solution)/shard_map/ppermute | solution.py:776
  429.0 10.0 %collective-permute-start.11 = (f32[4,24,768]{2,1,0:T(8,128)S(1)}, f32[4,24,768]{2,1,0:T(8,128)S(1)}, u32[]{:S(2)}, u32[]{:S(2)}) collective-permute-start(f32[4,24,768]{2,1,0:T(8,128)S(1)} %get-tuple-element.137), channel_id=1, source_target_pairs={{0,1},{1,0},{2,3},{3,2},{4,5},{5,4},{6,7},{7,6},{8,9},{9,8},{10,11... | collective-permute-start | bytes 884744 | tf_op jit(solution)/shard_map/ppermute | solution.py:776
  429.9 15.4 %collective-permute-start.15 = (f32[4,24,768]{2,1,0:T(8,128)S(1)}, f32[4,24,768]{2,1,0:T(8,128)S(1)}, u32[]{:S(2)}, u32[]{:S(2)}) collective-permute-start(f32[4,24,768]{2,1,0:T(8,128)S(1)} %get-tuple-element.136), channel_id=1, source_target_pairs={{0,1},{1,0},{2,3},{3,2},{4,5},{5,4},{6,7},{7,6},{8,9},{9,8},{10,11... | collective-permute-start | bytes 884744 | tf_op jit(solution)/shard_map/ppermute | solution.py:776
  431.1 16.1 %collective-permute-start.7 = (f32[4,24,768]{2,1,0:T(8,128)S(1)}, f32[4,24,768]{2,1,0:T(8,128)S(1)}, u32[]{:S(2)}, u32[]{:S(2)}) collective-permute-start(f32[4,24,768]{2,1,0:T(8,128)S(1)} %get-tuple-element.138), channel_id=1, source_target_pairs={{0,16},{8,24},{16,0},{24,8},{1,17},{9,25},{17,1},{25,9},{2,18},{10... | collective-permute-start | bytes 884744 | tf_op jit(solution)/shard_map/ppermute | solution.py:776
  434.0 89.5 %collective-permute-start.37 = (f32[8,96,768]{2,1,0:T(8,128)S(1)}, f32[8,96,768]{2,1,0:T(8,128)S(1)}, u32[]{:S(2)}, u32[]{:S(2)}) collective-permute-start(f32[8,96,768]{2,1,0:T(8,128)S(1)} %slice_add_fusion), channel_id=1, source_target_pairs={{0,16},{8,24},{16,0},{24,8},{1,17},{9,25},{17,1},{25,9},{2,18},{10... | collective-permute-start | bytes 7077896 | tf_op jit(solution)/shard_map/ppermute | solution.py:776
  435.9 26.9 %collective-permute-start.24 = (f32[8,24,1024]{2,1,0:T(8,128)S(1)}, f32[8,24,1024]{2,1,0:T(8,128)S(1)}, u32[]{:S(2)}, u32[]{:S(2)}) collective-permute-start(f32[8,24,1024]{2,1,0:T(8,128)S(1)} %get-tuple-element.125), channel_id=1, source_target_pairs={{0,1},{1,0},{2,3},{3,2},{4,5},{5,4},{6,7},{7,6},{8,9},{9,8},{10,11... | collective-permute-start | bytes 2359304 | tf_op jit(solution)/shard_map/ppermute | solution.py:776
  439.0 69.4 %collective-permute-start.28 = (f32[8,24,1024]{2,1,0:T(8,128)S(1)}, f32[8,24,1024]{2,1,0:T(8,128)S(1)}, u32[]{:S(2)}, u32[]{:S(2)}) collective-permute-start(f32[8,24,1024]{2,1,0:T(8,128)S(1)} %get-tuple-element.127), channel_id=1, source_target_pairs={{0,16},{8,24},{16,0},{24,8},{1,17},{9,25},{17,1},{25,9},{2,18},{10... | collective-permute-start | bytes 2359304 | tf_op jit(solution)/shard_map/ppermute | solution.py:776
  445.4 63.1 %collective-permute-start.32 = (f32[8,24,1024]{2,1,0:T(8,128)S(1)}, f32[8,24,1024]{2,1,0:T(8,128)S(1)}, u32[]{:S(2)}, u32[]{:S(2)}) collective-permute-start(f32[8,24,1024]{2,1,0:T(8,128)S(1)} %get-tuple-element.126), channel_id=1, source_target_pairs={{0,2},{1,3},{2,0},{3,1},{4,6},{5,7},{6,4},{7,5},{8,10},{9,11},{10,... | collective-permute-start | bytes 2359304 | tf_op jit(solution)/shard_map/ppermute | solution.py:776
  447.2 13.7 %collective-permute-start.45 = (f32[1,24,1536]{2,1,0:T(8,128)S(1)}, f32[1,24,1536]{2,1,0:T(8,128)S(1)}, u32[]{:S(2)}, u32[]{:S(2)}) collective-permute-start(f32[1,24,1536]{2,1,0:T(8,128)S(1)} %slice_add_fusion.50), channel_id=1, source_target_pairs={{0,4},{1,5},{2,6},{3,7},{4,0},{5,1},{6,2},{7,3},{8,12},{9,13},{10,... | collective-permute-start | bytes 442376 | tf_op jit(solution)/shard_map/ppermute | solution.py:776
  460.9 51.5 %collective-permute-start.16 = (f32[2,24,768]{2,1,0:T(8,128)S(1)}, f32[2,24,768]{2,1,0:T(8,128)S(1)}, u32[]{:S(2)}, u32[]{:S(2)}) collective-permute-start(f32[2,24,768]{2,1,0:T(8,128)S(1)} %get-tuple-element.133), channel_id=1, source_target_pairs={{0,16},{8,24},{16,0},{24,8},{1,17},{9,25},{17,1},{25,9},{2,18},{10... | collective-permute-start | bytes 442376 | tf_op jit(solution)/shard_map/ppermute | solution.py:776
  508.8 7.8 %collective-permute-start.25 = (f32[4,24,1024]{2,1,0:T(8,128)S(1)}, f32[4,24,1024]{2,1,0:T(8,128)S(1)}, u32[]{:S(2)}, u32[]{:S(2)}) collective-permute-start(f32[4,24,1024]{2,1,0:T(8,128)S(1)} %get-tuple-element.122), channel_id=1, source_target_pairs={{0,16},{8,24},{16,0},{24,8},{1,17},{9,25},{17,1},{25,9},{2,18},{10... | collective-permute-start | bytes 1179656 | tf_op jit(solution)/shard_map/ppermute | solution.py:776
  509.7 7.9 %collective-permute-start.29 = (f32[4,24,1024]{2,1,0:T(8,128)S(1)}, f32[4,24,1024]{2,1,0:T(8,128)S(1)}, u32[]{:S(2)}, u32[]{:S(2)}) collective-permute-start(f32[4,24,1024]{2,1,0:T(8,128)S(1)} %get-tuple-element.124), channel_id=1, source_target_pairs={{0,1},{1,0},{2,3},{3,2},{4,5},{5,4},{6,7},{7,6},{8,9},{9,8},{10,11... | collective-permute-start | bytes 1179656 | tf_op jit(solution)/shard_map/ppermute | solution.py:776
  510.6 11.3 %collective-permute-start.33 = (f32[4,24,1024]{2,1,0:T(8,128)S(1)}, f32[4,24,1024]{2,1,0:T(8,128)S(1)}, u32[]{:S(2)}, u32[]{:S(2)}) collective-permute-start(f32[4,24,1024]{2,1,0:T(8,128)S(1)} %get-tuple-element.123), channel_id=1, source_target_pairs={{0,1},{1,0},{2,3},{3,2},{4,5},{5,4},{6,7},{7,6},{8,9},{9,8},{10,11... | collective-permute-start | bytes 1179656 | tf_op jit(solution)/shard_map/ppermute | solution.py:776
  512.4 16.4 %collective-permute-start.12 = (f32[2,24,768]{2,1,0:T(8,128)S(1)}, f32[2,24,768]{2,1,0:T(8,128)S(1)}, u32[]{:S(2)}, u32[]{:S(2)}) collective-permute-start(f32[2,24,768]{2,1,0:T(8,128)S(1)} %get-tuple-element.134), channel_id=1, source_target_pairs={{0,2},{1,3},{2,0},{3,1},{4,6},{5,7},{6,4},{7,5},{8,10},{9,11},{10,... | collective-permute-start | bytes 442376 | tf_op jit(solution)/shard_map/ppermute | solution.py:776
  516.6 13.7 %collective-permute-start.8 = (f32[2,24,768]{2,1,0:T(8,128)S(1)}, f32[2,24,768]{2,1,0:T(8,128)S(1)}, u32[]{:S(2)}, u32[]{:S(2)}) collective-permute-start(f32[2,24,768]{2,1,0:T(8,128)S(1)} %get-tuple-element.135), channel_id=1, source_target_pairs={{0,2},{1,3},{2,0},{3,1},{4,6},{5,7},{6,4},{7,5},{8,10},{9,11},{10,... | collective-permute-start | bytes 442376 | tf_op jit(solution)/shard_map/ppermute | solution.py:776
  517.6 17.2 %collective-permute-start.17 = (f32[1,24,768]{2,1,0:T(8,128)S(1)}, f32[1,24,768]{2,1,0:T(8,128)S(1)}, u32[]{:S(2)}, u32[]{:S(2)}) collective-permute-start(f32[1,24,768]{2,1,0:T(8,128)S(1)} %slice_add_fusion.102), channel_id=1, source_target_pairs={{0,4},{1,5},{2,6},{3,7},{4,0},{5,1},{6,2},{7,3},{8,12},{9,13},{10,... | collective-permute-start | bytes 221192 | tf_op jit(solution)/shard_map/ppermute | solution.py:776
  522.0 5.9 collective-permute-start.26
  523.5 13.0 %collective-permute-start.30 = (f32[2,24,1024]{2,1,0:T(8,128)S(1)}, f32[2,24,1024]{2,1,0:T(8,128)S(1)}, u32[]{:S(2)}, u32[]{:S(2)}) collective-permute-start(f32[2,24,1024]{2,1,0:T(8,128)S(1)} %get-tuple-element.121), channel_id=1, source_target_pairs={{0,2},{1,3},{2,0},{3,1},{4,6},{5,7},{6,4},{7,5},{8,10},{9,11},{10,... | collective-permute-start | bytes 589832 | tf_op jit(solution)/shard_map/ppermute | solution.py:776
  527.9 22.5 %collective-permute-start.38 = (f32[4,96,768]{2,1,0:T(8,128)S(1)}, f32[4,96,768]{2,1,0:T(8,128)S(1)}, u32[]{:S(2)}, u32[]{:S(2)}) collective-permute-start(f32[4,96,768]{2,1,0:T(8,128)S(1)} %slice_add_fusion.2), channel_id=1, source_target_pairs={{0,1},{1,0},{2,3},{3,2},{4,5},{5,4},{6,7},{7,6},{8,9},{9,8},{10,11... | collective-permute-start | bytes 3538952 | tf_op jit(solution)/shard_map/ppermute | solution.py:776
  528.8 10.6 %collective-permute-start.34 = (f32[2,24,1024]{2,1,0:T(8,128)S(1)}, f32[2,24,1024]{2,1,0:T(8,128)S(1)}, u32[]{:S(2)}, u32[]{:S(2)}) collective-permute-start(f32[2,24,1024]{2,1,0:T(8,128)S(1)} %get-tuple-element.120), channel_id=1, source_target_pairs={{0,16},{8,24},{16,0},{24,8},{1,17},{9,25},{17,1},{25,9},{2,18},{10... | collective-permute-start | bytes 589832 | tf_op jit(solution)/shard_map/ppermute | solution.py:776
  530.3 10.6 %collective-permute-start.27 = (f32[1,24,1024]{2,1,0:T(8,128)S(1)}, f32[1,24,1024]{2,1,0:T(8,128)S(1)}, u32[]{:S(2)}, u32[]{:S(2)}) collective-permute-start(f32[1,24,1024]{2,1,0:T(8,128)S(1)} %slice_add_fusion.86), channel_id=1, source_target_pairs={{0,4},{1,5},{2,6},{3,7},{4,0},{5,1},{6,2},{7,3},{8,12},{9,13},{10,... | collective-permute-start | bytes 294920 | tf_op jit(solution)/shard_map/ppermute | solution.py:776
  536.5 7.5 %collective-permute-start.13 = (f32[1,24,768]{2,1,0:T(8,128)S(1)}, f32[1,24,768]{2,1,0:T(8,128)S(1)}, u32[]{:S(2)}, u32[]{:S(2)}) collective-permute-start(f32[1,24,768]{2,1,0:T(8,128)S(1)} %get-tuple-element.131), channel_id=1, source_target_pairs={{0,4},{1,5},{2,6},{3,7},{4,0},{5,1},{6,2},{7,3},{8,12},{9,13},{10,... | collective-permute-start | bytes 221192 | tf_op jit(solution)/shard_map/ppermute | solution.py:776
  536.5 8.0 %collective-permute-start.9 = (f32[1,24,768]{2,1,0:T(8,128)S(1)}, f32[1,24,768]{2,1,0:T(8,128)S(1)}, u32[]{:S(2)}, u32[]{:S(2)}) collective-permute-start(f32[1,24,768]{2,1,0:T(8,128)S(1)} %get-tuple-element.132), channel_id=1, source_target_pairs={{0,4},{1,5},{2,6},{3,7},{4,0},{5,1},{6,2},{7,3},{8,12},{9,13},{10,... | collective-permute-start | bytes 221192 | tf_op jit(solution)/shard_map/ppermute | solution.py:776
  541.1 6.3 %collective-permute-start.31 = (f32[1,24,1024]{2,1,0:T(8,128)S(1)}, f32[1,24,1024]{2,1,0:T(8,128)S(1)}, u32[]{:S(2)}, u32[]{:S(2)}) collective-permute-start(f32[1,24,1024]{2,1,0:T(8,128)S(1)} %get-tuple-element.118), channel_id=1, source_target_pairs={{0,4},{1,5},{2,6},{3,7},{4,0},{5,1},{6,2},{7,3},{8,12},{9,13},{10,... | collective-permute-start | bytes 294920 | tf_op jit(solution)/shard_map/ppermute | solution.py:776
  541.1 8.4 %collective-permute-start.35 = (f32[1,24,1024]{2,1,0:T(8,128)S(1)}, f32[1,24,1024]{2,1,0:T(8,128)S(1)}, u32[]{:S(2)}, u32[]{:S(2)}) collective-permute-start(f32[1,24,1024]{2,1,0:T(8,128)S(1)} %get-tuple-element.117), channel_id=1, source_target_pairs={{0,4},{1,5},{2,6},{3,7},{4,0},{5,1},{6,2},{7,3},{8,12},{9,13},{10,... | collective-permute-start | bytes 294920 | tf_op jit(solution)/shard_map/ppermute | solution.py:776
  551.5 13.0 %collective-permute-start.39 = (f32[2,96,768]{2,1,0:T(8,128)S(1)}, f32[2,96,768]{2,1,0:T(8,128)S(1)}, u32[]{:S(2)}, u32[]{:S(2)}) collective-permute-start(f32[2,96,768]{2,1,0:T(8,128)S(1)} %slice_add_fusion.9), channel_id=1, source_target_pairs={{0,2},{1,3},{2,0},{3,1},{4,6},{5,7},{6,4},{7,5},{8,10},{9,11},{10,... | collective-permute-start | bytes 1769480 | tf_op jit(solution)/shard_map/ppermute | solution.py:776
  565.7 12.0 %collective-permute-start.40 = (f32[1,96,768]{2,1,0:T(8,128)S(1)}, f32[1,96,768]{2,1,0:T(8,128)S(1)}, u32[]{:S(2)}, u32[]{:S(2)}) collective-permute-start(f32[1,96,768]{2,1,0:T(8,128)S(1)} %slice_add_fusion.25), channel_id=1, source_target_pairs={{0,4},{1,5},{2,6},{3,7},{4,0},{5,1},{6,2},{7,3},{8,12},{9,13},{10,... | collective-permute-start | bytes 884744 | tf_op jit(solution)/shard_map/ppermute | solution.py:776
  (107 other events, 914.6 us)
Sparse Core Ops, SparseCore 0:
  123.5 70.9 all-reduce.2
  344.0 47.3 reduce-scatter.1

commit v2 on v1

--- a/solution.py
+++ b/solution.py
@@ -19,14 +19,6 @@
 far_distance = 128
 epsilon = 1e-06
 highest = lax.Precision.HIGHEST
-
-
-def smooth_unit(values):
-    return jax.nn.gelu(values, approximate=True)
-
-
-def smooth_back(values, grad):
-    return jax.vjp(smooth_unit, values)[1](grad)[0]
 
 
 def bucket_of(offset, bidirectional):
@@ -49,63 +41,14 @@
     return base_bucket + min(exact_count + int(scaled), halves - 1)
 
 
-def causal_onehot(length):
-    table = np.zeros((length * length, BUCKETS), np.float32)
-    for query_pos in range(length):
-        for key_pos in range(length):
-            table[query_pos * length + key_pos, bucket_of(key_pos - query_pos, False)] = 1.0
-    return table
-
-
 def to_low(values):
     return values.astype(jnp.bfloat16)
-
-
-def product(left, right):
-    return jnp.dot(left, right, preferred_element_type=jnp.float32)
 
 
 def product_tn(left, right):
     return lax.dot_general(
         left, right, (((0,), (0,)), ((), ())), preferred_element_type=jnp.float32
     )
-
-
-def product_nt(left, right):
-    return lax.dot_general(
-        left, right, (((1,), (1,)), ((), ())), preferred_element_type=jnp.float32
-    )
-
-
-def exact_product(left, right):
-    return jnp.dot(left, right.astype(jnp.float32), precision=highest)
-
-
-def exact_tn(left, right):
-    return lax.dot_general(
-        left.astype(jnp.float32),
-        right.astype(jnp.float32),
-        (((0,), (0,)), ((), ())),
-        precision=highest,
-    )
-
-
-def exact_nt(left, right):
-    return lax.dot_general(
-        left, right.astype(jnp.float32), (((1,), (1,)), ((), ())), precision=highest
-    )
-
-
-def norm_forward(values, gain):
-    scale = lax.rsqrt(jnp.mean(values * values, axis=-1, keepdims=True) + epsilon)
-    return (values * scale * gain, scale)
-
-
-def norm_backward(values, scale, gain, grad):
-    scaled_grad = grad * gain
-    gain_grad = jnp.sum(grad * values * scale, axis=0)
-    inner = jnp.mean(scaled_grad * values, axis=-1, keepdims=True)
-    return (scaled_grad * scale - values * (scale * scale * scale) * inner, gain_grad)
 
 
 STRIP = 128
@@ -209,12 +152,10 @@
 
 
 def attn_backward_kernel(
-    lengths_ref, q_ref, k_ref, v_ref, o_ref, do_ref, lse_ref, base_ref,
+    beside, passage, passages, lengths_ref, q_ref, k_ref, v_ref, o_ref, do_ref, lse_ref, base_ref,
     dq_ref, dk_ref, dv_ref, fold_ref,
     strip_ref, gather_ref, dqT_ref,
 ):
-    passage = pl.program_id(1)
-
     @pl.when(passage == 0)
     def _():
         build_strip(base_ref, strip_ref)
@@ -236,6 +177,7 @@
     dks = []
     dvs = []
     for head in range(2):
+        beside(head)
         heads = slice(head * HEAD, (head + 1) * HEAD)
         delta = jnp.sum(weighed[heads], axis=0, keepdims=True)
         lse = lse_ref[0, 0, head : head + 1, :]
@@ -264,7 +206,7 @@
         dqT_ref[heads, :] = to_low(0.125 * acc)
     dq_ref[...] = dqT_ref[...].T
 
-    @pl.when(passage == pl.num_programs(1) - 1)
+    @pl.when(passage == passages - 1)
     def _():
         row = lax.broadcasted_iota(jnp.int32, (8, WIDE), 0)
         for head in range(2):
@@ -276,31 +218,6 @@
             fold_ref[0, head : head + 1, :] = jnp.sum(total, axis=0, keepdims=True)
 
 
-def attn_backward(lengths, q, k, v, o, do, lse, base):
-    passages = lengths.shape[0]
-    pairs = HEADS // 2
-    tile = pl.BlockSpec((PL, 128), lambda h, p, *_: (p, h))
-    row = pl.BlockSpec((1, 2, WIDE), lambda h, p, *_: (h, 0, 0))
-    big = jax.ShapeDtypeStruct((passages * PL, D), jnp.bfloat16)
-    return pl.pallas_call(
-        attn_backward_kernel,
-        grid_spec=pltpu.PrefetchScalarGridSpec(
-            num_scalar_prefetch=1,
-            grid=(pairs, passages),
-            in_specs=[tile] * 5 + [pl.BlockSpec((1, 1, 2, PL), lambda h, p, *_: (h, p, 0, 0)), row],
-            out_specs=[tile, tile, tile, row],
-            scratch_shapes=[
-                pltpu.VMEM((2, STRIP, WIDE), jnp.float32),
-                pltpu.VMEM((2, STRIP, WIDE), jnp.float32),
-                pltpu.VMEM((128, PL), jnp.bfloat16),
-            ],
-        ),
-        out_shape=[big, big, big, jax.ShapeDtypeStruct((pairs, 2, WIDE), jnp.float32)],
-        compiler_params=pltpu.CompilerParams(vmem_limit_bytes=32 * 2**20),
-        name="enc_attention_back",
-    )(lengths, q, k, v, o, do, lse, base)
-
-
 MIB = 2**20
 
 
@@ -345,10 +262,10 @@
     return pltpu.CompilerParams(vmem_limit_bytes=mib * MIB)
 
 
-def qkv_kernel(x_ref, gain_ref, wq_ref, wk_ref, wv_ref, low_ref, q_ref, k_ref, v_ref):
+def qkv_kernel(x_ref, gain_ref, wq_ref, wk_ref, wv_ref, turned_ref, q_ref, k_ref, v_ref):
     normed, _ = rms(x_ref[...].astype(jnp.float32), gain_ref[...])
     low = to_low(normed)
-    low_ref[...] = low
+    turned_ref[...] = low.T
     q_ref[...] = to_low(0.125 * to_low(nn(low, wq_ref[...])).astype(jnp.float32))
     k_ref[...] = to_low(nn(low, wk_ref[...]))
     v_ref[...] = to_low(nn(low, wv_ref[...]))
@@ -362,8 +279,8 @@
         qkv_kernel,
         grid=(tokens // tile,),
         in_specs=[rows_of(tile, D)] + [whole(a) for a in (gain, wq, wk, wv)],
-        out_specs=[rows_of(tile, D)] * 4,
-        out_shape=[big] * 4,
+        out_specs=[pl.BlockSpec((D, tile), lambda i: (0, i))] + [rows_of(tile, D)] * 3,
+        out_shape=[sds((D, tokens), jnp.bfloat16)] + [big] * 3,
         compiler_params=params(40),
         name="enc_qkv",
     )(x, gain, wq, wk, wv)
@@ -474,8 +391,8 @@
     )(gkv, y, mid, slope, cot, gain_ffn, gain_final, wck, wcv, wout, win, wo)
 
 
-def qkv_back_kernel(dq_ref, dk_ref, dv_ref, x_ref, grad_mid_ref, gain_ref, wq_ref, wk_ref, wv_ref, out_ref, gain_grad_ref):
-    @pl.when(pl.program_id(0) == 0)
+def qkv_back_kernel(opening, dq_ref, dk_ref, dv_ref, x_ref, grad_mid_ref, gain_ref, wq_ref, wk_ref, wv_ref, out_ref, gain_grad_ref):
+    @pl.when(opening)
     def _():
         gain_grad_ref[...] = jnp.zeros_like(gain_grad_ref)
 
@@ -485,21 +402,6 @@
     back, gain_grad = rms_back(x, scale, gain_ref[...], grad)
     gain_grad_ref[...] += gain_grad
     out_ref[...] = grad_mid_ref[...] + back
-
-
-def qkv_backward(dq, dk, dv, x, grad_mid, gain, wq, wk, wv):
-    tokens = x.shape[0]
-    tile = 256
-    d = rows_of(tile, D)
-    return pl.pallas_call(
-        qkv_back_kernel,
-        grid=(tokens // tile,),
-        in_specs=[d] * 5 + [whole(a) for a in (gain, wq, wk, wv)],
-        out_specs=[d, pl.BlockSpec((1, D), lambda i: (0, 0))],
-        out_shape=[sds((tokens, D), jnp.float32), sds((1, D), jnp.float32)],
-        compiler_params=params(40),
-        name="enc_qkv_back",
-    )(dq, dk, dv, x, grad_mid, gain, wq, wk, wv)
 
 
 def weight_grad_kernel(rows, pb, pa, tiles, per_chain, table_ref, left_ref, *refs):
@@ -739,6 +641,265 @@
     )(question_of, lengths, q, ck, cv, grad, att, lse)
 
 
+def causal_row(length):
+    table = np.zeros((128, BUCKETS), np.float32)
+    for back in range(length):
+        table[-back % 128, bucket_of(-back, False)] = 1.0
+    return table
+
+
+def in_three(values):
+    high = to_low(values)
+    rest = values - high.astype(jnp.float32)
+    middle = to_low(rest)
+    return high, middle, to_low(rest - middle.astype(jnp.float32))
+
+
+def dec_pre_kernel(
+    x_ref, gain_self_ref, gain_cross_ref, base_ref, wq_ref, wk_ref, wv_ref, wo_ref, wcq_ref,
+    low_ref, q_ref, k_ref, v_ref, probs_ref, att_ref, mid_ref, cross_low_ref, cross_q_ref,
+):
+    rows = x_ref.shape[0]
+    x = x_ref[...].astype(jnp.float32)
+    normed, _ = rms(x, gain_self_ref[...])
+    low = to_low(normed)
+    low_ref[...] = low
+    q = to_low(0.125 * to_low(nn(low, wq_ref[...])).astype(jnp.float32))
+    k = to_low(nn(low, wk_ref[...]))
+    v = to_low(nn(low, wv_ref[...]))
+    q_ref[...] = q
+    k_ref[...] = k
+    v_ref[...] = v
+    i = lax.broadcasted_iota(jnp.int32, (rows, rows), 0)
+    j = lax.broadcasted_iota(jnp.int32, (rows, rows), 1)
+    mask = (j <= i) & (i // ANS == j // ANS)
+    lane = lax.broadcasted_iota(jnp.int32, (rows, 128), 1)
+    for pair in range(HEADS // 2):
+        cols = slice(pair * 128, (pair + 1) * 128)
+        outs = []
+        for half in range(2):
+            head = 2 * pair + half
+            spread = jnp.broadcast_to(base_ref[head : head + 1, :], (rows, 128))
+            bias = pltpu.roll(spread, 0, 1, stride=1, stride_axis=0)[:, :rows]
+            s = jnp.where(mask, nt(head_lanes(q[:, cols], half), k[:, cols]) + bias, -1e9)
+            e = jnp.exp(s - jnp.max(s, axis=1, keepdims=True))
+            p = e / jnp.sum(e, axis=1, keepdims=True)
+            probs_ref[head] = p
+            outs.append(nn(to_low(p), v[:, cols]))
+        att_ref[:, cols] = to_low(jnp.where(lane < HEAD, outs[0], outs[1]))
+    mid = x + nn(att_ref[...], wo_ref[...])
+    mid_ref[...] = mid
+    normed, _ = rms(mid, gain_cross_ref[...])
+    low = to_low(normed)
+    cross_low_ref[...] = low
+    cross_q_ref[...] = to_low(nn(low, wcq_ref[...]))
+
+
+def in_vmem(kernel, outs, name, *args, smem=0):
+    vmem = pl.BlockSpec(memory_space=pltpu.VMEM)
+    return pl.pallas_call(
+        kernel,
+        in_specs=[pl.BlockSpec(memory_space=pltpu.SMEM)] * smem + [vmem] * (len(args) - smem),
+        out_specs=[vmem] * len(outs),
+        out_shape=outs,
+        compiler_params=params(56),
+        name=name,
+    )(*args)
+
+
+def dec_pre(x, gain_self, gain_cross, base, wq, wk, wv, wo, wcq):
+    rows = x.shape[0]
+    low = sds((rows, D), jnp.bfloat16)
+    full = sds((rows, D), jnp.float32)
+    outs = [low, low, low, low, sds((HEADS, rows, rows), jnp.float32), low, full, low, low]
+    return in_vmem(dec_pre_kernel, outs, "dec_pre", x, gain_self, gain_cross, base, wq, wk, wv, wo, wcq)
+
+
+def dec_mid_kernel(
+    merged_ref, mid_ref, cot_ref, gain_ref, wco_ref, win_ref, wout_ref,
+    out_ref, low_ref, hidden_ref, pre_grad_ref, after_low_ref, grad_after_ref, att_grad_ref, gain_grad_ref, slope_ref,
+):
+    rows = mid_ref.shape[0]
+    three = nn(jnp.concatenate(in_three(merged_ref[:, :D]), axis=0), wco_ref[...])
+    after = mid_ref[...] + (three[:rows] + three[rows : 2 * rows] + three[2 * rows :])
+    normed, scale = rms(after, gain_ref[...])
+    low = to_low(normed)
+    low_ref[...] = low
+    y = after
+    width = 768
+    chunks = [slice(c * width, (c + 1) * width) for c in range(win_ref.shape[1] // width)]
+    for cols in chunks:
+        hidden, slope = gelu_both(nn(low, win_ref[:, cols]))
+        hidden = to_low(hidden)
+        hidden_ref[:, cols] = hidden
+        slope_ref[:, cols] = slope
+        y = y + nn(hidden, wout_ref[cols, :])
+    out_ref[...] = to_low(y)
+    cot = cot_ref[...]
+    acc = None
+    for cols in chunks:
+        pre = to_low(slope_ref[:, cols] * nt(cot, wout_ref[cols, :]))
+        pre_grad_ref[:, cols] = pre
+        part = nt(pre, win_ref[:, cols])
+        acc = part if acc is None else acc + part
+    back, gain_grad = rms_back(after, scale, gain_ref[...], acc)
+    gain_grad_ref[...] = gain_grad
+    grad_after = cot.astype(jnp.float32) + back
+    grad_after_ref[...] = grad_after
+    after_low = to_low(grad_after)
+    after_low_ref[...] = after_low
+    att_grad_ref[...] = to_low(nt(after_low, wco_ref[...]))
+
+
+def dec_mid_call(merged, mid, cot, gain, wco, win, wout):
+    rows = mid.shape[0]
+    ff = win.shape[1]
+    low = sds((rows, D), jnp.bfloat16)
+    full = sds((rows, D), jnp.float32)
+    wide = sds((rows, ff), jnp.bfloat16)
+    outs = [low, low, wide, wide, low, full, low, sds((1, D), jnp.float32)]
+    vmem = pl.BlockSpec(memory_space=pltpu.VMEM)
+    return pl.pallas_call(
+        dec_mid_kernel,
+        in_specs=[vmem] * 7,
+        out_specs=[vmem] * len(outs),
+        out_shape=outs,
+        scratch_shapes=[pltpu.VMEM((rows, ff), jnp.float32)],
+        compiler_params=params(56),
+        name="dec_mid",
+    )(merged, mid, cot, gain, wco, win, wout)
+
+
+def dec_post_kernel(
+    gq_ref, grad_after_ref, mid_ref, x_ref, q_ref, k_ref, v_ref, probs_ref, gain_self_ref, gain_cross_ref,
+    wq_ref, wk_ref, wv_ref, wo_ref, wcq_ref, after_ref,
+    mid_low_ref, dq_ref, dk_ref, dv_ref, out_ref, gain_self_grad_ref, gain_cross_grad_ref, fold_ref,
+):
+    rows = x_ref.shape[0]
+    mid = mid_ref[...]
+    scale = lax.rsqrt(jnp.mean(mid * mid, axis=-1, keepdims=True) + epsilon)
+    three = nt(jnp.concatenate(in_three(gq_ref[...]), axis=0), wcq_ref[...])
+    back, gain_grad = rms_back(mid, scale, gain_cross_ref[...], three[:rows] + three[rows : 2 * rows] + three[2 * rows :])
+    gain_cross_grad_ref[...] = gain_grad
+    grad_mid = grad_after_ref[...] + back
+    mid_low = to_low(grad_mid)
+    mid_low_ref[...] = mid_low
+    att_grad = to_low(nt(mid_low, wo_ref[...]))
+    lane = lax.broadcasted_iota(jnp.int32, (rows, 128), 1)
+    row8 = lax.broadcasted_iota(jnp.int32, (8, 128), 0)
+    for pair in range(HEADS // 2):
+        cols = slice(pair * 128, (pair + 1) * 128)
+        q = q_ref[:, cols]
+        k = k_ref[:, cols]
+        v = v_ref[:, cols]
+        g = att_grad[:, cols]
+        dqs = []
+        scores = []
+        probs = []
+        for half in range(2):
+            head = 2 * pair + half
+            p = probs_ref[head]
+            dp = nt(head_lanes(g, half), v)
+            ds = p * (dp - jnp.sum(p * dp, axis=1, keepdims=True))
+            wide = jnp.concatenate([ds, jnp.zeros((rows, 128 - rows), jnp.float32)], axis=1)
+            total = wide[0:8]
+            for group in range(1, rows // 8):
+                total = total + pltpu.roll(wide[group * 8 : group * 8 + 8], 128 - group * 8, 1)
+            for bit in (1, 2, 4):
+                total = jnp.where((row8 // bit) % 2 == 1, pltpu.roll(total, 128 - bit, 1), total)
+            fold_ref[head : head + 1, :] = jnp.sum(total, axis=0, keepdims=True)
+            ds = to_low(ds)
+            dqs.append(nn(ds, k))
+            scores.append(ds)
+            probs.append(to_low(p))
+        dq_ref[:, cols] = to_low(0.125 * jnp.where(lane < HEAD, dqs[0], dqs[1]))
+        both_q = jnp.concatenate([head_lanes(q, 0), head_lanes(q, 1)], axis=0)
+        both_g = jnp.concatenate([head_lanes(g, 0), head_lanes(g, 1)], axis=0)
+        dk_ref[:, cols] = to_low(product_tn(jnp.concatenate(scores, axis=0), both_q))
+        dv_ref[:, cols] = to_low(product_tn(jnp.concatenate(probs, axis=0), both_g))
+    x = x_ref[...].astype(jnp.float32)
+    scale = lax.rsqrt(jnp.mean(x * x, axis=-1, keepdims=True) + epsilon)
+    grad = nt(dq_ref[...], wq_ref[...]) + nt(dk_ref[...], wk_ref[...]) + nt(dv_ref[...], wv_ref[...])
+    back, gain_grad = rms_back(x, scale, gain_self_ref[...], grad)
+    gain_self_grad_ref[...] = gain_grad
+    out_ref[...] = grad_mid + back
+
+
+def dec_post(gq, grad_after, mid, x, q, k, v, probs, gain_self, gain_cross, wq, wk, wv, wo, wcq, after):
+    rows = x.shape[0]
+    low = sds((rows, D), jnp.bfloat16)
+    gain = sds((1, D), jnp.float32)
+    outs = [low, low, low, low, sds((rows, D), jnp.float32), gain, gain, sds((HEADS, 128), jnp.float32)]
+    vmem = pl.BlockSpec(memory_space=pltpu.VMEM)
+    return pl.pallas_call(
+        dec_post_kernel,
+        in_specs=[vmem] * 15 + [pl.BlockSpec(memory_space=pl.ANY)],
+        out_specs=[vmem] * len(outs),
+        out_shape=outs,
+        compiler_params=params(60),
+        name="dec_post",
+    )(gq, grad_after, mid, x, q, k, v, probs, gain_self, gain_cross, wq, wk, wv, wo, wcq, after)
+
+
+def dec_weight_kernel(
+    pb, pa, column_ref, low_ref, dq_ref, dk_ref, dv_ref, att_ref, mid_low_ref, cross_low_ref, gq_ref, merged_ref, after_low_ref,
+    hidden_ref, cot_ref, dffn_low_ref, pre_grad_ref, out_ref, turned_ref, wide_ref,
+):
+    shards = pb * pa
+    column = column_ref[0]
+    rows = D // shards
+    depth = low_ref.shape[0]
+
+    def own(left, scratch):
+        height = left.shape[1]
+        here = height // shards
+        span = left.shape[0]
+        scratch[:, :span] = left.astype(jnp.float32).T
+        cut = [scratch[pl.ds((b * pa + column) * here, here), :span] for b in range(pb)]
+        return to_low(jnp.concatenate(cut, axis=0)), here
+
+    first = 0
+
+    def put(values, here):
+        nonlocal first
+        for b in range(pb):
+            out_ref[b, first : first + here, :] = values[b * here : (b + 1) * here]
+        first += here
+
+    left, here = own(low_ref[...], turned_ref)
+    for right_ref in (dq_ref, dk_ref, dv_ref):
+        put(nn(left, right_ref[...]), here)
+    left, here = own(att_ref[...], turned_ref)
+    put(nn(left, mid_low_ref[...]), here)
+    left, here = own(cross_low_ref[...], turned_ref)
+    a, b, c = in_three(gq_ref[...])
+    put(nn(left, a) + nn(left, b) + nn(left, c), here)
+    right = after_low_ref[...]
+    a, b, c = (own(part, turned_ref)[0] for part in in_three(merged_ref[:, :D]))
+    put(nn(a, right) + nn(b, right) + nn(c, right), here)
+    left, wide = own(hidden_ref[...], wide_ref)
+    put(nn(left, cot_ref[...]), wide)
+    left, here = own(dffn_low_ref[...], turned_ref)
+    for c in range(pre_grad_ref.shape[1] // D):
+        put(nn(left, pre_grad_ref[:, c * D : (c + 1) * D]), here)
+
+
+def dec_weight_grads(pb, pa, column, *args):
+    rows, ff = args[-1].shape
+    shards = pb * pa
+    height = (6 * D + ff + ff) // shards
+    vmem = pl.BlockSpec(memory_space=pltpu.VMEM)
+    return pl.pallas_call(
+        functools.partial(dec_weight_kernel, pb, pa),
+        in_specs=[pl.BlockSpec(memory_space=pltpu.SMEM)] + [vmem] * len(args),
+        out_specs=vmem,
+        out_shape=sds((pb, height, D), jnp.float32),
+        scratch_shapes=[pltpu.VMEM((D, rows), jnp.float32), pltpu.VMEM((ff, rows), jnp.float32)],
+        compiler_params=params(56),
+        name="dec_weight_grads",
+    )(column, *args)
+
+
 def bits_of(mesh_sizes):
     pb, pa = mesh_sizes
     pb_bits = pb.bit_length() - 1
@@ -771,61 +932,507 @@
     return jnp.stack(rows)
 
 
-def swap(values, axis, bit):
-    size = lax.axis_size(axis)
-    return lax.ppermute(values, axis, [(i, i ^ (1 << bit)) for i in range(size)])
-
-
-def summed(parts, first, last):
-    total = parts[0][first:last]
-    for part in parts[1:]:
-        total = total + part[first:last]
-    return total
-
-
-def scatter_chain(parts, order):
-    count = parts[0].shape[0]
+MESH = pl.DeviceIdType.MESH
+LINK = 0.088
+PAIR = 0.45
+NEAR = ("pb", 0)
+
+
+def link_of(step, sizes):
+    xs, ys, zs = bits_of(sizes)
+    if step == NEAR:
+        return "core"
+    if step in ys:
+        return "y"
+    return "x" if step in xs else "z"
+
+
+def link_time(step, megabytes, sizes):
+    if step == NEAR:
+        return megabytes / PAIR
+    return 2 * megabytes * (2 if step == bits_of(sizes)[2][-1] else 1) / LINK
+
+
+class Piece:
+    def __init__(self, array, first, width, order, place=None):
+        self.array, self.first, self.width, self.order, self.place = array, first, width, order, place
+
+
+def plan(pieces, shapes, starts, sizes, depth=2):
+    free, held, queues = {}, {}, {}
+    pending = [(start, i, -1) for i, start in enumerate(starts)]
+    events = []
+
+    def send(now, i, step, sends):
+        piece = pieces[i]
+        link = link_of(piece.order[step], sizes)
+        if held.get(link, 0) >= depth:
+            queues.setdefault(link, []).append((i, step))
+            return
+        held[link] = held.get(link, 0) + 1
+        half, rows = shapes[piece.array][:2]
+        megabytes = (half >> (step + piece.skip)) * rows * piece.width * 4e-6
+        begin = max(now, free.get(link, 0.0))
+        free[link] = begin + link_time(piece.order[step], megabytes, sizes)
+        pending.append((free[link] + 1.5, i, step))
+        sends.append((i, step))
+
+    while pending:
+        pending.sort()
+        now, i, step = pending.pop(0)
+        sends = []
+        if step >= 0:
+            link = link_of(pieces[i].order[step], sizes)
+            held[link] -= 1
+            waiting = queues.get(link, [])
+            if waiting:
+                send(now, *waiting.pop(0), sends)
+        if step + 1 < len(pieces[i].order):
+            send(now + 0.5, i, step + 1, sends)
+        events.append((now, i, step, sends))
+    return events
+
+
+def partner(step):
+    axis, bit = step
+    me = lax.axis_index(axis)
+    size = 1 << bit
+    there = me + size - 2 * size * lax.rem(me // size, 2)
+    return {"pb": lax.axis_index("pb"), "pa": lax.axis_index("pa"), axis: there}
+
+
+def all_steps(sizes):
+    xs, ys, zs = bits_of(sizes)
+    return [NEAR] + xs + ys + zs
+
+
+def greet(sizes):
+    barrier = pltpu.get_barrier_semaphore()
+    for step in all_steps(sizes):
+        pl.semaphore_signal(barrier, inc=1, device_id=partner(step), device_id_type=MESH)
+    pl.semaphore_wait(barrier, len(all_steps(sizes)))
+
+
+class Exchange:
+    def __init__(self, sizes, pieces, shapes, starts):
+        self.sizes, self.pieces, self.shapes = sizes, pieces, shapes
+        for piece in pieces:
+            piece.skip = 1 if piece.place is None else 0
+        self.events = plan(pieces, shapes, starts, sizes)
+        self.stages = len(all_steps(sizes))
+        self.own = [p for p in pieces if p.place is not None]
+        self.outside = [p for p in pieces if p.place is None]
+        self.staged = sorted({p.array for p in self.outside})
+
+    def scratch(self):
+        out = []
+        for array in self.staged:
+            half, rows = self.shapes[array][:2]
+            width = max(p.width for p in self.outside if p.array == array)
+            out += [pltpu.VMEM((half, rows, width), jnp.float32), pltpu.SemaphoreType.DMA]
+        for piece in self.outside:
+            half, rows = self.shapes[piece.array][:2]
+            out += [
+                pltpu.VMEM((half, rows, piece.width), jnp.float32),
+                pltpu.VMEM((half - 1, rows, piece.width), jnp.float32),
+                pltpu.SemaphoreType.DMA,
+            ]
+        if self.own:
+            half, rows = self.shapes[self.own[0].array][:2]
+            block = (rows, self.own[0].width)
+            count = len(self.own)
+            out += [
+                pltpu.VMEM((count, half) + block, jnp.float32),
+                pltpu.VMEM((count, half) + block, jnp.float32),
+                pltpu.VMEM((count, 2 * half - 1) + block, jnp.float32),
+            ]
+        count = len(self.pieces)
+        return out + [pltpu.SemaphoreType.DMA((count, self.stages)), pltpu.SemaphoreType.DMA((count, self.stages))]
+
+    def bind(self, keeps, nears, outs, scratch):
+        self.keeps, self.nears, self.outs = keeps, nears, outs
+        scratch = list(scratch)
+        self.stage_of = {array: (scratch.pop(0), scratch.pop(0)) for array in self.staged}
+        self.bufs, self.recvs, self.load_sems = {}, {}, {}
+        for i, piece in enumerate(self.pieces):
+            if piece.place is None:
+                self.bufs[i], self.recvs[i], self.load_sems[i] = scratch.pop(0), scratch.pop(0), scratch.pop(0)
+        if self.own:
+            self.keep_of, self.send_of, recv = scratch.pop(0), scratch.pop(0), scratch.pop(0)
+            for i, piece in enumerate(self.pieces):
+                if piece.place is not None:
+                    self.bufs[i], self.recvs[i] = self.keep_of.at[piece.place], recv.at[piece.place]
+        self.send_sems, self.recv_sems = scratch
+
+    def loads(self, i):
+        piece = self.pieces[i]
+        cols = pl.ds(piece.first, piece.width)
+        stage, sem = self.stage_of[piece.array]
+        return (
+            pltpu.make_async_copy(self.keeps[piece.array].at[:, :, cols], self.bufs[i], self.load_sems[i]),
+            pltpu.make_async_copy(self.nears[piece.array].at[:, :, cols], stage, sem),
+        )
+
+    def sizes_of(self, i, step):
+        piece = self.pieces[i]
+        half = self.shapes[piece.array][0]
+        count = half >> (step + piece.skip)
+        return count, (half >> piece.skip) * 2 - 2 * count
+
+    def copy(self, i, step):
+        piece = self.pieces[i]
+        count, first = self.sizes_of(i, step)
+        if step == 0 and piece.skip == 0:
+            source = self.send_of.at[piece.place]
+        else:
+            source = self.bufs[i].at[pl.ds(count, count)]
+        return pltpu.make_async_remote_copy(
+            src_ref=source, dst_ref=self.recvs[i].at[pl.ds(first, count)],
+            send_sem=self.send_sems.at[i, step], recv_sem=self.recv_sems.at[i, step],
+            device_id=partner(piece.order[step]), device_id_type=MESH,
+        )
+
+    def first_loads(self):
+        for array in self.staged:
+            self.start_load(next(i for i, p in enumerate(self.pieces) if p.array == array and p.place is None))
+
+    def start_load(self, i):
+        for load in self.loads(i):
+            load.start()
+
+    def event(self, i, step, sends):
+        piece = self.pieces[i]
+        buf, recv = self.bufs[i], self.recvs[i]
+        last = step + 1 == len(piece.order)
+        if step < 0 and piece.skip == 1:
+            for load in self.loads(i):
+                load.wait()
+            stage = self.stage_of[piece.array][0]
+            count = self.shapes[piece.array][0]
+
+            def add(slot, _):
+                buf[slot] = buf[slot] + stage[slot]
+                return 0
+
+        elif step >= 0:
+            count, first = self.sizes_of(i, step)
+            self.copy(i, step).wait_recv()
+
+            def add(slot, _):
+                buf[slot] = buf[slot] + recv[first + slot]
+                return 0
+
+        else:
+            count = 0
+        if last:
+            self.outs[piece.array][:, piece.first : piece.first + piece.width] = buf[0] + recv[first]
+        elif count:
+            lax.fori_loop(count // 2, count, add, 0)
+        for send in sends:
+            self.copy(*send).start()
+        if not last and count:
+            lax.fori_loop(0, count // 2, add, 0)
+        if step < 0 and piece.skip == 1:
+            rest = [j for j, p in enumerate(self.pieces) if p.array == piece.array and j > i]
+            if rest:
+                self.start_load(rest[0])
+
+    def finish(self):
+        for i, piece in enumerate(self.pieces):
+            for step in range(len(piece.order)):
+                self.copy(i, step).wait_send()
+
+    def points(self, times, ready):
+        out = [[] for _ in times]
+        place = 0
+        for when, i, step, sends in self.events:
+            while place < len(times) - 1 and times[place] < when:
+                place += 1
+            if step < 0 and self.pieces[i].place is not None:
+                place = max(place, ready[self.pieces[i].place])
+            out[place].append((i, step, sends))
+        return out
+
+
+class Everywhere:
+    def __init__(self, sizes, shape):
+        self.steps = all_steps(sizes)
+        self.shape = shape
+
+    def scratch(self):
+        count = len(self.steps)
+        return [
+            pltpu.VMEM((count + 1,) + self.shape, jnp.float32),
+            pltpu.VMEM((count,) + self.shape, jnp.float32),
+            pltpu.SemaphoreType.DMA((count,)),
+            pltpu.SemaphoreType.DMA((count,)),
+        ]
+
+    def bind(self, scratch):
+        self.sums, self.recvs, self.send_sems, self.recv_sems = scratch
+
+    def copy(self, k):
+        return pltpu.make_async_remote_copy(
+            src_ref=self.sums.at[k], dst_ref=self.recvs.at[k], send_sem=self.send_sems.at[k], recv_sem=self.recv_sems.at[k],
+            device_id=partner(self.steps[k]), device_id_type=MESH,
+        )
+
+    def arrive(self, k):
+        self.copy(k).wait_recv()
+        self.sums[k + 1] = self.sums[k] + self.recvs[k]
+        if k + 1 < len(self.steps):
+            self.copy(k + 1).start()
+
+    def finish(self):
+        for k in range(len(self.steps)):
+            self.copy(k).wait_send()
+
+
+SMALL = (32, 1024)
+ATTN_STEP = 3.6
+GRAD_STEP = 1.5
+BACK_STEP = 1.8
+
+
+def slots_of(sizes, order):
+    pb, pa = sizes
+    far = {}
     for axis, bit in order:
-        count //= 2
-        received = swap(summed(parts, count, 2 * count), axis, bit)
-        parts = [part[:count] for part in parts] + [received]
-    return summed(parts, 0, 1)[0]
-
-
-def scatter(pieces, orders, widths=None):
-    keep, send = pieces
-    received = swap(send, "pb", 0)
-    if widths is None:
-        return scatter_chain([keep, received], orders[0])
-    first = 0
-    done = []
-    for order, width in zip(orders, widths):
-        cols = slice(first, first + width)
-        done.append(scatter_chain([keep[:, :, cols], received[:, :, cols]], order))
-        first += width
-    return jnp.concatenate(done, axis=1)
-
-
-def scatter_small(values, orders, mesh_sizes):
-    pb, pa = mesh_sizes
-    full = [("pb", 0)] + list(orders[0])
-    count = pb * pa
-    width = -(-values.shape[1] // 128) * 128
-    values = jnp.pad(values, ((0, 0), (0, width - values.shape[1])))
-    pb_me = lax.axis_index("pb")
-    pa_me = lax.axis_index("pa")
-    cells = np.arange(count)
-    pb_of = jnp.zeros((count,), jnp.int32)
-    pa_of = jnp.zeros((count,), jnp.int32)
-    for place, (axis, bit) in enumerate(full):
-        one = jnp.asarray((cells >> (len(full) - 1 - place) & 1) << bit, jnp.int32)
-        if axis == "pb":
-            pb_of = pb_of + one
-        else:
-            pa_of = pa_of + one
-    shard = (pb_of ^ pb_me) * pa + (pa_of ^ pa_me)
-    ordered = jnp.take(values, shard, axis=0).reshape(count, width // 128, 128)
-    return scatter_chain([ordered], full).reshape(width)
+        me = lax.rem(lax.axis_index(axis) // (1 << bit), 2)
+        far[axis, bit] = (me, 1 - me)
+    cells = []
+    for y in range(pb // 2):
+        for a in range(pa):
+            slot = 0
+            for axis, bit in order:
+                slot = slot * 2 + far[axis, bit][(2 * y if axis == "pb" else a) >> bit & 1]
+            cells.append(slot)
+    return cells
+
+
+def last_kernel(
+    exchange, everywhere, points, orders, passages, share, arrays,
+    lengths_ref, q_ref, k_ref, v_ref, o_ref, do_ref, lse_ref, base_ref, turned_ref, x_ref, grad_mid_ref, gain_ref, wq_ref, wk_ref, wv_ref,
+    dec_fold_ref, *refs,
+):
+    gains, refs = refs[:5], refs[5:]
+    keeps, nears, refs = refs[:arrays], refs[arrays : 2 * arrays], refs[2 * arrays :]
+    after, refs = refs[0], refs[1:]
+    out_ref, small_ref = refs[:2]
+    moved, refs = refs[2 : 3 + arrays], refs[3 + arrays :]
+    strip_ref, gather_ref, dqT_ref, grads_ref, fold_ref, gain_grad_ref = refs[:6]
+    everywhere.bind(refs[6:10])
+    exchange.bind(keeps, nears, moved, refs[10:])
+    step = pl.program_id(0)
+    sizes = exchange.sizes
+    pb, pa = sizes
+    attn_steps = HEADS // 2 * passages
+    tiles = len(exchange.own)
+    grad_end = attn_steps + tiles
+
+    @pl.when(step == 0)
+    def _():
+        exchange.first_loads()
+        greet(sizes)
+
+    def beside(place):
+        for k, events in enumerate(points[:-1]):
+            if k < 2 * attn_steps and k % 2 == place and events:
+
+                @pl.when(step == k // 2)
+                def _(events=events):
+                    for event in events:
+                        exchange.event(*event)
+
+    def at_end(number, k):
+        if points[k]:
+
+            @pl.when(step == number)
+            def _():
+                for event in points[k]:
+                    exchange.event(*event)
+
+    @pl.when(step < attn_steps)
+    def _():
+        pair = step // passages
+        passage = lax.rem(step, passages)
+        place = pl.ds(pl.multiple_of(passage * PL, PL), PL), pl.ds(pl.multiple_of(pair * 128, 128), 128)
+        attn_backward_kernel(
+            beside, passage, passages, lengths_ref, q_ref, k_ref, v_ref, o_ref, do_ref, lse_ref, base_ref,
+            grads_ref.at[(0,) + place], grads_ref.at[(1,) + place], grads_ref.at[(2,) + place], fold_ref.at[pl.ds(pair, 1)],
+            strip_ref, gather_ref, dqT_ref,
+        )
+
+    @pl.when((step >= attn_steps) & (step < grad_end))
+    def _():
+        number = step - attn_steps
+        width = exchange.own[0].width
+        each = D // width
+        column = pl.ds(pl.multiple_of(lax.rem(number, each) * width, width), width)
+        right = grads_ref[number // each, :, column]
+        chain = lax.rem(number, len(orders))
+        choices = [slots_of(sizes, order) for order in orders]
+        core = lax.rem(lax.axis_index("pb"), 2)
+        rows = exchange.shapes[exchange.own[0].array][1]
+        half_rows = pa * rows
+        for y in range(pb // 2):
+            low_part = nn(turned_ref[2 * y * half_rows : (2 * y + 1) * half_rows, :], right)
+            high_part = nn(turned_ref[(2 * y + 1) * half_rows : (2 * y + 2) * half_rows, :], right)
+            mine = jnp.where(core == 0, low_part, high_part)
+            other = jnp.where(core == 0, high_part, low_part)
+            for a in range(pa):
+                slot = choices[0][y * pa + a]
+                for c in range(1, len(orders)):
+                    slot = jnp.where(chain == c, choices[c][y * pa + a], slot)
+                exchange.keep_of[number, slot] = mine[a * rows : (a + 1) * rows]
+                exchange.send_of[number, slot] = other[a * rows : (a + 1) * rows]
+
+    @pl.when(step >= grad_end)
+    def _():
+        rows = pl.ds(pl.multiple_of((step - grad_end) * x_ref.shape[0], x_ref.shape[0]), x_ref.shape[0])
+        qkv_back_kernel(
+            step == grad_end, grads_ref.at[0, rows], grads_ref.at[1, rows], grads_ref.at[2, rows],
+            x_ref, grad_mid_ref, gain_ref, wq_ref, wk_ref, wv_ref, out_ref, gain_grad_ref,
+        )
+
+    for k in range(2 * attn_steps, len(points) - 1):
+        at_end(k - attn_steps, k)
+
+    @pl.when(step == pl.num_programs(0) - 1)
+    def _():
+        first = everywhere.sums
+        first[0] = jnp.zeros(SMALL, jnp.float32)
+        first[0, 0:1, :D] = gain_grad_ref[...]
+        for r, ref in enumerate(gains):
+            first[0, r + 1 : r + 2, :D] = ref[...] if r < 2 else ref[...] * share
+        for pair in range(HEADS // 2):
+            first[0, 8 + 2 * pair : 10 + 2 * pair, :] = fold_ref[pair]
+        first[0, 8 + HEADS : 8 + 2 * HEADS, :128] = dec_fold_ref[...] * share
+        everywhere.copy(0).start()
+        left = points[-1]
+        steps = len(everywhere.steps)
+        every = max(1, len(left) // (steps + 1))
+        done = 0
+        for n, event in enumerate(left):
+            if n % every == every - 1 and done < steps:
+                everywhere.arrive(done)
+                done += 1
+            exchange.event(*event)
+        for k in range(done, steps):
+            everywhere.arrive(k)
+        small_ref[...] = everywhere.sums[steps]
+        exchange.finish()
+        everywhere.finish()
+
+
+def groups_of(orders, groups):
+    pieces, starts = [], []
+    for number, (_, _, widths) in enumerate(groups):
+        first = 0
+        for c, piece_width in enumerate(widths):
+            starts.append(4.0 + 1.5 * len(pieces))
+            pieces.append(Piece(number, first, piece_width, orders[c % len(orders)]))
+            first += piece_width
+    return pieces, starts
+
+
+def last_part(
+    sizes, orders, groups, after, lengths, q, k, v, o, do, lse, base, turned, x, grad_mid, gain, wq, wk, wv, dec_fold, gains,
+):
+    pb, pa = sizes
+    passages = lengths.shape[0]
+    tokens = x.shape[0]
+    pairs = HEADS // 2
+    tile_rows = 256
+    width = 256
+    attn_steps = pairs * passages
+    own_count = 3 * D // width
+    back_steps = tokens // tile_rows
+    steps = attn_steps + own_count + back_steps
+    half = pb * pa // 2
+    shapes = [g[0].shape for g in groups] + [(half, D // (pb * pa), 3 * D)]
+    pieces, starts = groups_of(orders, groups)
+    times = [ATTN_STEP * s / 2 for s in range(2 * attn_steps)]
+    ready = []
+    for n in range(own_count):
+        ready.append(len(times))
+        times.append(ATTN_STEP * attn_steps + GRAD_STEP * (n + 1))
+        starts.append(times[-1])
+        pieces.append(Piece(len(groups), n * width, width, [NEAR] + orders[n % len(orders)], n))
+    for s in range(back_steps - 1):
+        times.append(ATTN_STEP * attn_steps + GRAD_STEP * own_count + BACK_STEP * (s + 1))
+    exchange = Exchange(sizes, pieces, shapes, starts)
+    everywhere = Everywhere(sizes, SMALL)
+    points = exchange.points(times + [1e9], ready)
+
+    def attn_place(i):
+        at = jnp.minimum(i, attn_steps - 1)
+        return at // passages, lax.rem(at, passages)
+
+    def tile_map(i):
+        pair, passage = attn_place(i)
+        return passage, pair
+
+    def lse_map(i):
+        pair, passage = attn_place(i)
+        return pair, passage, 0, 0
+
+    def once(array):
+        return pl.BlockSpec(array.shape, lambda i: (0,) * array.ndim, pipeline_mode=pl.Buffered(1))
+
+    def row_map(i):
+        return jnp.maximum(i - attn_steps - own_count, 0), 0
+
+    tile = pl.BlockSpec((PL, 128), tile_map)
+    rows = pl.BlockSpec((tile_rows, D), row_map)
+    hbm = pl.BlockSpec(memory_space=pl.ANY)
+    keeps, nears = [g[0] for g in groups], [g[1] for g in groups]
+    return pl.pallas_call(
+        functools.partial(last_kernel, exchange, everywhere, points, orders, passages, 1.0 / pa, len(groups)),
+        grid=(steps,),
+        in_specs=[pl.BlockSpec(memory_space=pltpu.SMEM)]
+        + [tile] * 5
+        + [pl.BlockSpec((1, 1, 2, PL), lse_map), pl.BlockSpec((1, 2, WIDE), lambda i: (attn_place(i)[0], 0, 0)), once(turned), rows, rows]
+        + [once(a) for a in (gain, wq, wk, wv, dec_fold) + tuple(gains)]
+        + [hbm] * (2 * len(groups) + 1),
+        out_specs=[rows, pl.BlockSpec(SMALL, lambda i: (0, 0))] + [pl.BlockSpec(s[1:], lambda i: (0, 0)) for s in shapes],
+        out_shape=[sds((tokens, D), jnp.float32), sds(SMALL, jnp.float32)] + [sds(s[1:], jnp.float32) for s in shapes],
+        scratch_shapes=[
+            pltpu.VMEM((2, STRIP, WIDE), jnp.float32),
+            pltpu.VMEM((2, STRIP, WIDE), jnp.float32),
+            pltpu.VMEM((128, PL), jnp.bfloat16),
+            pltpu.VMEM((3, tokens, D), jnp.bfloat16),
+            pltpu.VMEM((pairs, 2, WIDE), jnp.float32),
+            pltpu.VMEM((1, D), jnp.float32),
+        ]
+        + everywhere.scratch()
+        + exchange.scratch(),
+        compiler_params=pltpu.CompilerParams(collective_id=1, has_side_effects=True, vmem_limit_bytes=63 * MIB),
+        name="enc_last",
+    )(lengths, q, k, v, o, do, lse, base, turned, x, grad_mid, gain, wq, wk, wv, dec_fold, *gains, *keeps, *nears, after)
+
+
+def exchange_kernel(exchange, arrays, *refs):
+    exchange.bind(refs[:arrays], refs[arrays : 2 * arrays], refs[2 * arrays : 3 * arrays], refs[3 * arrays :])
+    exchange.first_loads()
+    greet(exchange.sizes)
+    for _, *event in exchange.events:
+        exchange.event(*event)
+    exchange.finish()
+
+
+def exchange_only(sizes, orders, groups):
+    shapes = [g[0].shape for g in groups]
+    exchange = Exchange(sizes, *groups_of(orders, groups)[:1], shapes, groups_of(orders, groups)[1])
+    return pl.pallas_call(
+        functools.partial(exchange_kernel, exchange, len(groups)),
+        in_specs=[pl.BlockSpec(memory_space=pl.ANY)] * (2 * len(groups)),
+        out_specs=[pl.BlockSpec(memory_space=pltpu.VMEM)] * len(groups),
+        out_shape=[sds(s[1:], jnp.float32) for s in shapes],
+        scratch_shapes=exchange.scratch(),
+        compiler_params=pltpu.CompilerParams(collective_id=2, has_side_effects=True, vmem_limit_bytes=63 * MIB),
+        name="exchange",
+    )(*[g[0] for g in groups], *[g[1] for g in groups])
 
 
 def local(
@@ -838,150 +1445,88 @@
     sizes = (pb, pa)
     orders = orders_of(sizes)
     answer_rows = dec_in.shape[0]
-    questions = answer_rows // ANS
     gain_attn, gain_ffn, gain_final = (g.astype(jnp.float32)[None] for g in (enc_gain_attn, enc_gain_ffn, enc_gain_final))
-    gain_self = dec_gain_self.astype(jnp.float32)
-    gain_cross = dec_gain_cross.astype(jnp.float32)
-    gain_dffn = dec_gain_ffn.astype(jnp.float32)
+    gain_self, gain_cross, gain_dffn = (g.astype(jnp.float32)[None] for g in (dec_gain_self, dec_gain_cross, dec_gain_ffn))
     table = exchange_table(sizes, orders)
     enc_table = jnp.asarray(strip_table())
-    dec_table = jnp.asarray(causal_onehot(ANS))
+    dec_table = jnp.asarray(causal_row(ANS))
     base = jnp.dot(enc_table, enc_bias.astype(jnp.float32), precision=highest).T.reshape(HEADS // 2, 2, WIDE)
 
-    attn_low, enc_queries, enc_keys, enc_values = qkv_forward(enc_in, gain_attn, enc_query, enc_key, enc_value)
+    attn_turned, enc_queries, enc_keys, enc_values = qkv_forward(enc_in, gain_attn, enc_query, enc_key, enc_value)
     enc_attended, enc_lse = attn_forward(lengths, enc_queries, enc_keys, enc_values, base)
     enc_mid, ffn_low, enc_hidden, enc_slope, enc_y, enc_out, final_low, cross_keys, cross_values = post_forward(
         enc_in, enc_attended, gain_ffn, gain_final, enc_output, enc_ff_in, enc_ff_out, cross_key, cross_value
     )
 
-    dec_x = dec_in.astype(jnp.float32)
-    self_normed, self_scale = norm_forward(dec_x, gain_self)
-    self_low = to_low(self_normed)
-    dec_queries = to_low(product(self_low, dec_query)).reshape(questions, ANS, HEADS, HEAD)
-    dec_keys = to_low(product(self_low, dec_key)).reshape(questions, ANS, HEADS, HEAD)
-    dec_values = to_low(product(self_low, dec_value)).reshape(questions, ANS, HEADS, HEAD)
-    dec_position = jnp.dot(dec_table, dec_bias.astype(jnp.float32), precision=highest).T.reshape(HEADS, ANS, ANS)
-    causal = jnp.arange(ANS)[None, :] <= jnp.arange(ANS)[:, None]
-    raw_scores = 0.125 * jnp.einsum("qihd,qjhd->qhij", dec_queries, dec_keys, preferred_element_type=jnp.float32)
-    self_scores = jnp.where(causal, raw_scores + dec_position[None], -1000000000.0)
-    self_top = jnp.max(self_scores, axis=-1, keepdims=True)
-    self_exp = jnp.exp(self_scores - self_top)
-    dec_probs = self_exp / jnp.sum(self_exp, axis=-1, keepdims=True)
-    dec_attended = to_low(
-        jnp.einsum("qhij,qjhd->qihd", to_low(dec_probs), dec_values, preferred_element_type=jnp.float32).reshape(answer_rows, D)
+    dec_base = jnp.dot(dec_table, dec_bias.astype(jnp.float32), precision=highest).T
+    self_low, dec_queries, dec_keys, dec_values, dec_probs, dec_attended, dec_mid, cross_low, cross_queries = dec_pre(
+        dec_in, gain_self, gain_cross, dec_base, dec_query, dec_key, dec_value, dec_output, cross_query
     )
-    dec_mid = dec_x + product(dec_attended, dec_output)
-    cross_normed, cross_scale = norm_forward(dec_mid, gain_cross)
-    cross_low = to_low(cross_normed)
-    cross_queries = to_low(product(cross_low, cross_query))
 
     merged = merge(cross_part(question_of, lengths, cross_queries, cross_keys, cross_values), pa)
-    cross_attended = merged[:, :D]
-    dec_after = dec_mid + exact_product(cross_attended, cross_output)
-    dffn_normed, dffn_scale = norm_forward(dec_after, gain_dffn)
-    dffn_low = to_low(dffn_normed)
-    dec_pre = product(dffn_low, dec_ff_in)
-    dec_hidden = to_low(smooth_unit(dec_pre))
-    dec_y = dec_after + product(dec_hidden, dec_ff_out)
-    grad_dec_y = dec_cot.astype(jnp.float32)
-    out_grad_low = dec_cot
-    pre_grad_low = to_low(smooth_back(dec_pre, product_nt(out_grad_low, dec_ff_out)))
-    back_after, dec_gain_ffn_grad = norm_backward(dec_after, dffn_scale, gain_dffn, product_nt(pre_grad_low, dec_ff_in))
-    grad_after = grad_dec_y + back_after
-    after_low = to_low(grad_after)
-    cross_att_grad = to_low(product_nt(after_low, cross_output))
-
+    dec_out, dffn_low, dec_hidden, pre_grad_low, after_low, grad_after, cross_att_grad, dec_gain_ffn_grad = dec_mid_call(
+        merged, dec_mid, dec_cot, gain_dffn, cross_output, dec_ff_in, dec_ff_out
+    )
     query_part, grad_cross = cross_back(
-        question_of, lengths, cross_queries, cross_keys, cross_values, cross_att_grad, cross_attended, merged[:, D:]
+        question_of, lengths, cross_queries, cross_keys, cross_values, cross_att_grad, merged[:, :D], merged[:, D:]
     )
     grad_cross_q = lax.psum(query_part, "pa")
 
+    def near(terms):
+        keep, send = terms
+        return keep, lax.ppermute(send, "pb", [(i, i ^ 1) for i in range(pb)])
+
+    cross_terms = near(weight_grad(table, final_low, [grad_cross[0], grad_cross[1]], pb, pa, 256, 2))
     eout_low, epre_low, emid_low, grad_enc_mid, enc_att_grad, final_gain_grad, ffn_gain_grad = post_backward(
-        grad_cross, enc_y, enc_mid, enc_slope, enc_cot, gain_ffn, gain_final, cross_key, cross_value, enc_ff_out, enc_ff_in, enc_output
+        grad_cross, enc_y, enc_mid, enc_slope, enc_cot, gain_ffn, gain_final, cross_key, cross_value, enc_ff_out, enc_ff_in, enc_output,
     )
-    cross_terms = scatter(weight_grad(table, final_low, [grad_cross[0], grad_cross[1]], pb, pa, 256, 99), orders)
-    ff_out_term = scatter(weight_grad(table[jnp.array([0, 2])], enc_hidden, [eout_low], pb, pa, 256, 99), orders[1:])
-    ff_in_term = scatter(weight_grad(table, ffn_low, [epre_low], pb, pa, 512, 2), orders, (1024, 1024, 1024))
-    output_term = scatter(weight_grad(table[jnp.array([0, 3])], enc_attended, [emid_low], pb, pa, 256, 99), orders[2:])
-    grad_eq, grad_ek, grad_ev, fold = attn_backward(
-        lengths, enc_queries, enc_keys, enc_values, enc_attended, enc_att_grad, enc_lse, base
+    out_terms = near(weight_grad(table, enc_hidden, [eout_low], pb, pa, 256, 1))
+    in_terms = near(weight_grad(table, ffn_low, [epre_low], pb, pa, 512, 2))
+    mix_terms = near(weight_grad(table, enc_attended, [emid_low], pb, pa, 256, 1))
+
+    mid_low, grad_dq, grad_dk, grad_dv, dec_in_grad, dec_gain_self_grad, dec_gain_cross_grad, dec_fold = dec_post(
+        grad_cross_q, grad_after, dec_mid, dec_in, dec_queries, dec_keys, dec_values, dec_probs, gain_self, gain_cross,
+        dec_query, dec_key, dec_value, dec_output, cross_query, mix_terms[0],
     )
-    attn_terms = scatter(
-        weight_grad(table, attn_low, [grad_eq, grad_ek, grad_ev], pb, pa, 256, 3), orders, (768, 768, 768)
+    thin = dec_weight_grads(
+        pb, pa, lax.axis_index("pa").reshape(1), self_low, grad_dq, grad_dk, grad_dv, dec_attended, mid_low, cross_low, grad_cross_q,
+        merged, after_low, dec_hidden, dec_cot, dffn_low, pre_grad_low,
     )
-    enc_in_grad, attn_gain_grad = qkv_backward(
-        grad_eq, grad_ek, grad_ev, enc_in, grad_enc_mid, gain_attn, enc_query, enc_key, enc_value
-    )
-    enc_bias_grad = jnp.dot(fold.reshape(HEADS, WIDE), enc_table, precision=highest).T.reshape(BUCKETS * HEADS)
-
-    back_mid, dec_gain_cross_grad = norm_backward(dec_mid, cross_scale, gain_cross, exact_nt(grad_cross_q, cross_query))
-    grad_mid = grad_after + back_mid
-    mid_low = to_low(grad_mid)
-    dec_att_grad = to_low(product_nt(mid_low, dec_output)).reshape(questions, ANS, HEADS, HEAD)
-    dec_dprob = jnp.einsum("qihd,qjhd->qhij", dec_att_grad, dec_values, preferred_element_type=jnp.float32)
-    dec_dscore = dec_probs * (dec_dprob - jnp.sum(dec_probs * dec_dprob, axis=-1, keepdims=True))
-    dec_bias_grad = jnp.dot(
-        jnp.sum(dec_dscore, axis=0).reshape(HEADS, ANS * ANS), dec_table, precision=highest
-    ).T.reshape(BUCKETS * HEADS)
-    low_dscore = to_low(dec_dscore)
-    grad_dq = to_low(
-        0.125 * jnp.einsum("qhij,qjhd->qihd", low_dscore, dec_keys, preferred_element_type=jnp.float32)
-    ).reshape(answer_rows, D)
-    grad_dk = to_low(
-        0.125 * jnp.einsum("qhij,qihd->qjhd", low_dscore, dec_queries, preferred_element_type=jnp.float32)
-    ).reshape(answer_rows, D)
-    grad_dv = to_low(
-        jnp.einsum("qhij,qihd->qjhd", to_low(dec_probs), dec_att_grad, preferred_element_type=jnp.float32)
-    ).reshape(answer_rows, D)
-    self_back = product_nt(grad_dq, dec_query) + product_nt(grad_dk, dec_key) + product_nt(grad_dv, dec_value)
-    back_dec_in, dec_gain_self_grad = norm_backward(dec_x, self_scale, gain_self, self_back)
-    dec_in_grad = grad_mid + back_dec_in
-
-    column = lax.axis_index("pa")
-
-    def own_columns(values):
-        rows = values.shape[1] // (pb * pa)
-        cut = values.reshape(answer_rows, pb, pa, rows)
-        return lax.dynamic_slice_in_dim(cut, column, 1, 2).reshape(answer_rows, pb * rows)
-
-    def dec_term(left, right, times=product_tn):
-        left = own_columns(left)
-        return times(left, right).reshape(pb, left.shape[1] // pb, right.shape[1])
-
-    ff_rows = dec_hidden.shape[1]
-    thin = [
-        dec_term(self_low, grad_dq),
-        dec_term(self_low, grad_dk),
-        dec_term(self_low, grad_dv),
-        dec_term(dec_attended, mid_low),
-        dec_term(cross_low, grad_cross_q, exact_tn),
-        dec_term(cross_attended, after_low, exact_tn),
-        dec_term(dec_hidden, out_grad_low),
-    ]
-    wide = dec_term(dffn_low, pre_grad_low)
-    thin += [wide[:, :, c * D : (c + 1) * D] for c in range(ff_rows // D)]
-    heights = [t.shape[1] for t in thin]
-    dec_sum = lax.psum_scatter(jnp.concatenate(thin, axis=1), "pb", scatter_dimension=0, tiled=False)
-    cuts = np.cumsum([0] + heights)
+    dec_sum = lax.psum_scatter(thin, "pb", scatter_dimension=0, tiled=False)
+    small_height = D // (pb * pa)
+    wide_height = dec_hidden.shape[1] // (pb * pa)
+    cuts = np.cumsum([0] + [small_height] * 6 + [wide_height] + [small_height] * (dec_hidden.shape[1] // D))
     got = [dec_sum[a:b] for a, b in zip(cuts[:-1], cuts[1:])]
     dec_ff_in_grad = jnp.concatenate(got[7:], axis=1)
 
+    groups = [
+        cross_terms + ((512, 512, 512),), out_terms + ((256, 256, 256),), in_terms + ((1024, 1024, 1024),), mix_terms + ((256, 256, 256),),
+    ]
+    alone = [] if D // (pb * pa) % 8 == 0 else [groups.pop(2)]
+    enc_in_grad, small, *summed = last_part(
+        sizes, orders, groups, thin, lengths, enc_queries, enc_keys, enc_values, enc_attended, enc_att_grad, enc_lse, base,
+        attn_turned, enc_in, grad_enc_mid, gain_attn, enc_query, enc_key, enc_value, dec_fold,
+        (ffn_gain_grad, final_gain_grad, dec_gain_self_grad, dec_gain_cross_grad, dec_gain_ffn_grad),
+    )
+    summed[2:2] = exchange_only(sizes, orders, alone) if alone else []
+    cross_terms, ff_out_term, ff_in_term, output_term, attn_terms = summed
     shards = pb * pa
-    share = 1.0 / pa
-    small_list = [
-        attn_gain_grad[0], ffn_gain_grad[0], final_gain_grad[0], enc_bias_grad,
-        dec_gain_self_grad * share, dec_gain_cross_grad * share, dec_gain_ffn_grad * share, dec_bias_grad * share,
-    ]
-    small_rows = [s.shape[0] // shards for s in small_list]
-    small = scatter_small(jnp.concatenate([s.reshape(shards, -1) for s in small_list], axis=1), orders, sizes)
-    cuts = np.cumsum([0] + small_rows)
-    smalls = [small[a:b] for a, b in zip(cuts[:-1], cuts[1:])]
+    shard = lax.axis_index("pb") * pa + lax.axis_index("pa")
+    gains = lax.dynamic_slice_in_dim(small[:6, :D], shard * (D // shards), D // shards, 1)
+    width = BUCKETS * HEADS // shards
+
+    def bias_grad(folded, to_bucket):
+        flat = jnp.dot(folded, to_bucket, precision=highest).T.reshape(BUCKETS * HEADS)
+        return lax.dynamic_slice_in_dim(flat, shard * width, width)
+
+    enc_bias_grad = bias_grad(small[8 : 8 + HEADS], enc_table)
+    dec_bias_grad = bias_grad(small[8 + HEADS :, :128], dec_table)
 
     return (
-        enc_out, to_low(dec_y), enc_in_grad, dec_in_grad,
-        smalls[0], attn_terms[:, :D], attn_terms[:, D : 2 * D], attn_terms[:, 2 * D :], output_term, smalls[3],
-        smalls[1], ff_in_term, ff_out_term, smalls[2], cross_terms[:, :D], cross_terms[:, D:],
-        smalls[4], got[0], got[1], got[2], got[3], smalls[7], smalls[5], got[4], got[5], smalls[6], dec_ff_in_grad, got[6],
+        enc_out, dec_out, enc_in_grad, dec_in_grad,
+        gains[0], attn_terms[:, :D], attn_terms[:, D : 2 * D], attn_terms[:, 2 * D :], output_term, enc_bias_grad,
+        gains[1], ff_in_term, ff_out_term, gains[2], cross_terms[:, :D], cross_terms[:, D:],
+        gains[3], got[0], got[1], got[2], got[3], dec_bias_grad, gains[4], got[4], got[5], gains[5], dec_ff_in_grad, got[6],
     )
 
 

time: 597 us -> 456 us (0.76)
  Pallas kernels: 202 us -> 348 us
  waiting for transfers between devices: 127 us -> 43.7 us
  starting transfers between devices: 63.3 us -> 1.13 us
  matrix products: 52 us -> 5.76 us
  other arithmetic: 47.1 us -> 1.41 us
  local copies, waits for them, and re-layouts: 79.7 us -> 34.2 us
    pallas_call x2 -> x5, Pallas kernels: 44.9 us -> 203 us  [the longest x1 174 us: last_part(): pl.pallas_call(functools.partial(last_kernel, exchange, everywhere, point...]
    ppermute x46 -> x4, waiting for transfers between devices: 127 us -> 6.05 us  [near(): return (keep, lax.ppermute(send, 'pb', [(i, i ^ 1) for i in range(pb)]))]
    ppermute x46 -> x4, starting transfers between devices: 63.2 us -> 1.05 us  [near(): return (keep, lax.ppermute(send, 'pb', [(i, i ^ 1) for i in range(pb)]))]
    dot_general x32 -> x2, matrix products: 50.3 us -> 2.73 us  [bias_grad(): jnp.dot(folded, to_bucket, precision=highest).T.reshape(BUCKETS * HEADS)]
    psum x1, waiting for transfers between devices: 0.01 us -> 37.6 us  [local(): grad_cross_q = lax.psum(query_part, 'pa')]
    add x27 -> x0, other arithmetic: 27.7 us -> none  [the longest x24 25.7 us: summed(): total = total + part[first:last]]
    unnamed x217 -> x82, local copies, waits for them, and re-layouts: 31 us -> 16.6 us
    pallas_call x5 -> x4, Pallas kernels: 53 us -> 40.4 us  [weight_grad(): pl.pallas_call(functools.partial(weight_grad_kernel, rows, pb, pa, tiles,...]
  transfers between devices with their start and end apart: 48 -> 6, of which waited for: 22 -> 3; matrix products, arithmetic and copies ran while one was open for 20% -> 2% of each run, Pallas kernels for 21% -> 54%
where the time goes in v2:
time: 456 us; the launch traced here: 449 us
  Pallas kernels  348 us (76%)
  waiting for transfers between devices  43.7 us (10%)
  local copies, waits for them, and re-layouts  34.2 us (8%)
  between operations  15 us (3%)
  matrix products  5.76 us (1%)
    pallas_call x1, Pallas kernels, last_part(): pl.pallas_call(functools.partial(last_kernel, exchange, everywhere, point...  174 us
    pallas_call x4, Pallas kernels, weight_grad(): pl.pallas_call(functools.partial(weight_grad_kernel, rows, pb, pa, tiles,...  40.4 us
    psum x1, waiting for transfers between devices, local(): grad_cross_q = lax.psum(query_part, 'pa')  37.6 us
    pallas_call x1, Pallas kernels, post_backward(): pl.pallas_call(back_kernel, grid=(tokens // tile,), in_specs=[pl.BlockSpe...  26.5 us
    pallas_call x1, Pallas kernels, post_forward(): pl.pallas_call(post_kernel, grid=(tokens // tile,), in_specs=[d, d] + [wh...  25.7 us
    pallas_call x1, Pallas kernels, attn_forward(): pl.pallas_call(attn_forward_kernel, grid_spec=pltpu.PrefetchScalarGridSpe...  19.3 us
    pallas_call x1, Pallas kernels, merge(): pl.pallas_call(functools.partial(merge_kernel, pa), in_specs=[vmem], out_...  17.7 us
    unnamed x82, local copies, waits for them, and re-layouts  16.6 us
  transfers between devices with their start and end apart: 6, of which 3 were waited for; matrix products, arithmetic and copies ran while one was open for 2% of the time, Pallas kernels for 54%

profile of v2, /device:TPU:0, one launch (start us, length us, event | category | flops | bytes accessed | tf_op | source)
XLA Modules:
  0.0 449.2 jit_solution(8910108203099234768)
XLA Ops:
  7.3 0.7 reshape.91.gain_ref
  8.0 1.4 convolution_bitcast_fusion
  9.4 1.3 reshape.92.gain_ffn_ref
  10.7 1.3 reshape.93.gain_final_ref
  12.0 1.3 reshape.94.gain_self_ref
  13.2 1.3 reshape.95.gain_cross_ref
  14.5 1.6 convolution_bitcast_fusion.1.base_ref
  16.1 1.4 copy-done.3
  17.6 1.3 copy-done.11
  18.8 1.3 copy-done.12
  20.1 1.3 copy-done.13
  21.4 4.9 %enc_qkv.1 = (bf16[768,1024]{1,0:T(8,128)(2,1)S(1)}, bf16[1024,768]{1,0:T(8,128)(2,1)S(1)}, bf16[1024,768]{1,0:T(8,128)(2,1)S(1)}, bf16[1024,768]{1,0:T(8,128)(2,1)S(1)}) custom-call(bf16[1024,768]{1,0:T(8,128)(2,1)S(1)} %copy-done.3, f32[1,768]{1,0:T(1,128)S(1)} %reshape.91.gain_ref, bf16[768,768]{1,0:T(8,128)(2,1)S(1)} %copy-done.11, ...), custom_call_target="tpu_custom_call" | custom-call | tf_op jit(solution)/shard_map/enc_qkv/pallas_call | solution.py:278
  26.3 1.2 copy-done.14
  27.5 19.3 %enc_attention.1 = (bf16[1024,768]{1,0:T(8,128)(2,1)S(1)}, f32[6,2,2,512]{3,2,1,0:T(2,128)S(1)}) custom-call(s32[2]{0:T(128)S(1)} %copy-done.22, bf16[1024,768]{1,0:T(8,128)(2,1)S(1)} %get-tuple-element.92.q_ref, bf16[1024,768]{1,0:T(8,128)(2,1)S(1)} %get-tuple-element.93.k_ref, bf16[1024,768]{1,0:T(8,128)(2,1)S(1)} %get-tuple-element.94.v_ref, ...), custom_call_target="tpu_custom_call" | custom-call | tf_op jit(solution)/shard_map/enc_attention/pallas_call | solution.py:132
  46.8 1.2 copy-done.2
  48.6 25.7 %enc_post.1 = (f32[1024,768]{1,0:T(8,128)}, bf16[1024,768]{1,0:T(8,128)(2,1)}, bf16[1024,3072]{1,0:T(8,128)(2,1)}, bf16[1024,3072]{1,0:T(8,128)(2,1)}, f32[1024,...) custom-call(bf16[1024,768]{1,0:T(8,128)(2,1)} %x_ref.9, ...), custom_call_target="tpu_custom_call" | custom-call | tf_op jit(solution)/shard_map/enc_post/pallas_call | solution.py:325
  74.4 6.3 %dec_pre.1 = (bf16[48,768]{1,0:T(8,128)(2,1)}, bf16[48,768]{1,0:T(8,128)(2,1)}, bf16[48,768]{1,0:T(8,128)(2,1)}, bf16[48,768]{1,0:T(8,128)(2,1)}, f32[12,48,48]{...) custom-call(bf16[48,768]{1,0:T(8,128)(2,1)} %x_ref.8, ...), custom_call_target="tpu_custom_call" | custom-call | tf_op jit(solution)/shard_map/dec_pre/pallas_call | solution.py:700
  80.7 0.9 copy-done.17
  81.6 4.6 %cross_part.1 = f32[48,896]{1,0:T(8,128)S(1)} custom-call(s32[2]{0:T(128)S(1)} %copy-done.24, s32[2]{0:T(128)S(1)} %copy-done.22, bf16[48,768]{1,0:T(8,128)(2,1)S(1)} %copy-done.17, bf16[1024,768]{1,0:T(8,128)(2,1)S(1)} %copy-done.9, bf16[1024,768]{1,0:T(8,128)(2,1)S(1)} %copy-done.10), custom_call_target="tpu_custom_call" | custom-call | tf_op jit(solution)/shard_map/cross_part/pallas_call | solution.py:511
  86.3 17.7 %cross_merge.1 = f32[8,6,896]{2,1,0:T(8,128)S(1)} custom-call(f32[8,6,896]{2,1,0:T(8,128)S(1)} %reshape.86.part_ref), custom_call_target="tpu_custom_call" | custom-call | tf_op jit(solution)/shard_map/cross_merge/pallas_call | solution.py:581
  104.0 0.7 copy-done.15
  104.7 1.0 reshape.87.merged_ref
  106.3 10.6 %dec_mid.1 = (bf16[48,768]{1,0:T(8,128)(2,1)}, bf16[48,768]{1,0:T(8,128)(2,1)}, bf16[48,3072]{1,0:T(8,128)(2,1)}, bf16[48,3072]{1,0:T(8,128)(2,1)}, bf16[48,768]...) custom-call(f32[48,896]{1,0:T(8,128)} %copy-done.26, ...), custom_call_target="tpu_custom_call" | custom-call | tf_op jit(solution)/shard_map/dec_mid/pallas_call | solution.py:762
  117.0 0.9 copy-done.19
  117.9 5.7 %cross_back.1 = (f32[48,768]{1,0:T(8,128)}, bf16[2,1024,768]{2,1,0:T(8,128)(2,1)S(1)}) custom-call(s32[2]{0:T(128)S(1)} %copy-done.24, s32[2]{0:T(128)S(1)} %copy-done.23, bf16[48,768]{1,0:T(8,128)(2,1)S(1)} %copy-done.18, bf16[1024,768]{1,0:T(8,128)(2,1)S(1)} %copy-done.9, bf16[1024,768]{1,0:T(8,128)(2,1)S(1)} %copy-done.10, ...), custom_call_target="tpu_custom_call" | custom-call | tf_op jit(solution)/shard_map/cross_back/pallas_call | solution.py:634
  123.5 1.7 copy-done.4
  125.3 26.5 %enc_post_back.1 = (bf16[1024,768]{1,0:T(8,128)(2,1)}, bf16[1024,3072]{1,0:T(8,128)(2,1)}, bf16[1024,768]{1,0:T(8,128)(2,1)}, f32[1024,768]{1,0:T(8,128)}, bf16[...) custom-call(bf16[2,1024,768]{2,1,0:T(8,128)(2,1)} %copy-done.4, f32[1024,768]{1,0:T(8,128)} %get-tuple-element.104.y_ref, ...), custom_call_target="tpu_custom_call" | custom-call | tf_op jit(solution)/shard_map/enc_post_back/pallas_call | solution.py:381
  152.6 6.2 %weight_grad.4 = (f32[16,24,768]{2,1,0:T(8,128)}, f32[16,24,768]{2,1,0:T(8,128)}) custom-call(s32[4,16]{1,0:T(4,128)} %pad_add_fusion.table_ref, bf16[1024,768]{1,0:T(8,128)(2,1)} %copy-done.2, bf16[1024,768]{1,0:T(8,128)(2,1)} %get-tuple-element.117.refs_0_), custom_call_target="tpu_custom_call" | custom-call | tf_op jit(solution)/shard_map/weight_grad/pallas_call | solution.py:458
  158.8 37.6 %all-reduce.2.cloned.1.call-done.gq_ref = f32[48,768]{1,0:T(8,128)} async-done(((f32[48,768]{1,0:T(8,128)}), f32[48,768]{1,0:T(8,128)}) %all-reduce.2.cloned.1.call-update) | async-done | bytes 147472 | tf_op jit(solution)/shard_map/psum | solution.py:1473
  196.4 7.5 %dec_post.1 = (bf16[48,768]{1,0:T(8,128)(2,1)}, bf16[48,768]{1,0:T(8,128)(2,1)}, bf16[48,768]{1,0:T(8,128)(2,1)}, bf16[48,768]{1,0:T(8,128)(2,1)}, f32[48,768]{1...) custom-call(f32[48,768]{1,0:T(8,128)} %all-reduce.2.cloned.1.call-done.gq_ref, ...), custom_call_target="tpu_custom_call" | custom-call | tf_op jit(solution)/shard_map/dec_post/pallas_call | solution.py:834
  203.9 4.6 %dec_weight_grads.1.refs_13_ = f32[4,336,768]{2,1,0:T(8,128)} custom-call(s32[1]{0:T(128)} %bitcast.7.column_ref, bf16[48,768]{1,0:T(8,128)(2,1)} %get-tuple-element.137.low_ref, bf16[48,768]{1,0:T(8,128)(2,1)} %get-tuple-element.138.dq_ref, bf16[48,768]{1,0:T(8,128)(2,1)} %get-tuple-element.139.dk_ref, bf16[48,768]{1,0:T(8,128)(2,1)} %get-tuple-element.140.dv_ref, ...), custom_call_target="tpu_custom_call" | custom-call | tf_op jit(solution)/shard_map/dec_weight_grads/pallas_call | solution.py:892
  208.6 12.7 %weight_grad.6 = (f32[16,96,768]{2,1,0:T(8,128)}, f32[16,96,768]{2,1,0:T(8,128)}) custom-call(s32[4,16]{1,0:T(4,128)} %pad_add_fusion.table_ref, bf16[1024,3072]{1,0:T(8,128)(2,1)} %get-tuple-element.127.left_ref, bf16[1024,768]{1,0:T(8,128)(2,1)} %get-tuple-element.128.refs_0_), custom_call_target="tpu_custom_call" | custom-call | tf_op jit(solution)/shard_map/weight_grad/pallas_call | solution.py:458
  221.3 12.4 %weight_grad.7 = (f32[16,24,3072]{2,1,0:T(8,128)}, f32[16,24,3072]{2,1,0:T(8,128)}) custom-call(s32[4,16]{1,0:T(4,128)} %pad_add_fusion.table_ref, bf16[1024,768]{1,0:T(8,128)(2,1)} %get-tuple-element.130.left_ref, bf16[1024,3072]{1,0:T(8,128)(2,1)} %get-tuple-element.131.refs_0_), custom_call_target="tpu_custom_call" | custom-call | tf_op jit(solution)/shard_map/weight_grad/pallas_call | solution.py:458
  234.2 1.9 slice_bitcast_fusion
  236.1 9.1 %weight_grad.5 = (f32[16,24,1536]{2,1,0:T(8,128)}, f32[16,24,1536]{2,1,0:T(8,128)}) custom-call(s32[4,16]{1,0:T(4,128)} %pad_add_fusion.table_ref, bf16[1024,768]{1,0:T(8,128)(2,1)} %get-tuple-element.125.left_ref, bf16[1024,768]{1,0:T(8,128)(2,1)} %get-tuple-element.157.refs_0_, bf16[1024,768]{1,0:T(8,128)(2,1)} %get-tuple-element.156.refs_1_), custom_call_target="tpu_custom_call" | custom-call | tf_op jit(solution)/shard_map/weight_grad/pallas_call | solution.py:458
  245.8 5.4 %collective-permute-done.3.refs_12_ = f32[16,24,768]{2,1,0:T(8,128)S(1)} collective-permute-done((f32[16,24,768]{2,1,0:T(8,128)S(1)}, f32[16,24,768]{2,1,0:T(8,128)S(1)}, u32[]{:S(2)}, u32[]{:S(2)}) %collective-permute-start.3) | collective-permute-done | bytes 1179680 | tf_op jit(solution)/shard_map/ppermute | solution.py:1477
  251.2 0.7 collective-permute-done.refs_9_
  252.2 174.1 %enc_last.1 = (f32[1024,768]{1,0:T(8,128)}, f32[32,1024]{1,0:T(8,128)}, f32[24,1536]{1,0:T(8,128)}, f32[96,768]{1,0:T(8,128)}, f32[24,3072]{1,0:T(8,128)}, /*index=5*/f32[24,768]{1,0:T(8,128)}, f32[24,2304]{1,0:T(8,128)}) custom-call(s32[2]{0:T(128)} %lengths_ref.3, bf16[1024,768]{1,0:T(8,128)(2,1)} %copy-done.6, bf16[1024,768]{1,0:T(8,128)(2,1)} %copy-done.7, ...), custom_call_target="tpu_custom_call" | custom-call | tf_op jit(solution)/shard_map/enc_last/pallas_call | solution.py:1390
  426.3 0.7 slice.124
  427.1 1.8 fusion
  429.0 0.9 fusion.2
  431.9 1.9 fusion.4
  433.8 2.0 slice_bitcast_fusion.6
  435.7 0.7 pad_maximum_fusion
  436.5 1.7 slice_bitcast_fusion.2
  438.2 1.7 copy.71
  440.5 0.7 copy.73
  441.2 0.7 copy.74
  (94 shorter events, 6.3 us)
Async XLA Ops:
  7.2 0.8 copy-start
  7.2 189.2 %all-reduce.2.cloned.1.call-start = ((), (), s32[]{:S(2)}) async-start(), calls=%async_computation.1 | async-start | bytes 294912 | tf_op jit(solution)/shard_map/psum | solution.py:1473
  8.0 18.3 %copy-start.21 = (f32[1,768]{1,0:T(1,128)}, f32[1,768]{1,0:T(1,128)S(1)}, u32[]{:S(2)}) copy-start(f32[1,768]{1,0:T(1,128)S(1)} %reshape.91.gain_ref) | copy-start | bytes 9220
  9.4 18.1 %copy-start.16 = (f32[6,2,1024]{2,1,0:T(2,128)}, f32[6,2,1024]{2,1,0:T(2,128)S(1)}, u32[]{:S(2)}) copy-start(f32[6,2,1024]{2,1,0:T(2,128)S(1)} %reshape.85.base_ref) | copy-start | bytes 147460
  16.1 1.4 copy-start.3
  17.5 1.3 copy-start.11
  18.8 1.3 copy-start.12
  20.1 1.3 copy-start.13
  21.4 6.1 %copy-start.22 = (s32[2]{0:T(128)S(1)}, s32[2]{0:T(128)}, u32[]{:S(2)}) copy-start(s32[2]{0:T(128)} %lengths_ref.3) | copy-start | bytes 28
  26.3 1.2 copy-start.14
  27.5 19.3 %copy-start.6 = (bf16[1024,768]{1,0:T(8,128)(2,1)}, bf16[1024,768]{1,0:T(8,128)(2,1)S(1)}, u32[]{:S(2)}) copy-start(bf16[1024,768]{1,0:T(8,128)(2,1)S(1)} %get-tuple-element.92.q_ref) | copy-start | bytes 4718596
  27.5 19.3 %copy-start.7 = (bf16[1024,768]{1,0:T(8,128)(2,1)}, bf16[1024,768]{1,0:T(8,128)(2,1)S(1)}, u32[]{:S(2)}) copy-start(bf16[1024,768]{1,0:T(8,128)(2,1)S(1)} %get-tuple-element.93.k_ref) | copy-start | bytes 4718596
  27.5 19.3 %copy-start.8 = (bf16[1024,768]{1,0:T(8,128)(2,1)}, bf16[1024,768]{1,0:T(8,128)(2,1)S(1)}, u32[]{:S(2)}) copy-start(bf16[1024,768]{1,0:T(8,128)(2,1)S(1)} %get-tuple-element.94.v_ref) | copy-start | bytes 4718596
  46.8 1.2 copy-start.2
  48.0 0.6 copy-start.20
  74.3 6.4 %copy-start.9 = (bf16[1024,768]{1,0:T(8,128)(2,1)S(1)}, bf16[1024,768]{1,0:T(8,128)(2,1)}, u32[]{:S(2)}) copy-start(bf16[1024,768]{1,0:T(8,128)(2,1)} %get-tuple-element.98.ck_ref) | copy-start | bytes 4718596
  74.3 6.4 %copy-start.10 = (bf16[1024,768]{1,0:T(8,128)(2,1)S(1)}, bf16[1024,768]{1,0:T(8,128)(2,1)}, u32[]{:S(2)}) copy-start(bf16[1024,768]{1,0:T(8,128)(2,1)} %get-tuple-element.99.cv_ref) | copy-start | bytes 4718596
  74.3 6.4 %copy-start.24 = (s32[2]{0:T(128)S(1)}, s32[2]{0:T(128)}, u32[]{:S(2)}) copy-start(s32[2]{0:T(128)} %question_ref.3) | copy-start | bytes 28
  80.7 0.9 copy-start.17
  86.2 19.5 %copy-start.33 = (bf16[768]{0:T(1024)(128)(2,1)S(1)}, bf16[768]{0:T(1024)(128)(2,1)}, u32[]{:S(2)}) copy-start(bf16[768]{0:T(1024)(128)(2,1)} %param.59) | copy-start | bytes 4612
  104.0 0.7 copy-start.15
  105.7 0.7 copy-start.26
  106.3 10.6 %copy-start.18 = (bf16[48,768]{1,0:T(8,128)(2,1)S(1)}, bf16[48,768]{1,0:T(8,128)(2,1)}, u32[]{:S(2)}) copy-start(bf16[48,768]{1,0:T(8,128)(2,1)} %get-tuple-element.97.q_ref) | copy-start | bytes 221188
  106.3 10.6 %copy-start.23 = (s32[2]{0:T(128)S(1)}, s32[2]{0:T(128)}, u32[]{:S(2)}) copy-start(s32[2]{0:T(128)} %lengths_ref.3) | copy-start | bytes 28
  117.0 0.9 copy-start.19
  123.5 1.7 copy-start.4
  125.2 308.5 %reduce-scatter.2.cloned.1.call-start = ((), (), s32[]{:S(2)}) async-start(), calls=%async_computation.2 | async-start | bytes 5160960 | tf_op jit(solution)/shard_map/reduce_scatter | solution.py:1495
  125.3 26.5 %copy-start.34 = (s32[16]{0:T(128)S(1)}, s32[16]{0:T(128)}, u32[]{:S(2)}) copy-start(s32[16]{0:T(128)} %constant.50) | copy-start | bytes 196
  125.3 26.5 %copy-start.35 = (s32[16]{0:T(128)S(1)}, s32[16]{0:T(128)}, u32[]{:S(2)}) copy-start(s32[16]{0:T(128)} %constant.51) | copy-start | bytes 196
  125.3 26.5 %copy-start.36 = (s32[16]{0:T(128)S(1)}, s32[16]{0:T(128)}, u32[]{:S(2)}) copy-start(s32[16]{0:T(128)} %constant.52) | copy-start | bytes 196
  125.3 26.5 %copy-start.37 = (s32[16]{0:T(128)S(1)}, s32[16]{0:T(128)}, u32[]{:S(2)}) copy-start(s32[16]{0:T(128)} %constant.53) | copy-start | bytes 196
  221.2 30.6 %collective-permute-start.1 = (f32[16,96,768]{2,1,0:T(8,128)}, f32[16,96,768]{2,1,0:T(8,128)}, u32[]{:S(2)}, u32[]{:S(2)}) collective-permute-start(f32[16,96,768]{2,1,0:T(8,128)} %get-tuple-element.134), channel_id=1, source_target_pairs={{0,8},{8,0},{16,24},{24,16},{1,9},{9,1},{17,25},{25,17},{2,10},{10... | collective-permute-start | bytes 14155784 | tf_op jit(solution)/shard_map/ppermute | solution.py:1477
  221.2 13.0 %copy-start.5 = (bf16[2,1024,768]{2,1,0:T(8,128)(2,1)S(1)}, bf16[2,1024,768]{2,1,0:T(8,128)(2,1)}, u32[]{:S(2)}) copy-start(bf16[2,1024,768]{2,1,0:T(8,128)(2,1)} %copy-done.4) | copy-start | bytes 9437188
  233.7 18.2 %collective-permute-start.2 = (f32[16,24,3072]{2,1,0:T(8,128)}, f32[16,24,3072]{2,1,0:T(8,128)}, u32[]{:S(2)}, u32[]{:S(2)}) collective-permute-start(f32[16,24,3072]{2,1,0:T(8,128)} %get-tuple-element.135), channel_id=1, source_target_pairs={{0,8},{8,0},{16,24},{24,16},{1,9},{9,1},{17,25},{25,17},{2,10},{10... | collective-permute-start | bytes 14155784 | tf_op jit(solution)/shard_map/ppermute | solution.py:1477
  236.1 9.2 %copy-start.38 = (f32[16,24,768]{2,1,0:T(8,128)S(1)}, f32[16,24,768]{2,1,0:T(8,128)}, u32[]{:S(2)}) copy-start(f32[16,24,768]{2,1,0:T(8,128)} %get-tuple-element.136) | copy-start | bytes 3538948
  245.3 6.6 %collective-permute-start = (f32[16,24,1536]{2,1,0:T(8,128)}, f32[16,24,1536]{2,1,0:T(8,128)}, u32[]{:S(2)}, u32[]{:S(2)}) collective-permute-start(f32[16,24,1536]{2,1,0:T(8,128)} %get-tuple-element.133), channel_id=1, source_target_pairs={{0,8},{8,0},{16,24},{24,16},{1,9},{9,1},{17,25},{25,17},{2,10},{10... | collective-permute-start | bytes 7077896 | tf_op jit(solution)/shard_map/ppermute | solution.py:1477
  245.3 5.8 %collective-permute-start.3 = (f32[16,24,768]{2,1,0:T(8,128)S(1)}, f32[16,24,768]{2,1,0:T(8,128)S(1)}, u32[]{:S(2)}, u32[]{:S(2)}) collective-permute-start(f32[16,24,768]{2,1,0:T(8,128)S(1)} %copy-done.38), channel_id=1, source_target_pairs={{0,8},{8,0},{16,24},{24,16},{1,9},{9,1},{17,25},{25,17},{2,10},{10... | collective-permute-start | bytes 3538952 | tf_op jit(solution)/shard_map/ppermute | solution.py:1477
  251.2 1.0 copy-start.28
  252.2 174.9 %copy-start.27 = (f32[1024,32]{1,0:T(8,128)S(1)}, f32[1024,32]{1,0:T(8,128)}, u32[]{:S(2)}) copy-start(f32[1024,32]{1,0:T(8,128)} %constant.46.clone) | copy-start | bytes 393220
  252.2 176.8 %copy-start.31 = (f32[128,32]{1,0:T(8,128)S(1)}, f32[128,32]{1,0:T(8,128)}, u32[]{:S(2)}) copy-start(f32[128,32]{1,0:T(8,128)} %constant.47.clone) | copy-start | bytes 49156
  431.8 6.3 %copy-start.25 = (f32[1024,768]{1,0:T(8,128)S(1)}, f32[1024,768]{1,0:T(8,128)}, u32[]{:S(2)}) copy-start(f32[1024,768]{1,0:T(8,128)} %get-tuple-element.214) | copy-start | bytes 9437188
  438.2 1.7 copy-start.32
  438.2 2.3 copy-start.30
  438.2 3.0 copy-start.29
  438.2 3.8 copy-start.1
Sparse Core Ops, SparseCore 0:
  125.3 71.0 all-reduce.1
  208.7 43.1 reduce-scatter.1

commit v3 on v2

--- a/solution.py
+++ b/solution.py
@@ -89,8 +89,16 @@
         strip_ref[head] = pltpu.roll(spread, 0, 1, stride=1, stride_axis=0)
 
 
-def attn_forward_kernel(lengths_ref, q_ref, k_ref, v_ref, base_ref, out_ref, lse_ref, strip_ref, score_ref, outT_ref):
+def attn_forward_kernel(lengths_ref, q_ref, k_ref, v_ref, bias_ref, table_ref, out_ref, turned_ref, lse_ref, base_ref, rows_ref, strip_ref, score_ref):
     passage = pl.program_id(1)
+
+    @pl.when((passage == 0) & (pl.program_id(0) == 0))
+    def _():
+        every = product_tn(bias_ref[...], table_ref[...])
+        for pair in range(HEADS // 2):
+            rows_ref[pair] = every[2 * pair : 2 * pair + 2]
+
+    base_ref[...] = rows_ref[pl.ds(pl.program_id(0), 1)]
 
     @pl.when(passage == 0)
     def _():
@@ -120,12 +128,12 @@
             total = here if total is None else total + here
             part = nn(v_t[head * HEAD : (head + 1) * HEAD, rows], to_low(e))
             acc = part if acc is None else acc + part
-        outT_ref[head * HEAD : (head + 1) * HEAD, :] = to_low(acc * (1.0 / total))
+        turned_ref[head * HEAD : (head + 1) * HEAD, :] = to_low(acc * (1.0 / total))
         lse_ref[0, 0, head : head + 1, :] = top + jnp.log(total)
-    out_ref[...] = outT_ref[...].T
-
-
-def attn_forward(lengths, q, k, v, base):
+    out_ref[...] = turned_ref[...].T
+
+
+def attn_forward(lengths, q, k, v, bias, table):
     passages = lengths.shape[0]
     pairs = HEADS // 2
     tile = pl.BlockSpec((PL, 128), lambda h, p, *_: (p, h))
@@ -134,21 +142,28 @@
         grid_spec=pltpu.PrefetchScalarGridSpec(
             num_scalar_prefetch=1,
             grid=(pairs, passages),
-            in_specs=[tile, tile, tile, pl.BlockSpec((1, 2, WIDE), lambda h, p, *_: (h, 0, 0))],
-            out_specs=[tile, pl.BlockSpec((1, 1, 2, PL), lambda h, p, *_: (h, p, 0, 0))],
+            in_specs=[tile, tile, tile, pl.BlockSpec(bias.shape, lambda h, p, *_: (0, 0)), pl.BlockSpec(table.shape, lambda h, p, *_: (0, 0))],
+            out_specs=[
+                tile,
+                pl.BlockSpec((128, PL), lambda h, p, *_: (h, p)),
+                pl.BlockSpec((1, 1, 2, PL), lambda h, p, *_: (h, p, 0, 0)),
+                pl.BlockSpec((1, 2, WIDE), lambda h, p, *_: (h, 0, 0)),
+            ],
             scratch_shapes=[
+                pltpu.VMEM((pairs, 2, WIDE), jnp.float32),
                 pltpu.VMEM((2, STRIP, WIDE), jnp.float32),
                 pltpu.VMEM((2, PL, PL), jnp.float32),
-                pltpu.VMEM((128, PL), jnp.bfloat16),
             ],
         ),
         out_shape=[
             jax.ShapeDtypeStruct((passages * PL, D), jnp.bfloat16),
+            jax.ShapeDtypeStruct((D, passages * PL), jnp.bfloat16),
             jax.ShapeDtypeStruct((pairs, passages, 2, PL), jnp.float32),
+            jax.ShapeDtypeStruct((pairs, 2, WIDE), jnp.float32),
         ],
-        compiler_params=pltpu.CompilerParams(vmem_limit_bytes=32 * 2**20),
+        compiler_params=pltpu.CompilerParams(vmem_limit_bytes=62 * 2**20),
         name="enc_attention",
-    )(lengths, q, k, v, base)
+    )(lengths, q, k, v, bias, table)
 
 
 def attn_backward_kernel(
@@ -246,6 +261,13 @@
     return v * half, slope
 
 
+GAIN_ATTN, GAIN_FFN, GAIN_FINAL, GAIN_SELF, GAIN_CROSS, GAIN_DFFN = range(6)
+
+
+def gain_of(gains_ref, which):
+    return gains_ref[which : which + 1, :]
+
+
 def whole(array):
     return pl.BlockSpec(array.shape, lambda *_: (0,) * array.ndim)
 
@@ -262,8 +284,8 @@
     return pltpu.CompilerParams(vmem_limit_bytes=mib * MIB)
 
 
-def qkv_kernel(x_ref, gain_ref, wq_ref, wk_ref, wv_ref, turned_ref, q_ref, k_ref, v_ref):
-    normed, _ = rms(x_ref[...].astype(jnp.float32), gain_ref[...])
+def qkv_kernel(x_ref, gains_ref, wq_ref, wk_ref, wv_ref, turned_ref, q_ref, k_ref, v_ref):
+    normed, _ = rms(x_ref[...].astype(jnp.float32), gain_of(gains_ref, GAIN_ATTN))
     low = to_low(normed)
     turned_ref[...] = low.T
     q_ref[...] = to_low(0.125 * to_low(nn(low, wq_ref[...])).astype(jnp.float32))
@@ -271,49 +293,49 @@
     v_ref[...] = to_low(nn(low, wv_ref[...]))
 
 
-def qkv_forward(x, gain, wq, wk, wv):
+def qkv_forward(x, gains, wq, wk, wv):
     tokens = x.shape[0]
     tile = 256
     big = sds((tokens, D), jnp.bfloat16)
     return pl.pallas_call(
         qkv_kernel,
         grid=(tokens // tile,),
-        in_specs=[rows_of(tile, D)] + [whole(a) for a in (gain, wq, wk, wv)],
+        in_specs=[rows_of(tile, D)] + [whole(a) for a in (gains, wq, wk, wv)],
         out_specs=[pl.BlockSpec((D, tile), lambda i: (0, i))] + [rows_of(tile, D)] * 3,
         out_shape=[sds((D, tokens), jnp.bfloat16)] + [big] * 3,
-        compiler_params=params(40),
+        compiler_params=params(62),
         name="enc_qkv",
-    )(x, gain, wq, wk, wv)
+    )(x, gains, wq, wk, wv)
 
 
 def post_kernel(
-    x_ref, att_ref, gain_ffn_ref, gain_final_ref, wo_ref, win_ref, wout_ref, wck_ref, wcv_ref,
-    mid_ref, ffn_low_ref, hidden_ref, slope_ref, y_ref, out_ref, final_low_ref, ck_ref, cv_ref,
+    x_ref, att_ref, gains_ref, wo_ref, win_ref, wout_ref, wck_ref, wcv_ref,
+    mid_ref, ffn_turned_ref, hidden_turned_ref, slope_ref, y_ref, out_ref, final_turned_ref, ck_ref, cv_ref,
 ):
     mid = x_ref[...].astype(jnp.float32) + nn(att_ref[...], wo_ref[...])
     mid_ref[...] = mid
-    normed, _ = rms(mid, gain_ffn_ref[...])
+    normed, _ = rms(mid, gain_of(gains_ref, GAIN_FFN))
     low = to_low(normed)
-    ffn_low_ref[...] = low
+    ffn_turned_ref[...] = low.T
     y = mid
     width = 768
     for c in range(win_ref.shape[1] // width):
         cols = slice(c * width, (c + 1) * width)
         hidden, slope = gelu_both(nn(low, win_ref[:, cols]))
         hidden = to_low(hidden)
-        hidden_ref[:, cols] = hidden
+        hidden_turned_ref[cols, :] = hidden.T
         slope_ref[:, cols] = to_low(slope)
         y = y + nn(hidden, wout_ref[cols, :])
     y_ref[...] = y
     out_ref[...] = to_low(y)
-    final, _ = rms(y, gain_final_ref[...])
+    final, _ = rms(y, gain_of(gains_ref, GAIN_FINAL))
     final = to_low(final)
-    final_low_ref[...] = final
+    final_turned_ref[...] = final.T
     ck_ref[...] = to_low(nn(final, wck_ref[...]))
     cv_ref[...] = to_low(nn(final, wcv_ref[...]))
 
 
-def post_forward(x, att, gain_ffn, gain_final, wo, win, wout, wck, wcv):
+def post_forward(x, att, gains, wo, win, wout, wck, wcv):
     tokens = x.shape[0]
     tile = 256
     ff = win.shape[1]
@@ -322,22 +344,26 @@
     full = sds((tokens, D), jnp.float32)
     d = rows_of(tile, D)
     f = rows_of(tile, ff)
+    turned = pl.BlockSpec((D, tile), lambda i: (0, i))
+    flat = sds((D, tokens), jnp.bfloat16)
     return pl.pallas_call(
         post_kernel,
         grid=(tokens // tile,),
-        in_specs=[d, d] + [whole(a) for a in (gain_ffn, gain_final, wo, win, wout, wck, wcv)],
-        out_specs=[d, d, f, f, d, d, d, d, d],
-        out_shape=[full, low, wide, wide, full, low, low, low, low],
-        compiler_params=params(56),
+        in_specs=[d, d] + [whole(a) for a in (gains, wo, win, wout, wck, wcv)],
+        out_specs=[d, turned, pl.BlockSpec((ff, tile), lambda i: (0, i)), f, d, d, turned, d, d],
+        out_shape=[full, flat, sds((ff, tokens), jnp.bfloat16), wide, full, low, flat, low, low],
+        compiler_params=params(62),
         name="enc_post",
-    )(x, att, gain_ffn, gain_final, wo, win, wout, wck, wcv)
+    )(x, att, gains, wo, win, wout, wck, wcv)
 
 
 def back_kernel(
-    gkv_ref, y_ref, mid_ref, slope_ref, cot_ref, gain_ffn_ref, gain_final_ref,
-    wck_ref, wcv_ref, wout_ref, win_ref, wo_ref,
-    eout_ref, epre_ref, emid_ref, grad_mid_ref, att_grad_ref, gain_final_grad_ref, gain_ffn_grad_ref,
+    gkv_ref, y_ref, mid_ref, slope_ref, cot_ref, gains_ref,
+    wck_ref, wcv_ref, wout_ref, win_ref, wo_ref, after_ref,
+    eout_ref, epre_ref, emid_ref, grad_mid_ref, att_grad_ref, gain_final_grad_ref, gain_ffn_grad_ref, tick_ref,
 ):
+    tick_ref[...] = jnp.zeros_like(tick_ref)
+
     @pl.when(pl.program_id(0) == 0)
     def _():
         gain_final_grad_ref[...] = jnp.zeros_like(gain_final_grad_ref)
@@ -346,7 +372,7 @@
     y = y_ref[...]
     scale = lax.rsqrt(jnp.mean(y * y, axis=-1, keepdims=True) + epsilon)
     final_back = nt(gkv_ref[0], wck_ref[...]) + nt(gkv_ref[1], wcv_ref[...])
-    back, gain_grad = rms_back(y, scale, gain_final_ref[...], final_back)
+    back, gain_grad = rms_back(y, scale, gain_of(gains_ref, GAIN_FINAL), final_back)
     gain_final_grad_ref[...] += gain_grad
     grad_y = cot_ref[...].astype(jnp.float32) + back
     eout = to_low(grad_y)
@@ -361,7 +387,7 @@
         acc = part if acc is None else acc + part
     mid = mid_ref[...]
     scale = lax.rsqrt(jnp.mean(mid * mid, axis=-1, keepdims=True) + epsilon)
-    back, gain_grad = rms_back(mid, scale, gain_ffn_ref[...], acc)
+    back, gain_grad = rms_back(mid, scale, gain_of(gains_ref, GAIN_FFN), acc)
     gain_ffn_grad_ref[...] += gain_grad
     grad_mid = grad_y + back
     grad_mid_ref[...] = grad_mid
@@ -370,7 +396,7 @@
     att_grad_ref[...] = to_low(nt(emid, wo_ref[...]))
 
 
-def post_backward(gkv, y, mid, slope, cot, gain_ffn, gain_final, wck, wcv, wout, win, wo):
+def post_backward(gkv, y, mid, slope, cot, gains, wck, wcv, wout, win, wo, after):
     tokens = y.shape[0]
     tile = 256
     ff = win.shape[1]
@@ -382,16 +408,18 @@
         back_kernel,
         grid=(tokens // tile,),
         in_specs=[pl.BlockSpec((2, tile, D), lambda i: (0, i, 0)), d, d, f, d]
-        + [whole(a) for a in (gain_ffn, gain_final, wck, wcv, wout, win, wo)],
-        out_specs=[d, f, d, d, d, gain, gain],
+        + [whole(a) for a in (gains, wck, wcv, wout, win, wo)]
+        + [pl.BlockSpec(memory_space=pl.ANY)],
+        out_specs=[d, f, d, d, d, gain, gain, pl.BlockSpec((1, 128), lambda i: (0, 0))],
         out_shape=[low, sds((tokens, ff), jnp.bfloat16), low, sds((tokens, D), jnp.float32), low]
-        + [sds((1, D), jnp.float32)] * 2,
-        compiler_params=params(56),
+        + [sds((1, D), jnp.float32)] * 2
+        + [sds((1, 128), jnp.float32)],
+        compiler_params=params(62),
         name="enc_post_back",
-    )(gkv, y, mid, slope, cot, gain_ffn, gain_final, wck, wcv, wout, win, wo)
-
-
-def qkv_back_kernel(opening, dq_ref, dk_ref, dv_ref, x_ref, grad_mid_ref, gain_ref, wq_ref, wk_ref, wv_ref, out_ref, gain_grad_ref):
+    )(gkv, y, mid, slope, cot, gains, wck, wcv, wout, win, wo, after)
+
+
+def qkv_back_kernel(opening, dq_ref, dk_ref, dv_ref, x_ref, grad_mid_ref, gains_ref, wq_ref, wk_ref, wv_ref, out_ref, gain_grad_ref):
     @pl.when(opening)
     def _():
         gain_grad_ref[...] = jnp.zeros_like(gain_grad_ref)
@@ -399,26 +427,19 @@
     x = x_ref[...].astype(jnp.float32)
     scale = lax.rsqrt(jnp.mean(x * x, axis=-1, keepdims=True) + epsilon)
     grad = nt(dq_ref[...], wq_ref[...]) + nt(dk_ref[...], wk_ref[...]) + nt(dv_ref[...], wv_ref[...])
-    back, gain_grad = rms_back(x, scale, gain_ref[...], grad)
+    back, gain_grad = rms_back(x, scale, gain_of(gains_ref, GAIN_ATTN), grad)
     gain_grad_ref[...] += gain_grad
     out_ref[...] = grad_mid_ref[...] + back
 
 
-def weight_grad_kernel(rows, pb, pa, tiles, per_chain, table_ref, left_ref, *refs):
+def weight_grad_kernel(rows, pb, pa, tiles, per_chain, table_ref, turned_ref, *refs):
     rights = refs[: len(tiles)]
-    keep_ref, send_ref, turned_ref = refs[len(tiles) :]
+    keep_ref, send_ref, tick_ref = refs[-3:]
     step = pl.program_id(0)
-    depth, height = left_ref.shape
-
-    @pl.when(step == 0)
-    def _():
-        for c in range(height // 256):
-            cols = slice(c * 256, (c + 1) * 256)
-            turned_ref[cols, :] = left_ref[:, cols].T
-
     core = table_ref[0, 0]
     chain = step // per_chain
     half_rows = pa * rows
+    tick_ref[...] = jnp.zeros_like(tick_ref)
 
     def work(right):
         for y in range(pb // 2):
@@ -436,21 +457,29 @@
         if len(tiles) == 1:
             work(right_ref[...])
         else:
+
             @pl.when((step >= first) & (step < first + count))
             def _(right_ref=right_ref):
-                work(right_ref[...])
+                work(right_ref[...] if len(right_ref.shape) == 2 else right_ref[0])
+
         first += count
 
 
-def weight_grad(table, left, rights, pb, pa, width, per_chain):
-    tokens, height = left.shape
+def weight_grad(table, turned, rights, pb, pa, width, per_chain, after=()):
+    height, tokens = turned.shape
     rows = height // (pb * pa)
-    tiles = [r.shape[1] // width for r in rights]
+    arrays = [r[0] if isinstance(r, tuple) else r for r in rights]
+    tiles = [a.shape[-1] // width for a in arrays]
     total = sum(tiles)
     firsts = np.cumsum([0] + tiles)[:-1]
 
-    def spec(first, count):
-        return pl.BlockSpec((tokens, width), lambda i, *_: (0, jnp.clip(i - int(first), 0, count - 1)))
+    def spec(right, first, count):
+        def column(i):
+            return jnp.clip(i - int(first), 0, count - 1)
+
+        if isinstance(right, tuple):
+            return pl.BlockSpec((1, tokens, width), lambda i, *_: (right[1], 0, column(i)))
+        return pl.BlockSpec((tokens, width), lambda i, *_: (0, column(i)))
 
     half = pb * pa // 2
     out = pl.BlockSpec((half, rows, width), lambda i, *_: (0, 0, i))
@@ -460,14 +489,15 @@
         grid_spec=pltpu.PrefetchScalarGridSpec(
             num_scalar_prefetch=1,
             grid=(total,),
-            in_specs=[pl.BlockSpec((tokens, height), lambda i, *_: (0, 0))] + [spec(f, c) for f, c in zip(firsts, tiles)],
-            out_specs=[out, out],
-            scratch_shapes=[pltpu.VMEM((height, tokens), jnp.bfloat16)],
+            in_specs=[pl.BlockSpec((height, tokens), lambda i, *_: (0, 0))]
+            + [spec(r, f, c) for r, f, c in zip(rights, firsts, tiles)]
+            + [pl.BlockSpec(memory_space=pl.ANY)] * len(after),
+            out_specs=[out, out, pl.BlockSpec((1, 128), lambda i, *_: (0, 0))],
         ),
-        out_shape=[shape, shape],
-        compiler_params=params(56),
+        out_shape=[shape, shape, sds((1, 128), jnp.float32)],
+        compiler_params=params(62),
         name="weight_grad",
-    )(table, left, *rights)
+    )(table, turned, *arrays, *after)
 
 
 PACK = 896
@@ -656,12 +686,13 @@
 
 
 def dec_pre_kernel(
-    x_ref, gain_self_ref, gain_cross_ref, base_ref, wq_ref, wk_ref, wv_ref, wo_ref, wcq_ref,
+    x_ref, gains_ref, bias_ref, table_ref, wq_ref, wk_ref, wv_ref, wo_ref, wcq_ref,
     low_ref, q_ref, k_ref, v_ref, probs_ref, att_ref, mid_ref, cross_low_ref, cross_q_ref,
 ):
     rows = x_ref.shape[0]
+    base = product_tn(bias_ref[...], table_ref[...])
     x = x_ref[...].astype(jnp.float32)
-    normed, _ = rms(x, gain_self_ref[...])
+    normed, _ = rms(x, gain_of(gains_ref, GAIN_SELF))
     low = to_low(normed)
     low_ref[...] = low
     q = to_low(0.125 * to_low(nn(low, wq_ref[...])).astype(jnp.float32))
@@ -679,7 +710,7 @@
         outs = []
         for half in range(2):
             head = 2 * pair + half
-            spread = jnp.broadcast_to(base_ref[head : head + 1, :], (rows, 128))
+            spread = jnp.broadcast_to(base[head : head + 1, :], (rows, 128))
             bias = pltpu.roll(spread, 0, 1, stride=1, stride_axis=0)[:, :rows]
             s = jnp.where(mask, nt(head_lanes(q[:, cols], half), k[:, cols]) + bias, -1e9)
             e = jnp.exp(s - jnp.max(s, axis=1, keepdims=True))
@@ -689,7 +720,7 @@
         att_ref[:, cols] = to_low(jnp.where(lane < HEAD, outs[0], outs[1]))
     mid = x + nn(att_ref[...], wo_ref[...])
     mid_ref[...] = mid
-    normed, _ = rms(mid, gain_cross_ref[...])
+    normed, _ = rms(mid, gain_of(gains_ref, GAIN_CROSS))
     low = to_low(normed)
     cross_low_ref[...] = low
     cross_q_ref[...] = to_low(nn(low, wcq_ref[...]))
@@ -702,27 +733,27 @@
         in_specs=[pl.BlockSpec(memory_space=pltpu.SMEM)] * smem + [vmem] * (len(args) - smem),
         out_specs=[vmem] * len(outs),
         out_shape=outs,
-        compiler_params=params(56),
+        compiler_params=params(62),
         name=name,
     )(*args)
 
 
-def dec_pre(x, gain_self, gain_cross, base, wq, wk, wv, wo, wcq):
+def dec_pre(x, gains, bias, table, wq, wk, wv, wo, wcq):
     rows = x.shape[0]
     low = sds((rows, D), jnp.bfloat16)
     full = sds((rows, D), jnp.float32)
     outs = [low, low, low, low, sds((HEADS, rows, rows), jnp.float32), low, full, low, low]
-    return in_vmem(dec_pre_kernel, outs, "dec_pre", x, gain_self, gain_cross, base, wq, wk, wv, wo, wcq)
+    return in_vmem(dec_pre_kernel, outs, "dec_pre", x, gains, bias, table, wq, wk, wv, wo, wcq)
 
 
 def dec_mid_kernel(
-    merged_ref, mid_ref, cot_ref, gain_ref, wco_ref, win_ref, wout_ref,
+    merged_ref, mid_ref, cot_ref, gains_ref, wco_ref, win_ref, wout_ref,
     out_ref, low_ref, hidden_ref, pre_grad_ref, after_low_ref, grad_after_ref, att_grad_ref, gain_grad_ref, slope_ref,
 ):
     rows = mid_ref.shape[0]
     three = nn(jnp.concatenate(in_three(merged_ref[:, :D]), axis=0), wco_ref[...])
     after = mid_ref[...] + (three[:rows] + three[rows : 2 * rows] + three[2 * rows :])
-    normed, scale = rms(after, gain_ref[...])
+    normed, scale = rms(after, gain_of(gains_ref, GAIN_DFFN))
     low = to_low(normed)
     low_ref[...] = low
     y = after
@@ -742,7 +773,7 @@
         pre_grad_ref[:, cols] = pre
         part = nt(pre, win_ref[:, cols])
         acc = part if acc is None else acc + part
-    back, gain_grad = rms_back(after, scale, gain_ref[...], acc)
+    back, gain_grad = rms_back(after, scale, gain_of(gains_ref, GAIN_DFFN), acc)
     gain_grad_ref[...] = gain_grad
     grad_after = cot.astype(jnp.float32) + back
     grad_after_ref[...] = grad_after
@@ -765,13 +796,13 @@
         out_specs=[vmem] * len(outs),
         out_shape=outs,
         scratch_shapes=[pltpu.VMEM((rows, ff), jnp.float32)],
-        compiler_params=params(56),
+        compiler_params=params(62),
         name="dec_mid",
     )(merged, mid, cot, gain, wco, win, wout)
 
 
 def dec_post_kernel(
-    gq_ref, grad_after_ref, mid_ref, x_ref, q_ref, k_ref, v_ref, probs_ref, gain_self_ref, gain_cross_ref,
+    gq_ref, grad_after_ref, mid_ref, x_ref, q_ref, k_ref, v_ref, probs_ref, gains_ref,
     wq_ref, wk_ref, wv_ref, wo_ref, wcq_ref, after_ref,
     mid_low_ref, dq_ref, dk_ref, dv_ref, out_ref, gain_self_grad_ref, gain_cross_grad_ref, fold_ref,
 ):
@@ -779,7 +810,7 @@
     mid = mid_ref[...]
     scale = lax.rsqrt(jnp.mean(mid * mid, axis=-1, keepdims=True) + epsilon)
     three = nt(jnp.concatenate(in_three(gq_ref[...]), axis=0), wcq_ref[...])
-    back, gain_grad = rms_back(mid, scale, gain_cross_ref[...], three[:rows] + three[rows : 2 * rows] + three[2 * rows :])
+    back, gain_grad = rms_back(mid, scale, gain_of(gains_ref, GAIN_CROSS), three[:rows] + three[rows : 2 * rows] + three[2 * rows :])
     gain_cross_grad_ref[...] = gain_grad
     grad_mid = grad_after_ref[...] + back
     mid_low = to_low(grad_mid)
@@ -820,12 +851,12 @@
     x = x_ref[...].astype(jnp.float32)
     scale = lax.rsqrt(jnp.mean(x * x, axis=-1, keepdims=True) + epsilon)
     grad = nt(dq_ref[...], wq_ref[...]) + nt(dk_ref[...], wk_ref[...]) + nt(dv_ref[...], wv_ref[...])
-    back, gain_grad = rms_back(x, scale, gain_self_ref[...], grad)
+    back, gain_grad = rms_back(x, scale, gain_of(gains_ref, GAIN_SELF), grad)
     gain_self_grad_ref[...] = gain_grad
     out_ref[...] = grad_mid + back
 
 
-def dec_post(gq, grad_after, mid, x, q, k, v, probs, gain_self, gain_cross, wq, wk, wv, wo, wcq, after):
+def dec_post(gq, grad_after, mid, x, q, k, v, probs, gains, wq, wk, wv, wo, wcq, after):
     rows = x.shape[0]
     low = sds((rows, D), jnp.bfloat16)
     gain = sds((1, D), jnp.float32)
@@ -833,20 +864,21 @@
     vmem = pl.BlockSpec(memory_space=pltpu.VMEM)
     return pl.pallas_call(
         dec_post_kernel,
-        in_specs=[vmem] * 15 + [pl.BlockSpec(memory_space=pl.ANY)],
+        in_specs=[vmem] * 14 + [pl.BlockSpec(memory_space=pl.ANY)],
         out_specs=[vmem] * len(outs),
         out_shape=outs,
-        compiler_params=params(60),
+        compiler_params=params(62),
         name="dec_post",
-    )(gq, grad_after, mid, x, q, k, v, probs, gain_self, gain_cross, wq, wk, wv, wo, wcq, after)
+    )(gq, grad_after, mid, x, q, k, v, probs, gains, wq, wk, wv, wo, wcq, after)
 
 
 def dec_weight_kernel(
-    pb, pa, column_ref, low_ref, dq_ref, dk_ref, dv_ref, att_ref, mid_low_ref, cross_low_ref, gq_ref, merged_ref, after_low_ref,
-    hidden_ref, cot_ref, dffn_low_ref, pre_grad_ref, out_ref, turned_ref, wide_ref,
+    pb, pa, place_ref, low_ref, dq_ref, dk_ref, dv_ref, att_ref, mid_low_ref, cross_low_ref, gq_ref, merged_ref, after_low_ref,
+    hidden_ref, cot_ref, dffn_low_ref, pre_grad_ref, keep_ref, send_ref, turned_ref, wide_ref,
 ):
     shards = pb * pa
-    column = column_ref[0]
+    column = place_ref[0]
+    core = place_ref[1]
     rows = D // shards
     depth = low_ref.shape[0]
 
@@ -862,8 +894,12 @@
 
     def put(values, here):
         nonlocal first
-        for b in range(pb):
-            out_ref[b, first : first + here, :] = values[b * here : (b + 1) * here]
+        for y in range(pb // 2):
+            low_part = values[2 * y * here : (2 * y + 1) * here]
+            high_part = values[(2 * y + 1) * here : (2 * y + 2) * here]
+            slot = place_ref[2 + y]
+            keep_ref[slot, first : first + here, :] = jnp.where(core == 0, low_part, high_part)
+            send_ref[slot, first : first + here, :] = jnp.where(core == 0, high_part, low_part)
         first += here
 
     left, here = own(low_ref[...], turned_ref)
@@ -884,7 +920,7 @@
         put(nn(left, pre_grad_ref[:, c * D : (c + 1) * D]), here)
 
 
-def dec_weight_grads(pb, pa, column, *args):
+def dec_weight_grads(pb, pa, place, *args):
     rows, ff = args[-1].shape
     shards = pb * pa
     height = (6 * D + ff + ff) // shards
@@ -892,12 +928,55 @@
     return pl.pallas_call(
         functools.partial(dec_weight_kernel, pb, pa),
         in_specs=[pl.BlockSpec(memory_space=pltpu.SMEM)] + [vmem] * len(args),
-        out_specs=vmem,
-        out_shape=sds((pb, height, D), jnp.float32),
+        out_specs=[vmem, vmem],
+        out_shape=[sds((pb // 2, height, D), jnp.float32)] * 2,
         scratch_shapes=[pltpu.VMEM((D, rows), jnp.float32), pltpu.VMEM((ff, rows), jnp.float32)],
-        compiler_params=params(56),
+        compiler_params=params(62),
         name="dec_weight_grads",
-    )(column, *args)
+    )(place, *args)
+
+
+def finish_kernel(pb, pa, heights, small_ref, dec_ref, enc_table_ref, dec_table_ref, *outs):
+    shards = pb * pa
+    shard = lax.axis_index("pb") * pa + lax.axis_index("pa")
+    width = D // shards
+    rolled = pltpu.roll(small_ref[0:8, :D], lax.rem(D - shard * width, D), 1)
+    for r in range(6):
+        outs[r][...] = rolled[r, :width]
+    share = BUCKETS * HEADS // shards
+    bucket = shard * share // HEADS
+    head = lax.rem(shard * share, HEADS)
+
+    def bias_grad(folded, table_ref, out_ref):
+        table = table_ref[...]
+        by_bucket = sum(nt(table, part) for part in in_three(folded))
+        row = lax.broadcasted_iota(jnp.int32, by_bucket.shape, 0)
+        mine = jnp.sum(jnp.where(row == bucket, by_bucket, 0.0), axis=0, keepdims=True)
+        mine = jnp.concatenate([mine, jnp.zeros((1, 128 - HEADS), jnp.float32)], axis=1)
+        mine = jnp.broadcast_to(mine, (8, 128))
+        out_ref[...] = pltpu.roll(mine, lax.rem(128 - head, 128), 1)[0, :share]
+
+    bias_grad(small_ref[8 : 8 + HEADS, :], enc_table_ref, outs[6])
+    dec_fold = jnp.concatenate([small_ref[0:6, D : D + 128], small_ref[0:6, D + 128 : D + 256]], axis=0)
+    bias_grad(dec_fold, dec_table_ref, outs[7])
+    first = 0
+    for number, height in enumerate(heights):
+        outs[8 + number][...] = dec_ref[first : first + height]
+        first += height
+    wide_ref = outs[8 + len(heights)]
+    for c in range(wide_ref.shape[1] // D):
+        wide_ref[:, c * D : (c + 1) * D] = dec_ref[first : first + width]
+        first += width
+
+
+def finish(pb, pa, small, dec_sum, enc_table, dec_table, ff):
+    shards = pb * pa
+    width = D // shards
+    share = BUCKETS * HEADS // shards
+    heights = [width] * 6 + [ff // shards]
+    outs = [sds((width,), jnp.float32)] * 6 + [sds((share,), jnp.float32)] * 2
+    outs += [sds((h, D), jnp.float32) for h in heights] + [sds((width, ff), jnp.float32)]
+    return in_vmem(functools.partial(finish_kernel, pb, pa, heights), outs, "finish", small, dec_sum, enc_table, dec_table)
 
 
 def bits_of(mesh_sizes):
@@ -912,7 +991,7 @@
 
 def orders_of(mesh_sizes):
     xs, ys, zs = bits_of(mesh_sizes)
-    return (xs + ys + zs, ys + xs + zs, zs[:1] + xs + ys + zs[1:])
+    return (xs + ys + zs, ys + xs + zs, zs[:1] + xs + ys + zs[1:], zs[:1] + ys + xs + zs[1:])
 
 
 def exchange_table(mesh_sizes, orders):
@@ -933,7 +1012,7 @@
 
 
 MESH = pl.DeviceIdType.MESH
-LINK = 0.088
+LINK = 0.11
 PAIR = 0.45
 NEAR = ("pb", 0)
 
@@ -944,7 +1023,9 @@
         return "core"
     if step in ys:
         return "y"
-    return "x" if step in xs else "z"
+    if step in xs:
+        return "x"
+    return "z far" if step == zs[-1] else "z"
 
 
 def link_time(step, megabytes, sizes):
@@ -954,42 +1035,61 @@
 
 
 class Piece:
-    def __init__(self, array, first, width, order, place=None):
-        self.array, self.first, self.width, self.order, self.place = array, first, width, order, place
-
-
-def plan(pieces, shapes, starts, sizes, depth=2):
+    def __init__(self, array, first, width, order, place=None, start=0.0, met=False):
+        self.array, self.first, self.width, self.order = array, first, width, [NEAR] + list(order)
+        self.place, self.start, self.met = place, start, met
+
+
+DEPTH = 3
+
+
+def block_of(piece, shapes):
+    return tuple(shapes[piece.array][:2]) + (piece.width,)
+
+
+def plan(pieces, shapes, sizes):
     free, held, queues = {}, {}, {}
-    pending = [(start, i, -1) for i, start in enumerate(starts)]
+    pending = [(piece.start, i, "ready", 0) for i, piece in enumerate(pieces)]
     events = []
 
-    def send(now, i, step, sends):
-        piece = pieces[i]
-        link = link_of(piece.order[step], sizes)
-        if held.get(link, 0) >= depth:
-            queues.setdefault(link, []).append((i, step))
+    def key_of(what, i, step):
+        return ("load", block_of(pieces[i], shapes)) if what == "load" else link_of(pieces[i].order[step], sizes)
+
+    def start(now, what, i, step, starts):
+        key = key_of(what, i, step)
+        if key != "core" and held.get(key, 0) >= (1 if what == "load" else DEPTH):
+            queues.setdefault(key, []).append((what, i, step))
             return
-        held[link] = held.get(link, 0) + 1
-        half, rows = shapes[piece.array][:2]
-        megabytes = (half >> (step + piece.skip)) * rows * piece.width * 4e-6
-        begin = max(now, free.get(link, 0.0))
-        free[link] = begin + link_time(piece.order[step], megabytes, sizes)
-        pending.append((free[link] + 1.5, i, step))
-        sends.append((i, step))
+        held[key] = held.get(key, 0) + 1
+        half, rows = shapes[pieces[i].array][:2]
+        megabytes = (half >> step) * rows * pieces[i].width * 4e-6
+        begin = max(now, free.get(key, 0.0))
+        if what == "load":
+            free[key] = begin + 1.0 + megabytes * 0.8
+            pending.append((free[key], i, "loaded", 0))
+        else:
+            free[key] = begin + link_time(pieces[i].order[step], megabytes, sizes)
+            pending.append((free[key] + 1.5, i, "arrived", step))
+        starts.append((what, i, step))
 
     while pending:
         pending.sort()
-        now, i, step = pending.pop(0)
-        sends = []
-        if step >= 0:
-            link = link_of(pieces[i].order[step], sizes)
-            held[link] -= 1
-            waiting = queues.get(link, [])
-            if waiting:
-                send(now, *waiting.pop(0), sends)
-        if step + 1 < len(pieces[i].order):
-            send(now + 0.5, i, step + 1, sends)
-        events.append((now, i, step, sends))
+        now, i, what, step = pending.pop(0)
+        starts = []
+        if what != "ready":
+            key = key_of("load" if what == "loaded" else "send", i, step)
+            held[key] -= 1
+            if queues.get(key):
+                start(now, *queues[key].pop(0), starts)
+        if what == "ready":
+            start(now, "load" if pieces[i].met else "send", i, 0, starts)
+        elif what == "arrived" and step == 0:
+            start(now, "load", i, 0, starts)
+        elif what == "loaded":
+            start(now + 0.5, "send", i, 1, starts)
+        elif step + 1 < len(pieces[i].order):
+            start(now + 0.5, "send", i, step + 1, starts)
+        events.append((now, what, i, step, starts))
     return events
 
 
@@ -1014,146 +1114,141 @@
 
 
 class Exchange:
-    def __init__(self, sizes, pieces, shapes, starts):
+    def __init__(self, sizes, pieces, shapes):
         self.sizes, self.pieces, self.shapes = sizes, pieces, shapes
-        for piece in pieces:
-            piece.skip = 1 if piece.place is None else 0
-        self.events = plan(pieces, shapes, starts, sizes)
+        self.events = plan(pieces, shapes, sizes)
         self.stages = len(all_steps(sizes))
-        self.own = [p for p in pieces if p.place is not None]
-        self.outside = [p for p in pieces if p.place is None]
-        self.staged = sorted({p.array for p in self.outside})
+        self.arrays = range(len(shapes))
+        self.own = [a for a in self.arrays if any(p.array == a and p.place is not None for p in pieces)]
+        self.block = [block_of(pieces[self.of(a)[0]], shapes) for a in self.arrays]
+        self.blocks = sorted(set(self.block))
+        self.before = {}
+        for n, a in enumerate(self.own):
+            earlier = [b for b in self.own[:n] if self.block[b] == self.block[a]]
+            if earlier:
+                self.before[a] = earlier[-1]
+
+    def of(self, array):
+        return [i for i, p in enumerate(self.pieces) if p.array == array]
 
     def scratch(self):
-        out = []
-        for array in self.staged:
-            half, rows = self.shapes[array][:2]
-            width = max(p.width for p in self.outside if p.array == array)
-            out += [pltpu.VMEM((half, rows, width), jnp.float32), pltpu.SemaphoreType.DMA]
-        for piece in self.outside:
-            half, rows = self.shapes[piece.array][:2]
+        out = [pltpu.VMEM(block, jnp.float32) for block in self.blocks]
+        for array in self.arrays:
+            half, *block = self.block[array]
+            count = len(self.of(array))
             out += [
-                pltpu.VMEM((half, rows, piece.width), jnp.float32),
-                pltpu.VMEM((half - 1, rows, piece.width), jnp.float32),
-                pltpu.SemaphoreType.DMA,
-            ]
-        if self.own:
-            half, rows = self.shapes[self.own[0].array][:2]
-            block = (rows, self.own[0].width)
-            count = len(self.own)
-            out += [
-                pltpu.VMEM((count, half) + block, jnp.float32),
-                pltpu.VMEM((count, half) + block, jnp.float32),
-                pltpu.VMEM((count, 2 * half - 1) + block, jnp.float32),
+                pltpu.VMEM((count, half, *block), jnp.float32),
+                pltpu.VMEM((count, half - 1, *block), jnp.float32),
             ]
         count = len(self.pieces)
-        return out + [pltpu.SemaphoreType.DMA((count, self.stages)), pltpu.SemaphoreType.DMA((count, self.stages))]
-
-    def bind(self, keeps, nears, outs, scratch):
-        self.keeps, self.nears, self.outs = keeps, nears, outs
-        scratch = list(scratch)
-        self.stage_of = {array: (scratch.pop(0), scratch.pop(0)) for array in self.staged}
-        self.bufs, self.recvs, self.load_sems = {}, {}, {}
-        for i, piece in enumerate(self.pieces):
-            if piece.place is None:
-                self.bufs[i], self.recvs[i], self.load_sems[i] = scratch.pop(0), scratch.pop(0), scratch.pop(0)
-        if self.own:
-            self.keep_of, self.send_of, recv = scratch.pop(0), scratch.pop(0), scratch.pop(0)
-            for i, piece in enumerate(self.pieces):
-                if piece.place is not None:
-                    self.bufs[i], self.recvs[i] = self.keep_of.at[piece.place], recv.at[piece.place]
-        self.send_sems, self.recv_sems = scratch
+        return out + [
+            pltpu.SemaphoreType.DMA((count,)),
+            pltpu.SemaphoreType.DMA((count,)),
+            pltpu.SemaphoreType.DMA((count, self.stages)),
+            pltpu.SemaphoreType.DMA((count, self.stages)),
+        ]
+
+    def bind(self, keeps, sends, nears, outs, staging, scratch):
+        self.keeps, self.sends, self.nears, self.outs, self.staging = keeps, sends, nears, outs, staging
+        places = dict(zip(self.blocks, scratch))
+        self.loaded = [places[block] for block in self.block]
+        scratch = scratch[len(self.blocks) :]
+        self.kept = [scratch[2 * a] for a in self.arrays]
+        recvs = [scratch[2 * a + 1] for a in self.arrays]
+        self.near_sems, self.keep_sems, self.send_sems, self.recv_sems = scratch[2 * len(self.shapes) :]
+        self.bufs, self.recvs = {}, {}
+        for array in self.arrays:
+            for number, i in enumerate(self.of(array)):
+                self.bufs[i], self.recvs[i] = self.kept[array].at[number], recvs[array].at[number]
 
     def loads(self, i):
         piece = self.pieces[i]
         cols = pl.ds(piece.first, piece.width)
-        stage, sem = self.stage_of[piece.array]
-        return (
-            pltpu.make_async_copy(self.keeps[piece.array].at[:, :, cols], self.bufs[i], self.load_sems[i]),
-            pltpu.make_async_copy(self.nears[piece.array].at[:, :, cols], stage, sem),
-        )
+        out = [pltpu.make_async_copy(self.nears[piece.array].at[:, :, cols], self.loaded[piece.array], self.near_sems.at[i])]
+        if piece.place is None:
+            out.append(pltpu.make_async_copy(self.keeps[piece.array].at[:, :, cols], self.bufs[i], self.keep_sems.at[i]))
+        return out
 
     def sizes_of(self, i, step):
-        piece = self.pieces[i]
-        half = self.shapes[piece.array][0]
-        count = half >> (step + piece.skip)
-        return count, (half >> piece.skip) * 2 - 2 * count
+        half = self.shapes[self.pieces[i].array][0]
+        count = half >> step
+        return count, half - 2 * count
 
     def copy(self, i, step):
         piece = self.pieces[i]
         count, first = self.sizes_of(i, step)
-        if step == 0 and piece.skip == 0:
-            source = self.send_of.at[piece.place]
+        if step == 0:
+            if piece.place is None:
+                source = self.sends[piece.array].at[:, :, pl.ds(piece.first, piece.width)]
+            else:
+                source = self.staging[piece.array].at[piece.place % 2]
+            target = self.nears[piece.array].at[:, :, pl.ds(piece.first, piece.width)]
         else:
             source = self.bufs[i].at[pl.ds(count, count)]
+            target = self.recvs[i].at[pl.ds(first, count)]
         return pltpu.make_async_remote_copy(
-            src_ref=source, dst_ref=self.recvs[i].at[pl.ds(first, count)],
-            send_sem=self.send_sems.at[i, step], recv_sem=self.recv_sems.at[i, step],
+            src_ref=source, dst_ref=target, send_sem=self.send_sems.at[i, step], recv_sem=self.recv_sems.at[i, step],
             device_id=partner(piece.order[step]), device_id_type=MESH,
         )
 
-    def first_loads(self):
-        for array in self.staged:
-            self.start_load(next(i for i, p in enumerate(self.pieces) if p.array == array and p.place is None))
-
-    def start_load(self, i):
-        for load in self.loads(i):
-            load.start()
-
-    def event(self, i, step, sends):
+    def free_staging(self, array, place):
+        if place >= 2:
+            self.copy(self.of(array)[place - 2], 0).wait_send()
+        elif array in self.before:
+            self.copy([i for i in self.of(self.before[array]) if self.pieces[i].place % 2 == place][-1], 0).wait_send()
+
+    def event(self, what, i, step, starts):
         piece = self.pieces[i]
-        buf, recv = self.bufs[i], self.recvs[i]
-        last = step + 1 == len(piece.order)
-        if step < 0 and piece.skip == 1:
+        buf = self.bufs[i]
+        last = what == "arrived" and step + 1 == len(piece.order)
+        count = 0
+        if what == "loaded":
             for load in self.loads(i):
                 load.wait()
-            stage = self.stage_of[piece.array][0]
-            count = self.shapes[piece.array][0]
-
-            def add(slot, _):
-                buf[slot] = buf[slot] + stage[slot]
-                return 0
-
-        elif step >= 0:
-            count, first = self.sizes_of(i, step)
+            source, first, count = self.loaded[piece.array], 0, self.shapes[piece.array][0]
+        elif what == "arrived":
             self.copy(i, step).wait_recv()
-
-            def add(slot, _):
-                buf[slot] = buf[slot] + recv[first + slot]
-                return 0
-
-        else:
-            count = 0
+            if step > 0:
+                source = self.recvs[i]
+                count, first = self.sizes_of(i, step)
+
+        def add(slot, _):
+            buf[slot] = buf[slot] + source[first + slot]
+            return 0
+
         if last:
-            self.outs[piece.array][:, piece.first : piece.first + piece.width] = buf[0] + recv[first]
+            self.outs[piece.array][:, piece.first : piece.first + piece.width] = buf[0] + source[first]
         elif count:
-            lax.fori_loop(count // 2, count, add, 0)
-        for send in sends:
-            self.copy(*send).start()
+            lax.fori_loop(count // 2, count, add, 0, unroll=min(4, count // 2))
+        mine = [s for s in starts if s[0] == "send"]
+        for _, j, k in mine:
+            self.copy(j, k).start()
         if not last and count:
-            lax.fori_loop(0, count // 2, add, 0)
-        if step < 0 and piece.skip == 1:
-            rest = [j for j, p in enumerate(self.pieces) if p.array == piece.array and j > i]
-            if rest:
-                self.start_load(rest[0])
+            lax.fori_loop(0, count // 2, add, 0, unroll=min(4, count // 2))
+        for kind, j, _ in starts:
+            if kind == "load":
+                for load in self.loads(j):
+                    load.start()
 
     def finish(self):
         for i, piece in enumerate(self.pieces):
-            for step in range(len(piece.order)):
+            waited = piece.place is not None and (
+                piece.place + 2 < len(self.of(piece.array)) or piece.array in self.before.values()
+            )
+            first = 1 if waited or piece.met else 0
+            for step in range(first, len(piece.order)):
                 self.copy(i, step).wait_send()
 
     def points(self, times, ready):
         out = [[] for _ in times]
         place = 0
-        for when, i, step, sends in self.events:
+        for when, what, i, step, starts in self.events:
             while place < len(times) - 1 and times[place] < when:
                 place += 1
-            if step < 0 and self.pieces[i].place is not None:
-                place = max(place, ready[self.pieces[i].place])
-            out[place].append((i, step, sends))
+            if what == "ready" and i in ready:
+                place = max(place, ready[i])
+            out[place].append((what, i, step, starts))
         return out
-
-
 class Everywhere:
     def __init__(self, sizes, shape):
         self.steps = all_steps(sizes)
@@ -1188,10 +1283,11 @@
             self.copy(k).wait_send()
 
 
-SMALL = (32, 1024)
+SMALL = (24, 1024)
 ATTN_STEP = 3.6
-GRAD_STEP = 1.5
-BACK_STEP = 1.8
+OPENING = 7.0
+TILE_US = 0.0052
+BACK_STEP = 1.2
 
 
 def slots_of(sizes, order):
@@ -1210,93 +1306,122 @@
     return cells
 
 
+class Phase:
+    def __init__(self, name, first, count, us):
+        self.name, self.first, self.count, self.us = name, first, count, us
+
+
 def last_kernel(
-    exchange, everywhere, points, orders, passages, share, arrays,
-    lengths_ref, q_ref, k_ref, v_ref, o_ref, do_ref, lse_ref, base_ref, turned_ref, x_ref, grad_mid_ref, gain_ref, wq_ref, wk_ref, wv_ref,
+    exchange, everywhere, points, orders, phases, passages, share, outside, gradients,
+    lengths_ref, q_ref, k_ref, v_ref, o_ref, do_ref, lse_ref, base_ref, x_ref, grad_mid_ref, gains_ref, wq_ref, wk_ref, wv_ref,
     dec_fold_ref, *refs,
 ):
-    gains, refs = refs[:5], refs[5:]
-    keeps, nears, refs = refs[:arrays], refs[arrays : 2 * arrays], refs[2 * arrays :]
-    after, refs = refs[0], refs[1:]
-    out_ref, small_ref = refs[:2]
-    moved, refs = refs[2 : 3 + arrays], refs[3 + arrays :]
-    strip_ref, gather_ref, dqT_ref, grads_ref, fold_ref, gain_grad_ref = refs[:6]
-    everywhere.bind(refs[6:10])
-    exchange.bind(keeps, nears, moved, refs[10:])
+    refs = list(refs)
+
+    def take(count):
+        out = refs[:count]
+        del refs[:count]
+        return out
+
+    gains = take(5)
+    lefts = take(len(gradients))
+    rights = take(len(gradients) - 1)
+    keeps, others = take(len(outside)), take(len(outside))
+    out_ref, small_ref = take(2)
+    moved = take(len(exchange.shapes))
+    nears = [other if met else take(1)[0] for other, met in zip(others, outside)] + take(len(gradients))
+    strip_ref, gather_ref, dqT_ref, grads_ref, fold_ref, gain_grad_ref = take(6)
+    staging = {}
+    for array in exchange.own:
+        staging[array] = staging[exchange.before[array]] if array in exchange.before else take(1)[0]
+    everywhere.bind(take(4))
+    exchange.bind(keeps, others, nears, moved, staging, refs)
     step = pl.program_id(0)
     sizes = exchange.sizes
     pb, pa = sizes
-    attn_steps = HEADS // 2 * passages
-    tiles = len(exchange.own)
-    grad_end = attn_steps + tiles
 
     @pl.when(step == 0)
     def _():
-        exchange.first_loads()
         greet(sizes)
-
-    def beside(place):
-        for k, events in enumerate(points[:-1]):
-            if k < 2 * attn_steps and k % 2 == place and events:
-
-                @pl.when(step == k // 2)
+        for event in points["start"][0]:
+            exchange.event(*event)
+
+    def run(place):
+        for at, events in points.get(place, {}).items():
+            if events:
+
+                @pl.when(step == at)
                 def _(events=events):
                     for event in events:
                         exchange.event(*event)
 
-    def at_end(number, k):
-        if points[k]:
-
-            @pl.when(step == number)
-            def _():
-                for event in points[k]:
-                    exchange.event(*event)
-
-    @pl.when(step < attn_steps)
-    def _():
-        pair = step // passages
-        passage = lax.rem(step, passages)
+    def attention(phase):
+        number = step - phase.first
+        pair = number // passages
+        passage = lax.rem(number, passages)
         place = pl.ds(pl.multiple_of(passage * PL, PL), PL), pl.ds(pl.multiple_of(pair * 128, 128), 128)
         attn_backward_kernel(
-            beside, passage, passages, lengths_ref, q_ref, k_ref, v_ref, o_ref, do_ref, lse_ref, base_ref,
+            lambda head: run(("attention", head)), passage, passages, lengths_ref, q_ref, k_ref, v_ref, o_ref, do_ref, lse_ref, base_ref,
             grads_ref.at[(0,) + place], grads_ref.at[(1,) + place], grads_ref.at[(2,) + place], fold_ref.at[pl.ds(pair, 1)],
             strip_ref, gather_ref, dqT_ref,
         )
 
-    @pl.when((step >= attn_steps) & (step < grad_end))
-    def _():
-        number = step - attn_steps
-        width = exchange.own[0].width
-        each = D // width
-        column = pl.ds(pl.multiple_of(lax.rem(number, each) * width, width), width)
-        right = grads_ref[number // each, :, column]
-        chain = lax.rem(number, len(orders))
+    def gradient(phase, array, left_ref, right_ref):
+        number = step - phase.first
+        width = exchange.pieces[exchange.of(array)[0]].width
+        if right_ref is None:
+            each = D // width
+            column = pl.ds(pl.multiple_of(lax.rem(number, each) * width, width), width)
+            right = grads_ref[number // each, :, column]
+        else:
+            right = right_ref[...]
+        for place in range(0 if array in exchange.before else 2, phase.count):
+
+            @pl.when(number == place)
+            def _(place=place):
+                exchange.free_staging(array, place)
+
+        chain = 0
+        for place, c in enumerate(gradients[array - len(outside)][3]):
+            chain = jnp.where(number == place, c, chain)
         choices = [slots_of(sizes, order) for order in orders]
         core = lax.rem(lax.axis_index("pb"), 2)
-        rows = exchange.shapes[exchange.own[0].array][1]
+        rows = exchange.shapes[array][1]
         half_rows = pa * rows
+        kept, staged = exchange.kept[array], exchange.staging[array]
         for y in range(pb // 2):
-            low_part = nn(turned_ref[2 * y * half_rows : (2 * y + 1) * half_rows, :], right)
-            high_part = nn(turned_ref[(2 * y + 1) * half_rows : (2 * y + 2) * half_rows, :], right)
+            low_part = nn(left_ref[2 * y * half_rows : (2 * y + 1) * half_rows, :], right)
+            high_part = nn(left_ref[(2 * y + 1) * half_rows : (2 * y + 2) * half_rows, :], right)
             mine = jnp.where(core == 0, low_part, high_part)
             other = jnp.where(core == 0, high_part, low_part)
             for a in range(pa):
                 slot = choices[0][y * pa + a]
                 for c in range(1, len(orders)):
                     slot = jnp.where(chain == c, choices[c][y * pa + a], slot)
-                exchange.keep_of[number, slot] = mine[a * rows : (a + 1) * rows]
-                exchange.send_of[number, slot] = other[a * rows : (a + 1) * rows]
-
-    @pl.when(step >= grad_end)
-    def _():
-        rows = pl.ds(pl.multiple_of((step - grad_end) * x_ref.shape[0], x_ref.shape[0]), x_ref.shape[0])
+                kept[number, slot] = mine[a * rows : (a + 1) * rows]
+                staged[lax.rem(number, 2), slot] = other[a * rows : (a + 1) * rows]
+
+    def back(phase):
+        height = x_ref.shape[0]
+        rows = pl.ds(pl.multiple_of((step - phase.first) * height, height), height)
         qkv_back_kernel(
-            step == grad_end, grads_ref.at[0, rows], grads_ref.at[1, rows], grads_ref.at[2, rows],
-            x_ref, grad_mid_ref, gain_ref, wq_ref, wk_ref, wv_ref, out_ref, gain_grad_ref,
+            step == phase.first, grads_ref.at[0, rows], grads_ref.at[1, rows], grads_ref.at[2, rows],
+            x_ref, grad_mid_ref, gains_ref, wq_ref, wk_ref, wv_ref, out_ref, gain_grad_ref,
         )
 
-    for k in range(2 * attn_steps, len(points) - 1):
-        at_end(k - attn_steps, k)
+    for phase in phases:
+
+        @pl.when((step >= phase.first) & (step < phase.first + phase.count))
+        def _(phase=phase):
+            if phase.name == "attention":
+                attention(phase)
+            elif phase.name == "back":
+                back(phase)
+            else:
+                k = phase.name
+                gradient(phase, exchange.own[k], lefts[k], rights[k] if k < len(rights) else None)
+
+    run("end")
 
     @pl.when(step == pl.num_programs(0) - 1)
     def _():
@@ -1307,9 +1432,11 @@
             first[0, r + 1 : r + 2, :D] = ref[...] if r < 2 else ref[...] * share
         for pair in range(HEADS // 2):
             first[0, 8 + 2 * pair : 10 + 2 * pair, :] = fold_ref[pair]
-        first[0, 8 + HEADS : 8 + 2 * HEADS, :128] = dec_fold_ref[...] * share
+        for part in range(2):
+            lanes = slice(D + part * 128, D + (part + 1) * 128)
+            first[0, 0:6, lanes] = dec_fold_ref[6 * part : 6 * part + 6] * share
         everywhere.copy(0).start()
-        left = points[-1]
+        left = points["rest"]
         steps = len(everywhere.steps)
         every = max(1, len(left) // (steps + 1))
         done = 0
@@ -1325,78 +1452,111 @@
         everywhere.finish()
 
 
-def groups_of(orders, groups):
-    pieces, starts = [], []
-    for number, (_, _, widths) in enumerate(groups):
-        first = 0
-        for c, piece_width in enumerate(widths):
-            starts.append(4.0 + 1.5 * len(pieces))
-            pieces.append(Piece(number, first, piece_width, orders[c % len(orders)]))
-            first += piece_width
-    return pieces, starts
+def outside_pieces(orders, groups):
+    pieces = []
+    for number, (_, _, met, chains, width) in enumerate(groups):
+        for c, chain in enumerate(chains):
+            order = chain if isinstance(chain, list) else orders[chain]
+            pieces.append(Piece(number, c * width, width, order, start=0.1 * number + 0.01 * c, met=met))
+    return pieces
 
 
 def last_part(
-    sizes, orders, groups, after, lengths, q, k, v, o, do, lse, base, turned, x, grad_mid, gain, wq, wk, wv, dec_fold, gains,
+    sizes, orders, groups, gradients, lengths, q, k, v, o, do, lse, base, x, grad_mid, gains, wq, wk, wv, dec_fold, grads_of_gains,
 ):
     pb, pa = sizes
     passages = lengths.shape[0]
     tokens = x.shape[0]
     pairs = HEADS // 2
-    tile_rows = 256
-    width = 256
-    attn_steps = pairs * passages
-    own_count = 3 * D // width
-    back_steps = tokens // tile_rows
-    steps = attn_steps + own_count + back_steps
+    tile_rows = 128
     half = pb * pa // 2
-    shapes = [g[0].shape for g in groups] + [(half, D // (pb * pa), 3 * D)]
-    pieces, starts = groups_of(orders, groups)
-    times = [ATTN_STEP * s / 2 for s in range(2 * attn_steps)]
-    ready = []
-    for n in range(own_count):
-        ready.append(len(times))
-        times.append(ATTN_STEP * attn_steps + GRAD_STEP * (n + 1))
-        starts.append(times[-1])
-        pieces.append(Piece(len(groups), n * width, width, [NEAR] + orders[n % len(orders)], n))
-    for s in range(back_steps - 1):
-        times.append(ATTN_STEP * attn_steps + GRAD_STEP * own_count + BACK_STEP * (s + 1))
-    exchange = Exchange(sizes, pieces, shapes, starts)
+    shapes = [g[0].shape for g in groups]
+    widths = [right.shape[1] if right is not None else 3 * D for _, right, *_ in gradients]
+    shapes += [(half, left.shape[0] // (pb * pa), w) for (left, *_), w in zip(gradients, widths)]
+
+    phases = []
+    names = list(range(len(gradients) - 1)) + ["attention", len(gradients) - 1, "back"]
+    step = 0
+    for name in names:
+        if name == "attention":
+            count, us = pairs * passages, ATTN_STEP
+        elif name == "back":
+            count, us = tokens // tile_rows, BACK_STEP
+        else:
+            count, us = widths[name] // gradients[name][2], TILE_US * gradients[name][2]
+        phases.append(Phase(name, step, count, us))
+        step += count
+    steps = step
+    pieces = outside_pieces(orders, groups)
+    times, labels, ready = [OPENING], [("start", 0)], {}
+    now = OPENING
+    for phase in phases:
+        for n in range(phase.count):
+            number = phase.first + n
+            if phase.name == "attention":
+                times += [now, now + phase.us / 2]
+                labels += [(("attention", 0), number), (("attention", 1), number)]
+            now += phase.us
+            if phase.name != "attention" and number < steps - 1:
+                times.append(now)
+                labels.append(("end", number))
+            if isinstance(phase.name, int):
+                ready[len(pieces)] = len(times) - 1
+                width = gradients[phase.name][2]
+                pieces.append(Piece(len(groups) + phase.name, n * width, width, orders[gradients[phase.name][3][n]], n, now))
+    exchange = Exchange(sizes, pieces, shapes)
     everywhere = Everywhere(sizes, SMALL)
-    points = exchange.points(times + [1e9], ready)
-
-    def attn_place(i):
-        at = jnp.minimum(i, attn_steps - 1)
-        return at // passages, lax.rem(at, passages)
-
-    def tile_map(i):
-        pair, passage = attn_place(i)
-        return passage, pair
-
-    def lse_map(i):
-        pair, passage = attn_place(i)
-        return pair, passage, 0, 0
+    points = {}
+    found = exchange.points(times + [1e9], ready)
+    for (place, number), events in zip(labels, found):
+        points.setdefault(place, {})[number] = events
+    points["rest"] = found[-1]
+    by_name = {phase.name: phase for phase in phases}
+
+    def at(name, i):
+        phase = by_name[name]
+        return jnp.clip(i - phase.first, 0, phase.count - 1)
+
+    def pair_of(i):
+        return at("attention", i) // passages
+
+    def passage_of(i):
+        return lax.rem(at("attention", i), passages)
 
     def once(array):
         return pl.BlockSpec(array.shape, lambda i: (0,) * array.ndim, pipeline_mode=pl.Buffered(1))
 
-    def row_map(i):
-        return jnp.maximum(i - attn_steps - own_count, 0), 0
-
-    tile = pl.BlockSpec((PL, 128), tile_map)
-    rows = pl.BlockSpec((tile_rows, D), row_map)
+    tile = pl.BlockSpec((PL, 128), lambda i: (passage_of(i), pair_of(i)))
+    rows = pl.BlockSpec((tile_rows, D), lambda i: (at("back", i), 0))
     hbm = pl.BlockSpec(memory_space=pl.ANY)
-    keeps, nears = [g[0] for g in groups], [g[1] for g in groups]
+    keeps, others = [g[0] for g in groups], [g[1] for g in groups]
+    outside = [g[2] for g in groups]
+    lefts = [left for left, *_ in gradients]
+    rights = [right for _, right, *_ in gradients[:-1]]
+    right_specs = [
+        pl.BlockSpec((tokens, width), lambda i, name=name: (0, at(name, i)), pipeline_mode=pl.Buffered(1)) for name, (_, _, width, _) in enumerate(gradients[:-1])
+    ]
+    own_shapes = shapes[len(groups) :]
+    near_shapes = [s for s, met in zip(shapes, outside) if not met] + own_shapes
     return pl.pallas_call(
-        functools.partial(last_kernel, exchange, everywhere, points, orders, passages, 1.0 / pa, len(groups)),
+        functools.partial(
+            last_kernel, exchange, everywhere, points, orders, phases, passages, 1.0 / pa, outside, gradients
+        ),
         grid=(steps,),
         in_specs=[pl.BlockSpec(memory_space=pltpu.SMEM)]
         + [tile] * 5
-        + [pl.BlockSpec((1, 1, 2, PL), lse_map), pl.BlockSpec((1, 2, WIDE), lambda i: (attn_place(i)[0], 0, 0)), once(turned), rows, rows]
-        + [once(a) for a in (gain, wq, wk, wv, dec_fold) + tuple(gains)]
-        + [hbm] * (2 * len(groups) + 1),
-        out_specs=[rows, pl.BlockSpec(SMALL, lambda i: (0, 0))] + [pl.BlockSpec(s[1:], lambda i: (0, 0)) for s in shapes],
-        out_shape=[sds((tokens, D), jnp.float32), sds(SMALL, jnp.float32)] + [sds(s[1:], jnp.float32) for s in shapes],
+        + [pl.BlockSpec((1, 1, 2, PL), lambda i: (pair_of(i), passage_of(i), 0, 0)), pl.BlockSpec((1, 2, WIDE), lambda i: (pair_of(i), 0, 0))]
+        + [rows, rows]
+        + [once(a) for a in (gains, wq, wk, wv, dec_fold) + tuple(grads_of_gains)]
+        + [once(left) for left in lefts]
+        + right_specs
+        + [hbm] * (2 * len(groups)),
+        out_specs=[rows, pl.BlockSpec(SMALL, lambda i: (0, 0), pipeline_mode=pl.Buffered(1))]
+        + [pl.BlockSpec(s[1:], lambda i: (0, 0), pipeline_mode=pl.Buffered(1)) for s in shapes]
+        + [hbm] * len(near_shapes),
+        out_shape=[sds((tokens, D), jnp.float32), sds(SMALL, jnp.float32)]
+        + [sds(s[1:], jnp.float32) for s in shapes]
+        + [sds(s, jnp.float32) for s in near_shapes],
         scratch_shapes=[
             pltpu.VMEM((2, STRIP, WIDE), jnp.float32),
             pltpu.VMEM((2, STRIP, WIDE), jnp.float32),
@@ -1405,16 +1565,18 @@
             pltpu.VMEM((pairs, 2, WIDE), jnp.float32),
             pltpu.VMEM((1, D), jnp.float32),
         ]
+        + [pltpu.VMEM((2,) + exchange.block[a], jnp.float32) for a in exchange.own if a not in exchange.before]
         + everywhere.scratch()
         + exchange.scratch(),
-        compiler_params=pltpu.CompilerParams(collective_id=1, has_side_effects=True, vmem_limit_bytes=63 * MIB),
+        compiler_params=pltpu.CompilerParams(collective_id=1, has_side_effects=True, vmem_limit_bytes=63 * MIB + MIB // 2),
         name="enc_last",
-    )(lengths, q, k, v, o, do, lse, base, turned, x, grad_mid, gain, wq, wk, wv, dec_fold, *gains, *keeps, *nears, after)
+    )(
+        lengths, q, k, v, o, do, lse, base, x, grad_mid, gains, wq, wk, wv, dec_fold, *grads_of_gains, *lefts, *rights, *keeps, *others
+    )[: 2 + len(shapes)]
 
 
 def exchange_kernel(exchange, arrays, *refs):
-    exchange.bind(refs[:arrays], refs[arrays : 2 * arrays], refs[2 * arrays : 3 * arrays], refs[3 * arrays :])
-    exchange.first_loads()
+    exchange.bind(refs[:arrays], {}, refs[arrays : 2 * arrays], refs[2 * arrays : 3 * arrays], {}, refs[3 * arrays :])
     greet(exchange.sizes)
     for _, *event in exchange.events:
         exchange.event(*event)
@@ -1423,7 +1585,7 @@
 
 def exchange_only(sizes, orders, groups):
     shapes = [g[0].shape for g in groups]
-    exchange = Exchange(sizes, *groups_of(orders, groups)[:1], shapes, groups_of(orders, groups)[1])
+    exchange = Exchange(sizes, outside_pieces(orders, groups), shapes)
     return pl.pallas_call(
         functools.partial(exchange_kernel, exchange, len(groups)),
         in_specs=[pl.BlockSpec(memory_space=pl.ANY)] * (2 * len(groups)),
@@ -1445,88 +1607,96 @@
     sizes = (pb, pa)
     orders = orders_of(sizes)
     answer_rows = dec_in.shape[0]
-    gain_attn, gain_ffn, gain_final = (g.astype(jnp.float32)[None] for g in (enc_gain_attn, enc_gain_ffn, enc_gain_final))
-    gain_self, gain_cross, gain_dffn = (g.astype(jnp.float32)[None] for g in (dec_gain_self, dec_gain_cross, dec_gain_ffn))
+    gains = jnp.concatenate([enc_gain_attn, enc_gain_ffn, enc_gain_final, dec_gain_self, dec_gain_cross, dec_gain_ffn])
+    gains = gains.astype(jnp.float32).reshape(6, D)
     table = exchange_table(sizes, orders)
-    enc_table = jnp.asarray(strip_table())
-    dec_table = jnp.asarray(causal_row(ANS))
-    base = jnp.dot(enc_table, enc_bias.astype(jnp.float32), precision=highest).T.reshape(HEADS // 2, 2, WIDE)
-
-    attn_turned, enc_queries, enc_keys, enc_values = qkv_forward(enc_in, gain_attn, enc_query, enc_key, enc_value)
-    enc_attended, enc_lse = attn_forward(lengths, enc_queries, enc_keys, enc_values, base)
-    enc_mid, ffn_low, enc_hidden, enc_slope, enc_y, enc_out, final_low, cross_keys, cross_values = post_forward(
-        enc_in, enc_attended, gain_ffn, gain_final, enc_output, enc_ff_in, enc_ff_out, cross_key, cross_value
+    enc_table = jnp.asarray(strip_table().T, jnp.bfloat16)
+    dec_table = jnp.asarray(causal_row(ANS).T, jnp.bfloat16)
+
+    attn_turned, enc_queries, enc_keys, enc_values = qkv_forward(enc_in, gains, enc_query, enc_key, enc_value)
+    enc_attended, attended_turned, enc_lse, base = attn_forward(lengths, enc_queries, enc_keys, enc_values, enc_bias, enc_table)
+    enc_mid, ffn_turned, hidden_turned, enc_slope, enc_y, enc_out, final_turned, cross_keys, cross_values = post_forward(
+        enc_in, enc_attended, gains, enc_output, enc_ff_in, enc_ff_out, cross_key, cross_value
     )
 
-    dec_base = jnp.dot(dec_table, dec_bias.astype(jnp.float32), precision=highest).T
     self_low, dec_queries, dec_keys, dec_values, dec_probs, dec_attended, dec_mid, cross_low, cross_queries = dec_pre(
-        dec_in, gain_self, gain_cross, dec_base, dec_query, dec_key, dec_value, dec_output, cross_query
+        dec_in, gains, dec_bias, dec_table, dec_query, dec_key, dec_value, dec_output, cross_query
     )
 
     merged = merge(cross_part(question_of, lengths, cross_queries, cross_keys, cross_values), pa)
     dec_out, dffn_low, dec_hidden, pre_grad_low, after_low, grad_after, cross_att_grad, dec_gain_ffn_grad = dec_mid_call(
-        merged, dec_mid, dec_cot, gain_dffn, cross_output, dec_ff_in, dec_ff_out
+        merged, dec_mid, dec_cot, gains, cross_output, dec_ff_in, dec_ff_out
     )
     query_part, grad_cross = cross_back(
         question_of, lengths, cross_queries, cross_keys, cross_values, cross_att_grad, merged[:, :D], merged[:, D:]
     )
-    grad_cross_q = lax.psum(query_part, "pa")
-
     def near(terms):
-        keep, send = terms
+        keep, send, _ = terms
         return keep, lax.ppermute(send, "pb", [(i, i ^ 1) for i in range(pb)])
 
-    cross_terms = near(weight_grad(table, final_low, [grad_cross[0], grad_cross[1]], pb, pa, 256, 2))
-    eout_low, epre_low, emid_low, grad_enc_mid, enc_att_grad, final_gain_grad, ffn_gain_grad = post_backward(
-        grad_cross, enc_y, enc_mid, enc_slope, enc_cot, gain_ffn, gain_final, cross_key, cross_value, enc_ff_out, enc_ff_in, enc_output,
+    def doubled(values, bits, tick):
+        for bit in bits:
+            values = values + lax.ppermute(values, "pa", [(i, i ^ (1 << bit)) for i in range(pa)])
+        return values + tick[0, 0]
+
+    pa_bits = range(pa.bit_length() - 1)
+    terms = weight_grad(table, final_turned, [(grad_cross, 0), (grad_cross, 1)], pb, pa, 256, 2)
+    cross_terms = near(terms)
+    grad_cross_q = doubled(query_part, pa_bits[:-2], terms[2])
+    eout_low, epre_low, emid_low, grad_enc_mid, enc_att_grad, final_gain_grad, ffn_gain_grad, tick = post_backward(
+        grad_cross, enc_y, enc_mid, enc_slope, enc_cot, gains, cross_key, cross_value, enc_ff_out, enc_ff_in, enc_output, grad_cross_q
     )
-    out_terms = near(weight_grad(table, enc_hidden, [eout_low], pb, pa, 256, 1))
-    in_terms = near(weight_grad(table, ffn_low, [epre_low], pb, pa, 512, 2))
-    mix_terms = near(weight_grad(table, enc_attended, [emid_low], pb, pa, 256, 1))
+    grad_cross_q = doubled(grad_cross_q, pa_bits[-2:-1], tick)
+    terms = weight_grad(table, hidden_turned, [eout_low], pb, pa, 256, 1, (grad_cross_q,))
+    out_terms = terms[:2]
+    grad_cross_q = doubled(grad_cross_q, pa_bits[-1:], terms[2])
 
     mid_low, grad_dq, grad_dk, grad_dv, dec_in_grad, dec_gain_self_grad, dec_gain_cross_grad, dec_fold = dec_post(
-        grad_cross_q, grad_after, dec_mid, dec_in, dec_queries, dec_keys, dec_values, dec_probs, gain_self, gain_cross,
-        dec_query, dec_key, dec_value, dec_output, cross_query, mix_terms[0],
+        grad_cross_q, grad_after, dec_mid, dec_in, dec_queries, dec_keys, dec_values, dec_probs, gains,
+        dec_query, dec_key, dec_value, dec_output, cross_query, out_terms[0],
     )
-    thin = dec_weight_grads(
-        pb, pa, lax.axis_index("pa").reshape(1), self_low, grad_dq, grad_dk, grad_dv, dec_attended, mid_low, cross_low, grad_cross_q,
+    far = lax.axis_index("pb") // 2
+    places = [lax.axis_index("pa"), lax.axis_index("pb") % 2]
+    for y in range(pb // 2):
+        slot = 0
+        for _, bit in bits_of(sizes)[1]:
+            slot = slot * 2 + ((far >> (bit - 1)) + (y >> (bit - 1))) % 2
+        places.append(slot)
+    dec_terms = dec_weight_grads(
+        pb, pa, jnp.stack(places).astype(jnp.int32), self_low, grad_dq, grad_dk, grad_dv, dec_attended, mid_low, cross_low, grad_cross_q,
         merged, after_low, dec_hidden, dec_cot, dffn_low, pre_grad_low,
     )
-    dec_sum = lax.psum_scatter(thin, "pb", scatter_dimension=0, tiled=False)
-    small_height = D // (pb * pa)
-    wide_height = dec_hidden.shape[1] // (pb * pa)
-    cuts = np.cumsum([0] + [small_height] * 6 + [wide_height] + [small_height] * (dec_hidden.shape[1] // D))
-    got = [dec_sum[a:b] for a, b in zip(cuts[:-1], cuts[1:])]
-    dec_ff_in_grad = jnp.concatenate(got[7:], axis=1)
-
+    ys = bits_of(sizes)[1]
     groups = [
-        cross_terms + ((512, 512, 512),), out_terms + ((256, 256, 256),), in_terms + ((1024, 1024, 1024),), mix_terms + ((256, 256, 256),),
+        tuple(cross_terms) + (True, (0, 1, 2), 512),
+        tuple(out_terms) + (False, (0, 1, 2), 256),
+        tuple(dec_terms) + (False, (ys, ys, ys), 256),
     ]
-    alone = [] if D // (pb * pa) % 8 == 0 else [groups.pop(2)]
+    gradients = [
+        (ffn_turned, epre_low, 512, (0, 1, 2, 0, 2, 3)),
+        (attended_turned, emid_low, 256, (0, 1, 2)),
+        (attn_turned, None, 256, (0, 1, 2, 0, 1, 3, 0, 1, 2)),
+    ]
+    roomy = D // (pb * pa) % 8 == 0
+    if not roomy:
+        del gradients[0]
+        in_terms = near(weight_grad(table, ffn_turned, [epre_low], pb, pa, 512, 2))
     enc_in_grad, small, *summed = last_part(
-        sizes, orders, groups, thin, lengths, enc_queries, enc_keys, enc_values, enc_attended, enc_att_grad, enc_lse, base,
-        attn_turned, enc_in, grad_enc_mid, gain_attn, enc_query, enc_key, enc_value, dec_fold,
+        sizes, orders, groups, gradients, lengths, enc_queries, enc_keys, enc_values, enc_attended, enc_att_grad, enc_lse, base,
+        enc_in, grad_enc_mid, gains, enc_query, enc_key, enc_value, dec_fold,
         (ffn_gain_grad, final_gain_grad, dec_gain_self_grad, dec_gain_cross_grad, dec_gain_ffn_grad),
     )
-    summed[2:2] = exchange_only(sizes, orders, alone) if alone else []
-    cross_terms, ff_out_term, ff_in_term, output_term, attn_terms = summed
-    shards = pb * pa
-    shard = lax.axis_index("pb") * pa + lax.axis_index("pa")
-    gains = lax.dynamic_slice_in_dim(small[:6, :D], shard * (D // shards), D // shards, 1)
-    width = BUCKETS * HEADS // shards
-
-    def bias_grad(folded, to_bucket):
-        flat = jnp.dot(folded, to_bucket, precision=highest).T.reshape(BUCKETS * HEADS)
-        return lax.dynamic_slice_in_dim(flat, shard * width, width)
-
-    enc_bias_grad = bias_grad(small[8 : 8 + HEADS], enc_table)
-    dec_bias_grad = bias_grad(small[8 + HEADS :, :128], dec_table)
+    if not roomy:
+        summed[3:3] = exchange_only(sizes, orders, [tuple(in_terms) + (True, (0, 1, 2), 1024)])
+    cross_terms, ff_out_term, dec_sum, ff_in_term, output_term, attn_terms = summed
+    ends = finish(pb, pa, small, dec_sum, enc_table, dec_table, dec_hidden.shape[1])
+    gain_grads, (enc_bias_grad, dec_bias_grad), got = ends[:6], ends[6:8], ends[8:]
 
     return (
         enc_out, dec_out, enc_in_grad, dec_in_grad,
-        gains[0], attn_terms[:, :D], attn_terms[:, D : 2 * D], attn_terms[:, 2 * D :], output_term, enc_bias_grad,
-        gains[1], ff_in_term, ff_out_term, gains[2], cross_terms[:, :D], cross_terms[:, D:],
-        gains[3], got[0], got[1], got[2], got[3], dec_bias_grad, gains[4], got[4], got[5], gains[5], dec_ff_in_grad, got[6],
+        gain_grads[0], attn_terms[:, :D], attn_terms[:, D : 2 * D], attn_terms[:, 2 * D :], output_term, enc_bias_grad,
+        gain_grads[1], ff_in_term, ff_out_term, gain_grads[2], cross_terms[:, :D], cross_terms[:, D:],
+        gain_grads[3], got[0], got[1], got[2], got[3], dec_bias_grad, gain_grads[4], got[4], got[5], gain_grads[5], got[7], got[6],
     )
 
 

time: 456 us -> 375 us (0.82)
  waiting for transfers between devices: 43.7 us -> 5.35 us
  Pallas kernels: 348 us -> 327 us
  between operations: 15 us -> 1.39 us
  local copies, waits for them, and re-layouts: 34.2 us -> 23.8 us
  matrix products: 5.76 us -> 0 us
  starting transfers between devices: 1.13 us -> 5.7 us
    psum x1 -> x0, waiting for transfers between devices: 37.6 us -> none  [local(): grad_cross_q = lax.psum(query_part, 'pa')]
    pallas_call x4 -> x2, Pallas kernels: 40.4 us -> 19.7 us  [weight_grad(): pl.pallas_call(functools.partial(weight_grad_kernel, rows, pb, pa, tiles,...]
    pallas_call x1, Pallas kernels: 174 us -> 168 us  [last_part(): pl.pallas_call(functools.partial(last_kernel, exchange, everywhere, point...]
    broadcast_in_dim x6 -> x0, local copies, waits for them, and re-layouts: 6.36 us -> none  [local(): g.astype(jnp.float32)[None]]
    ppermute x4 -> x1, waiting for transfers between devices: 6.05 us -> 0.01 us  [near(): return (keep, lax.ppermute(send, 'pb', [(i, i ^ 1) for i in range(pb)]))]
    dot_general x4 -> x0, matrix products: 5.76 us -> none  [the longest x2 2.73 us: bias_grad(): jnp.dot(folded, to_bucket, precision=highest).T.reshape(BUCKETS * HEADS)]
    ppermute x0 -> x3, starting transfers between devices: none -> 5.7 us  [doubled(): lax.ppermute(values, 'pa', [(i, i ^ 1 << bit) for i in range(pa)])]
    ppermute x0 -> x3, waiting for transfers between devices: none -> 5.35 us  [doubled(): lax.ppermute(values, 'pa', [(i, i ^ 1 << bit) for i in range(pa)])]
  transfers between devices with their start and end apart: 6 -> 4, of which waited for: 3 -> 1; matrix products, arithmetic and copies ran while one was open for 2% -> 1% of each run, Pallas kernels for 54% -> 13%
where the time goes in v3:
time: 375 us; the launch traced here: 368 us
  Pallas kernels  327 us (87%)
  local copies, waits for them, and re-layouts  23.8 us (6%)
  starting transfers between devices  5.7 us (2%)
  waiting for transfers between devices  5.35 us (1%)
  other arithmetic  5.07 us (1%)
    pallas_call x1, Pallas kernels, last_part(): pl.pallas_call(functools.partial(last_kernel, exchange, everywhere, point...  168 us
    pallas_call x1, Pallas kernels, post_backward(): pl.pallas_call(back_kernel, grid=(tokens // tile,), in_specs=[pl.BlockSpe...  26.3 us
    pallas_call x1, Pallas kernels, post_forward(): pl.pallas_call(post_kernel, grid=(tokens // tile,), in_specs=[d, d] + [wh...  25.9 us
    pallas_call x1, Pallas kernels, attn_forward(): pl.pallas_call(attn_forward_kernel, grid_spec=pltpu.PrefetchScalarGridSpe...  20.5 us
    unnamed x49, local copies, waits for them, and re-layouts  19.8 us
    pallas_call x2, Pallas kernels, weight_grad(): pl.pallas_call(functools.partial(weight_grad_kernel, rows, pb, pa, tiles,...  19.7 us
    pallas_call x1, Pallas kernels, merge(): pl.pallas_call(functools.partial(merge_kernel, pa), in_specs=[vmem], out_...  17.7 us
    pallas_call x1, Pallas kernels, dec_mid_call(): pl.pallas_call(dec_mid_kernel, in_specs=[vmem] * 7, out_specs=[vmem] * le...  10.6 us
  transfers between devices with their start and end apart: 4, of which 1 were waited for; matrix products, arithmetic and copies ran while one was open for 1% of the time, Pallas kernels for 13%

profile of v3, /device:TPU:0, one launch (start us, length us, event | category | flops | bytes accessed | tf_op | source)
XLA Modules:
  0.0 368.2 jit_solution(3153174414467331986)
XLA Ops:
  0.7 1.4 copy.64.bias_ref
  2.1 1.4 copy.65.bias_ref
  3.4 0.8 dynamic-update-slice
  4.3 0.8 dynamic-update-slice.1
  5.1 0.9 dynamic-update-slice.2
  6.0 0.9 dynamic-update-slice.3
  6.8 0.9 dynamic-update-slice.4
  7.7 0.8 dynamic-update-slice.5
  8.5 0.6 reshape.68.gains_ref
  9.2 7.7 %enc_qkv.1 = (bf16[768,1024]{1,0:T(8,128)(2,1)}, bf16[1024,768]{1,0:T(8,128)(2,1)}, bf16[1024,768]{1,0:T(8,128)(2,1)}, bf16[1024,768]{1,0:T(8,128)(2,1)}) custom-call(bf16[1024,768]{1,0:T(8,128)(2,1)} %x_ref.9, f32[6,768]{1,0:T(8,128)} %reshape.68.gains_ref, bf16[768,768]{1,0:T(8,128)(2,1)} %wq_ref.7, bf16[768,768]{1,0:T(8,128)(2,1)} %wk_ref.7, ...), custom_call_target="tpu_custom_call" | custom-call | tf_op jit(solution)/shard_map/enc_qkv/pallas_call | solution.py:300
  16.9 20.5 %enc_attention.1 = (bf16[1024,768]{1,0:T(8,128)(2,1)}, bf16[768,1024]{1,0:T(8,128)(2,1)}, f32[6,2,2,512]{3,2,1,0:T(2,128)}, f32[6,2,1024]{2,1,0:T(2,128)}) custom-call(s32[2]{0:T(128)} %lengths_ref.3, bf16[1024,768]{1,0:T(8,128)(2,1)} %get-tuple-element.112.q_ref, bf16[1024,768]{1,0:T(8,128)(2,1)} %get-tuple-element.113.k_ref, ...), custom_call_target="tpu_custom_call" | custom-call | tf_op jit(solution)/shard_map/enc_attention/pallas_call | solution.py:140
  37.4 25.9 %enc_post.1 = (f32[1024,768]{1,0:T(8,128)}, bf16[768,1024]{1,0:T(8,128)(2,1)}, bf16[3072,1024]{1,0:T(8,128)(2,1)}, bf16[1024,3072]{1,0:T(8,128)(2,1)}, f32[1024,...) custom-call(bf16[1024,768]{1,0:T(8,128)(2,1)} %x_ref.9, ...), custom_call_target="tpu_custom_call" | custom-call | tf_op jit(solution)/shard_map/enc_post/pallas_call | solution.py:349
  63.3 0.0 copy-start.7
  63.3 0.0 copy-start.8
  63.3 6.4 %dec_pre.1 = (bf16[48,768]{1,0:T(8,128)(2,1)}, bf16[48,768]{1,0:T(8,128)(2,1)}, bf16[48,768]{1,0:T(8,128)(2,1)}, bf16[48,768]{1,0:T(8,128)(2,1)}, f32[12,48,48]{...) custom-call(bf16[48,768]{1,0:T(8,128)(2,1)} %x_ref.8, ...), custom_call_target="tpu_custom_call" | custom-call | tf_op jit(solution)/shard_map/dec_pre/pallas_call | solution.py:731
  69.7 1.4 copy-done.2
  71.1 0.9 copy-done.4
  72.0 4.6 %cross_part.1 = f32[48,896]{1,0:T(8,128)S(1)} custom-call(s32[2]{0:T(128)S(1)} %copy-done.8, s32[2]{0:T(128)S(1)} %copy-done.7, bf16[48,768]{1,0:T(8,128)(2,1)S(1)} %copy-done.4, bf16[1024,768]{1,0:T(8,128)(2,1)S(1)} %copy-done.1, bf16[1024,768]{1,0:T(8,128)(2,1)S(1)} %copy-done.2), custom_call_target="tpu_custom_call" | custom-call | tf_op jit(solution)/shard_map/cross_part/pallas_call | solution.py:541
  76.7 17.7 %cross_merge.1 = f32[8,6,896]{2,1,0:T(8,128)S(1)} custom-call(f32[8,6,896]{2,1,0:T(8,128)S(1)} %reshape.66.part_ref), custom_call_target="tpu_custom_call" | custom-call | tf_op jit(solution)/shard_map/cross_merge/pallas_call | solution.py:611
  94.5 0.6 copy-done.9
  95.1 10.6 %dec_mid.1 = (bf16[48,768]{1,0:T(8,128)(2,1)}, bf16[48,768]{1,0:T(8,128)(2,1)}, bf16[48,3072]{1,0:T(8,128)(2,1)}, bf16[48,3072]{1,0:T(8,128)(2,1)}, bf16[48,768]...) custom-call(f32[48,896]{1,0:T(8,128)} %copy-done.9, ...), custom_call_target="tpu_custom_call" | custom-call | tf_op jit(solution)/shard_map/dec_mid/pallas_call | solution.py:793
  105.7 1.4 copy-done.3
  107.1 0.9 copy-done.6
  108.0 5.2 %cross_back.1 = (f32[48,768]{1,0:T(8,128)S(1)}, bf16[2,1024,768]{2,1,0:T(8,128)(2,1)S(1)}) custom-call(s32[2]{0:T(128)S(1)} %copy-done.8, s32[2]{0:T(128)S(1)} %copy-done.7, bf16[48,768]{1,0:T(8,128)(2,1)S(1)} %copy-done.5, bf16[1024,768]{1,0:T(8,128)(2,1)S(1)} %copy-done.1, bf16[1024,768]{1,0:T(8,128)(2,1)S(1)} %copy-done.3, bf16[48,768]{1,0:T(8,128)(2,1)S(1)} %copy-done.6, ...), custom_call_target="tpu_custom_call" | custom-call | tf_op jit(solution)/shard_map/cross_back/pallas_call | solution.py:664
  113.2 1.7 copy-done
  115.0 0.6 stack.34.table_ref
  115.6 8.8 %weight_grad.2 = (f32[16,24,1536]{2,1,0:T(8,128)}, f32[16,24,1536]{2,1,0:T(8,128)}, f32[1,128]{1,0:T(1,128)}) custom-call(s32[5,16]{1,0:T(8,128)} %stack.34.table_ref, bf16[768,1024]{1,0:T(8,128)(2,1)} %get-tuple-element.128.turned_ref, bf16[2,1024,768]{2,1,0:T(8,128)(2,1)} %copy-done, bf16[2,1024,768]{2,1,0:T(8,128)(2,1)} %copy-done), custom_call_target="tpu_custom_call" | custom-call | tf_op jit(solution)/shard_map/weight_grad/pallas_call | solution.py:487
  124.3 0.9 collective-permute-start
  125.3 5.3 %collective-permute-done = f32[48,768]{1,0:T(8,128)S(1)} collective-permute-done((f32[48,768]{1,0:T(8,128)S(1)}, f32[48,768]{1,0:T(8,128)S(1)}, u32[]{:S(2)}, u32[]{:S(2)}) %collective-permute-start) | collective-permute-done | bytes 147488 | tf_op jit(solution)/shard_map/ppermute | solution.py:1639
  130.6 0.7 add_add_fusion.2.after_ref
  131.3 0.0 copy-start.10
  131.3 1.2 collective-permute-start.1
  132.5 26.3 %enc_post_back.1 = (bf16[1024,768]{1,0:T(8,128)(2,1)}, bf16[1024,3072]{1,0:T(8,128)(2,1)}, bf16[1024,768]{1,0:T(8,128)(2,1)}, f32[1024,768]{1,0:T(8,128)}, bf16[...) custom-call(bf16[2,1024,768]{2,1,0:T(8,128)(2,1)} %copy-done, ...), custom_call_target="tpu_custom_call" | custom-call | tf_op jit(solution)/shard_map/enc_post_back/pallas_call | solution.py:407
  158.8 1.6 add_add_fusion.1.refs_1_
  160.4 0.0 copy-start.11
  160.4 3.5 collective-permute-start.2
  164.0 0.6 pad_add_fusion.place_ref
  164.6 11.0 %weight_grad.3 = (f32[16,96,768]{2,1,0:T(8,128)}, f32[16,96,768]{2,1,0:T(8,128)}, f32[1,128]{1,0:T(1,128)}) custom-call(s32[5,16]{1,0:T(8,128)} %stack.34.table_ref, bf16[3072,1024]{1,0:T(8,128)(2,1)} %get-tuple-element.135.turned_ref, bf16[1024,768]{1,0:T(8,128)(2,1)} %get-tuple-element.136.refs_0_, f32[48,768]{1,0:T(8,128)} %copy-done.11), custom_call_target="tpu_custom_call" | custom-call | tf_op jit(solution)/shard_map/weight_grad/pallas_call | solution.py:487
  175.5 2.2 add_add_fusion.gq_ref
  177.7 7.5 %dec_post.1 = (bf16[48,768]{1,0:T(8,128)(2,1)}, bf16[48,768]{1,0:T(8,128)(2,1)}, bf16[48,768]{1,0:T(8,128)(2,1)}, bf16[48,768]{1,0:T(8,128)(2,1)}, f32[48,768]{1...) custom-call(f32[48,768]{1,0:T(8,128)} %add_add_fusion.gq_ref, ...), custom_call_target="tpu_custom_call" | custom-call | tf_op jit(solution)/shard_map/dec_post/pallas_call | solution.py:865
  185.3 4.8 %dec_weight_grads.1 = (f32[2,336,768]{2,1,0:T(8,128)}, f32[2,336,768]{2,1,0:T(8,128)}) custom-call(s32[4]{0:T(128)} %pad_add_fusion.place_ref, bf16[48,768]{1,0:T(8,128)(2,1)} %get-tuple-element.156.low_ref, bf16[48,768]{1,0:T(8,128)(2,1)} %get-tuple-element.157.dq_ref, bf16[48,768]{1,0:T(8,128)(2,1)} %get-tuple-element.158.dk_ref, ...), custom_call_target="tpu_custom_call" | custom-call | tf_op jit(solution)/shard_map/dec_weight_grads/pallas_call | solution.py:928
  190.0 167.7 %enc_last.1 = (f32[1024,768]{1,0:T(8,128)}, f32[24,1024]{1,0:T(8,128)}, f32[24,1536]{1,0:T(8,128)}, f32[96,768]{1,0:T(8,128)}, f32[336,768]{1,0:T(8,128)}, /*ind...) custom-call(s32[2]{0:T(128)} %lengths_ref.3, ...), custom_call_target="tpu_custom_call" | custom-call | tf_op jit(solution)/shard_map/enc_last/pallas_call | solution.py:1541
  357.7 1.8 fusion
  359.5 2.4 finish.1
  361.9 3.8 %copy.76 = f32[1024,768]{1,0:T(8,128)} copy(f32[1024,768]{1,0:T(8,128)} %get-tuple-element.237) | data formatting | bytes 6291456
  365.7 0.6 copy.77
  366.3 0.7 copy.78
  367.1 0.7 copy.79
  (39 shorter events, 0.2 us)
Async XLA Ops:
  63.3 6.4 %copy-start.1 = (bf16[1024,768]{1,0:T(8,128)(2,1)S(1)}, bf16[1024,768]{1,0:T(8,128)(2,1)}, u32[]{:S(2)}) copy-start(bf16[1024,768]{1,0:T(8,128)(2,1)} %get-tuple-element.118.ck_ref) | copy-start | bytes 4718596
  63.3 6.4 %copy-start.7 = (s32[2]{0:T(128)S(1)}, s32[2]{0:T(128)}, u32[]{:S(2)}) copy-start(s32[2]{0:T(128)} %lengths_ref.3) | copy-start | bytes 28
  63.3 6.4 %copy-start.8 = (s32[2]{0:T(128)S(1)}, s32[2]{0:T(128)}, u32[]{:S(2)}) copy-start(s32[2]{0:T(128)} %question_ref.3) | copy-start | bytes 28
  69.7 1.4 copy-start.2
  71.1 0.9 copy-start.4
  94.4 0.7 copy-start.9
  95.1 10.6 %copy-start.5 = (bf16[48,768]{1,0:T(8,128)(2,1)S(1)}, bf16[48,768]{1,0:T(8,128)(2,1)}, u32[]{:S(2)}) copy-start(bf16[48,768]{1,0:T(8,128)(2,1)} %get-tuple-element.117.q_ref) | copy-start | bytes 221188
  105.7 1.4 copy-start.3
  107.1 0.9 copy-start.6
  108.0 6.9 %copy-start.15 = (s32[16]{0:T(128)S(1)}, s32[16]{0:T(128)}, u32[]{:S(2)}) copy-start(s32[16]{0:T(128)} %constant.64) | copy-start | bytes 196
  108.0 6.9 %copy-start.16 = (s32[16]{0:T(128)S(1)}, s32[16]{0:T(128)}, u32[]{:S(2)}) copy-start(s32[16]{0:T(128)} %constant.63) | copy-start | bytes 196
  108.0 6.9 %copy-start.17 = (s32[16]{0:T(128)S(1)}, s32[16]{0:T(128)}, u32[]{:S(2)}) copy-start(s32[16]{0:T(128)} %constant.62) | copy-start | bytes 196
  108.0 6.9 %copy-start.18 = (s32[16]{0:T(128)S(1)}, s32[16]{0:T(128)}, u32[]{:S(2)}) copy-start(s32[16]{0:T(128)} %constant.61) | copy-start | bytes 196
  113.2 1.7 copy-start
  124.3 65.7 %collective-permute-start.3 = (f32[16,24,1536]{2,1,0:T(8,128)}, f32[16,24,1536]{2,1,0:T(8,128)}, u32[]{:S(2)}, u32[]{:S(2)}) collective-permute-start(f32[16,24,1536]{2,1,0:T(8,128)} %get-tuple-element.168), channel_id=1, source_target_pairs={{0,8},{8,0},{16,24},{24,16},{1,9},{9,1},{17,25},{25,17},{2,10},{10... | collective-permute-start | bytes 7077896 | tf_op jit(solution)/shard_map/ppermute | solution.py:1635
  124.3 6.3 %collective-permute-start = (f32[48,768]{1,0:T(8,128)S(1)}, f32[48,768]{1,0:T(8,128)S(1)}, u32[]{:S(2)}, u32[]{:S(2)}) collective-permute-start(f32[48,768]{1,0:T(8,128)S(1)} %get-tuple-element.127), channel_id=1, source_target_pairs={{0,1},{1,0},{2,3},{3,2},{4,5},{5,4},{6,7},{7,6},{8,9},{9,8},{10,11... | collective-permute-start | bytes 442376 | tf_op jit(solution)/shard_map/ppermute | solution.py:1639
  131.3 1.3 copy-start.10
  131.3 27.6 %collective-permute-start.1 = (f32[48,768]{1,0:T(8,128)S(1)}, f32[48,768]{1,0:T(8,128)S(1)}, u32[]{:S(2)}, u32[]{:S(2)}) collective-permute-start(f32[48,768]{1,0:T(8,128)S(1)} %add_add_fusion.2.after_ref), channel_id=1, source_target_pairs={{0,2},{1,3},{2,0},{3,1},{4,6},{5,7},{6,4},{7,5},{8,10},{9,11},{10,... | collective-permute-start | bytes 442376 | tf_op jit(solution)/shard_map/ppermute | solution.py:1639
  160.4 4.1 %copy-start.11 = (f32[48,768]{1,0:T(8,128)}, f32[48,768]{1,0:T(8,128)S(1)}, u32[]{:S(2)}) copy-start(f32[48,768]{1,0:T(8,128)S(1)} %add_add_fusion.1.refs_1_) | copy-start | bytes 442372
  160.4 15.1 %collective-permute-start.2 = (f32[48,768]{1,0:T(8,128)S(1)}, f32[48,768]{1,0:T(8,128)S(1)}, u32[]{:S(2)}, u32[]{:S(2)}) collective-permute-start(f32[48,768]{1,0:T(8,128)S(1)} %add_add_fusion.1.refs_1_), channel_id=1, source_target_pairs={{0,4},{1,5},{2,6},{3,7},{4,0},{5,1},{6,2},{7,3},{8,12},{9,13},{10,... | collective-permute-start | bytes 442376 | tf_op jit(solution)/shard_map/ppermute | solution.py:1639
  361.8 3.9 %copy-start.14 = (f32[24,768]{1,0:T(8,128)S(1)}, f32[24,768]{1,0:T(8,128)}, u32[]{:S(2)}) copy-start(f32[24,768]{1,0:T(8,128)} %get-tuple-element.243) | copy-start | bytes 221188
  361.9 4.5 %copy-start.13 = (f32[24,3072]{1,0:T(8,128)S(1)}, f32[24,3072]{1,0:T(8,128)}, u32[]{:S(2)}) copy-start(f32[24,3072]{1,0:T(8,128)} %get-tuple-element.246) | copy-start | bytes 884740
  361.9 5.2 %copy-start.12 = (f32[96,768]{1,0:T(8,128)S(1)}, f32[96,768]{1,0:T(8,128)}, u32[]{:S(2)}) copy-start(f32[96,768]{1,0:T(8,128)} %get-tuple-element.247) | copy-start | bytes 884740

commit v4 on v3

--- a/solution.py
+++ b/solution.py
@@ -94,7 +94,7 @@
 
     @pl.when((passage == 0) & (pl.program_id(0) == 0))
     def _():
-        every = product_tn(bias_ref[...], table_ref[...])
+        every = nn(bias_ref[...], table_ref[...])
         for pair in range(HEADS // 2):
             rows_ref[pair] = every[2 * pair : 2 * pair + 2]
 
@@ -359,10 +359,9 @@
 
 def back_kernel(
     gkv_ref, y_ref, mid_ref, slope_ref, cot_ref, gains_ref,
-    wck_ref, wcv_ref, wout_ref, win_ref, wo_ref, after_ref,
-    eout_ref, epre_ref, emid_ref, grad_mid_ref, att_grad_ref, gain_final_grad_ref, gain_ffn_grad_ref, tick_ref,
+    wck_ref, wcv_ref, wout_ref, win_ref, wo_ref,
+    eout_ref, epre_ref, emid_ref, grad_mid_ref, att_grad_ref, gain_final_grad_ref, gain_ffn_grad_ref,
 ):
-    tick_ref[...] = jnp.zeros_like(tick_ref)
 
     @pl.when(pl.program_id(0) == 0)
     def _():
@@ -396,29 +395,6 @@
     att_grad_ref[...] = to_low(nt(emid, wo_ref[...]))
 
 
-def post_backward(gkv, y, mid, slope, cot, gains, wck, wcv, wout, win, wo, after):
-    tokens = y.shape[0]
-    tile = 256
-    ff = win.shape[1]
-    low = sds((tokens, D), jnp.bfloat16)
-    d = rows_of(tile, D)
-    f = rows_of(tile, ff)
-    gain = pl.BlockSpec((1, D), lambda i: (0, 0))
-    return pl.pallas_call(
-        back_kernel,
-        grid=(tokens // tile,),
-        in_specs=[pl.BlockSpec((2, tile, D), lambda i: (0, i, 0)), d, d, f, d]
-        + [whole(a) for a in (gains, wck, wcv, wout, win, wo)]
-        + [pl.BlockSpec(memory_space=pl.ANY)],
-        out_specs=[d, f, d, d, d, gain, gain, pl.BlockSpec((1, 128), lambda i: (0, 0))],
-        out_shape=[low, sds((tokens, ff), jnp.bfloat16), low, sds((tokens, D), jnp.float32), low]
-        + [sds((1, D), jnp.float32)] * 2
-        + [sds((1, 128), jnp.float32)],
-        compiler_params=params(62),
-        name="enc_post_back",
-    )(gkv, y, mid, slope, cot, gains, wck, wcv, wout, win, wo, after)
-
-
 def qkv_back_kernel(opening, dq_ref, dk_ref, dv_ref, x_ref, grad_mid_ref, gains_ref, wq_ref, wk_ref, wv_ref, out_ref, gain_grad_ref):
     @pl.when(opening)
     def _():
@@ -432,14 +408,15 @@
     out_ref[...] = grad_mid_ref[...] + back
 
 
-def weight_grad_kernel(rows, pb, pa, tiles, per_chain, table_ref, turned_ref, *refs):
+def weight_grad_kernel(rows, pb, pa, tiles, chains, table_ref, turned_ref, *refs):
     rights = refs[: len(tiles)]
-    keep_ref, send_ref, tick_ref = refs[-3:]
+    keep_ref, send_ref = refs[-2:]
     step = pl.program_id(0)
     core = table_ref[0, 0]
-    chain = step // per_chain
+    chain = chains[0]
+    for place, c in enumerate(chains):
+        chain = jnp.where(step == place, c, chain)
     half_rows = pa * rows
-    tick_ref[...] = jnp.zeros_like(tick_ref)
 
     def work(right):
         for y in range(pb // 2):
@@ -465,7 +442,7 @@
         first += count
 
 
-def weight_grad(table, turned, rights, pb, pa, width, per_chain, after=()):
+def weight_grad(table, turned, rights, pb, pa, width, chains):
     height, tokens = turned.shape
     rows = height // (pb * pa)
     arrays = [r[0] if isinstance(r, tuple) else r for r in rights]
@@ -485,19 +462,34 @@
     out = pl.BlockSpec((half, rows, width), lambda i, *_: (0, 0, i))
     shape = sds((half, rows, total * width), jnp.float32)
     return pl.pallas_call(
-        functools.partial(weight_grad_kernel, rows, pb, pa, tiles, per_chain),
+        functools.partial(weight_grad_kernel, rows, pb, pa, tiles, chains),
         grid_spec=pltpu.PrefetchScalarGridSpec(
             num_scalar_prefetch=1,
             grid=(total,),
             in_specs=[pl.BlockSpec((height, tokens), lambda i, *_: (0, 0))]
-            + [spec(r, f, c) for r, f, c in zip(rights, firsts, tiles)]
-            + [pl.BlockSpec(memory_space=pl.ANY)] * len(after),
-            out_specs=[out, out, pl.BlockSpec((1, 128), lambda i, *_: (0, 0))],
+            + [spec(r, f, c) for r, f, c in zip(rights, firsts, tiles)],
+            out_specs=[out, out],
         ),
-        out_shape=[shape, shape, sds((1, 128), jnp.float32)],
+        out_shape=[shape, shape],
         compiler_params=params(62),
         name="weight_grad",
-    )(table, turned, *arrays, *after)
+    )(table, turned, *arrays)
+
+
+def gains_kernel(*refs):
+    for row, ref in enumerate(refs[:-1]):
+        refs[-1][row] = ref[...].astype(jnp.float32)
+
+
+def gains_together(*gains):
+    vmem = pl.BlockSpec(memory_space=pltpu.VMEM)
+    return pl.pallas_call(
+        gains_kernel,
+        in_specs=[vmem] * len(gains),
+        out_specs=vmem,
+        out_shape=sds((len(gains), D), jnp.float32),
+        name="gains",
+    )(*gains)
 
 
 PACK = 896
@@ -690,7 +682,7 @@
     low_ref, q_ref, k_ref, v_ref, probs_ref, att_ref, mid_ref, cross_low_ref, cross_q_ref,
 ):
     rows = x_ref.shape[0]
-    base = product_tn(bias_ref[...], table_ref[...])
+    base = nn(bias_ref[...], table_ref[...])
     x = x_ref[...].astype(jnp.float32)
     normed, _ = rms(x, gain_of(gains_ref, GAIN_SELF))
     low = to_low(normed)
@@ -936,7 +928,8 @@
     )(place, *args)
 
 
-def finish_kernel(pb, pa, heights, small_ref, dec_ref, enc_table_ref, dec_table_ref, *outs):
+def finish_kernel(pb, pa, heights, cuts, small_ref, dec_ref, enc_table_ref, dec_table_ref, *refs):
+    pieces, outs = refs[: len(cuts)], refs[len(cuts) :]
     shards = pb * pa
     shard = lax.axis_index("pb") * pa + lax.axis_index("pa")
     width = D // shards
@@ -963,20 +956,36 @@
     for number, height in enumerate(heights):
         outs[8 + number][...] = dec_ref[first : first + height]
         first += height
-    wide_ref = outs[8 + len(heights)]
+    at = 8 + len(heights)
+    wide_ref = outs[at]
     for c in range(wide_ref.shape[1] // D):
         wide_ref[:, c * D : (c + 1) * D] = dec_ref[first : first + width]
         first += width
-
-
-def finish(pb, pa, small, dec_sum, enc_table, dec_table, ff):
+    for piece_ref, count in zip(pieces, cuts):
+        columns = piece_ref.shape[1] // count
+        for c in range(count):
+            at += 1
+            outs[at][...] = piece_ref[:, c * columns : (c + 1) * columns]
+
+
+def finish(pb, pa, small, dec_sum, enc_table, dec_table, ff, pieces, cuts):
     shards = pb * pa
     width = D // shards
     share = BUCKETS * HEADS // shards
     heights = [width] * 6 + [ff // shards]
     outs = [sds((width,), jnp.float32)] * 6 + [sds((share,), jnp.float32)] * 2
     outs += [sds((h, D), jnp.float32) for h in heights] + [sds((width, ff), jnp.float32)]
-    return in_vmem(functools.partial(finish_kernel, pb, pa, heights), outs, "finish", small, dec_sum, enc_table, dec_table)
+    for piece, count in zip(pieces, cuts):
+        outs += [sds((piece.shape[0], piece.shape[1] // count), jnp.float32)] * count
+    vmem = pl.BlockSpec(memory_space=pltpu.VMEM)
+    return pl.pallas_call(
+        functools.partial(finish_kernel, pb, pa, heights, cuts),
+        in_specs=[vmem] * (4 + len(pieces)),
+        out_specs=[vmem] * len(outs),
+        out_shape=outs,
+        compiler_params=params(62),
+        name="finish",
+    )(small, dec_sum, enc_table, dec_table, *pieces)
 
 
 def bits_of(mesh_sizes):
@@ -1028,10 +1037,10 @@
     return "z far" if step == zs[-1] else "z"
 
 
-def link_time(step, megabytes, sizes):
+def link_time(step, megabytes, sizes, rate=None):
     if step == NEAR:
         return megabytes / PAIR
-    return 2 * megabytes * (2 if step == bits_of(sizes)[2][-1] else 1) / LINK
+    return 2 * megabytes * (2 if step == bits_of(sizes)[2][-1] else 1) / (rate or LINK)
 
 
 class Piece:
@@ -1047,7 +1056,7 @@
     return tuple(shapes[piece.array][:2]) + (piece.width,)
 
 
-def plan(pieces, shapes, sizes):
+def plan(pieces, shapes, sizes, rate=None):
     free, held, queues = {}, {}, {}
     pending = [(piece.start, i, "ready", 0) for i, piece in enumerate(pieces)]
     events = []
@@ -1068,7 +1077,7 @@
             free[key] = begin + 1.0 + megabytes * 0.8
             pending.append((free[key], i, "loaded", 0))
         else:
-            free[key] = begin + link_time(pieces[i].order[step], megabytes, sizes)
+            free[key] = begin + link_time(pieces[i].order[step], megabytes, sizes, rate)
             pending.append((free[key] + 1.5, i, "arrived", step))
         starts.append((what, i, step))
 
@@ -1114,9 +1123,9 @@
 
 
 class Exchange:
-    def __init__(self, sizes, pieces, shapes):
+    def __init__(self, sizes, pieces, shapes, rate=None):
         self.sizes, self.pieces, self.shapes = sizes, pieces, shapes
-        self.events = plan(pieces, shapes, sizes)
+        self.events = plan(pieces, shapes, sizes, rate)
         self.stages = len(all_steps(sizes))
         self.arrays = range(len(shapes))
         self.own = [a for a in self.arrays if any(p.array == a and p.place is not None for p in pieces)]
@@ -1250,8 +1259,8 @@
             out[place].append((what, i, step, starts))
         return out
 class Everywhere:
-    def __init__(self, sizes, shape):
-        self.steps = all_steps(sizes)
+    def __init__(self, steps, shape):
+        self.steps = steps
         self.shape = shape
 
     def scratch(self):
@@ -1304,6 +1313,70 @@
                 slot = slot * 2 + far[axis, bit][(2 * y if axis == "pb" else a) >> bit & 1]
             cells.append(slot)
     return cells
+
+
+def outside_pieces(orders, groups):
+    pieces = []
+    for number, (_, _, met, chains, width) in enumerate(groups):
+        for c, chain in enumerate(chains):
+            order = chain if isinstance(chain, list) else orders[chain]
+            pieces.append(Piece(number, c * width, width, order, start=0.1 * number + 0.01 * c, met=met))
+    return pieces
+
+
+def back_host_kernel(adding, sizes, *refs):
+    own, part_ref, outs, total_ref, scratch = refs[:11], refs[11], refs[12:19], refs[19], refs[20:]
+    adding.bind(scratch)
+    step = pl.program_id(0)
+    last = pl.num_programs(0) - 1
+    steps = len(adding.steps)
+
+    @pl.when(step == 0)
+    def _():
+        adding.sums[0] = part_ref[...]
+        greet(sizes)
+        adding.copy(0).start()
+
+    for k in range(steps):
+
+        @pl.when(step == jnp.minimum(k + 1, last))
+        def _(k=k):
+            adding.arrive(k)
+
+    back_kernel(*own, *outs)
+
+    @pl.when(step == last)
+    def _():
+        total_ref[...] = adding.sums[steps]
+        adding.finish()
+
+
+def post_backward(sizes, part, gkv, y, mid, slope, cot, gains, wck, wcv, wout, win, wo):
+    tokens = y.shape[0]
+    tile = 256
+    ff = win.shape[1]
+    low = sds((tokens, D), jnp.bfloat16)
+    d = rows_of(tile, D)
+    f = rows_of(tile, ff)
+    gain = pl.BlockSpec((1, D), lambda i: (0, 0))
+    xs, _, zs = bits_of(sizes)
+    adding = Everywhere(xs + zs, part.shape)
+
+    def once(array):
+        return pl.BlockSpec(array.shape, lambda i: (0,) * array.ndim, pipeline_mode=pl.Buffered(1))
+
+    return pl.pallas_call(
+        functools.partial(back_host_kernel, adding, sizes),
+        grid=(tokens // tile,),
+        in_specs=[pl.BlockSpec((2, tile, D), lambda i: (0, i, 0)), d, d, f, d] + [once(a) for a in (gains, wck, wcv, wout, win, wo, part)],
+        out_specs=[d, f, d, d, d, gain, gain, pl.BlockSpec(part.shape, lambda i: (0, 0))],
+        out_shape=[low, sds((tokens, ff), jnp.bfloat16), low, sds((tokens, D), jnp.float32), low]
+        + [sds((1, D), jnp.float32)] * 2
+        + [sds(part.shape, jnp.float32)],
+        scratch_shapes=adding.scratch(),
+        compiler_params=pltpu.CompilerParams(collective_id=3, has_side_effects=True, vmem_limit_bytes=62 * MIB),
+        name="enc_post_back",
+    )(gkv, y, mid, slope, cot, gains, wck, wcv, wout, win, wo, part)
 
 
 class Phase:
@@ -1450,15 +1523,6 @@
         small_ref[...] = everywhere.sums[steps]
         exchange.finish()
         everywhere.finish()
-
-
-def outside_pieces(orders, groups):
-    pieces = []
-    for number, (_, _, met, chains, width) in enumerate(groups):
-        for c, chain in enumerate(chains):
-            order = chain if isinstance(chain, list) else orders[chain]
-            pieces.append(Piece(number, c * width, width, order, start=0.1 * number + 0.01 * c, met=met))
-    return pieces
 
 
 def last_part(
@@ -1505,7 +1569,7 @@
                 width = gradients[phase.name][2]
                 pieces.append(Piece(len(groups) + phase.name, n * width, width, orders[gradients[phase.name][3][n]], n, now))
     exchange = Exchange(sizes, pieces, shapes)
-    everywhere = Everywhere(sizes, SMALL)
+    everywhere = Everywhere(all_steps(sizes), SMALL)
     points = {}
     found = exchange.points(times + [1e9], ready)
     for (place, number), events in zip(labels, found):
@@ -1607,20 +1671,19 @@
     sizes = (pb, pa)
     orders = orders_of(sizes)
     answer_rows = dec_in.shape[0]
-    gains = jnp.concatenate([enc_gain_attn, enc_gain_ffn, enc_gain_final, dec_gain_self, dec_gain_cross, dec_gain_ffn])
-    gains = gains.astype(jnp.float32).reshape(6, D)
+    gains = gains_together(enc_gain_attn, enc_gain_ffn, enc_gain_final, dec_gain_self, dec_gain_cross, dec_gain_ffn)
     table = exchange_table(sizes, orders)
     enc_table = jnp.asarray(strip_table().T, jnp.bfloat16)
     dec_table = jnp.asarray(causal_row(ANS).T, jnp.bfloat16)
 
     attn_turned, enc_queries, enc_keys, enc_values = qkv_forward(enc_in, gains, enc_query, enc_key, enc_value)
-    enc_attended, attended_turned, enc_lse, base = attn_forward(lengths, enc_queries, enc_keys, enc_values, enc_bias, enc_table)
+    enc_attended, attended_turned, enc_lse, base = attn_forward(lengths, enc_queries, enc_keys, enc_values, enc_bias.T, enc_table)
     enc_mid, ffn_turned, hidden_turned, enc_slope, enc_y, enc_out, final_turned, cross_keys, cross_values = post_forward(
         enc_in, enc_attended, gains, enc_output, enc_ff_in, enc_ff_out, cross_key, cross_value
     )
 
     self_low, dec_queries, dec_keys, dec_values, dec_probs, dec_attended, dec_mid, cross_low, cross_queries = dec_pre(
-        dec_in, gains, dec_bias, dec_table, dec_query, dec_key, dec_value, dec_output, cross_query
+        dec_in, gains, dec_bias.T, dec_table, dec_query, dec_key, dec_value, dec_output, cross_query
     )
 
     merged = merge(cross_part(question_of, lengths, cross_queries, cross_keys, cross_values), pa)
@@ -1631,25 +1694,15 @@
         question_of, lengths, cross_queries, cross_keys, cross_values, cross_att_grad, merged[:, :D], merged[:, D:]
     )
     def near(terms):
-        keep, send, _ = terms
+        keep, send = terms
         return keep, lax.ppermute(send, "pb", [(i, i ^ 1) for i in range(pb)])
 
-    def doubled(values, bits, tick):
-        for bit in bits:
-            values = values + lax.ppermute(values, "pa", [(i, i ^ (1 << bit)) for i in range(pa)])
-        return values + tick[0, 0]
-
-    pa_bits = range(pa.bit_length() - 1)
-    terms = weight_grad(table, final_turned, [(grad_cross, 0), (grad_cross, 1)], pb, pa, 256, 2)
-    cross_terms = near(terms)
-    grad_cross_q = doubled(query_part, pa_bits[:-2], terms[2])
-    eout_low, epre_low, emid_low, grad_enc_mid, enc_att_grad, final_gain_grad, ffn_gain_grad, tick = post_backward(
-        grad_cross, enc_y, enc_mid, enc_slope, enc_cot, gains, cross_key, cross_value, enc_ff_out, enc_ff_in, enc_output, grad_cross_q
+    cross_terms = near(weight_grad(table, final_turned, [(grad_cross, 0), (grad_cross, 1)], pb, pa, 256, (0, 0, 1, 1, 2, 2)))
+    eout_low, epre_low, emid_low, grad_enc_mid, enc_att_grad, final_gain_grad, ffn_gain_grad, grad_cross_q = post_backward(
+        sizes, query_part,
+        grad_cross, enc_y, enc_mid, enc_slope, enc_cot, gains, cross_key, cross_value, enc_ff_out, enc_ff_in, enc_output,
     )
-    grad_cross_q = doubled(grad_cross_q, pa_bits[-2:-1], tick)
-    terms = weight_grad(table, hidden_turned, [eout_low], pb, pa, 256, 1, (grad_cross_q,))
-    out_terms = terms[:2]
-    grad_cross_q = doubled(grad_cross_q, pa_bits[-1:], terms[2])
+    out_terms = near(weight_grad(table, hidden_turned, [eout_low], pb, pa, 256, (0, 1, 3)))
 
     mid_low, grad_dq, grad_dk, grad_dv, dec_in_grad, dec_gain_self_grad, dec_gain_cross_grad, dec_fold = dec_post(
         grad_cross_q, grad_after, dec_mid, dec_in, dec_queries, dec_keys, dec_values, dec_probs, gains,
@@ -1668,19 +1721,20 @@
     )
     ys = bits_of(sizes)[1]
     groups = [
-        tuple(cross_terms) + (True, (0, 1, 2), 512),
-        tuple(out_terms) + (False, (0, 1, 2), 256),
+        cross_terms + (True, (0, 1, 2), 512),
+        out_terms + (True, (0, 1, 3), 256),
         tuple(dec_terms) + (False, (ys, ys, ys), 256),
     ]
     gradients = [
-        (ffn_turned, epre_low, 512, (0, 1, 2, 0, 2, 3)),
+        (ffn_turned, epre_low, 512, (0, 1, 2, 0, 1, 3)),
         (attended_turned, emid_low, 256, (0, 1, 2)),
         (attn_turned, None, 256, (0, 1, 2, 0, 1, 3, 0, 1, 2)),
     ]
     roomy = D // (pb * pa) % 8 == 0
     if not roomy:
         del gradients[0]
-        in_terms = near(weight_grad(table, ffn_turned, [epre_low], pb, pa, 512, 2))
+        keep, send = weight_grad(table, ffn_turned, [epre_low], pb, pa, 512, (0, 0, 1, 1, 2, 2))
+        in_terms = keep, lax.ppermute(send, "pb", [(i, i ^ 1) for i in range(pb)])
     enc_in_grad, small, *summed = last_part(
         sizes, orders, groups, gradients, lengths, enc_queries, enc_keys, enc_values, enc_attended, enc_att_grad, enc_lse, base,
         enc_in, grad_enc_mid, gains, enc_query, enc_key, enc_value, dec_fold,
@@ -1688,14 +1742,17 @@
     )
     if not roomy:
         summed[3:3] = exchange_only(sizes, orders, [tuple(in_terms) + (True, (0, 1, 2), 1024)])
-    cross_terms, ff_out_term, dec_sum, ff_in_term, output_term, attn_terms = summed
-    ends = finish(pb, pa, small, dec_sum, enc_table, dec_table, dec_hidden.shape[1])
-    gain_grads, (enc_bias_grad, dec_bias_grad), got = ends[:6], ends[6:8], ends[8:]
+    cross_sum, ff_out_sum, dec_sum, *summed = summed
+    ends = finish(
+        pb, pa, small, dec_sum, enc_table, dec_table, dec_hidden.shape[1], [cross_sum, ff_out_sum] + summed, [2, 1, 1, 1, 3]
+    )
+    gain_grads, (enc_bias_grad, dec_bias_grad), got = ends[:6], ends[6:8], ends[8:16]
+    cross_key_grad, cross_value_grad, ff_out_grad, ff_in_grad, output_grad, query_grad, key_grad, value_grad = ends[16:]
 
     return (
         enc_out, dec_out, enc_in_grad, dec_in_grad,
-        gain_grads[0], attn_terms[:, :D], attn_terms[:, D : 2 * D], attn_terms[:, 2 * D :], output_term, enc_bias_grad,
-        gain_grads[1], ff_in_term, ff_out_term, gain_grads[2], cross_terms[:, :D], cross_terms[:, D:],
+        gain_grads[0], query_grad, key_grad, value_grad, output_grad, enc_bias_grad,
+        gain_grads[1], ff_in_grad, ff_out_grad, gain_grads[2], cross_key_grad, cross_value_grad,
         gain_grads[3], got[0], got[1], got[2], got[3], dec_bias_grad, gain_grads[4], got[4], got[5], gain_grads[5], got[7], got[6],
     )
 

time: 375 us -> 351 us (0.936)
  local copies, waits for them, and re-layouts: 23.8 us -> 12 us
  waiting for transfers between devices: 5.35 us -> 0.01 us
  starting transfers between devices: 5.7 us -> 0.5 us
  other arithmetic: 5.07 us -> 0.61 us
    pallas_call x1 -> x3, Pallas kernels: 26.3 us -> 38.5 us  [the longest x1 34 us: post_backward(): pl.pallas_call(functools.partial(back_host_kernel, adding, sizes), grid=(...]
    unnamed x49 -> x31, local copies, waits for them, and re-layouts: 19.8 us -> 11.4 us
    pallas_call x1, Pallas kernels: 168 us -> 161 us  [last_part(): pl.pallas_call(functools.partial(last_kernel, exchange, everywhere, point...]
    ppermute x3 -> x0, starting transfers between devices: 5.7 us -> none  [doubled(): lax.ppermute(values, 'pa', [(i, i ^ 1 << bit) for i in range(pa)])]
    ppermute x3 -> x0, waiting for transfers between devices: 5.35 us -> none  [doubled(): lax.ppermute(values, 'pa', [(i, i ^ 1 << bit) for i in range(pa)])]
    add x3 -> x0, other arithmetic: 4.46 us -> none  [doubled(): return values + tick[0, 0]]
    pallas_call x2 -> x1, Pallas kernels: 8.73 us -> 6.32 us  [in_vmem(): pl.pallas_call(kernel, in_specs=[pl.BlockSpec(memory_space=pltpu.SMEM)] *...]
  transfers between devices with their start and end apart: 4 -> 2, of which waited for: 1 -> 0; matrix products, arithmetic and copies ran while one was open for 1% -> 0% of each run, Pallas kernels for 13% -> 6%
where the time goes in v4:
time: 351 us; the launch traced here: 345 us
  Pallas kernels  330 us (94%)
  local copies, waits for them, and re-layouts  12 us (3%)
    pallas_call x1, Pallas kernels, last_part(): pl.pallas_call(functools.partial(last_kernel, exchange, everywhere, point...  161 us
    pallas_call x1, Pallas kernels, post_backward(): pl.pallas_call(functools.partial(back_host_kernel, adding, sizes), grid=(...  34 us
    pallas_call x1, Pallas kernels, post_forward(): pl.pallas_call(post_kernel, grid=(tokens // tile,), in_specs=[d, d] + [wh...  25.9 us
    pallas_call x1, Pallas kernels, attn_forward(): pl.pallas_call(attn_forward_kernel, grid_spec=pltpu.PrefetchScalarGridSpe...  20.5 us
    pallas_call x2, Pallas kernels, weight_grad(): pl.pallas_call(functools.partial(weight_grad_kernel, rows, pb, pa, tiles,...  19.5 us
    pallas_call x1, Pallas kernels, merge(): pl.pallas_call(functools.partial(merge_kernel, pa), in_specs=[vmem], out_...  17.7 us
    unnamed x31, local copies, waits for them, and re-layouts  11.4 us
    pallas_call x1, Pallas kernels, dec_mid_call(): pl.pallas_call(dec_mid_kernel, in_specs=[vmem] * 7, out_specs=[vmem] * le...  10.6 us
  transfers between devices with their start and end apart: 2, of which 0 were waited for; matrix products, arithmetic and copies ran while one was open for 0% of the time, Pallas kernels for 6%

profile of v4, /device:TPU:0, one launch (start us, length us, event | category | flops | bytes accessed | tf_op | source)
XLA Modules:
  0.0 344.6 jit_solution(2119341906281019486)
XLA Ops:
  0.7 1.4 gains.1.gains_ref.refs_5_
  2.1 7.7 %enc_qkv.1 = (bf16[768,1024]{1,0:T(8,128)(2,1)}, bf16[1024,768]{1,0:T(8,128)(2,1)}, bf16[1024,768]{1,0:T(8,128)(2,1)}, bf16[1024,768]{1,0:T(8,128)(2,1)}) custom-call(bf16[1024,768]{1,0:T(8,128)(2,1)} %x_ref.9, f32[6,768]{1,0:T(8,128)} %gains.1.gains_ref.refs_5_, bf16[768,768]{1,0:T(8,128)(2,1)} %wq_ref.7, bf16[768,768]{1,0:T(8,128)(2,1)} %wk_ref.7, ...), custom_call_target="tpu_custom_call" | custom-call | tf_op jit(solution)/shard_map/enc_qkv/pallas_call | solution.py:300
  9.8 20.5 %enc_attention.1 = (bf16[1024,768]{1,0:T(8,128)(2,1)}, bf16[768,1024]{1,0:T(8,128)(2,1)}, f32[6,2,2,512]{3,2,1,0:T(2,128)}, f32[6,2,1024]{2,1,0:T(2,128)}) custom-call(s32[2]{0:T(128)} %lengths_ref.3, bf16[1024,768]{1,0:T(8,128)(2,1)} %get-tuple-element.118.q_ref, bf16[1024,768]{1,0:T(8,128)(2,1)} %get-tuple-element.119.k_ref, ...), custom_call_target="tpu_custom_call" | custom-call | tf_op jit(solution)/shard_map/enc_attention/pallas_call | solution.py:140
  30.3 25.9 %enc_post.1 = (f32[1024,768]{1,0:T(8,128)}, bf16[768,1024]{1,0:T(8,128)(2,1)}, bf16[3072,1024]{1,0:T(8,128)(2,1)}, bf16[1024,3072]{1,0:T(8,128)(2,1)}, f32[1024,...) custom-call(bf16[1024,768]{1,0:T(8,128)(2,1)} %x_ref.9, ...), custom_call_target="tpu_custom_call" | custom-call | tf_op jit(solution)/shard_map/enc_post/pallas_call | solution.py:349
  56.2 0.0 copy-start.1
  56.2 0.0 copy-start.8
  56.2 0.0 copy-start.9
  56.3 6.3 %dec_pre.1 = (bf16[48,768]{1,0:T(8,128)(2,1)}, bf16[48,768]{1,0:T(8,128)(2,1)}, bf16[48,768]{1,0:T(8,128)(2,1)}, bf16[48,768]{1,0:T(8,128)(2,1)}, f32[12,48,48]{...) custom-call(bf16[48,768]{1,0:T(8,128)(2,1)} %x_ref.8, ...), custom_call_target="tpu_custom_call" | custom-call | tf_op jit(solution)/shard_map/dec_pre/pallas_call | solution.py:723
  62.6 0.0 copy-done.1
  62.6 0.0 copy-done.8
  62.6 0.0 copy-done.9
  62.6 0.0 copy-start.2
  62.6 1.4 copy-done.2
  64.0 0.0 copy-start.4
  64.0 0.9 copy-done.4
  64.9 4.6 %cross_part.1 = f32[48,896]{1,0:T(8,128)S(1)} custom-call(s32[2]{0:T(128)S(1)} %copy-done.9, s32[2]{0:T(128)S(1)} %copy-done.8, bf16[48,768]{1,0:T(8,128)(2,1)S(1)} %copy-done.4, bf16[1024,768]{1,0:T(8,128)(2,1)S(1)} %copy-done.1, bf16[1024,768]{1,0:T(8,128)(2,1)S(1)} %copy-done.2), custom_call_target="tpu_custom_call" | custom-call | tf_op jit(solution)/shard_map/cross_part/pallas_call | solution.py:533
  69.6 17.7 %cross_merge.1 = f32[8,6,896]{2,1,0:T(8,128)S(1)} custom-call(f32[8,6,896]{2,1,0:T(8,128)S(1)} %reshape.62.part_ref), custom_call_target="tpu_custom_call" | custom-call | tf_op jit(solution)/shard_map/cross_merge/pallas_call | solution.py:603
  87.3 0.0 copy-start.10
  87.4 0.6 copy-done.10
  88.0 0.0 copy-start.5
  88.0 10.6 %dec_mid.1 = (bf16[48,768]{1,0:T(8,128)(2,1)}, bf16[48,768]{1,0:T(8,128)(2,1)}, bf16[48,3072]{1,0:T(8,128)(2,1)}, bf16[48,3072]{1,0:T(8,128)(2,1)}, bf16[48,768]...) custom-call(f32[48,896]{1,0:T(8,128)} %copy-done.10, ...), custom_call_target="tpu_custom_call" | custom-call | tf_op jit(solution)/shard_map/dec_mid/pallas_call | solution.py:785
  98.6 0.0 copy-done.5
  98.6 0.0 copy-start.3
  98.6 1.4 copy-done.3
  100.0 0.0 copy-start.7
  100.0 0.9 copy-done.7
  100.9 5.2 %cross_back.1 = (f32[48,768]{1,0:T(8,128)S(1)}, bf16[2,1024,768]{2,1,0:T(8,128)(2,1)S(1)}) custom-call(s32[2]{0:T(128)S(1)} %copy-done.9, s32[2]{0:T(128)S(1)} %copy-done.8, bf16[48,768]{1,0:T(8,128)(2,1)S(1)} %copy-done.5, bf16[1024,768]{1,0:T(8,128)(2,1)S(1)} %copy-done.1, bf16[1024,768]{1,0:T(8,128)(2,1)S(1)} %copy-done.3, bf16[48,768]{1,0:T(8,128)(2,1)S(1)} %copy-done.7, ...), custom_call_target="tpu_custom_call" | custom-call | tf_op jit(solution)/shard_map/cross_back/pallas_call | solution.py:656
  106.1 0.0 copy-start
  106.1 1.7 copy-done
  107.8 0.7 copy-done.6
  108.5 0.0 copy-done.11
  108.5 0.0 copy-done.12
  108.5 0.0 copy-done.13
  108.5 0.0 copy-done.14
  108.5 0.6 stack.34.table_ref
  109.1 34.0 %enc_post_back.1 = (bf16[1024,768]{1,0:T(8,128)(2,1)}, bf16[1024,3072]{1,0:T(8,128)(2,1)}, bf16[1024,768]{1,0:T(8,128)(2,1)}, f32[1024,768]{1,0:T(8,128)}, bf16[...) custom-call(bf16[2,1024,768]{2,1,0:T(8,128)(2,1)} %copy-done, ...), custom_call_target="tpu_custom_call" | custom-call | tf_op jit(solution)/shard_map/enc_post_back/pallas_call | solution.py:1368
  143.2 10.9 %weight_grad.2 = (f32[16,96,768]{2,1,0:T(8,128)}, f32[16,96,768]{2,1,0:T(8,128)}) custom-call(s32[5,16]{1,0:T(8,128)} %stack.34.table_ref, bf16[3072,1024]{1,0:T(8,128)(2,1)} %get-tuple-element.144.turned_ref, bf16[1024,768]{1,0:T(8,128)(2,1)} %get-tuple-element.145.refs_0_), custom_call_target="tpu_custom_call" | custom-call | tf_op jit(solution)/shard_map/weight_grad/pallas_call | solution.py:464
  154.1 0.0 collective-permute-start.1
  154.1 8.5 %weight_grad.3 = (f32[16,24,1536]{2,1,0:T(8,128)}, f32[16,24,1536]{2,1,0:T(8,128)}) custom-call(s32[5,16]{1,0:T(8,128)} %stack.34.table_ref, bf16[768,1024]{1,0:T(8,128)(2,1)} %get-tuple-element.158.turned_ref, bf16[2,1024,768]{2,1,0:T(8,128)(2,1)} %copy-done, bf16[2,1024,768]{2,1,0:T(8,128)(2,1)} %copy-done), custom_call_target="tpu_custom_call" | custom-call | tf_op jit(solution)/shard_map/weight_grad/pallas_call | solution.py:464
  162.6 0.5 collective-permute-start
  163.1 7.5 %dec_post.1 = (bf16[48,768]{1,0:T(8,128)(2,1)}, bf16[48,768]{1,0:T(8,128)(2,1)}, bf16[48,768]{1,0:T(8,128)(2,1)}, bf16[48,768]{1,0:T(8,128)(2,1)}, f32[48,768]{1...) custom-call(f32[48,768]{1,0:T(8,128)} %get-tuple-element.138.gq_ref, ...), custom_call_target="tpu_custom_call" | custom-call | tf_op jit(solution)/shard_map/dec_post/pallas_call | solution.py:857
  170.7 0.6 pad_add_fusion.place_ref
  171.2 4.8 %dec_weight_grads.1 = (f32[2,336,768]{2,1,0:T(8,128)}, f32[2,336,768]{2,1,0:T(8,128)}) custom-call(s32[4]{0:T(128)} %pad_add_fusion.place_ref, bf16[48,768]{1,0:T(8,128)(2,1)} %get-tuple-element.160.low_ref, bf16[48,768]{1,0:T(8,128)(2,1)} %get-tuple-element.161.dq_ref, bf16[48,768]{1,0:T(8,128)(2,1)} %get-tuple-element.162.dk_ref, ...), custom_call_target="tpu_custom_call" | custom-call | tf_op jit(solution)/shard_map/dec_weight_grads/pallas_call | solution.py:920
  176.0 0.0 collective-permute-done.refs_13_
  176.0 0.0 collective-permute-done.1.refs_14_
  176.1 161.2 %enc_last.1 = (f32[1024,768]{1,0:T(8,128)}, f32[24,1024]{1,0:T(8,128)}, f32[24,1536]{1,0:T(8,128)}, f32[96,768]{1,0:T(8,128)}, f32[336,768]{1,0:T(8,128)}, /*ind...) custom-call(s32[2]{0:T(128)} %lengths_ref.3, ...), custom_call_target="tpu_custom_call" | custom-call | tf_op jit(solution)/shard_map/enc_last/pallas_call | solution.py:1605
  337.3 3.1 finish.1
  340.4 3.8 %copy.63 = f32[1024,768]{1,0:T(8,128)} copy(f32[1024,768]{1,0:T(8,128)} %get-tuple-element.242) | data formatting | bytes 6291456
  (11 shorter events, 0.1 us)
Async XLA Ops:
  56.2 6.4 %copy-start.1 = (bf16[1024,768]{1,0:T(8,128)(2,1)S(1)}, bf16[1024,768]{1,0:T(8,128)(2,1)}, u32[]{:S(2)}) copy-start(bf16[1024,768]{1,0:T(8,128)(2,1)} %get-tuple-element.124.ck_ref) | copy-start | bytes 4718596
  56.2 6.4 %copy-start.8 = (s32[2]{0:T(128)S(1)}, s32[2]{0:T(128)}, u32[]{:S(2)}) copy-start(s32[2]{0:T(128)} %lengths_ref.3) | copy-start | bytes 28
  56.2 6.3 %copy-start.9 = (s32[2]{0:T(128)S(1)}, s32[2]{0:T(128)}, u32[]{:S(2)}) copy-start(s32[2]{0:T(128)} %question_ref.3) | copy-start | bytes 28
  62.6 1.4 copy-start.2
  64.0 0.9 copy-start.4
  87.3 0.7 copy-start.10
  88.0 10.6 %copy-start.5 = (bf16[48,768]{1,0:T(8,128)(2,1)S(1)}, bf16[48,768]{1,0:T(8,128)(2,1)}, u32[]{:S(2)}) copy-start(bf16[48,768]{1,0:T(8,128)(2,1)} %get-tuple-element.123.q_ref) | copy-start | bytes 221188
  98.6 1.4 copy-start.3
  100.0 0.9 copy-start.7
  100.9 7.6 %copy-start.11 = (s32[16]{0:T(128)S(1)}, s32[16]{0:T(128)}, u32[]{:S(2)}) copy-start(s32[16]{0:T(128)} %constant.64) | copy-start | bytes 196
  100.9 7.6 %copy-start.12 = (s32[16]{0:T(128)S(1)}, s32[16]{0:T(128)}, u32[]{:S(2)}) copy-start(s32[16]{0:T(128)} %constant.63) | copy-start | bytes 196
  100.9 7.6 %copy-start.13 = (s32[16]{0:T(128)S(1)}, s32[16]{0:T(128)}, u32[]{:S(2)}) copy-start(s32[16]{0:T(128)} %constant.62) | copy-start | bytes 196
  100.9 7.6 %copy-start.14 = (s32[16]{0:T(128)S(1)}, s32[16]{0:T(128)}, u32[]{:S(2)}) copy-start(s32[16]{0:T(128)} %constant.61) | copy-start | bytes 196
  106.1 1.7 copy-start
  107.8 0.7 copy-start.6
  154.1 22.0 %collective-permute-start.1 = (f32[16,96,768]{2,1,0:T(8,128)}, f32[16,96,768]{2,1,0:T(8,128)}, u32[]{:S(2)}, u32[]{:S(2)}) collective-permute-start(f32[16,96,768]{2,1,0:T(8,128)} %get-tuple-element.173), channel_id=1, source_target_pairs={{0,8},{8,0},{16,24},{24,16},{1,9},{9,1},{17,25},{25,17},{2,10},{10... | collective-permute-start | bytes 14155784 | tf_op jit(solution)/shard_map/ppermute | solution.py:1698
  162.6 13.4 %collective-permute-start = (f32[16,24,1536]{2,1,0:T(8,128)}, f32[16,24,1536]{2,1,0:T(8,128)}, u32[]{:S(2)}, u32[]{:S(2)}) collective-permute-start(f32[16,24,1536]{2,1,0:T(8,128)} %get-tuple-element.172), channel_id=1, source_target_pairs={{0,8},{8,0},{16,24},{24,16},{1,9},{9,1},{17,25},{25,17},{2,10},{10... | collective-permute-start | bytes 7077896 | tf_op jit(solution)/shard_map/ppermute | solution.py:1698

commit v5 on v4

--- a/solution.py
+++ b/solution.py
@@ -504,38 +504,50 @@
     )
 
 
-def cross_part_kernel(question_ref, length_ref, q_ref, ck_ref, cv_ref, part_ref):
+def cross_part_kernel(question_ref, length_ref, q_ref, ck_ref, cv_ref, part_ref, stats_ref, all_ref):
+    pair = pl.program_id(0)
     rows = q_ref.shape[0]
     mask = permitted_mask(question_ref, length_ref, rows, ck_ref.shape[0] // PL)
     lane = lax.broadcasted_iota(jnp.int32, (rows, 128), 1)
-    stats = jnp.zeros((rows, 128), jnp.float32)
-    for pair in range(HEADS // 2):
-        cols = slice(pair * 128, (pair + 1) * 128)
-        q = q_ref[:, cols]
-        k = ck_ref[:, cols]
-        v = cv_ref[:, cols]
-        outs = []
-        for head in range(2):
-            s = jnp.where(mask, 0.125 * nt(head_lanes(q, head), k), -1e9)
-            top = jnp.max(s, axis=1, keepdims=True)
-            e = jnp.exp(s - top)
-            total = jnp.sum(e, axis=1, keepdims=True)
-            outs.append(nn(to_low(e), v))
-            place = 2 * pair + head
-            stats = jnp.where(lane == place, top, jnp.where(lane == HEADS + place, total, stats))
-        part_ref[:, cols] = jnp.where(lane < HEAD, outs[0], outs[1])
-    part_ref[:, D:] = stats
-
-
-def cross_part(question_of, lengths, q, ck, cv):
-    vmem = pl.BlockSpec(memory_space=pltpu.VMEM)
+
+    @pl.when(pair == 0)
+    def _():
+        all_ref[...] = jnp.zeros_like(all_ref)
+
+    q = q_ref[...]
+    k = ck_ref[...]
+    v = cv_ref[...]
+    stats = all_ref[...]
+    outs = []
+    for head in range(2):
+        s = jnp.where(mask, 0.125 * nt(head_lanes(q, head), k), -1e9)
+        top = jnp.max(s, axis=1, keepdims=True)
+        e = jnp.exp(s - top)
+        total = jnp.sum(e, axis=1, keepdims=True)
+        outs.append(nn(to_low(e), v))
+        place = 2 * pair + head
+        stats = jnp.where(lane == place, top, jnp.where(lane == HEADS + place, total, stats))
+    all_ref[...] = stats
+    part = jnp.where(lane < HEAD, outs[0], outs[1])
+    each = part_ref.shape[1]
+    for r in range(part_ref.shape[0]):
+        part_ref[r] = part[r * each : (r + 1) * each]
+        stats_ref[r] = stats[r * each : (r + 1) * each]
+
+
+def cross_part(pa, question_of, lengths, q, ck, cv):
     smem = pl.BlockSpec(memory_space=pltpu.SMEM)
+    rows, tokens = q.shape[0], ck.shape[0]
+    short = pl.BlockSpec((rows, 128), lambda h: (0, h))
+    tall = pl.BlockSpec((tokens, 128), lambda h: (0, h))
     return pl.pallas_call(
         cross_part_kernel,
-        in_specs=[smem, smem, vmem, vmem, vmem],
-        out_specs=vmem,
-        out_shape=sds((q.shape[0], PACK), jnp.float32),
-        compiler_params=params(40),
+        grid=(HEADS // 2,),
+        in_specs=[smem, smem, short, tall, tall],
+        out_specs=[pl.BlockSpec((pa, rows // pa, 128), lambda h: (0, 0, h)), pl.BlockSpec((pa, rows // pa, 128), lambda h: (0, 0, 0))],
+        out_shape=[sds((pa, rows // pa, D), jnp.float32), sds((pa, rows // pa, 128), jnp.float32)],
+        scratch_shapes=[pltpu.VMEM((rows, 128), jnp.float32)],
+        compiler_params=params(62),
         name="cross_part",
     )(question_of, lengths, q, ck, cv)
 
@@ -548,9 +560,11 @@
     )
 
 
-def merge_kernel(pa, part_ref, out_ref, recv_ref, mine_ref, send_sem, recv_sem, send2_sem, recv2_sem):
+def merge_kernel(pa, sums_ref, stats_ref, out_ref, part_ref, recv_ref, mine_ref, send_sem, recv_sem, send2_sem, recv2_sem):
     me = lax.axis_index("pa")
     rows = part_ref.shape[1]
+    part_ref[:, :, :D] = sums_ref[...]
+    part_ref[:, :, D:] = stats_ref[...]
     barrier = pltpu.get_barrier_semaphore()
     for off in range(1, pa):
         pl.semaphore_signal(barrier, inc=1, device_id={"pa": lax.rem(me + off, pa)}, device_id_type=pl.DeviceIdType.MESH)
@@ -595,17 +609,18 @@
         second(off).wait()
 
 
-def merge(part, pa):
-    answer_rows = part.shape[0]
-    rows = answer_rows // pa
+def merge(part, stats, pa):
+    rows = part.shape[1]
+    answer_rows = pa * rows
     block = (pa, rows, PACK)
     vmem = pl.BlockSpec(memory_space=pltpu.VMEM)
     out = pl.pallas_call(
         functools.partial(merge_kernel, pa),
-        in_specs=[vmem],
+        in_specs=[vmem, vmem],
         out_specs=vmem,
         out_shape=sds(block, jnp.float32),
         scratch_shapes=[
+            pltpu.VMEM(block, jnp.float32),
             pltpu.VMEM(block, jnp.float32),
             pltpu.VMEM((rows, PACK), jnp.float32),
             pltpu.SemaphoreType.DMA((pa,)),
@@ -615,52 +630,54 @@
         ],
         compiler_params=pltpu.CompilerParams(collective_id=0, has_side_effects=True, vmem_limit_bytes=16 * MIB),
         name="cross_merge",
-    )(part.reshape(block))
+    )(part, stats)
     return out.reshape(answer_rows, PACK)
 
 
 def cross_back_kernel(question_ref, length_ref, q_ref, ck_ref, cv_ref, grad_ref, att_ref, lse_ref, gq_ref, gkv_ref):
+    pair = pl.program_id(0)
     rows = q_ref.shape[0]
     mask = permitted_mask(question_ref, length_ref, rows, ck_ref.shape[0] // PL)
     lane = lax.broadcasted_iota(jnp.int32, (rows, 128), 1)
-    for pair in range(HEADS // 2):
-        cols = slice(pair * 128, (pair + 1) * 128)
-        q = q_ref[:, cols]
-        k = ck_ref[:, cols]
-        v = cv_ref[:, cols]
-        g = grad_ref[:, cols]
-        weighed = g.astype(jnp.float32) * att_ref[:, cols]
-        gqs = []
-        scores = []
-        probs = []
-        for head in range(2):
-            place = 2 * pair + head
-            s = jnp.where(mask, 0.125 * nt(head_lanes(q, head), k), -1e9)
-            p = jnp.exp(s - lse_ref[:, place : place + 1])
-            dp = nt(head_lanes(g, head), v)
-            delta = jnp.sum(head_lanes(weighed, head), axis=1, keepdims=True)
-            ds = to_low(p * (dp - delta))
-            gqs.append(nn(ds, k))
-            scores.append(ds)
-            probs.append(to_low(p))
-        gq_ref[:, cols] = 0.125 * jnp.where(lane < HEAD, gqs[0], gqs[1])
-        both_q = jnp.concatenate([head_lanes(q, 0), head_lanes(q, 1)], axis=0)
-        both_g = jnp.concatenate([head_lanes(g, 0), head_lanes(g, 1)], axis=0)
-        gkv_ref[0, :, cols] = to_low(0.125 * product_tn(jnp.concatenate(scores, axis=0), both_q))
-        gkv_ref[1, :, cols] = to_low(product_tn(jnp.concatenate(probs, axis=0), both_g))
-
-
-def cross_back(question_of, lengths, q, ck, cv, grad, att, lse):
-    vmem = pl.BlockSpec(memory_space=pltpu.VMEM)
+    q = q_ref[...]
+    k = ck_ref[...]
+    v = cv_ref[...]
+    g = grad_ref[...]
+    weighed = g.astype(jnp.float32) * att_ref[...]
+    gqs = []
+    scores = []
+    probs = []
+    for head in range(2):
+        lse = jnp.sum(jnp.where(lane == 2 * pair + head, lse_ref[...], 0.0), axis=1, keepdims=True)
+        s = jnp.where(mask, 0.125 * nt(head_lanes(q, head), k), -1e9)
+        p = jnp.exp(s - lse)
+        dp = nt(head_lanes(g, head), v)
+        delta = jnp.sum(head_lanes(weighed, head), axis=1, keepdims=True)
+        ds = to_low(p * (dp - delta))
+        gqs.append(nn(ds, k))
+        scores.append(ds)
+        probs.append(to_low(p))
+    gq_ref[...] = 0.125 * jnp.where(lane < HEAD, gqs[0], gqs[1])
+    both_q = jnp.concatenate([head_lanes(q, 0), head_lanes(q, 1)], axis=0)
+    both_g = jnp.concatenate([head_lanes(g, 0), head_lanes(g, 1)], axis=0)
+    gkv_ref[0] = to_low(0.125 * product_tn(jnp.concatenate(scores, axis=0), both_q))
+    gkv_ref[1] = to_low(product_tn(jnp.concatenate(probs, axis=0), both_g))
+
+
+def cross_back(question_of, lengths, q, ck, cv, grad, merged):
     smem = pl.BlockSpec(memory_space=pltpu.SMEM)
+    rows, tokens = q.shape[0], ck.shape[0]
+    short = pl.BlockSpec((rows, 128), lambda h: (0, h))
+    tall = pl.BlockSpec((tokens, 128), lambda h: (0, h))
     return pl.pallas_call(
         cross_back_kernel,
-        in_specs=[smem, smem] + [vmem] * 6,
-        out_specs=[vmem, vmem],
-        out_shape=[sds((q.shape[0], D), jnp.float32), sds((2, ck.shape[0], D), jnp.bfloat16)],
-        compiler_params=params(40),
+        grid=(HEADS // 2,),
+        in_specs=[smem, smem, short, tall, tall, short, short, pl.BlockSpec((rows, 128), lambda h: (0, D // 128))],
+        out_specs=[short, pl.BlockSpec((2, tokens, 128), lambda h: (0, 0, h))],
+        out_shape=[sds((rows, D), jnp.float32), sds((2, tokens, D), jnp.bfloat16)],
+        compiler_params=params(62),
         name="cross_back",
-    )(question_of, lengths, q, ck, cv, grad, att, lse)
+    )(question_of, lengths, q, ck, cv, grad, merged, merged)
 
 
 def causal_row(length):
@@ -929,7 +946,15 @@
 
 
 def finish_kernel(pb, pa, heights, cuts, small_ref, dec_ref, enc_table_ref, dec_table_ref, *refs):
-    pieces, outs = refs[: len(cuts)], refs[len(cuts) :]
+    pieces, big_ref, outs = refs[: len(cuts)], refs[len(cuts)], refs[len(cuts) + 1 :]
+    outs[-1][...] = big_ref[...]
+
+    @pl.when(pl.program_id(0) == 0)
+    def _():
+        finish_small(pb, pa, heights, small_ref, dec_ref, enc_table_ref, dec_table_ref, pieces, cuts, outs)
+
+
+def finish_small(pb, pa, heights, small_ref, dec_ref, enc_table_ref, dec_table_ref, pieces, cuts, outs):
     shards = pb * pa
     shard = lax.axis_index("pb") * pa + lax.axis_index("pa")
     width = D // shards
@@ -968,7 +993,7 @@
             outs[at][...] = piece_ref[:, c * columns : (c + 1) * columns]
 
 
-def finish(pb, pa, small, dec_sum, enc_table, dec_table, ff, pieces, cuts):
+def finish(pb, pa, small, dec_sum, enc_table, dec_table, ff, pieces, cuts, big):
     shards = pb * pa
     width = D // shards
     share = BUCKETS * HEADS // shards
@@ -977,15 +1002,17 @@
     outs += [sds((h, D), jnp.float32) for h in heights] + [sds((width, ff), jnp.float32)]
     for piece, count in zip(pieces, cuts):
         outs += [sds((piece.shape[0], piece.shape[1] // count), jnp.float32)] * count
-    vmem = pl.BlockSpec(memory_space=pltpu.VMEM)
+    args = [small, dec_sum, enc_table, dec_table, *pieces]
+    tile = pl.BlockSpec((256, big.shape[1]), lambda i: (i, 0))
     return pl.pallas_call(
         functools.partial(finish_kernel, pb, pa, heights, cuts),
-        in_specs=[vmem] * (4 + len(pieces)),
-        out_specs=[vmem] * len(outs),
-        out_shape=outs,
+        grid=(big.shape[0] // 256,),
+        in_specs=[whole(a) for a in args] + [tile],
+        out_specs=[whole(o) for o in outs] + [tile],
+        out_shape=outs + [sds(big.shape, big.dtype)],
         compiler_params=params(62),
         name="finish",
-    )(small, dec_sum, enc_table, dec_table, *pieces)
+    )(*args, big)
 
 
 def bits_of(mesh_sizes):
@@ -1337,7 +1364,7 @@
         greet(sizes)
         adding.copy(0).start()
 
-    for k in range(steps):
+    for k in range(steps - 1):
 
         @pl.when(step == jnp.minimum(k + 1, last))
         def _(k=k):
@@ -1347,6 +1374,7 @@
 
     @pl.when(step == last)
     def _():
+        adding.arrive(steps - 1)
         total_ref[...] = adding.sums[steps]
         adding.finish()
 
@@ -1686,12 +1714,12 @@
         dec_in, gains, dec_bias.T, dec_table, dec_query, dec_key, dec_value, dec_output, cross_query
     )
 
-    merged = merge(cross_part(question_of, lengths, cross_queries, cross_keys, cross_values), pa)
+    merged = merge(*cross_part(pa, question_of, lengths, cross_queries, cross_keys, cross_values), pa)
     dec_out, dffn_low, dec_hidden, pre_grad_low, after_low, grad_after, cross_att_grad, dec_gain_ffn_grad = dec_mid_call(
         merged, dec_mid, dec_cot, gains, cross_output, dec_ff_in, dec_ff_out
     )
     query_part, grad_cross = cross_back(
-        question_of, lengths, cross_queries, cross_keys, cross_values, cross_att_grad, merged[:, :D], merged[:, D:]
+        question_of, lengths, cross_queries, cross_keys, cross_values, cross_att_grad, merged
     )
     def near(terms):
         keep, send = terms
@@ -1744,10 +1772,10 @@
         summed[3:3] = exchange_only(sizes, orders, [tuple(in_terms) + (True, (0, 1, 2), 1024)])
     cross_sum, ff_out_sum, dec_sum, *summed = summed
     ends = finish(
-        pb, pa, small, dec_sum, enc_table, dec_table, dec_hidden.shape[1], [cross_sum, ff_out_sum] + summed, [2, 1, 1, 1, 3]
+        pb, pa, small, dec_sum, enc_table, dec_table, dec_hidden.shape[1], [cross_sum, ff_out_sum] + summed, [2, 1, 1, 1, 3], enc_in_grad
     )
     gain_grads, (enc_bias_grad, dec_bias_grad), got = ends[:6], ends[6:8], ends[8:16]
-    cross_key_grad, cross_value_grad, ff_out_grad, ff_in_grad, output_grad, query_grad, key_grad, value_grad = ends[16:]
+    cross_key_grad, cross_value_grad, ff_out_grad, ff_in_grad, output_grad, query_grad, key_grad, value_grad, enc_in_grad = ends[16:]
 
     return (
         enc_out, dec_out, enc_in_grad, dec_in_grad,

time: 351 us -> 342 us (0.974); the launches traced: 345 us -> 340 us
  local copies, waits for them, and re-layouts: 12 us -> 3.01 us
  Pallas kernels: 330 us -> 335 us
    unnamed x31 -> x12, local copies, waits for them, and re-layouts: 11.4 us -> 1.7 us
    pallas_call x4, Pallas kernels: 30.6 us -> 39.1 us  [the longest x1 17.7 us: merge(): pl.pallas_call(functools.partial(merge_kernel, pa), in_specs=[vmem, vmem]...]
where the time goes in v5:
time: 342 us; the launch traced here: 340 us
  Pallas kernels  335 us (98%)
    pallas_call x1, Pallas kernels, last_part(): pl.pallas_call(functools.partial(last_kernel, exchange, everywhere, point...  161 us
    pallas_call x1, Pallas kernels, post_backward(): pl.pallas_call(functools.partial(back_host_kernel, adding, sizes), grid=(...  30.9 us
    pallas_call x1, Pallas kernels, post_forward(): pl.pallas_call(post_kernel, grid=(tokens // tile,), in_specs=[d, d] + [wh...  25.8 us
    pallas_call x1, Pallas kernels, attn_forward(): pl.pallas_call(attn_forward_kernel, grid_spec=pltpu.PrefetchScalarGridSpe...  20.5 us
    pallas_call x2, Pallas kernels, weight_grad(): pl.pallas_call(functools.partial(weight_grad_kernel, rows, pb, pa, tiles,...  19.6 us
    pallas_call x1, Pallas kernels, merge(): pl.pallas_call(functools.partial(merge_kernel, pa), in_specs=[vmem, vmem]...  17.7 us
    pallas_call x1, Pallas kernels, dec_mid_call(): pl.pallas_call(dec_mid_kernel, in_specs=[vmem] * 7, out_specs=[vmem] * le...  10.6 us
    pallas_call x1, Pallas kernels, cross_back(): pl.pallas_call(cross_back_kernel, grid=(HEADS // 2,), in_specs=[smem, sme...  8.28 us
  transfers between devices with their start and end apart: 2, of which 0 were waited for; matrix products, arithmetic and copies ran while one was open for 0% of the time, Pallas kernels for 6%

profile of v5, /device:TPU:0, one launch (start us, length us, event | category | flops | bytes accessed | tf_op | source)
XLA Modules:
  0.0 340.3 jit_solution(5150517382313982142)
XLA Ops:
  0.7 1.4 gains.1.gains_ref.refs_5_
  2.1 7.7 %enc_qkv.1 = (bf16[768,1024]{1,0:T(8,128)(2,1)}, bf16[1024,768]{1,0:T(8,128)(2,1)}, bf16[1024,768]{1,0:T(8,128)(2,1)}, bf16[1024,768]{1,0:T(8,128)(2,1)}) custom-call(bf16[1024,768]{1,0:T(8,128)(2,1)} %x_ref.9, f32[6,768]{1,0:T(8,128)} %gains.1.gains_ref.refs_5_, bf16[768,768]{1,0:T(8,128)(2,1)} %wq_ref.7, bf16[768,768]{1,0:T(8,128)(2,1)} %wk_ref.7, ...), custom_call_target="tpu_custom_call" | custom-call | tf_op jit(solution)/shard_map/enc_qkv/pallas_call | solution.py:300
  9.8 20.5 %enc_attention.1 = (bf16[1024,768]{1,0:T(8,128)(2,1)}, bf16[768,1024]{1,0:T(8,128)(2,1)}, f32[6,2,2,512]{3,2,1,0:T(2,128)}, f32[6,2,1024]{2,1,0:T(2,128)}) custom-call(s32[2]{0:T(128)} %lengths_ref.3, bf16[1024,768]{1,0:T(8,128)(2,1)} %get-tuple-element.121.q_ref, bf16[1024,768]{1,0:T(8,128)(2,1)} %get-tuple-element.122.k_ref, ...), custom_call_target="tpu_custom_call" | custom-call | tf_op jit(solution)/shard_map/enc_attention/pallas_call | solution.py:140
  30.3 25.8 %enc_post.1 = (f32[1024,768]{1,0:T(8,128)}, bf16[768,1024]{1,0:T(8,128)(2,1)}, bf16[3072,1024]{1,0:T(8,128)(2,1)}, bf16[1024,3072]{1,0:T(8,128)(2,1)}, f32[1024,...) custom-call(bf16[1024,768]{1,0:T(8,128)(2,1)} %x_ref.9, ...), custom_call_target="tpu_custom_call" | custom-call | tf_op jit(solution)/shard_map/enc_post/pallas_call | solution.py:349
  56.1 6.2 %dec_pre.1 = (bf16[48,768]{1,0:T(8,128)(2,1)}, bf16[48,768]{1,0:T(8,128)(2,1)}, bf16[48,768]{1,0:T(8,128)(2,1)}, bf16[48,768]{1,0:T(8,128)(2,1)}, f32[12,48,48]{...) custom-call(bf16[48,768]{1,0:T(8,128)(2,1)} %x_ref.8, ...), custom_call_target="tpu_custom_call" | custom-call | tf_op jit(solution)/shard_map/dec_pre/pallas_call | solution.py:740
  62.3 7.1 %cross_part.1 = (f32[8,6,768]{2,1,0:T(8,128)}, f32[8,6,128]{2,1,0:T(8,128)}) custom-call(s32[2]{0:T(128)} %question_ref.3, s32[2]{0:T(128)} %lengths_ref.3, bf16[48,768]{1,0:T(8,128)(2,1)} %get-tuple-element.126.q_ref, bf16[1024,768]{1,0:T(8,128)(2,1)} %get-tuple-element.127.ck_ref, bf16[1024,768]{1,0:T(8,128)(2,1)} %get-tuple-element.128.cv_ref), custom_call_target="tpu_custom_call" | custom-call | tf_op jit(solution)/shard_map/cross_part/pallas_call | solution.py:543
  69.4 0.0 copy-start
  69.4 0.9 copy-done
  70.3 0.0 copy-start.1
  70.3 0.8 copy-done.1
  71.0 17.7 %cross_merge.1 = f32[8,6,896]{2,1,0:T(8,128)S(1)} custom-call(f32[8,6,768]{2,1,0:T(8,128)S(1)} %copy-done, f32[8,6,128]{2,1,0:T(8,128)S(1)} %copy-done.1), custom_call_target="tpu_custom_call" | custom-call | tf_op jit(solution)/shard_map/cross_merge/pallas_call | solution.py:617
  88.8 0.7 reshape.59.merged_ref.att_ref.lse_ref
  89.5 10.6 %dec_mid.1 = (bf16[48,768]{1,0:T(8,128)(2,1)}, bf16[48,768]{1,0:T(8,128)(2,1)}, bf16[48,3072]{1,0:T(8,128)(2,1)}, bf16[48,3072]{1,0:T(8,128)(2,1)}, bf16[48,768]...) custom-call(f32[48,896]{1,0:T(8,128)} %reshape.59.merged_ref.att_ref.lse_ref, ...), custom_call_target="tpu_custom_call" | custom-call | tf_op jit(solution)/shard_map/dec_mid/pallas_call | solution.py:802
  100.1 0.0 copy-start.2
  100.1 0.0 copy-start.3
  100.1 0.0 copy-start.4
  100.1 0.0 copy-start.5
  100.1 8.3 %cross_back.1 = (f32[48,768]{1,0:T(8,128)}, bf16[2,1024,768]{2,1,0:T(8,128)(2,1)}) custom-call(s32[2]{0:T(128)} %question_ref.3, s32[2]{0:T(128)} %lengths_ref.3, bf16[48,768]{1,0:T(8,128)(2,1)} %get-tuple-element.126.q_ref, bf16[1024,768]{1,0:T(8,128)(2,1)} %get-tuple-element.127.ck_ref, bf16[1024,768]{1,0:T(8,128)(2,1)} %get-tuple-element.128.cv_ref, ...), custom_call_target="tpu_custom_call" | custom-call | tf_op jit(solution)/shard_map/cross_back/pallas_call | solution.py:672
  108.4 0.0 copy-done.2
  108.4 0.0 copy-done.3
  108.4 0.0 copy-done.4
  108.4 0.0 copy-done.5
  108.5 0.6 stack.34.table_ref
  109.1 30.9 %enc_post_back.1 = (bf16[1024,768]{1,0:T(8,128)(2,1)}, bf16[1024,3072]{1,0:T(8,128)(2,1)}, bf16[1024,768]{1,0:T(8,128)(2,1)}, f32[1024,768]{1,0:T(8,128)}, bf16[...) custom-call(bf16[2,1024,768]{2,1,0:T(8,128)(2,1)} %get-tuple-element.134.refs_0_.refs_1_, ...), custom_call_target="tpu_custom_call" | custom-call | tf_op jit(solution)/shard_map/enc_post_back/pallas_call | solution.py:1396
  140.0 11.0 %weight_grad.2 = (f32[16,96,768]{2,1,0:T(8,128)}, f32[16,96,768]{2,1,0:T(8,128)}) custom-call(s32[5,16]{1,0:T(8,128)} %stack.34.table_ref, bf16[3072,1024]{1,0:T(8,128)(2,1)} %get-tuple-element.149.turned_ref, bf16[1024,768]{1,0:T(8,128)(2,1)} %get-tuple-element.150.refs_0_), custom_call_target="tpu_custom_call" | custom-call | tf_op jit(solution)/shard_map/weight_grad/pallas_call | solution.py:464
  151.1 0.0 collective-permute-start.1
  151.1 8.5 %weight_grad.3 = (f32[16,24,1536]{2,1,0:T(8,128)}, f32[16,24,1536]{2,1,0:T(8,128)}) custom-call(s32[5,16]{1,0:T(8,128)} %stack.34.table_ref, bf16[768,1024]{1,0:T(8,128)(2,1)} %get-tuple-element.163.turned_ref, bf16[2,1024,768]{2,1,0:T(8,128)(2,1)} %get-tuple-element.134.refs_0_.refs_1_, bf16[2,1024,768]{2,1,0:T(8,128)(2,1)} %get-tuple-element.134.refs_0_.refs_1_), custom_call_target="tpu_custom_call" | custom-call | tf_op jit(solution)/shard_map/weight_grad/pallas_call | solution.py:464
  159.6 0.5 collective-permute-start
  160.1 7.5 %dec_post.1 = (bf16[48,768]{1,0:T(8,128)(2,1)}, bf16[48,768]{1,0:T(8,128)(2,1)}, bf16[48,768]{1,0:T(8,128)(2,1)}, bf16[48,768]{1,0:T(8,128)(2,1)}, f32[48,768]{1...) custom-call(f32[48,768]{1,0:T(8,128)} %get-tuple-element.143.gq_ref, ...), custom_call_target="tpu_custom_call" | custom-call | tf_op jit(solution)/shard_map/dec_post/pallas_call | solution.py:874
  167.6 0.6 pad_add_fusion.place_ref
  168.2 4.8 %dec_weight_grads.1 = (f32[2,336,768]{2,1,0:T(8,128)}, f32[2,336,768]{2,1,0:T(8,128)}) custom-call(s32[4]{0:T(128)} %pad_add_fusion.place_ref, bf16[48,768]{1,0:T(8,128)(2,1)} %get-tuple-element.165.low_ref, bf16[48,768]{1,0:T(8,128)(2,1)} %get-tuple-element.166.dq_ref, bf16[48,768]{1,0:T(8,128)(2,1)} %get-tuple-element.167.dk_ref, ...), custom_call_target="tpu_custom_call" | custom-call | tf_op jit(solution)/shard_map/dec_weight_grads/pallas_call | solution.py:937
  173.0 0.0 collective-permute-done.refs_13_
  173.0 0.0 collective-permute-done.1.refs_14_
  173.0 161.1 %enc_last.1 = (f32[1024,768]{1,0:T(8,128)}, f32[24,1024]{1,0:T(8,128)}, f32[24,1536]{1,0:T(8,128)}, f32[96,768]{1,0:T(8,128)}, f32[336,768]{1,0:T(8,128)}, /*ind...) custom-call(s32[2]{0:T(128)} %lengths_ref.3, ...), custom_call_target="tpu_custom_call" | custom-call | tf_op jit(solution)/shard_map/enc_last/pallas_call | solution.py:1633
  334.2 6.0 %finish.1 = (f32[24]{0:T(128)}, f32[24]{0:T(128)}, f32[24]{0:T(128)}, f32[24]{0:T(128)}, f32[24]{0:T(128)}, /*index=5*/f32[24]{0:T(128)}, f32[12]{0:T(128)}, f32...) custom-call(f32[24,1024]{1,0:T(8,128)} %get-tuple-element.180.small_, ...), custom_call_target="tpu_custom_call" | custom-call | tf_op jit(solution)/shard_map/finish/pallas_call | solution.py:1007
  (2 shorter events, 0.0 us)
Async XLA Ops:
  69.4 0.9 copy-start
  70.3 0.8 copy-start.1
  100.1 8.3 %copy-start.2 = (s32[16]{0:T(128)S(1)}, s32[16]{0:T(128)}, u32[]{:S(2)}) copy-start(s32[16]{0:T(128)} %constant.64) | copy-start | bytes 196
  100.1 8.3 %copy-start.3 = (s32[16]{0:T(128)S(1)}, s32[16]{0:T(128)}, u32[]{:S(2)}) copy-start(s32[16]{0:T(128)} %constant.63) | copy-start | bytes 196
  100.1 8.3 %copy-start.4 = (s32[16]{0:T(128)S(1)}, s32[16]{0:T(128)}, u32[]{:S(2)}) copy-start(s32[16]{0:T(128)} %constant.62) | copy-start | bytes 196
  100.1 8.3 %copy-start.5 = (s32[16]{0:T(128)S(1)}, s32[16]{0:T(128)}, u32[]{:S(2)}) copy-start(s32[16]{0:T(128)} %constant.61) | copy-start | bytes 196
  151.1 22.0 %collective-permute-start.1 = (f32[16,96,768]{2,1,0:T(8,128)}, f32[16,96,768]{2,1,0:T(8,128)}, u32[]{:S(2)}, u32[]{:S(2)}) collective-permute-start(f32[16,96,768]{2,1,0:T(8,128)} %get-tuple-element.178), channel_id=1, source_target_pairs={{0,8},{8,0},{16,24},{24,16},{1,9},{9,1},{17,25},{25,17},{2,10},{10... | collective-permute-start | bytes 14155784 | tf_op jit(solution)/shard_map/ppermute | solution.py:1726
  159.6 13.4 %collective-permute-start = (f32[16,24,1536]{2,1,0:T(8,128)}, f32[16,24,1536]{2,1,0:T(8,128)}, u32[]{:S(2)}, u32[]{:S(2)}) collective-permute-start(f32[16,24,1536]{2,1,0:T(8,128)} %get-tuple-element.177), channel_id=1, source_target_pairs={{0,8},{8,0},{16,24},{24,16},{1,9},{9,1},{17,25},{25,17},{2,10},{10... | collective-permute-start | bytes 7077896 | tf_op jit(solution)/shard_map/ppermute | solution.py:1726

commit v6 on v5

--- a/solution.py
+++ b/solution.py
@@ -1076,7 +1076,7 @@
         self.place, self.start, self.met = place, start, met
 
 
-DEPTH = 3
+DEPTH = 4
 
 
 def block_of(piece, shapes):

time: 342 us -> 345 us (level)
  no operation moved by 1% of the time
where the time goes in v6:
time: 345 us; the launch traced here: 343 us
  Pallas kernels  338 us (98%)
    pallas_call x1, Pallas kernels, last_part(): pl.pallas_call(functools.partial(last_kernel, exchange, everywhere, point...  164 us
    pallas_call x1, Pallas kernels, post_backward(): pl.pallas_call(functools.partial(back_host_kernel, adding, sizes), grid=(...  30.9 us
    pallas_call x1, Pallas kernels, post_forward(): pl.pallas_call(post_kernel, grid=(tokens // tile,), in_specs=[d, d] + [wh...  25.8 us
    pallas_call x1, Pallas kernels, attn_forward(): pl.pallas_call(attn_forward_kernel, grid_spec=pltpu.PrefetchScalarGridSpe...  20.5 us
    pallas_call x2, Pallas kernels, weight_grad(): pl.pallas_call(functools.partial(weight_grad_kernel, rows, pb, pa, tiles,...  19.6 us
    pallas_call x1, Pallas kernels, merge(): pl.pallas_call(functools.partial(merge_kernel, pa), in_specs=[vmem, vmem]...  17.7 us
    pallas_call x1, Pallas kernels, dec_mid_call(): pl.pallas_call(dec_mid_kernel, in_specs=[vmem] * 7, out_specs=[vmem] * le...  10.6 us
    pallas_call x1, Pallas kernels, cross_back(): pl.pallas_call(cross_back_kernel, grid=(HEADS // 2,), in_specs=[smem, sme...  8.28 us
  transfers between devices with their start and end apart: 2, of which 0 were waited for; matrix products, arithmetic and copies ran while one was open for 0% of the time, Pallas kernels for 6%

profile of v6, /device:TPU:0, one launch (start us, length us, event | category | flops | bytes accessed | tf_op | source)
XLA Modules:
  0.0 343.5 jit_solution(7299492724277086630)
XLA Ops:
  0.7 1.4 gains.1.gains_ref.refs_5_
  2.1 7.7 %enc_qkv.1 = (bf16[768,1024]{1,0:T(8,128)(2,1)}, bf16[1024,768]{1,0:T(8,128)(2,1)}, bf16[1024,768]{1,0:T(8,128)(2,1)}, bf16[1024,768]{1,0:T(8,128)(2,1)}) custom-call(bf16[1024,768]{1,0:T(8,128)(2,1)} %x_ref.9, f32[6,768]{1,0:T(8,128)} %gains.1.gains_ref.refs_5_, bf16[768,768]{1,0:T(8,128)(2,1)} %wq_ref.7, bf16[768,768]{1,0:T(8,128)(2,1)} %wk_ref.7, ...), custom_call_target="tpu_custom_call" | custom-call | tf_op jit(solution)/shard_map/enc_qkv/pallas_call | solution.py:300
  9.8 20.5 %enc_attention.1 = (bf16[1024,768]{1,0:T(8,128)(2,1)}, bf16[768,1024]{1,0:T(8,128)(2,1)}, f32[6,2,2,512]{3,2,1,0:T(2,128)}, f32[6,2,1024]{2,1,0:T(2,128)}) custom-call(s32[2]{0:T(128)} %lengths_ref.3, bf16[1024,768]{1,0:T(8,128)(2,1)} %get-tuple-element.121.q_ref, bf16[1024,768]{1,0:T(8,128)(2,1)} %get-tuple-element.122.k_ref, ...), custom_call_target="tpu_custom_call" | custom-call | tf_op jit(solution)/shard_map/enc_attention/pallas_call | solution.py:140
  30.3 25.8 %enc_post.1 = (f32[1024,768]{1,0:T(8,128)}, bf16[768,1024]{1,0:T(8,128)(2,1)}, bf16[3072,1024]{1,0:T(8,128)(2,1)}, bf16[1024,3072]{1,0:T(8,128)(2,1)}, f32[1024,...) custom-call(bf16[1024,768]{1,0:T(8,128)(2,1)} %x_ref.9, ...), custom_call_target="tpu_custom_call" | custom-call | tf_op jit(solution)/shard_map/enc_post/pallas_call | solution.py:349
  56.1 6.2 %dec_pre.1 = (bf16[48,768]{1,0:T(8,128)(2,1)}, bf16[48,768]{1,0:T(8,128)(2,1)}, bf16[48,768]{1,0:T(8,128)(2,1)}, bf16[48,768]{1,0:T(8,128)(2,1)}, f32[12,48,48]{...) custom-call(bf16[48,768]{1,0:T(8,128)(2,1)} %x_ref.8, ...), custom_call_target="tpu_custom_call" | custom-call | tf_op jit(solution)/shard_map/dec_pre/pallas_call | solution.py:740
  62.3 7.1 %cross_part.1 = (f32[8,6,768]{2,1,0:T(8,128)}, f32[8,6,128]{2,1,0:T(8,128)}) custom-call(s32[2]{0:T(128)} %question_ref.3, s32[2]{0:T(128)} %lengths_ref.3, bf16[48,768]{1,0:T(8,128)(2,1)} %get-tuple-element.126.q_ref, bf16[1024,768]{1,0:T(8,128)(2,1)} %get-tuple-element.127.ck_ref, bf16[1024,768]{1,0:T(8,128)(2,1)} %get-tuple-element.128.cv_ref), custom_call_target="tpu_custom_call" | custom-call | tf_op jit(solution)/shard_map/cross_part/pallas_call | solution.py:543
  69.4 0.0 copy-start
  69.4 0.9 copy-done
  70.3 0.0 copy-start.1
  70.3 0.8 copy-done.1
  71.0 17.7 %cross_merge.1 = f32[8,6,896]{2,1,0:T(8,128)S(1)} custom-call(f32[8,6,768]{2,1,0:T(8,128)S(1)} %copy-done, f32[8,6,128]{2,1,0:T(8,128)S(1)} %copy-done.1), custom_call_target="tpu_custom_call" | custom-call | tf_op jit(solution)/shard_map/cross_merge/pallas_call | solution.py:617
  88.8 0.7 reshape.59.merged_ref.att_ref.lse_ref
  89.5 10.6 %dec_mid.1 = (bf16[48,768]{1,0:T(8,128)(2,1)}, bf16[48,768]{1,0:T(8,128)(2,1)}, bf16[48,3072]{1,0:T(8,128)(2,1)}, bf16[48,3072]{1,0:T(8,128)(2,1)}, bf16[48,768]...) custom-call(f32[48,896]{1,0:T(8,128)} %reshape.59.merged_ref.att_ref.lse_ref, ...), custom_call_target="tpu_custom_call" | custom-call | tf_op jit(solution)/shard_map/dec_mid/pallas_call | solution.py:802
  100.1 0.0 copy-start.2
  100.1 0.0 copy-start.3
  100.1 0.0 copy-start.4
  100.1 0.0 copy-start.5
  100.1 8.3 %cross_back.1 = (f32[48,768]{1,0:T(8,128)}, bf16[2,1024,768]{2,1,0:T(8,128)(2,1)}) custom-call(s32[2]{0:T(128)} %question_ref.3, s32[2]{0:T(128)} %lengths_ref.3, bf16[48,768]{1,0:T(8,128)(2,1)} %get-tuple-element.126.q_ref, bf16[1024,768]{1,0:T(8,128)(2,1)} %get-tuple-element.127.ck_ref, bf16[1024,768]{1,0:T(8,128)(2,1)} %get-tuple-element.128.cv_ref, ...), custom_call_target="tpu_custom_call" | custom-call | tf_op jit(solution)/shard_map/cross_back/pallas_call | solution.py:672
  108.4 0.0 copy-done.2
  108.4 0.0 copy-done.3
  108.4 0.0 copy-done.4
  108.4 0.0 copy-done.5
  108.5 0.6 stack.34.table_ref
  109.1 30.9 %enc_post_back.1 = (bf16[1024,768]{1,0:T(8,128)(2,1)}, bf16[1024,3072]{1,0:T(8,128)(2,1)}, bf16[1024,768]{1,0:T(8,128)(2,1)}, f32[1024,768]{1,0:T(8,128)}, bf16[...) custom-call(bf16[2,1024,768]{2,1,0:T(8,128)(2,1)} %get-tuple-element.134.refs_0_.refs_1_, ...), custom_call_target="tpu_custom_call" | custom-call | tf_op jit(solution)/shard_map/enc_post_back/pallas_call | solution.py:1396
  140.0 11.0 %weight_grad.2 = (f32[16,96,768]{2,1,0:T(8,128)}, f32[16,96,768]{2,1,0:T(8,128)}) custom-call(s32[5,16]{1,0:T(8,128)} %stack.34.table_ref, bf16[3072,1024]{1,0:T(8,128)(2,1)} %get-tuple-element.149.turned_ref, bf16[1024,768]{1,0:T(8,128)(2,1)} %get-tuple-element.150.refs_0_), custom_call_target="tpu_custom_call" | custom-call | tf_op jit(solution)/shard_map/weight_grad/pallas_call | solution.py:464
  151.1 0.0 collective-permute-start.1
  151.1 8.5 %weight_grad.3 = (f32[16,24,1536]{2,1,0:T(8,128)}, f32[16,24,1536]{2,1,0:T(8,128)}) custom-call(s32[5,16]{1,0:T(8,128)} %stack.34.table_ref, bf16[768,1024]{1,0:T(8,128)(2,1)} %get-tuple-element.163.turned_ref, bf16[2,1024,768]{2,1,0:T(8,128)(2,1)} %get-tuple-element.134.refs_0_.refs_1_, bf16[2,1024,768]{2,1,0:T(8,128)(2,1)} %get-tuple-element.134.refs_0_.refs_1_), custom_call_target="tpu_custom_call" | custom-call | tf_op jit(solution)/shard_map/weight_grad/pallas_call | solution.py:464
  159.6 0.5 collective-permute-start
  160.1 7.5 %dec_post.1 = (bf16[48,768]{1,0:T(8,128)(2,1)}, bf16[48,768]{1,0:T(8,128)(2,1)}, bf16[48,768]{1,0:T(8,128)(2,1)}, bf16[48,768]{1,0:T(8,128)(2,1)}, f32[48,768]{1...) custom-call(f32[48,768]{1,0:T(8,128)} %get-tuple-element.143.gq_ref, ...), custom_call_target="tpu_custom_call" | custom-call | tf_op jit(solution)/shard_map/dec_post/pallas_call | solution.py:874
  167.6 0.6 pad_add_fusion.place_ref
  168.2 4.8 %dec_weight_grads.1 = (f32[2,336,768]{2,1,0:T(8,128)}, f32[2,336,768]{2,1,0:T(8,128)}) custom-call(s32[4]{0:T(128)} %pad_add_fusion.place_ref, bf16[48,768]{1,0:T(8,128)(2,1)} %get-tuple-element.165.low_ref, bf16[48,768]{1,0:T(8,128)(2,1)} %get-tuple-element.166.dq_ref, bf16[48,768]{1,0:T(8,128)(2,1)} %get-tuple-element.167.dk_ref, ...), custom_call_target="tpu_custom_call" | custom-call | tf_op jit(solution)/shard_map/dec_weight_grads/pallas_call | solution.py:937
  173.0 0.0 collective-permute-done.refs_13_
  173.0 0.0 collective-permute-done.1.refs_14_
  173.0 164.3 %enc_last.1 = (f32[1024,768]{1,0:T(8,128)}, f32[24,1024]{1,0:T(8,128)}, f32[24,1536]{1,0:T(8,128)}, f32[96,768]{1,0:T(8,128)}, f32[336,768]{1,0:T(8,128)}, /*ind...) custom-call(s32[2]{0:T(128)} %lengths_ref.3, ...), custom_call_target="tpu_custom_call" | custom-call | tf_op jit(solution)/shard_map/enc_last/pallas_call | solution.py:1633
  337.3 6.0 %finish.1 = (f32[24]{0:T(128)}, f32[24]{0:T(128)}, f32[24]{0:T(128)}, f32[24]{0:T(128)}, f32[24]{0:T(128)}, /*index=5*/f32[24]{0:T(128)}, f32[12]{0:T(128)}, f32...) custom-call(f32[24,1024]{1,0:T(8,128)} %get-tuple-element.180.small_, ...), custom_call_target="tpu_custom_call" | custom-call | tf_op jit(solution)/shard_map/finish/pallas_call | solution.py:1007
  (2 shorter events, 0.0 us)
Async XLA Ops:
  69.4 0.9 copy-start
  70.3 0.8 copy-start.1
  100.1 8.3 %copy-start.2 = (s32[16]{0:T(128)S(1)}, s32[16]{0:T(128)}, u32[]{:S(2)}) copy-start(s32[16]{0:T(128)} %constant.64) | copy-start | bytes 196
  100.1 8.3 %copy-start.3 = (s32[16]{0:T(128)S(1)}, s32[16]{0:T(128)}, u32[]{:S(2)}) copy-start(s32[16]{0:T(128)} %constant.63) | copy-start | bytes 196
  100.1 8.3 %copy-start.4 = (s32[16]{0:T(128)S(1)}, s32[16]{0:T(128)}, u32[]{:S(2)}) copy-start(s32[16]{0:T(128)} %constant.62) | copy-start | bytes 196
  100.1 8.3 %copy-start.5 = (s32[16]{0:T(128)S(1)}, s32[16]{0:T(128)}, u32[]{:S(2)}) copy-start(s32[16]{0:T(128)} %constant.61) | copy-start | bytes 196
  151.1 22.0 %collective-permute-start.1 = (f32[16,96,768]{2,1,0:T(8,128)}, f32[16,96,768]{2,1,0:T(8,128)}, u32[]{:S(2)}, u32[]{:S(2)}) collective-permute-start(f32[16,96,768]{2,1,0:T(8,128)} %get-tuple-element.178), channel_id=1, source_target_pairs={{0,8},{8,0},{16,24},{24,16},{1,9},{9,1},{17,25},{25,17},{2,10},{10... | collective-permute-start | bytes 14155784 | tf_op jit(solution)/shard_map/ppermute | solution.py:1726
  159.6 13.4 %collective-permute-start = (f32[16,24,1536]{2,1,0:T(8,128)}, f32[16,24,1536]{2,1,0:T(8,128)}, u32[]{:S(2)}, u32[]{:S(2)}) collective-permute-start(f32[16,24,1536]{2,1,0:T(8,128)} %get-tuple-element.177), channel_id=1, source_target_pairs={{0,8},{8,0},{16,24},{24,16},{1,9},{9,1},{17,25},{25,17},{2,10},{10... | collective-permute-start | bytes 7077896 | tf_op jit(solution)/shard_map/ppermute | solution.py:1726
